TPU v7x, 32 devices: a whole 2x2x4 slice. The times are simulated.
32 devices in a mesh: ctx: 16 (over z, y, core), fsdp: 2 (over x).
Axes of the slice: x: 2, y: 2, z: 4, core: 2. Of those that a mesh axis runs over, the one named last changes fastest.
Arguments:
- tokens: bfloat16 [4, 2048, 512], P('fsdp', 'ctx'), may hold values from -6 to 6
- encoder: bfloat16 [4, 512, 512], P('fsdp', 'ctx'), may hold values from -6 to 6
- step_ids: int32 [4], P('fsdp'), may hold values from 0 to 49
- out_grad: bfloat16 [4, 2048, 512], P('fsdp', 'ctx'), may hold values from -6 to 6
- self_in: bfloat16 [512, 1536], P('fsdp'), may hold values from -0.25 to 0.25
- self_out: bfloat16 [512, 512], P('fsdp'), may hold values from -6 to 6
- cross_query: bfloat16 [512, 512], P('fsdp'), may hold values from -0.25 to 0.25
- cross_keyval: bfloat16 [512, 1024], P('fsdp'), may hold values from -0.25 to 0.25
- cross_out: bfloat16 [512, 512], P('fsdp'), may hold values from -3.5 to 3.5
- ffn_up: bfloat16 [512, 2048], P('fsdp'), may hold values from -0.25 to 0.25
- up_bias: bfloat16 [2048], P('fsdp'), may hold values from -4 to 4
- ffn_down: bfloat16 [2048, 512], P('fsdp'), may hold values from -0.125 to 0.125
- down_bias: bfloat16 [512], P('fsdp'), may hold values from -4 to 4
- norm_gain: bfloat16 [3, 512], P(None, 'fsdp'), may hold values from 0.5 to 1.5
- norm_shift: bfloat16 [3, 512], P(None, 'fsdp'), may hold values from -4 to 4
- step_table: bfloat16 [50, 512], P(None, 'fsdp'), may hold values from -6 to 6
Outputs:
- mixed: bfloat16 [4, 2048, 512], P('fsdp', 'ctx')
- tokens_grad: float32 [4, 2048, 512], P('fsdp', 'ctx')
- encoder_grad: float32 [4, 512, 512], P('fsdp', 'ctx')
- self_in_grad: float32 [512, 1536], P('fsdp')
- self_out_grad: float32 [512, 512], P('fsdp')
- cross_query_grad: float32 [512, 512], P('fsdp')
- cross_keyval_grad: float32 [512, 1024], P('fsdp')
- cross_out_grad: float32 [512, 512], P('fsdp')
- ffn_up_grad: float32 [512, 2048], P('fsdp')
- up_bias_grad: float32 [2048], P('fsdp')
- ffn_down_grad: float32 [2048, 512], P('fsdp')
- down_bias_grad: float32 [512], P('fsdp')
- norm_gain_grad: float32 [3, 512], P(None, 'fsdp')
- norm_shift_grad: float32 [3, 512], P(None, 'fsdp')
- step_table_grad: float32 [50, 512], P(None, 'fsdp')
All inputs are finite; a program needn't handle non-finite values.
Results may differ from a plain program's by a relative error of at most 0.025.
Values may be sent and summed in bfloat16 or wider, within the bound.
No kernel may reach another device: no remote copies, remote signals or barrier semaphores. Data moves between devices by JAX's collectives and lax.ppermute only.
A program may use at most 192 MiB of HBM per device.

v0:
```python
import math

import jax
import jax.numpy as jnp
from jax import lax
from jax.sharding import PartitionSpec as P

H = 8


norm_epsilon = 1e-05
far_below = -1e30


def layer_norm(values, gain, shift):
    centre = jnp.mean(values, axis=-1, keepdims=True)
    centred = values - centre
    spread = jnp.mean(centred * centred, axis=-1, keepdims=True)
    return centred * lax.rsqrt(spread + norm_epsilon) * gain + shift


def matmul(left, right):
    return jnp.dot(left, right, preferred_element_type=jnp.float32)


def weight_grad(inputs, grads):
    return jnp.einsum("rd,re->de", inputs, grads, preferred_element_type=jnp.float32)


def input_grad(grads, weight):
    return jnp.einsum("re,de->rd", grads, weight, preferred_element_type=jnp.float32)


def key_block(count):
    return math.gcd(count, 512)


def scores_of(queries, keys, scale):
    return scale * jnp.einsum("qhd,khd->qhk", queries, keys, preferred_element_type=jnp.float32)


def whole_zeros(shard_part, split_dim, count):
    shape = list(shard_part.shape)
    shape[split_dim] = shape[split_dim] * count
    return jnp.zeros(tuple(shape), jnp.float32)


def forward_step(queries, scale, carry, piece):
    head_count = queries.shape[1]
    head_width = queries.shape[2]
    count = piece.shape[0]
    size = key_block(count)
    blocks = piece.reshape(count // size, size, 2, head_count, head_width)

    def forward_inner(state, block):
        summed, peak_score, totals = state
        scores = scores_of(queries, block[:, 0], scale)
        new_peak = jnp.maximum(peak_score, jnp.max(scores, axis=-1))
        decay = jnp.exp(peak_score - new_peak)
        shares = jnp.exp(scores - new_peak[..., None])
        totals = totals * decay + jnp.sum(shares, axis=-1)
        summed = summed * decay[..., None] + jnp.einsum(
            "qhk,khd->qhd",
            shares.astype(jnp.bfloat16),
            block[:, 1],
            preferred_element_type=jnp.float32,
        )
        return ((summed, new_peak, totals), None)

    result, unused = lax.scan(forward_inner, carry, blocks)
    return result


def query_grad_step(queries, grad_out, log_total, row_delta, scale, carry, piece):
    head_count = queries.shape[1]
    head_width = queries.shape[2]
    count = piece.shape[0]
    size = key_block(count)
    blocks = piece.reshape(count // size, size, 2, head_count, head_width)

    def query_inner(query_acc, block):
        scores = scores_of(queries, block[:, 0], scale)
        shares = jnp.exp(scores - log_total[..., None])
        share_grad = jnp.einsum(
            "qhd,khd->qhk", grad_out, block[:, 1], preferred_element_type=jnp.float32
        )
        score_grad = (shares * (share_grad - row_delta[..., None])).astype(jnp.bfloat16)
        query_acc = query_acc + scale * jnp.einsum(
            "qhk,khd->qhd", score_grad, block[:, 0], preferred_element_type=jnp.float32
        )
        return (query_acc, None)

    result, unused = lax.scan(query_inner, carry, blocks)
    return result


def key_grad_step(keyval, lse_all, delta_all, scale, carry, pieces):
    row_count = keyval.shape[0]
    head_count = lse_all.shape[1]
    head_width = keyval.shape[1] // (2 * head_count)
    owned = keyval.reshape(row_count, 2, head_count, head_width)
    own_keys = owned[:, 0]
    own_values = owned[:, 1]
    query_piece, grad_piece = pieces
    count = query_piece.shape[0]
    size = key_block(count)
    number = count // size
    lse_rows = lse_all.reshape(number, size, head_count)
    delta_rows = delta_all.reshape(number, size, head_count)
    blocks = (
        query_piece.reshape(number, size, head_count, head_width),
        grad_piece.reshape(number, size, head_count, head_width),
        lse_rows,
        delta_rows,
    )

    def key_inner(state, block):
        key_acc, value_acc = state
        query_rows, grad_rows, lse_block, delta_block = block
        scores = scores_of(query_rows, own_keys, scale)
        shares = jnp.exp(scores - lse_block[..., None])
        share_grad = jnp.einsum(
            "qhd,khd->qhk", grad_rows, own_values, preferred_element_type=jnp.float32
        )
        score_grad = (shares * (share_grad - delta_block[..., None])).astype(jnp.bfloat16)
        value_acc = value_acc + jnp.einsum(
            "qhk,qhd->khd",
            shares.astype(jnp.bfloat16),
            grad_rows,
            preferred_element_type=jnp.float32,
        )
        key_acc = key_acc + scale * jnp.einsum(
            "qhk,qhd->khd", score_grad, query_rows, preferred_element_type=jnp.float32
        )
        return ((key_acc, value_acc), None)

    result, unused = lax.scan(key_inner, carry, blocks)
    return result


def layer_pass(token_rows, enc_rows, step_index, grad_rows, weights):
    (
        weight_in,
        weight_out,
        weight_cross_query,
        weight_cross_kv,
        weight_cross_out,
        weight_up,
        bias_up,
        weight_down,
        bias_down,
        gain_rows,
        shift_rows,
        table_rows,
    ) = weights
    row_count, width = token_rows.shape
    head_width = width // H
    scale = 1.0 / math.sqrt(head_width)
    gains = gain_rows.astype(jnp.float32)
    shifts = shift_rows.astype(jnp.float32)
    onehot = (jnp.arange(table_rows.shape[0], dtype=jnp.int32) == step_index).astype(jnp.bfloat16)
    step_row = jnp.dot(onehot, table_rows, preferred_element_type=jnp.float32)
    start = token_rows.astype(jnp.float32) + step_row[None, :]
    normed0, back_norm0 = jax.vjp(layer_norm, start, gains[0], shifts[0])
    normed0_low = normed0.astype(jnp.bfloat16)
    joined = matmul(normed0_low, weight_in).astype(jnp.bfloat16)
    queries = joined[:, :width].reshape(row_count, H, head_width)
    keyval = joined[:, width:]
    initial = (
        jnp.zeros((row_count, H, head_width), jnp.float32),
        jnp.full((row_count, H), far_below, jnp.float32),
        jnp.zeros((row_count, H), jnp.float32),
    )
    summed, peak_score, share_total = forward_step(
        queries, scale, initial, lax.all_gather(keyval, "ctx", axis=0, tiled=True)
    )
    attended = summed / share_total[..., None]
    log_total = peak_score + jnp.log(share_total)
    attended_low = attended.reshape(row_count, width).astype(jnp.bfloat16)
    hidden1 = start + matmul(attended_low, weight_out)
    normed1, back_norm1 = jax.vjp(layer_norm, hidden1, gains[1], shifts[1])
    normed1_low = normed1.astype(jnp.bfloat16)
    cross_q = (
        matmul(normed1_low, weight_cross_query)
        .astype(jnp.bfloat16)
        .reshape(row_count, H, head_width)
    )
    cross_local = matmul(enc_rows, weight_cross_kv).astype(jnp.bfloat16)
    cross_kv = lax.all_gather(cross_local, "ctx", axis=0, tiled=True)
    enc_count = cross_kv.shape[0]
    cross_keys = cross_kv[:, :width].reshape(enc_count, H, head_width)
    cross_values = cross_kv[:, width:].reshape(enc_count, H, head_width)
    cross_scores = scores_of(cross_q, cross_keys, scale)
    cross_peak = jnp.max(cross_scores, axis=-1, keepdims=True)
    cross_exp = jnp.exp(cross_scores - cross_peak)
    cross_shares = cross_exp / jnp.sum(cross_exp, axis=-1, keepdims=True)
    cross_shares_low = cross_shares.astype(jnp.bfloat16)
    crossed = jnp.einsum(
        "qhk,khd->qhd", cross_shares_low, cross_values, preferred_element_type=jnp.float32
    )
    crossed_low = crossed.reshape(row_count, width).astype(jnp.bfloat16)
    hidden2 = hidden1 + matmul(crossed_low, weight_cross_out)
    normed2, back_norm2 = jax.vjp(layer_norm, hidden2, gains[2], shifts[2])
    normed2_low = normed2.astype(jnp.bfloat16)
    pre_act = matmul(normed2_low, weight_up) + bias_up.astype(jnp.float32)
    activated, back_act = jax.vjp(jax.nn.gelu, pre_act)
    act_low = activated.astype(jnp.bfloat16)
    mixed = hidden2 + matmul(act_low, weight_down) + bias_down.astype(jnp.float32)
    grad_top = grad_rows.astype(jnp.float32)
    down_grad = weight_grad(act_low, grad_rows)
    down_bias_grad = jnp.sum(grad_top, axis=0)
    (pre_grad,) = back_act(input_grad(grad_rows, weight_down))
    pre_low = pre_grad.astype(jnp.bfloat16)
    up_grad = weight_grad(normed2_low, pre_low)
    up_bias_grad = jnp.sum(pre_low.astype(jnp.float32), axis=0)
    hidden2_part, gain2_grad, shift2_grad = back_norm2(input_grad(pre_low, weight_up))
    hidden2_grad = grad_top + hidden2_part
    hidden2_low = hidden2_grad.astype(jnp.bfloat16)
    cross_out_grad = weight_grad(crossed_low, hidden2_low)
    crossed_grad = (
        input_grad(hidden2_low, weight_cross_out)
        .astype(jnp.bfloat16)
        .reshape(row_count, H, head_width)
    )
    share_grad = jnp.einsum(
        "qhd,khd->qhk", crossed_grad, cross_values, preferred_element_type=jnp.float32
    )
    share_mean = jnp.sum(cross_shares * share_grad, axis=-1, keepdims=True)
    cross_score_grad = (cross_shares * (share_grad - share_mean)).astype(jnp.bfloat16)
    cross_q_grad = (
        (
            scale
            * jnp.einsum(
                "qhk,khd->qhd", cross_score_grad, cross_keys, preferred_element_type=jnp.float32
            )
        )
        .astype(jnp.bfloat16)
        .reshape(row_count, width)
    )
    cross_key_part = scale * jnp.einsum(
        "qhk,qhd->khd", cross_score_grad, cross_q, preferred_element_type=jnp.float32
    )
    cross_value_part = jnp.einsum(
        "qhk,qhd->khd", cross_shares_low, crossed_grad, preferred_element_type=jnp.float32
    )
    cross_kv_part = jnp.concatenate(
        [cross_key_part.reshape(enc_count, width), cross_value_part.reshape(enc_count, width)],
        axis=1,
    )
    cross_kv_grad = lax.psum_scatter(
        cross_kv_part.astype(jnp.bfloat16), "ctx", scatter_dimension=0, tiled=True
    )
    cross_keyval_grad = weight_grad(enc_rows, cross_kv_grad)
    enc_grad = input_grad(cross_kv_grad, weight_cross_kv)
    cross_query_grad = weight_grad(normed1_low, cross_q_grad)
    hidden1_part, gain1_grad, shift1_grad = back_norm1(input_grad(cross_q_grad, weight_cross_query))
    hidden1_grad = hidden2_grad + hidden1_part
    hidden1_low = hidden1_grad.astype(jnp.bfloat16)
    self_out_grad = weight_grad(attended_low, hidden1_low)
    attended_grad = input_grad(hidden1_low, weight_out).astype(jnp.bfloat16)
    attended_heads = attended_grad.reshape(row_count, H, head_width)
    row_delta = jnp.sum(attended_heads.astype(jnp.float32) * attended, axis=-1)
    gathered_stats = (
        lax.all_gather(log_total, "ctx", axis=0, tiled=True),
        lax.all_gather(row_delta, "ctx", axis=0, tiled=True),
    )
    query_acc = query_grad_step(
        queries,
        attended_heads,
        log_total,
        row_delta,
        scale,
        jnp.zeros((row_count, H, head_width), jnp.float32),
        lax.all_gather(keyval, "ctx", axis=0, tiled=True),
    )
    blank = jnp.zeros((row_count, H, head_width), jnp.float32)
    key_acc, value_acc = key_grad_step(
        keyval,
        gathered_stats[0],
        gathered_stats[1],
        scale,
        (blank, blank),
        (
            lax.all_gather(joined[:, :width], "ctx", axis=0, tiled=True),
            lax.all_gather(attended_grad, "ctx", axis=0, tiled=True),
        ),
    )
    query_part = query_acc.reshape(row_count, width)
    key_part = key_acc.reshape(row_count, width)
    value_part = value_acc.reshape(row_count, width)
    joined_grad = jnp.concatenate([query_part, key_part, value_part], axis=1).astype(jnp.bfloat16)
    self_in_grad = weight_grad(normed0_low, joined_grad)
    start_part, gain0_grad, shift0_grad = back_norm0(input_grad(joined_grad, weight_in))
    start_grad = hidden1_grad + start_part
    table_grad = onehot.astype(jnp.float32)[:, None] * jnp.sum(start_grad, axis=0)[None, :]
    fresh = (
        self_in_grad,
        self_out_grad,
        cross_query_grad,
        cross_keyval_grad,
        cross_out_grad,
        up_grad,
        up_bias_grad,
        down_grad,
        down_bias_grad,
        jnp.stack([gain0_grad, gain1_grad, gain2_grad]),
        jnp.stack([shift0_grad, shift1_grad, shift2_grad]),
        table_grad,
    )
    return (fresh, (mixed.astype(jnp.bfloat16), start_grad, enc_grad))


def shards(
    tokens,
    encoder,
    step_ids,
    out_grad,
    self_in,
    self_out,
    cross_query,
    cross_keyval,
    cross_out,
    ffn_up,
    up_bias,
    ffn_down,
    down_bias,
    norm_gain,
    norm_shift,
    step_table,
):
    shard_list = (
        self_in,
        self_out,
        cross_query,
        cross_keyval,
        cross_out,
        ffn_up,
        up_bias,
        ffn_down,
        down_bias,
        norm_gain,
        norm_shift,
        step_table,
    )
    split_dims = (0, 0, 0, 0, 0, 0, 0, 0, 0, 1, 1, 1)
    fsdp_count = lax.axis_size("fsdp")
    zero_grads = tuple(
        (
            whole_zeros(shard_part, split_dim, fsdp_count)
            for shard_part, split_dim in zip(shard_list, split_dims)
        )
    )

    def micro_batch(totals, inputs):
        token_rows, enc_rows, step_index, grad_rows = inputs
        weights = (
            lax.all_gather(self_in, "fsdp", axis=0, tiled=True),
            lax.all_gather(self_out, "fsdp", axis=0, tiled=True),
            lax.all_gather(cross_query, "fsdp", axis=0, tiled=True),
            lax.all_gather(cross_keyval, "fsdp", axis=0, tiled=True),
            lax.all_gather(cross_out, "fsdp", axis=0, tiled=True),
            lax.all_gather(ffn_up, "fsdp", axis=0, tiled=True),
            lax.all_gather(up_bias, "fsdp", axis=0, tiled=True),
            lax.all_gather(ffn_down, "fsdp", axis=0, tiled=True),
            lax.all_gather(down_bias, "fsdp", axis=0, tiled=True),
            lax.all_gather(norm_gain, "fsdp", axis=1, tiled=True),
            lax.all_gather(norm_shift, "fsdp", axis=1, tiled=True),
            lax.all_gather(step_table, "fsdp", axis=1, tiled=True),
        )
        fresh, outputs = layer_pass(token_rows, enc_rows, step_index, grad_rows, weights)
        totals = jax.tree.map(jnp.add, totals, fresh)
        return (totals, outputs)

    totals, results = lax.scan(micro_batch, zero_grads, (tokens, encoder, step_ids, out_grad))
    mixed, tokens_grad, encoder_grad = results
    owned = (
        lax.psum_scatter(
            totals[0].astype(jnp.bfloat16), "fsdp", scatter_dimension=0, tiled=True
        ).astype(jnp.float32),
        lax.psum_scatter(
            totals[1].astype(jnp.bfloat16), "fsdp", scatter_dimension=0, tiled=True
        ).astype(jnp.float32),
        lax.psum_scatter(
            totals[2].astype(jnp.bfloat16), "fsdp", scatter_dimension=0, tiled=True
        ).astype(jnp.float32),
        lax.psum_scatter(
            totals[3].astype(jnp.bfloat16), "fsdp", scatter_dimension=0, tiled=True
        ).astype(jnp.float32),
        lax.psum_scatter(
            totals[4].astype(jnp.bfloat16), "fsdp", scatter_dimension=0, tiled=True
        ).astype(jnp.float32),
        lax.psum_scatter(
            totals[5].astype(jnp.bfloat16), "fsdp", scatter_dimension=0, tiled=True
        ).astype(jnp.float32),
        lax.psum_scatter(
            totals[6].astype(jnp.bfloat16), "fsdp", scatter_dimension=0, tiled=True
        ).astype(jnp.float32),
        lax.psum_scatter(
            totals[7].astype(jnp.bfloat16), "fsdp", scatter_dimension=0, tiled=True
        ).astype(jnp.float32),
        lax.psum_scatter(
            totals[8].astype(jnp.bfloat16), "fsdp", scatter_dimension=0, tiled=True
        ).astype(jnp.float32),
        lax.psum_scatter(
            totals[9].astype(jnp.bfloat16), "fsdp", scatter_dimension=1, tiled=True
        ).astype(jnp.float32),
        lax.psum_scatter(
            totals[10].astype(jnp.bfloat16), "fsdp", scatter_dimension=1, tiled=True
        ).astype(jnp.float32),
        lax.psum_scatter(
            totals[11].astype(jnp.bfloat16), "fsdp", scatter_dimension=1, tiled=True
        ).astype(jnp.float32),
    )
    finals = (
        lax.psum(owned[0].astype(jnp.bfloat16), "ctx").astype(jnp.float32),
        lax.psum(owned[1].astype(jnp.bfloat16), "ctx").astype(jnp.float32),
        lax.psum(owned[2].astype(jnp.bfloat16), "ctx").astype(jnp.float32),
        lax.psum(owned[3].astype(jnp.bfloat16), "ctx").astype(jnp.float32),
        lax.psum(owned[4].astype(jnp.bfloat16), "ctx").astype(jnp.float32),
        lax.psum(owned[5].astype(jnp.bfloat16), "ctx").astype(jnp.float32),
        lax.psum(owned[6].astype(jnp.bfloat16), "ctx").astype(jnp.float32),
        lax.psum(owned[7].astype(jnp.bfloat16), "ctx").astype(jnp.float32),
        lax.psum(owned[8].astype(jnp.bfloat16), "ctx").astype(jnp.float32),
        lax.psum(owned[9].astype(jnp.bfloat16), "ctx").astype(jnp.float32),
        lax.psum(owned[10].astype(jnp.bfloat16), "ctx").astype(jnp.float32),
        lax.psum(owned[11].astype(jnp.bfloat16), "ctx").astype(jnp.float32),
    )
    return (
        mixed,
        tokens_grad,
        encoder_grad,
        finals[0],
        finals[1],
        finals[2],
        finals[3],
        finals[4],
        finals[5],
        finals[6],
        finals[7],
        finals[8],
        finals[9],
        finals[10],
        finals[11],
    )


def solution(mesh):
    in_specs = (
        P("fsdp", "ctx", None),
        P("fsdp", "ctx", None),
        P("fsdp"),
        P("fsdp", "ctx", None),
        P("fsdp", None),
        P("fsdp", None),
        P("fsdp", None),
        P("fsdp", None),
        P("fsdp", None),
        P("fsdp", None),
        P("fsdp"),
        P("fsdp", None),
        P("fsdp"),
        P(None, "fsdp"),
        P(None, "fsdp"),
        P(None, "fsdp"),
    )
    out_specs = (
        P("fsdp", "ctx", None),
        P("fsdp", "ctx", None),
        P("fsdp", "ctx", None),
        P("fsdp", None),
        P("fsdp", None),
        P("fsdp", None),
        P("fsdp", None),
        P("fsdp", None),
        P("fsdp", None),
        P("fsdp"),
        P("fsdp", None),
        P("fsdp"),
        P(None, "fsdp"),
        P(None, "fsdp"),
        P(None, "fsdp"),
    )
    return jax.shard_map(shards, mesh=mesh, in_specs=in_specs, out_specs=out_specs, check_vma=False)
```

profile of v0, /device:TPU:0, one launch (start us, length us, event | category | flops | bytes accessed | tf_op | source)
XLA Modules:
  0.0 1188.9 jit_solution(17851124461466329279)
XLA Ops:
  8.2 834.6 %while.122 = (s32[]{:T(128)}, f32[512,1536]{1,0:T(8,128)}, f32[512,512]{1,0:T(8,128)}, f32[512,512]{1,0:T(8,128)}, f32[512,1024]{1,0:T(8,128)}, /*index=5*/f32[5...) while((s32[]{:T(128)}, f32[512,1536]{1,0:T(8,128)}, ...), condition=%wide.region_35.36_spmd.clone, body=%wide.region_0.35_spmd.clone.sunk | while | flops 3978741760 | bytes 400288224 | solution.py:374
  9.8 24.9 %all-gather.19.cloned.1.call-done = bf16[512,1024]{1,0:T(8,128)(2,1)} async-done(((bf16[256,1024]{1,0:T(8,128)(2,1)}), bf16[512,1024]{1,0:T(8,128)(2,1)}) %all-gather.19.cloned.1.call-update) | async-done | bytes 1048592 | tf_op jit(solution)/shard_map/while/body/eval_jaxpr/all_gather | solution.py:360
  53.6 10.4 all-gather.13.cloned.1.call-done
  70.1 8.8 all_gather.150
  79.0 7.9 all_gather.153
  86.9 7.1 all_gather.154
  108.1 39.6 %all-gather.15.cloned.1.call-done = bf16[2048,512]{1,0:T(8,128)(2,1)} async-done(((bf16[128,512]{1,0:T(8,128)(2,1)}), bf16[2048,512]{1,0:T(8,128)(2,1)}) %all-gather.15.cloned.1.call-update) | async-done | bytes 2097168 | tf_op jit(solution)/shard_map/while/body/eval_jaxpr/all_gather | solution.py:284
  147.7 6.2 reshape.334
  159.4 40.5 %all-gather.17.cloned.1.call-done = bf16[2048,1024]{1,0:T(8,128)(2,1)} async-done(((bf16[128,1024]{1,0:T(8,128)(2,1)}), bf16[2048,1024]{1,0:T(8,128)(2,1)}) %all-gather.17.cloned.1.call-update) | async-done | bytes 4194320 | tf_op jit(solution)/shard_map/while/body/eval_jaxpr/all_gather | solution.py:274
  199.8 11.7 reshape.335
  211.5 9.7 copy.126
  221.2 11.3 while.123
  244.0 23.6 %all-gather.25.cloned.1.call-done = bf16[2048,512]{1,0:T(8,128)(2,1)} async-done(((bf16[1024,512]{1,0:T(8,128)(2,1)}), bf16[2048,512]{1,0:T(8,128)(2,1)}) %all-gather.25.cloned.1.call-update) | async-done | bytes 2097168 | tf_op jit(solution)/shard_map/while/body/eval_jaxpr/all_gather | solution.py:364
  285.8 18.2 %while.125 = (s32[]{:T(128)}, f32[128,8,64]{0,2,1:T(8,128)}, bf16[4,512,2,8,64]{1,4,3,2,0:T(8,128)(2,1)}, bf16[128,8,64]{0,2,1:T(8,128)(2,1)S(1)}, f32[128,8]{0,...) while((s32[]{:T(128)}, f32[128,8,64]{0,2,1:T(8,128)}, ...), condition=%wide.region_20.20_spmd.clone, body=%wide.region_19.19_spmd.clone.sunk | while | flops 204144640 | bytes 8691875 | solution.py:93
  305.7 23.1 %all_gather.159 = f32[2048,8]{0,1:T(8,128)} all-gather(f32[128,8]{0,1:T(8,128)} %get-tuple-element.1771), channel_id=1, replica_groups=mesh['ctx'=16,'fsdp'=2] {'ctx'}, dimensions={0}, use_global_device_ids=true | all-gather | bytes 69632 | tf_op jit(solution)/shard_map/while/body/eval_jaxpr/all_gather | solution.py:265
  328.8 19.3 %all_gather.149 = f32[2048,8]{0,1:T(8,128)} all-gather(f32[128,8]{0,1:T(8,128)} %get-tuple-element.1772), channel_id=1, replica_groups=mesh['ctx'=16,'fsdp'=2] {'ctx'}, dimensions={0}, use_global_device_ids=true | all-gather | bytes 69632 | tf_op jit(solution)/shard_map/while/body/eval_jaxpr/all_gather | solution.py:264
  368.3 12.6 %all-gather.27.cloned.1.call-done = bf16[2048,512]{1,0:T(8,128)(2,1)} async-done(((bf16[128,512]{1,0:T(8,128)(2,1)}), bf16[2048,512]{1,0:T(8,128)(2,1)}) %all-gather.27.cloned.1.call-update) | async-done | bytes 2097168 | tf_op jit(solution)/shard_map/while/body/eval_jaxpr/all_gather | solution.py:285
  380.9 6.2 reshape.336
  387.1 5.5 copy.132
  392.6 28.8 %while.124 = (s32[]{:T(128)}, f32[128,8,64]{0,2,1:T(8,128)S(1)}, f32[128,8,64]{0,2,1:T(8,128)S(1)}, bf16[4,512,8,64]{1,3,2,0:T(8,128)(2,1)}, bf16[128,8,64]{0,2,...) while((s32[]{:T(128)}, f32[128,8,64]{0,2,1:T(8,128)S(1)}, ...), condition=%wide.region_22.22_spmd.clone, body=%wide.region_21.21_spmd.clone.sunk | while | flops 272957440 | bytes 9816188 | solution.py:137
  429.1 20.9 %all-gather.19.cloned.1.call-done = bf16[512,1024]{1,0:T(8,128)(2,1)} async-done(((bf16[256,1024]{1,0:T(8,128)(2,1)}), bf16[512,1024]{1,0:T(8,128)(2,1)}) %all-gather.19.cloned.1.call-update) | async-done | bytes 1048592 | tf_op jit(solution)/shard_map/while/body/eval_jaxpr/all_gather | solution.py:360
  469.0 10.5 all-gather.13.cloned.1.call-done
  485.4 8.8 all_gather.150
  494.2 7.9 all_gather.153
  502.1 7.1 all_gather.154
  523.4 39.7 %all-gather.15.cloned.1.call-done = bf16[2048,512]{1,0:T(8,128)(2,1)} async-done(((bf16[128,512]{1,0:T(8,128)(2,1)}), bf16[2048,512]{1,0:T(8,128)(2,1)}) %all-gather.15.cloned.1.call-update) | async-done | bytes 2097168 | tf_op jit(solution)/shard_map/while/body/eval_jaxpr/all_gather | solution.py:284
  563.1 6.2 reshape.334
  574.7 40.3 %all-gather.17.cloned.1.call-done = bf16[2048,1024]{1,0:T(8,128)(2,1)} async-done(((bf16[128,1024]{1,0:T(8,128)(2,1)}), bf16[2048,1024]{1,0:T(8,128)(2,1)}) %all-gather.17.cloned.1.call-update) | async-done | bytes 4194320 | tf_op jit(solution)/shard_map/while/body/eval_jaxpr/all_gather | solution.py:274
  615.0 11.7 reshape.335
  626.7 9.7 copy.126
  636.5 11.3 while.123
  659.2 23.4 %all-gather.25.cloned.1.call-done = bf16[2048,512]{1,0:T(8,128)(2,1)} async-done(((bf16[1024,512]{1,0:T(8,128)(2,1)}), bf16[2048,512]{1,0:T(8,128)(2,1)}) %all-gather.25.cloned.1.call-update) | async-done | bytes 2097168 | tf_op jit(solution)/shard_map/while/body/eval_jaxpr/all_gather | solution.py:364
  700.8 18.2 %while.125 = (s32[]{:T(128)}, f32[128,8,64]{0,2,1:T(8,128)}, bf16[4,512,2,8,64]{1,4,3,2,0:T(8,128)(2,1)}, bf16[128,8,64]{0,2,1:T(8,128)(2,1)S(1)}, f32[128,8]{0,...) while((s32[]{:T(128)}, f32[128,8,64]{0,2,1:T(8,128)}, ...), condition=%wide.region_20.20_spmd.clone, body=%wide.region_19.19_spmd.clone.sunk | while | flops 204144640 | bytes 8691875 | solution.py:93
  720.8 23.1 %all_gather.159 = f32[2048,8]{0,1:T(8,128)} all-gather(f32[128,8]{0,1:T(8,128)} %get-tuple-element.1771), channel_id=1, replica_groups=mesh['ctx'=16,'fsdp'=2] {'ctx'}, dimensions={0}, use_global_device_ids=true | all-gather | bytes 69632 | tf_op jit(solution)/shard_map/while/body/eval_jaxpr/all_gather | solution.py:265
  743.9 19.3 %all_gather.149 = f32[2048,8]{0,1:T(8,128)} all-gather(f32[128,8]{0,1:T(8,128)} %get-tuple-element.1772), channel_id=1, replica_groups=mesh['ctx'=16,'fsdp'=2] {'ctx'}, dimensions={0}, use_global_device_ids=true | all-gather | bytes 69632 | tf_op jit(solution)/shard_map/while/body/eval_jaxpr/all_gather | solution.py:264
  786.9 9.1 all-gather.27.cloned.1.call-done
  796.0 6.2 reshape.336
  807.7 28.8 %while.124 = (s32[]{:T(128)}, f32[128,8,64]{0,2,1:T(8,128)S(1)}, f32[128,8,64]{0,2,1:T(8,128)S(1)}, bf16[4,512,8,64]{1,3,2,0:T(8,128)(2,1)}, bf16[128,8,64]{0,2,...) while((s32[]{:T(128)}, f32[128,8,64]{0,2,1:T(8,128)S(1)}, ...), condition=%wide.region_22.22_spmd.clone, body=%wide.region_21.21_spmd.clone.sunk | while | flops 272957440 | bytes 9816188 | solution.py:137
  862.4 14.2 %reduce-scatter.24.cloned.1.call-done = bf16[256,512]{1,0:T(8,128)(2,1)} async-done(((bf16[512,512]{1,0:T(8,128)(2,1)}), bf16[256,512]{1,0:T(8,128)(2,1)}) %reduce-scatter.24.cloned.1.call-update) | async-done | bytes 262160 | tf_op jit(solution)/shard_map/reduce_scatter | solution.py:383
  876.6 17.2 %reduce-scatter.28.cloned.1.call-done = bf16[256,512]{1,0:T(8,128)(2,1)} async-done(((bf16[512,512]{1,0:T(8,128)(2,1)}), bf16[256,512]{1,0:T(8,128)(2,1)}) %reduce-scatter.28.cloned.1.call-update) | async-done | bytes 262160 | tf_op jit(solution)/shard_map/reduce_scatter | solution.py:389
  893.8 23.2 %reduce-scatter.26.cloned.1.call-done = bf16[256,1024]{1,0:T(8,128)(2,1)} async-done(((bf16[512,1024]{1,0:T(8,128)(2,1)}), bf16[256,1024]{1,0:T(8,128)(2,1)}) %reduce-scatter.26.cloned.1.call-update) | async-done | bytes 524304 | tf_op jit(solution)/shard_map/reduce_scatter | solution.py:386
  917.0 28.8 %reduce-scatter.20.cloned.1.call-done = bf16[256,1536]{1,0:T(8,128)(2,1)} async-done(((bf16[512,1536]{1,0:T(8,128)(2,1)}), bf16[256,1536]{1,0:T(8,128)(2,1)}) %reduce-scatter.20.cloned.1.call-update) | async-done | bytes 786448 | tf_op jit(solution)/shard_map/reduce_scatter | solution.py:377
  945.8 34.7 %reduce-scatter.30.cloned.1.call-done = bf16[256,2048]{1,0:T(8,128)(2,1)} async-done(((bf16[512,2048]{1,0:T(8,128)(2,1)}), bf16[256,2048]{1,0:T(8,128)(2,1)}) %reduce-scatter.30.cloned.1.call-update) | async-done | bytes 1048592 | tf_op jit(solution)/shard_map/reduce_scatter | solution.py:392
  980.5 34.5 %reduce-scatter.32.cloned.1.call-done = bf16[1024,512]{1,0:T(8,128)(2,1)} async-done(((bf16[2048,512]{1,0:T(8,128)(2,1)}), bf16[1024,512]{1,0:T(8,128)(2,1)}) %reduce-scatter.32.cloned.1.call-update) | async-done | bytes 1048592 | tf_op jit(solution)/shard_map/reduce_scatter | solution.py:398
  1028.2 11.5 reduce-scatter.38.cloned.1.call-done
  1040.6 11.8 reduce-scatter.34.cloned.1.call-done
  1052.5 62.2 %all-reduce.2 = (bf16[1024]{0:T(1024)(128)(2,1)S(1)}, bf16[256]{0:T(256)(128)(2,1)S(1)}, bf16[3,256]{1,0:T(4,128)(2,1)S(1)}, bf16[3,256]{1,0:T(4,128)(2,1)S(1)}, bf16[50,256]{1,0:T(8,128)(2,1)S(1)}) all-reduce(bf16[1024]{0:T(1024)(128)(2,1)S(1)} %dynamic-slice.1, ...), channel_id=1, replica_groups=mesh['ctx'=16,'fsdp'=2] {'ctx'}, use_global_device_ids=true, to_apply=%region_49.50 | all-reduce | flops 15616 | bytes 62464 | tf_op jit(solution)/shard_map/psum | solution.py:421
  1117.7 54.1 %all-reduce.7.cloned.1.call-done = (bf16[256,1536]{1,0:T(8,128)(2,1)}, bf16[256,512]{1,0:T(8,128)(2,1)}, bf16[256,512]{1,0:T(8,128)(2,1)}, bf16[256,1024]{1,0:T(...) async-done(((bf16[256,1536]{1,0:T(8,128)(2,1)}, bf16[256,512]{1,0:T(8,128)(2,1)}, bf16[256,512]{1,0:T(8,128)(2,1)}, ...) | async-done | bytes 4194320 | tf_op jit(solution)/shard_map/psum | solution.py:415
  (928 shorter events, 373.9 us)
Async XLA Ops:
  8.2 33.6 %copy-start.108 = (bf16[3,256]{1,0:T(4,128)(2,1)S(1)}, bf16[3,256]{1,0:T(4,128)(2,1)}, u32[]{:S(2)}) copy-start(bf16[3,256]{1,0:T(4,128)(2,1)} %get-tuple-element.1658) | copy-start | bytes 4612 | tf_op jit(solution)/shard_map/while
  8.2 37.9 %copy-start.65 = (bf16[50,256]{1,0:T(8,128)(2,1)S(1)}, bf16[50,256]{1,0:T(8,128)(2,1)}, u32[]{:S(2)}) copy-start(bf16[50,256]{1,0:T(8,128)(2,1)} %get-tuple-element.1656) | copy-start | bytes 76804 | tf_op jit(solution)/shard_map/while
  8.2 43.8 %copy-start.20 = (bf16[2,128,512]{2,1,0:T(8,128)(2,1)S(1)}, bf16[2,128,512]{2,1,0:T(8,128)(2,1)}, u32[]{:S(2)}) copy-start(bf16[2,128,512]{2,1,0:T(8,128)(2,1)} %get-tuple-element.1654) | copy-start | bytes 786436 | tf_op jit(solution)/shard_map/while
  8.2 26.4 %all-gather.19.cloned.1.call-start = ((), (), s32[]{:S(2)}) async-start(), calls=%async_computation.25 | async-start | bytes 1572864 | tf_op jit(solution)/shard_map/while/body/eval_jaxpr/all_gather | solution.py:360
  9.0 55.1 %all-gather.13.cloned.1.call-start = ((), (), s32[]{:S(2)}) async-start(), calls=%async_computation.22 | async-start | bytes 2359296 | tf_op jit(solution)/shard_map/while/body/eval_jaxpr/all_gather | solution.py:357
  9.7 95.1 %all-gather.21.cloned.1.call-start = ((), (), s32[]{:S(2)}) async-start(), calls=%async_computation.26 | async-start | bytes 1114112 | tf_op jit(solution)/shard_map/while/body/eval_jaxpr/all_gather | solution.py:189
  36.8 110.9 %all-gather.15.cloned.1.call-start = ((), (), s32[]{:S(2)}) async-start(), calls=%async_computation.23 | async-start | bytes 2228224 | tf_op jit(solution)/shard_map/while/body/eval_jaxpr/all_gather | solution.py:284
  66.6 133.2 %all-gather.17.cloned.1.call-start = ((), (), s32[]{:S(2)}) async-start(), calls=%async_computation.24 | async-start | bytes 4456448 | tf_op jit(solution)/shard_map/while/body/eval_jaxpr/all_gather | solution.py:274
  67.4 173.1 %all-gather.23.cloned.1.call-start = ((), (), s32[]{:S(2)}) async-start(), calls=%async_computation.27 | async-start | bytes 3145728 | tf_op jit(solution)/shard_map/while/body/eval_jaxpr/all_gather | solution.py:362
  67.5 31.5 %copy-start.126 = (bf16[256]{0:T(256)(128)(2,1)S(1)}, bf16[256]{0:T(256)(128)(2,1)}, u32[]{:S(2)}) copy-start(bf16[256]{0:T(256)(128)(2,1)} %get-tuple-element.1669) | copy-start | bytes 1540 | tf_op jit(solution)/shard_map/while
  67.5 36.3 %copy-start.35 = (bf16[128,512]{1,0:T(8,128)(2,1)S(1)}, bf16[128,512]{1,0:T(8,128)(2,1)}, u32[]{:S(2)}) copy-start(bf16[128,512]{1,0:T(8,128)(2,1)} %slice.165) | copy-start | bytes 393220 | tf_op jit(solution)/shard_map/while
  68.0 35.9 %copy-start.19 = (bf16[128,1024]{1,0:T(8,128)(2,1)S(1)}, bf16[128,1024]{1,0:T(8,128)(2,1)}, u32[]{:S(2)}) copy-start(bf16[128,1024]{1,0:T(8,128)(2,1)} %slice.166) | copy-start | bytes 786436 | tf_op jit(solution)/shard_map/while
  68.0 199.5 %all-gather.25.cloned.1.call-start = ((), (), s32[]{:S(2)}) async-start(), calls=%async_computation.28 | async-start | bytes 3145728 | tf_op jit(solution)/shard_map/while/body/eval_jaxpr/all_gather | solution.py:364
  68.8 295.5 %reduce-scatter.40.cloned.1.call-start = ((), (), s32[]{:S(2)}) async-start(), calls=%async_computation.30 | async-start | bytes 1114112 | tf_op jit(solution)/shard_map/while
  240.3 32.5 %copy-start.3 = (f32[128,512]{1,0:T(8,128)}, f32[128,512]{1,0:T(8,128)S(1)}, u32[]{:S(2)}) copy-start(f32[128,512]{1,0:T(8,128)S(1)} %get-tuple-element.1411) | copy-start | bytes 786436 | tf_op jit(solution)/shard_map/while
  280.6 100.3 %all-gather.27.cloned.1.call-start = ((), (), s32[]{:S(2)}) async-start(), calls=%async_computation.29 | async-start | bytes 2228224 | tf_op jit(solution)/shard_map/while/body/eval_jaxpr/all_gather | solution.py:285
  304.0 49.0 %copy-start.7 = (f32[128,512]{1,0:T(8,128)S(1)}, f32[128,512]{1,0:T(8,128)}, u32[]{:S(2)}) copy-start(f32[128,512]{1,0:T(8,128)} %copy-done.6) | copy-start | bytes 786436 | tf_op jit(solution)/shard_map/while
  304.0 49.0 %copy-start.29 = (f32[512,512]{1,0:T(8,128)S(1)}, f32[512,512]{1,0:T(8,128)}, u32[]{:S(2)}) copy-start(f32[512,512]{1,0:T(8,128)} %get-tuple-element.1600) | copy-start | bytes 3145732 | tf_op jit(solution)/shard_map/while
  304.0 49.0 %copy-start.40 = (bf16[128,8,64]{0,2,1:T(8,128)(2,1)S(1)}, bf16[128,8,64]{0,2,1:T(8,128)(2,1)}, u32[]{:S(2)}) copy-start(bf16[128,8,64]{0,2,1:T(8,128)(2,1)} %copy-done.39) | copy-start | bytes 393220 | tf_op jit(solution)/shard_map/while
  427.7 33.8 %copy-start.65 = (bf16[50,256]{1,0:T(8,128)(2,1)S(1)}, bf16[50,256]{1,0:T(8,128)(2,1)}, u32[]{:S(2)}) copy-start(bf16[50,256]{1,0:T(8,128)(2,1)} %get-tuple-element.1656) | copy-start | bytes 76804 | tf_op jit(solution)/shard_map/while
  427.7 39.7 %copy-start.20 = (bf16[2,128,512]{2,1,0:T(8,128)(2,1)S(1)}, bf16[2,128,512]{2,1,0:T(8,128)(2,1)}, u32[]{:S(2)}) copy-start(bf16[2,128,512]{2,1,0:T(8,128)(2,1)} %get-tuple-element.1654) | copy-start | bytes 786436 | tf_op jit(solution)/shard_map/while
  427.7 22.3 %all-gather.19.cloned.1.call-start = ((), (), s32[]{:S(2)}) async-start(), calls=%async_computation.25 | async-start | bytes 1572864 | tf_op jit(solution)/shard_map/while/body/eval_jaxpr/all_gather | solution.py:360
  428.3 51.1 %all-gather.13.cloned.1.call-start = ((), (), s32[]{:S(2)}) async-start(), calls=%async_computation.22 | async-start | bytes 2359296 | tf_op jit(solution)/shard_map/while/body/eval_jaxpr/all_gather | solution.py:357
  429.0 91.0 %all-gather.21.cloned.1.call-start = ((), (), s32[]{:S(2)}) async-start(), calls=%async_computation.26 | async-start | bytes 1114112 | tf_op jit(solution)/shard_map/while/body/eval_jaxpr/all_gather | solution.py:189
  452.2 110.9 %all-gather.15.cloned.1.call-start = ((), (), s32[]{:S(2)}) async-start(), calls=%async_computation.23 | async-start | bytes 2228224 | tf_op jit(solution)/shard_map/while/body/eval_jaxpr/all_gather | solution.py:284
  482.0 133.0 %all-gather.17.cloned.1.call-start = ((), (), s32[]{:S(2)}) async-start(), calls=%async_computation.24 | async-start | bytes 4456448 | tf_op jit(solution)/shard_map/while/body/eval_jaxpr/all_gather | solution.py:274
  482.8 173.0 %all-gather.23.cloned.1.call-start = ((), (), s32[]{:S(2)}) async-start(), calls=%async_computation.27 | async-start | bytes 3145728 | tf_op jit(solution)/shard_map/while/body/eval_jaxpr/all_gather | solution.py:362
  482.9 31.3 %copy-start.126 = (bf16[256]{0:T(256)(128)(2,1)S(1)}, bf16[256]{0:T(256)(128)(2,1)}, u32[]{:S(2)}) copy-start(bf16[256]{0:T(256)(128)(2,1)} %get-tuple-element.1669) | copy-start | bytes 1540 | tf_op jit(solution)/shard_map/while
  482.9 36.1 %copy-start.35 = (bf16[128,512]{1,0:T(8,128)(2,1)S(1)}, bf16[128,512]{1,0:T(8,128)(2,1)}, u32[]{:S(2)}) copy-start(bf16[128,512]{1,0:T(8,128)(2,1)} %slice.165) | copy-start | bytes 393220 | tf_op jit(solution)/shard_map/while
  483.4 35.7 %copy-start.19 = (bf16[128,1024]{1,0:T(8,128)(2,1)S(1)}, bf16[128,1024]{1,0:T(8,128)(2,1)}, u32[]{:S(2)}) copy-start(bf16[128,1024]{1,0:T(8,128)(2,1)} %slice.166) | copy-start | bytes 786436 | tf_op jit(solution)/shard_map/while
  483.4 199.2 %all-gather.25.cloned.1.call-start = ((), (), s32[]{:S(2)}) async-start(), calls=%async_computation.28 | async-start | bytes 3145728 | tf_op jit(solution)/shard_map/while/body/eval_jaxpr/all_gather | solution.py:364
  484.0 298.1 %reduce-scatter.40.cloned.1.call-start = ((), (), s32[]{:S(2)}) async-start(), calls=%async_computation.30 | async-start | bytes 1114112 | tf_op jit(solution)/shard_map/while
  655.5 32.3 %copy-start.3 = (f32[128,512]{1,0:T(8,128)}, f32[128,512]{1,0:T(8,128)S(1)}, u32[]{:S(2)}) copy-start(f32[128,512]{1,0:T(8,128)S(1)} %get-tuple-element.1411) | copy-start | bytes 786436 | tf_op jit(solution)/shard_map/while
  695.7 100.3 %all-gather.27.cloned.1.call-start = ((), (), s32[]{:S(2)}) async-start(), calls=%async_computation.29 | async-start | bytes 2228224 | tf_op jit(solution)/shard_map/while/body/eval_jaxpr/all_gather | solution.py:285
  719.0 49.5 %copy-start.7 = (f32[128,512]{1,0:T(8,128)S(1)}, f32[128,512]{1,0:T(8,128)}, u32[]{:S(2)}) copy-start(f32[128,512]{1,0:T(8,128)} %copy-done.6) | copy-start | bytes 786436 | tf_op jit(solution)/shard_map/while
  719.0 49.5 %copy-start.29 = (f32[512,512]{1,0:T(8,128)S(1)}, f32[512,512]{1,0:T(8,128)}, u32[]{:S(2)}) copy-start(f32[512,512]{1,0:T(8,128)} %get-tuple-element.1600) | copy-start | bytes 3145732 | tf_op jit(solution)/shard_map/while
  719.0 49.5 %copy-start.40 = (bf16[128,8,64]{0,2,1:T(8,128)(2,1)S(1)}, bf16[128,8,64]{0,2,1:T(8,128)(2,1)}, u32[]{:S(2)}) copy-start(bf16[128,8,64]{0,2,1:T(8,128)(2,1)} %copy-done.39) | copy-start | bytes 393220 | tf_op jit(solution)/shard_map/while
  842.8 19.6 %reduce-scatter.22.cloned.1.call-start = ((), (), s32[]{:S(2)}) async-start(), calls=%async_computation.12 | async-start | bytes 786432 | tf_op jit(solution)/shard_map/reduce_scatter | solution.py:380
  845.1 31.5 %reduce-scatter.24.cloned.1.call-start = ((), (), s32[]{:S(2)}) async-start(), calls=%async_computation.13 | async-start | bytes 786432 | tf_op jit(solution)/shard_map/reduce_scatter | solution.py:383
  846.0 47.7 %reduce-scatter.28.cloned.1.call-start = ((), (), s32[]{:S(2)}) async-start(), calls=%async_computation.15 | async-start | bytes 786432 | tf_op jit(solution)/shard_map/reduce_scatter | solution.py:389
  847.0 70.0 %reduce-scatter.26.cloned.1.call-start = ((), (), s32[]{:S(2)}) async-start(), calls=%async_computation.14 | async-start | bytes 1572864 | tf_op jit(solution)/shard_map/reduce_scatter | solution.py:386
  850.0 95.8 %reduce-scatter.20.cloned.1.call-start = ((), (), s32[]{:S(2)}) async-start(), calls=%async_computation.11 | async-start | bytes 2359296 | tf_op jit(solution)/shard_map/reduce_scatter | solution.py:377
  851.4 129.1 %reduce-scatter.30.cloned.1.call-start = ((), (), s32[]{:S(2)}) async-start(), calls=%async_computation.16 | async-start | bytes 3145728 | tf_op jit(solution)/shard_map/reduce_scatter | solution.py:392
  855.3 159.7 %reduce-scatter.32.cloned.1.call-start = ((), (), s32[]{:S(2)}) async-start(), calls=%async_computation.17 | async-start | bytes 3145728 | tf_op jit(solution)/shard_map/reduce_scatter | solution.py:398
  859.2 168.2 %reduce-scatter.36.cloned.1.call-start = ((), (), s32[]{:S(2)}) async-start(), calls=%async_computation.19 | async-start | bytes 196608
  860.7 179.1 %reduce-scatter.38.cloned.1.call-start = ((), (), s32[]{:S(2)}) async-start(), calls=%async_computation.20 | async-start | bytes 196608
  861.6 190.9 %reduce-scatter.34.cloned.1.call-start = ((), (), s32[]{:S(2)}) async-start(), calls=%async_computation.18 | async-start | bytes 86016 | tf_op jit(solution)/shard_map/reduce_scatter | solution.py:410
  862.3 309.5 %all-reduce.7.cloned.1.call-start = ((), (), s32[]{:S(2)}) async-start(), calls=%async_computation.21 | async-start | bytes 8388608 | tf_op jit(solution)/shard_map/psum | solution.py:415
  (238 other events, 1345.1 us)
Sparse Core Ops, SparseCore 0:
  10.6 23.9 all-gather.18
  36.2 27.8 all-gather.12
  66.8 37.9 all-gather.20
  107.4 40.2 all-gather.14
  150.3 49.4 all-gather.16
  201.2 31.5 all-gather.22
  234.4 33.1 all-gather.24
  280.7 57.5 reduce-scatter.39
  340.7 40.1 all-gather.26
  429.8 20.1 all-gather.18
  451.6 27.8 all-gather.12
  482.0 37.9 all-gather.20
  522.7 40.3 all-gather.14
  565.7 49.3 all-gather.16
  616.4 31.5 all-gather.22
  649.5 33.1 all-gather.24
  695.8 57.5 reduce-scatter.39
  755.6 40.3 all-gather.26
Sparse Core Ops, SparseCore 1:
  846.1 13.2 reduce-scatter.21
  862.1 14.4 reduce-scatter.23
  879.3 14.5 reduce-scatter.27
  896.7 20.2 reduce-scatter.25
  919.8 25.9 reduce-scatter.19
  948.7 31.7 reduce-scatter.29
  983.2 31.7 reduce-scatter.31
  1017.1 10.2 reduce-scatter.35
  1029.5 10.2 reduce-scatter.37
  1042.6 9.8 reduce-scatter.33
  1057.7 114.1 all-reduce.6
where the time goes:
time: 1190 us
  waiting for transfers between devices  535 us (45%)
  blocking collectives  244 us (21%)
  matrix products  169 us (14%)
  local copies, waits for them, and re-layouts  162 us (14%)
  other arithmetic  55.3 us (5%)
  between operations  17.3 us (1%)
    all_gather x2, waiting for transfers between devices, layer_pass(): lax.all_gather(keyval, 'ctx', axis=0, tiled=True)  80.8 us
    all_gather x2, waiting for transfers between devices, layer_pass(): lax.all_gather(joined[:, :width], 'ctx', axis=0, tiled=True)  79.3 us
    while x502, local copies, waits for them, and re-layouts  64.4 us
    psum x1, blocking collectives, shards(): lax.psum(owned[6].astype(jnp.bfloat16), 'ctx').astype(jnp.float32)  62.2 us
    psum x1, waiting for transfers between devices, shards(): lax.psum(owned[0].astype(jnp.bfloat16), 'ctx').astype(jnp.float32)  54.1 us
    all_gather x2, waiting for transfers between devices, micro_batch(): lax.all_gather(ffn_down, 'fsdp', axis=0, tiled=True)  46.9 us
    all_gather x2, blocking collectives, layer_pass(): lax.all_gather(row_delta, 'ctx', axis=0, tiled=True)  46.3 us
    all_gather x2, waiting for transfers between devices, micro_batch(): lax.all_gather(cross_keyval, 'fsdp', axis=0, tiled=True)  45.8 us
  transfers between devices with their start and end apart: 29, of which 22 were waited for; matrix products, arithmetic and copies ran while one was open for 20% of the time, Pallas kernels for 0%

commit v1 on v0

v1 whole, which is shorter than its diff:
```python
import functools
import math

import jax
import jax.numpy as jnp
from jax import lax
from jax.experimental import pallas as pl
from jax.experimental.pallas import tpu as pltpu
from jax.sharding import PartitionSpec as P

H = 8
EPS = 1e-05
F32 = jnp.float32
BF = jnp.bfloat16
LOG2E = 1.4426950408889634
VMEM_LIMIT = 56 * 1024 * 1024


def nn(a, b):
    return lax.dot_general(a, b, (((1,), (0,)), ((), ())), preferred_element_type=F32)


def nt(a, b):
    return lax.dot_general(a, b, (((1,), (1,)), ((), ())), preferred_element_type=F32)


def flip(v):
    return jnp.transpose(v)


def normalise(v):
    centred = v - jnp.mean(v, axis=-1, keepdims=True)
    r = lax.rsqrt(jnp.mean(centred * centred, axis=-1, keepdims=True) + EPS)
    return centred * r, r


def norm_back(grad, gain, xhat, r):
    u = grad * gain
    return r * (u - jnp.mean(u, axis=-1, keepdims=True) - xhat * jnp.mean(u * xhat, axis=-1, keepdims=True))


def aligned(index, size):
    return pl.ds(pl.multiple_of(index, size), size)


VM = pl.BlockSpec(memory_space=pltpu.VMEM)
SM = pl.BlockSpec(memory_space=pltpu.SMEM)
ANY = pl.BlockSpec(memory_space=pl.ANY)


def call(kernel, name, outs, in_specs, scratch, args, flops, nbytes, exps=0, out_specs=None):
    return pl.pallas_call(
        kernel,
        name=name,
        out_shape=[jax.ShapeDtypeStruct(s, d) for s, d in outs],
        in_specs=in_specs,
        out_specs=out_specs or [VM] * len(outs),
        scratch_shapes=scratch,
        compiler_params=pltpu.CompilerParams(vmem_limit_bytes=VMEM_LIMIT),
        cost_estimate=pl.CostEstimate(flops=flops, bytes_accessed=nbytes, transcendentals=exps),
    )(*args)


class Placer:
    def __init__(self, sems, x, c):
        self.sems, self.x, self.c, self.used = sems, x, c, 0

    def copy(self, src, dst):
        copy = pltpu.make_async_copy(src, dst, self.sems.at[self.used])
        self.used += 1
        copy.start()
        return copy

    def lay(self, own, near, far, dst, row0, blocks):
        rows = own.shape[0]
        half = rows // 2
        base = (1 - self.x) * rows
        copies = [self.copy(own, dst.at[aligned(self.x * rows, rows)])]
        for b in range(blocks):
            cols = pl.ds(b * 512, 512)
            part = pl.ds(row0 + b * half, half)
            copies.append(self.copy(near.at[part], dst.at[aligned(base + self.c * half, half), cols]))
            copies.append(self.copy(far.at[part], dst.at[aligned(base + (1 - self.c) * half, half), cols]))
        return copies


def wait(copies):
    for copy in copies:
        copy.wait()


def attend_kernel(
    meta, place, even, odd, step, gain, shift, wh_own, wh_other, xhat_out, joined_out, heads_out, full_out, stats_out,
    wh, normed, keys,
):
    x = meta[0]
    n, width = xhat_out.shape
    half = wh_own.shape[1]
    hd = joined_out.shape[0] // 3
    blocks, rows = even.shape[0], even.shape[1]
    wh[:, aligned(x * half, half)] = wh_own[...]
    wh[:, aligned((1 - x) * half, half)] = wh_other[...]
    stats_out[...] = jnp.zeros_like(stats_out)
    for k in range(2 * blocks):
        block = even[k] if k < blocks else odd[k - blocks]
        xhat, r = normalise(block.astype(F32) + step[...])
        at = aligned(place[k] * rows, rows)
        xhat_out[at, :] = xhat.astype(BF)
        normed[at, :] = (xhat * gain[...] + shift[...]).astype(BF)
        stats_out[1:2, at] = flip(jnp.broadcast_to(r, (rows, 128)))[0:1, :]
    for b in range(n // 512):
        cols = pl.ds(b * 512, 512)
        joined_out[:, cols] = nt(wh[...], normed[cols, :]).astype(BF)
    keys[...] = flip(joined_out[hd : 2 * hd, :].astype(F32)).astype(BF)
    factor = LOG2E / math.sqrt(hd)
    wide = 256

    def query_block(b, carry):
        cols = aligned(b * wide, wide)
        scores = nn(keys[...], joined_out[0:hd, cols]) * factor
        peak = jnp.max(scores, axis=0, keepdims=True)
        shares = jnp.exp2(scores - peak)
        total = jnp.sum(shares, axis=0, keepdims=True)
        out = nn(joined_out[2 * hd : 3 * hd, :], shares.astype(BF)) / total
        full_out[:, cols] = out
        stats_out[0:1, cols] = peak + jnp.log2(total)
        for part in range(wide // rows):
            heads_out[b * (wide // rows) + part] = out[:, part * rows : (part + 1) * rows].astype(BF)
        return carry

    lax.fori_loop(0, n // wide, query_block, 0)


def attend_back_kernel(
    meta, joined, full, stats, grads, xhat, gain, shift, wh_own, wh_other, extra, joined_grad_out, keep_out, send_out,
    wh, keys, values, gout, lhs, query_acc, whole,
):
    x, active, slot = meta[0], meta[3], meta[4]
    n, width = xhat.shape
    half = wh_own.shape[1]
    hd = joined.shape[0] // 3
    rows = grads.shape[2]
    scale = 1.0 / math.sqrt(hd)
    factor = LOG2E * scale
    wh[:, aligned(x * half, half)] = wh_own[...]
    wh[:, aligned((1 - x) * half, half)] = wh_other[...]
    for j in range(grads.shape[0]):
        gout[:, j * rows : (j + 1) * rows] = grads[j]
    keys[...] = flip(joined[hd : 2 * hd, :].astype(F32)).astype(BF)
    values[...] = flip(joined[2 * hd : 3 * hd, :].astype(F32)).astype(BF)
    delta = jnp.sum(gout[...].astype(F32) * full[...], axis=0, keepdims=True)
    lse = stats[0:1, :]
    query_acc[...] = jnp.zeros_like(query_acc)
    wide = 256

    def key_block(b, carry):
        at = aligned(b * wide, wide)
        queries = joined[0:hd, :]
        shares = jnp.exp2(nn(keys[at, :], queries) * factor - lse)
        share_grad = nn(values[at, :], gout[...])
        score_grad = (shares * (share_grad - delta)).astype(BF)
        lhs[hd : 2 * hd, at] = (nt(queries, score_grad) * scale).astype(BF)
        lhs[2 * hd : 3 * hd, at] = nt(gout[...], shares.astype(BF)).astype(BF)
        query_acc[...] += nn(joined[hd : 2 * hd, at], score_grad)
        return carry

    lax.fori_loop(0, n // wide, key_block, 0)
    lhs[0:hd, :] = (query_acc[...] * scale).astype(BF)
    for j in range(joined_grad_out.shape[0]):
        joined_grad_out[j] = lhs[0 : 3 * hd, j * rows : (j + 1) * rows]

    grad = lhs[0 : 3 * hd, :].astype(F32)
    r = stats[1:2, :]
    weight = wh[...].astype(F32)
    bias = jnp.sum(weight * shift[...], axis=1, keepdims=True)
    mixed_mean = jnp.sum(grad * (joined[...].astype(F32) - bias), axis=0, keepdims=True) * (1.0 / width)
    tail = lhs.shape[0] - 3 * hd
    first = lax.broadcasted_iota(jnp.int32, (tail, n), 0) == 0
    lhs[3 * hd :, :] = jnp.where(first, mixed_mean * r, 0.0).astype(BF)
    product = nn(lhs[...], xhat[...])
    m = product[0 : 3 * hd]
    sums = jnp.sum(grad, axis=1, keepdims=True)
    scaled_sums = jnp.sum(grad * r, axis=1, keepdims=True)
    lead = gain[...] * jnp.sum(weight * scaled_sums, axis=0, keepdims=True)
    start_sum = lead - jnp.mean(lead, axis=1, keepdims=True) - product[3 * hd : 3 * hd + 1]
    on = active.astype(F32)
    whole[0 : 3 * hd, :] = (m * gain[...] + sums * shift[...]) * on
    gain_grad = jnp.sum(weight * m, axis=0, keepdims=True) * on
    shift_grad = jnp.sum(weight * sums, axis=0, keepdims=True) * on
    row = lax.broadcasted_iota(jnp.int32, extra.shape, 0)
    more = jnp.where(row == 0, gain_grad, 0.0) + jnp.where(row == 1, shift_grad, 0.0)
    more = more + jnp.where(row == 2 + slot, start_sum * on, 0.0)
    whole[3 * hd :, :] = extra[...] + more
    keep_out[...] = whole[:, aligned(x * half, half)]
    send_out[...] = whole[:, aligned((1 - x) * half, half)].astype(BF)


def encoder_kernel(meta, enc, own, near, far, kvt_out, weight_out, sems):
    put = Placer(sems, meta[0], meta[1])
    wait(put.lay(own, near, far, weight_out, 0, 2))
    for s in range(enc.shape[0]):
        for b in range(2):
            kv = nn(enc[s], weight_out[:, b * 512 : (b + 1) * 512])
            kvt_out[s, b * 512 : (b + 1) * 512, :] = flip(kv).astype(BF)


def chunk_at(meta, k, xr):
    x, c = meta[0], meta[1]
    return x ^ xr, c ^ k


def forward_kernel(
    meta, tokens, steps, att, kvt, gains, shifts, up_bias, down_bias, out_grad,
    own_out, own_query, own_cross, own_up, own_down, near2, far2, near3, far3,
    mixed_out, h2g_out, h1_out, q_out, crossed_out, shares_out, extra_out, keep_out, send_out,
    w_out, w_query, w_cross, w_up, w_down, act_t, n2_t, pre_low, sems,
):
    seqs, rows, width = tokens.shape
    hd = width // H
    ff = w_down.shape[0]
    slots = extra_out.shape[0]
    put = Placer(sems, meta[0], meta[1])
    half = own_out.shape[0] // 2
    c_out = put.lay(own_out, near2, far2, w_out, 2 * half, 1)
    c_query = put.lay(own_query, near2, far2, w_query, 3 * half, 1)
    c_cross = put.lay(own_cross, near2, far2, w_cross, 4 * half, 1)
    c_up = put.lay(own_up, near3, far3, w_up, 0, 4)
    c_down = put.lay(own_down, near3, far3, w_down, 4 * half, 1)
    factor = LOG2E / math.sqrt(hd)

    wait(c_out)
    for s in range(seqs):
        at = pl.ds(s * rows, rows)
        start = tokens[s].astype(F32) + steps[s : s + 1, :]
        h1_out[at, :] = start + nn(flip(att[s]), w_out[...])
    hidden1 = h1_out[...]
    xhat1, unused = normalise(hidden1)
    wait(c_query)
    q_out[...] = nn((xhat1 * gains[1:2, :] + shifts[1:2, :]).astype(BF), w_query[...]).astype(BF)
    for s in range(seqs):
        for h in range(H):
            q = q_out[s * rows : (s + 1) * rows, h * hd : (h + 1) * hd]
            scores = nn(q, kvt[s, h * hd : (h + 1) * hd, :]) * factor
            shares = jnp.exp2(scores - jnp.max(scores, axis=1, keepdims=True))
            shares = (shares * (1.0 / jnp.sum(shares, axis=1, keepdims=True))).astype(BF)
            shares_out[s * H + h] = shares
            got = nt(kvt[s, width + h * hd : width + (h + 1) * hd, :], shares)
            crossed_out[s, h * hd : (h + 1) * hd, :] = got.astype(BF)
    wait(c_cross)
    crossed = jnp.concatenate([flip(crossed_out[s]) for s in range(seqs)], axis=0)
    hidden2 = hidden1 + nn(crossed, w_cross[...])
    xhat2, r2 = normalise(hidden2)
    n2 = (xhat2 * gains[2:3, :] + shifts[2:3, :]).astype(BF)
    n2_t[...] = flip(n2)
    grad = jnp.concatenate([out_grad[s] for s in range(seqs)], axis=0)
    top = grad.astype(F32)
    wait(c_up)
    wait(c_down)
    mixed = hidden2 + down_bias[...]
    n2_grad = jnp.zeros_like(hidden2)
    extra_out[...] = jnp.zeros_like(extra_out)
    root = math.sqrt(2.0 / math.pi)
    bias_row = slots - 10
    for b in range(ff // 512):
        cols = pl.ds(b * 512, 512)
        pre = nn(n2, w_up[:, cols]) + up_bias[:, cols]
        square = pre * pre
        bent = jnp.tanh(root * pre * (1.0 + 0.044715 * square))
        act = (0.5 * pre * (1.0 + bent)).astype(BF)
        slope = 0.5 * (1.0 + bent) + 0.5 * root * pre * (1.0 - bent * bent) * (1.0 + 3.0 * 0.044715 * square)
        mixed = mixed + nn(act, w_down[cols, :])
        act_t[cols, :] = flip(act)
        low = (nt(grad, w_down[cols, :]) * slope).astype(BF)
        pre_low[:, cols] = low
        n2_grad = n2_grad + nt(low, w_up[:, cols])
        sums = jnp.sum(low.astype(F32), axis=0, keepdims=True)
        per_half = ff // 512 // 2
        lanes = pl.ds((b // per_half) * 256, 256)
        for piece in range(2):
            row = bias_row + 1 + (b % per_half) * 2 + piece
            extra_out[row : row + 1, lanes] = sums[:, piece * 256 : (piece + 1) * 256]
    for s in range(seqs):
        mixed_out[s] = mixed[s * rows : (s + 1) * rows].astype(BF)
    h2g_out[...] = top + norm_back(n2_grad, gains[2:3, :], xhat2, r2)
    extra_out[bias_row : bias_row + 1, :] = jnp.sum(top, axis=0, keepdims=True)
    extra_out[bias_row + 5 : bias_row + 6, :] = jnp.sum(n2_grad * xhat2, axis=0, keepdims=True)
    extra_out[bias_row + 6 : bias_row + 7, :] = jnp.sum(n2_grad, axis=0, keepdims=True)

    me = meta[2]
    for k in (1, 0):
        out = send_out if k else keep_out
        for xr in (1, 0):
            xa, ca = chunk_at(meta, k, xr)
            down = nn(act_t[aligned(xa * (ff // 2) + ca * (ff // 4), ff // 4), :], grad).astype(BF)
            up = nn(n2_t[aligned(xa * (width // 2), width // 2), :], pre_low[:, aligned(ca * (ff // 2), ff // 2)])
            up = up.astype(BF)
            for a in range(8):
                out[xr, a ^ me, 0:64, :] = down[a * 64 : (a + 1) * 64]
                out[xr, a ^ me, 64:128, :] = up[(a % 4) * 64 : (a % 4 + 1) * 64, (a // 4) * 512 : (a // 4 + 1) * 512]


def backward_kernel(
    meta, h2g, hidden1, q, crossed, shares, kvt, att, enc, gains, shifts, extra_in,
    own_out, own_query, own_cross, near2, far2,
    h1g_out, att_grad_out, kv_keep, kv_send, extra_out, keep_out, send_out,
    w_out, w_query, w_cross, dc, dq, n1_t, part, enc_t, sems,
):
    width = h2g.shape[1]
    seqs, unused, rows = att.shape
    hd = width // H
    enc_rows = enc.shape[1]
    scale = 1.0 / math.sqrt(hd)
    put = Placer(sems, meta[0], meta[1])
    half = own_out.shape[0] // 2
    c_cross = put.lay(own_cross, near2, far2, w_cross, 4 * half, 1)
    c_query = put.lay(own_query, near2, far2, w_query, 3 * half, 1)
    c_out = put.lay(own_out, near2, far2, w_out, 2 * half, 1)
    grad2 = h2g[...]
    low2 = grad2.astype(BF)
    wait(c_cross)
    dc[...] = nt(low2, w_cross[...]).astype(BF)
    for s in range(seqs):
        at = slice(s * rows, (s + 1) * rows)
        q_t = flip(q[at, :])
        dc_t = flip(dc[at, :])
        enc_t[s] = flip(enc[s])
        for h in range(H):
            head = slice(h * hd, (h + 1) * hd)
            low = shares[s * H + h]
            wide = low.astype(F32)
            share_grad = nn(dc[at, head], kvt[s, width + h * hd : width + (h + 1) * hd, :])
            mean = jnp.sum(wide * share_grad, axis=1, keepdims=True)
            score_grad = (wide * (share_grad - mean)).astype(BF)
            dq[at, head] = (nt(score_grad, kvt[s, head, :]) * scale).astype(BF)
            part[s, head, :] = (nn(q_t[head], score_grad) * scale).astype(BF)
            part[s, width + h * hd : width + (h + 1) * hd, :] = nn(dc_t[head], low).astype(BF)
    kv_keep[...] = part[:, :, 0 : enc_rows // 2]
    kv_send[...] = part[:, :, enc_rows // 2 :]
    xhat1, r1 = normalise(hidden1[...])
    n1_t[...] = flip((xhat1 * gains[1:2, :] + shifts[1:2, :]).astype(BF))
    wait(c_query)
    n1_grad = nt(dq[...], w_query[...])
    grad1 = grad2 + norm_back(n1_grad, gains[1:2, :], xhat1, r1)
    h1g_out[...] = grad1
    low1 = grad1.astype(BF)
    wait(c_out)
    for s in range(seqs):
        att_grad_out[s] = nt(w_out[...], low1[s * rows : (s + 1) * rows]).astype(BF)
    extra_out[...] = extra_in[...]
    last = extra_out.shape[0] - 10
    extra_out[last + 7 : last + 8, :] = jnp.sum(n1_grad * xhat1, axis=0, keepdims=True)
    extra_out[last + 8 : last + 9, :] = jnp.sum(n1_grad, axis=0, keepdims=True)
    row = lax.broadcasted_iota(jnp.int32, extra_out.shape, 0)
    more = jnp.zeros(extra_out.shape, F32)
    for s in range(seqs):
        token_sum = jnp.sum(grad1[s * rows : (s + 1) * rows], axis=0, keepdims=True)
        more = more + jnp.where(row == 2 + meta[5] + s, token_sum, 0.0)
    extra_out[...] += more

    me = meta[2]
    for k in (1, 0):
        out = send_out if k else keep_out
        for xr in (1, 0):
            xa, ca = chunk_at(meta, k, xr)
            at = aligned(xa * (width // 2) + ca * (width // 4), width // 4)
            outer = jnp.zeros((width // 4, width), F32)
            cross = jnp.zeros((width // 4, width), F32)
            keyval = jnp.zeros((width // 2, width), F32)
            for s in range(seqs):
                mine = slice(s * rows, (s + 1) * rows)
                outer = outer + nn(att[s, at, :], low1[mine])
                cross = cross + nn(crossed[s, at, :], low2[mine])
                keyval = keyval + nt(enc_t[s, aligned(xa * (width // 2), width // 2), :], part[s, aligned(ca * width, width), :])
            query = nn(n1_t[at, :], dq[...]).astype(BF)
            outer, cross, keyval = outer.astype(BF), cross.astype(BF), keyval.astype(BF)
            for a in range(8):
                out[xr, a ^ me, 0:16, :] = outer[a * 16 : (a + 1) * 16]
                out[xr, a ^ me, 16:32, :] = query[a * 16 : (a + 1) * 16]
                out[xr, a ^ me, 32:48, :] = cross[a * 16 : (a + 1) * 16]
                out[xr, a ^ me, 48:80, :] = keyval[a * 32 : (a + 1) * 32]


def start_kernel(meta, grads, tokens, steps, gains, h1g, own, near, far, grad_out, weight, turned, sems):
    seqs, rows, width = tokens.shape
    hd = width // H
    put = Placer(sems, meta[0], meta[1])
    copies = put.lay(own, near, far, weight, 0, 3)
    for s in range(seqs):
        for h in range(H):
            for j in range(3):
                turned[s, j * width + h * hd : j * width + (h + 1) * hd, :] = grads[s, h, j * hd : (j + 1) * hd, :]
    wait(copies)
    for s in range(seqs):
        xhat, r = normalise(tokens[s].astype(F32) + steps[s : s + 1, :])
        grad = nt(flip(turned[s]), weight[...])
        grad_out[s] = h1g[s * rows : (s + 1) * rows, :] + norm_back(grad, gains[0:1, :], xhat, r)


def place_ffn_kernel(meta, *refs):
    pieces, (up_out, down_out) = refs[:-2], refs[-2:]
    c, me = meta[1], meta[2]
    for k, (core, mask, index) in enumerate(PIECES):
        block = pieces[k // 2][index].astype(F32)
        a = me ^ mask
        ca = c ^ core
        down_out[aligned(ca * 512 + a * 64, 64), :] = block[0:64]
        up_out[aligned((a % 4) * 64, 64), aligned(ca * 1024 + (a // 4) * 512, 512)] = block[64:128]


def place_cross_kernel(meta, *refs):
    pieces, (out_out, query_out, cross_out, keyval_out) = refs[:-4], refs[-4:]
    c, me = meta[1], meta[2]
    for k, (core, mask, index) in enumerate(PIECES):
        block = pieces[k // 2][index].astype(F32)
        a = me ^ mask
        ca = c ^ core
        at = aligned(ca * 128 + a * 16, 16)
        out_out[at, :] = block[0:16]
        query_out[at, :] = block[16:32]
        cross_out[at, :] = block[32:48]
        keyval_out[aligned(a * 32, 32), aligned(ca * 512, 512)] = block[48:80]


PIECES = [(core, mask + far, far) for core in (0, 1) for mask in (0, 2, 4, 6) for far in (0, 1)]


def place_joined_kernel(meta, *refs):
    pieces, (grad_out, extra_out, stacked) = refs[:-3], refs[-3:]
    low = meta[6]
    total = jnp.zeros(extra_out.shape, F32)
    hd = 64
    for k, mask in enumerate((0, 4, 2, 6, 1, 5, 3, 7)):
        block = pieces[k][...].astype(F32)
        head = low ^ mask
        for j in range(3):
            stacked[aligned(j * H * hd + head * hd, hd), :] = block[j * hd : (j + 1) * hd]
        total = total + block[3 * hd :]
    extra_out[...] = total
    for b in range(3):
        grad_out[:, b * 512 : (b + 1) * 512] = flip(stacked[b * 512 : (b + 1) * 512, :])


def over_ctx(value, mask):
    return lax.ppermute(value, "ctx", [(i, i ^ mask) for i in range(16)])


def over_x(value):
    return lax.ppermute(value, "fsdp", [(0, 1), (1, 0)])


def half_rows(weight, c):
    half = weight.shape[0] // 2
    part = lax.dynamic_slice_in_dim(weight, c * half, half, 0)
    return [part[:, b : b + 512] for b in range(0, weight.shape[1], 512)]


def fetch_group(weights, c):
    near = over_x(jnp.concatenate([p for w in weights for p in half_rows(w, c)], axis=0))
    return near, over_ctx(near, 1)


def add_low(*terms):
    return sum(t.astype(F32) for t in terms).astype(BF)


def reduce_blocks(keep, send):
    got = over_ctx(send, 1)
    got_x = over_x(add_low(keep[1], got[1]))
    kept = add_low(keep[0], got[0], got_x)
    kept = add_low(kept[0:4], over_ctx(kept[4:8], 2))
    kept = add_low(kept[0:2], over_ctx(kept[2:4], 4))
    return add_low(kept[0], over_ctx(kept[1], 8))


def gather_blocks(block):
    pair = jnp.stack([block, over_ctx(block, 8)])
    pieces = [pair] + [over_ctx(pair, mask) for mask in (4, 2, 6)]
    return pieces + [over_ctx(piece, 1) for piece in pieces]


def shards(
    tokens, encoder, step_ids, out_grad, self_in, self_out, cross_query, cross_keyval, cross_out,
    ffn_up, up_bias, ffn_down, down_bias, norm_gain, norm_shift, step_table,
):
    nctx, nx = lax.axis_size("ctx"), lax.axis_size("fsdp")
    i, x = lax.axis_index("ctx"), lax.axis_index("fsdp")
    seqs, rows, width = tokens.shape
    hd = width // H
    units = seqs * H
    rep = nctx // units
    unit = i // rep
    s_mine, head = unit // H, unit % H
    n = rows * nctx
    ff = 2048
    fast = nctx == 16 and nx == 2
    steps_count = step_table.shape[0]
    slots = seqs * nx
    extra_rows = -(-(slots + 12) // 16) * 16
    zero = jnp.int32(0)

    def small_rows(w):
        by_head = w.reshape(w.shape[0], 3, H, hd)
        mine = lax.dynamic_index_in_dim(by_head, head, 2, False).reshape(w.shape[0], 3 * hd)
        return mine.T

    if fast:
        c = i & 1
        me = ((i >> 1) & 1) * 4 + ((i >> 2) & 1) * 2 + ((i >> 3) & 1)
        ids = jnp.pad(step_ids.astype(BF)[None, :], ((0, 0), (0, width // 2 - seqs)))
        small = jnp.concatenate(
            [norm_gain, norm_shift, step_table, down_bias[None, :], up_bias.reshape(4, width // 2), ids,
             jnp.zeros((2, width // 2), BF)], axis=0)
        wh_own = small_rows(self_in)
        other_small = over_x(jnp.concatenate([wh_own, small], axis=0))
        wh_other = other_small[: 3 * hd]
        other = other_small[3 * hd :]
        swap = x == 1
        first = jnp.where(swap, other, small)
        second = jnp.where(swap, small, other)
        both = jnp.concatenate([first, second], axis=1)
        gains, shifts = both[0:3].astype(F32), both[3:6].astype(F32)
        table = both[6 : 6 + steps_count]
        bias_d = both[6 + steps_count : 7 + steps_count].astype(F32)
        at = 7 + steps_count
        bias_u = jnp.concatenate([first[at : at + 4].reshape(1, ff // 2), second[at : at + 4].reshape(1, ff // 2)], axis=1)
        bias_u = bias_u.astype(F32)
        all_ids = jnp.concatenate([first[at + 4, :seqs], second[at + 4, :seqs]])

        mine = lax.dynamic_index_in_dim(tokens, s_mine, 0, False)
        others = lax.dynamic_index_in_dim(tokens, 1 - s_mine, 0, False)
        got = over_ctx(others, 8)
        near = [mine] + [over_ctx(mine, mask) for mask in (4, 2, 6)]
        far = [got] + [over_ctx(got, mask) for mask in (4, 2, 6)]
        even = jnp.stack(near + far)
        odd = over_ctx(even, 1)
        place = i ^ jnp.array([0, 4, 2, 6, 8, 12, 10, 14, 1, 5, 3, 7, 9, 13, 11, 15], jnp.int32)

        enc8 = over_ctx(encoder, 8)
        pair = jnp.stack([encoder, enc8])
        through = {mask: over_ctx(pair, mask) for mask in (4, 2, 6)}
        enc_even = jnp.concatenate([pair, through[4], through[2], through[6]], axis=0)
        enc_all = jnp.concatenate([enc_even, over_ctx(enc_even, 1)], axis=0)
        enc_all = enc_all.transpose(1, 0, 2, 3).reshape(seqs, -1, width)

        own = dict(keyval=cross_keyval, out=self_out, query=cross_query, cross=cross_out, up=ffn_up, down=ffn_down, joined=self_in)
        near2, far2 = fetch_group([cross_keyval, self_out, cross_query, cross_out], c)
        near3, far3 = fetch_group([ffn_up, ffn_down], c)
        near4, far4 = fetch_group([self_in], c)
        xk, first_slot = x, seqs * x
    else:
        c, me, xk, first_slot = zero, zero, zero, seqs * x

        def gather(w, axis=0):
            return lax.all_gather(w, "fsdp", axis=axis, tiled=True)

        gains, shifts = gather(norm_gain, 1).astype(F32), gather(norm_shift, 1).astype(F32)
        table = gather(step_table, 1)
        bias_d, bias_u = gather(down_bias)[None, :].astype(F32), gather(up_bias)[None, :].astype(F32)
        all_ids = gather(step_ids.astype(BF))
        full = dict(keyval=gather(cross_keyval), out=gather(self_out), query=gather(cross_query), cross=gather(cross_out),
                    up=gather(ffn_up), down=gather(ffn_down), joined=gather(self_in))
        half_of = {name: w.shape[0] // 2 for name, w in full.items()}
        own = {name: w[: half_of[name]] for name, w in full.items()}

        def group(names, which):
            parts = []
            for name in names:
                rest = full[name][half_of[name] :]
                quarter = half_of[name] // 2
                part = rest[which * quarter : (which + 1) * quarter]
                parts += [part[:, b : b + 512] for b in range(0, part.shape[1], 512)]
            return jnp.concatenate(parts, axis=0)

        near2, far2 = (group(["keyval", "out", "query", "cross"], w) for w in (0, 1))
        near3, far3 = (group(["up", "down"], w) for w in (0, 1))
        near4, far4 = (group(["joined"], w) for w in (0, 1))
        wh = small_rows(full["joined"])
        wh_own, wh_other = wh[:, : width // 2], wh[:, width // 2 :]
        every = lax.all_gather(tokens, "ctx", axis=0, tiled=False)
        chosen = lax.dynamic_index_in_dim(every, s_mine, 1, False)
        even, odd = chosen[: nctx // 2], chosen[nctx // 2 :]
        place = jnp.arange(nctx, dtype=jnp.int32)
        enc_all = lax.all_gather(encoder, "ctx", axis=1, tiled=True)

    active = (i % rep == 0).astype(jnp.int32)
    slot = first_slot + s_mine
    meta = jnp.stack([xk, c, me, active, slot, jnp.int32(first_slot), i & 7, zero]).astype(jnp.int32)
    onehot = (jnp.arange(steps_count, dtype=jnp.int32)[None, :] == step_ids[:, None]).astype(BF)
    steps = jnp.dot(onehot, table, preferred_element_type=F32)
    step_mine = lax.dynamic_index_in_dim(steps, s_mine, 0, True)

    xhat0, joined, heads, attended_full, stats = call(
        attend_kernel, "attend",
        [((n, width), BF), ((3 * hd, n), BF), ((nctx, hd, rows), BF), ((hd, n), F32), ((8, n), F32)],
        [SM, SM] + [VM] * 7,
        [pltpu.VMEM((3 * hd, width), BF), pltpu.VMEM((n, width), BF), pltpu.VMEM((n, hd), BF)],
        (meta, place, even, odd, step_mine, gains[0:1], shifts[0:1], wh_own, wh_other),
        2 * n * width * 3 * hd + 4 * n * n * hd, 8 * n * width, n * n,
    )
    back = lax.all_to_all(heads, "ctx", 0, 0, tiled=True)
    att = back.reshape(units, rep, hd, rows)[:, 0].reshape(seqs, width, rows)

    kvt, w_keyval = call(
        encoder_kernel, "encoder_rows",
        [((seqs, 2 * width, enc_all.shape[1]), BF), ((width, 2 * width), BF)],
        [SM, VM, ANY, ANY, ANY],
        [pltpu.SemaphoreType.DMA((5,))],
        (meta, enc_all, own["keyval"], near2, far2),
        4 * seqs * enc_all.shape[1] * width * width, 4 << 20,
    )

    tall = seqs * rows
    enc_rows = enc_all.shape[1]
    mixed, h2g, hidden1, q, crossed, shares, extra1, f_keep, f_send = call(
        forward_kernel, "forward",
        [((seqs, rows, width), BF), ((tall, width), F32), ((tall, width), F32), ((tall, width), BF), ((seqs, width, rows), BF),
         ((units, rows, enc_rows), BF), ((extra_rows, width), F32), ((2, 8, 128, width), BF), ((2, 8, 128, width), BF)],
        [SM] + [VM] * 9 + [ANY] * 9,
        [pltpu.VMEM((width, width), BF)] * 3
        + [pltpu.VMEM((width, ff), BF), pltpu.VMEM((ff, width), BF), pltpu.VMEM((ff, tall), BF),
           pltpu.VMEM((width, tall), BF), pltpu.VMEM((tall, ff), BF), pltpu.SemaphoreType.DMA((21,))],
        (meta, tokens, steps, att, kvt, gains, shifts, bias_u, bias_d, out_grad,
         own["out"], own["query"], own["cross"], own["up"], own["down"], near2, far2, near3, far3),
        2 * tall * width * (2 * width + 2 * enc_rows + 6 * ff), 24 << 20, tall * (H * enc_rows + ff),
    )
    h1g, att_grad, kv_keep, kv_send, extra2, c_keep, c_send = call(
        backward_kernel, "backward",
        [((tall, width), F32), ((seqs, width, rows), BF), ((seqs, 2 * width, enc_rows // 2), BF),
         ((seqs, 2 * width, enc_rows // 2), BF), ((extra_rows, width), F32), ((2, 8, 80, width), BF), ((2, 8, 80, width), BF)],
        [SM] + [VM] * 11 + [ANY] * 5,
        [pltpu.VMEM((width, width), BF)] * 3
        + [pltpu.VMEM((tall, width), BF), pltpu.VMEM((tall, width), BF), pltpu.VMEM((width, tall), BF),
           pltpu.VMEM((seqs, 2 * width, enc_rows), BF), pltpu.VMEM((seqs, width, enc_rows), BF), pltpu.SemaphoreType.DMA((9,))],
        (meta, h2g, hidden1, q, crossed, shares, kvt, att, enc_all, gains, shifts, extra1,
         own["out"], own["query"], own["cross"], near2, far2),
        2 * tall * width * (6 * width + 4 * enc_rows) + 4 * seqs * enc_rows * width * width, 24 << 20, 0,
    )

    by_unit = att_grad.reshape(units, 1, hd, rows)
    grads = lax.all_to_all(jnp.broadcast_to(by_unit, (units, rep, hd, rows)).reshape(nctx, hd, rows), "ctx", 0, 0, tiled=True)
    joined_grad, u_keep, u_send = call(
        attend_back_kernel, "attend_back",
        [((nctx, 3 * hd, rows), BF), ((3 * hd + extra_rows, width // 2), F32), ((3 * hd + extra_rows, width // 2), BF)],
        [SM] + [VM] * 10,
        [pltpu.VMEM((3 * hd, width), BF), pltpu.VMEM((n, hd), BF), pltpu.VMEM((n, hd), BF), pltpu.VMEM((hd, n), BF),
         pltpu.VMEM((3 * hd + 16, n), BF), pltpu.VMEM((hd, n), F32), pltpu.VMEM((3 * hd + extra_rows, width), F32)],
        (meta, joined, attended_full, stats, grads, xhat0, gains[0:1], shifts[0:1], wh_own, wh_other, extra2),
        10 * n * n * hd + 2 * n * width * 3 * hd, 8 << 20, n * n,
    )
    dj = lax.all_to_all(joined_grad, "ctx", 0, 0, tiled=True)
    dj = dj.reshape(units, rep, 3 * hd, rows)[:, 0].reshape(seqs, H, 3 * hd, rows)
    (tokens_grad,) = call(
        start_kernel, "start_grad",
        [((seqs, rows, width), F32)],
        [SM] + [VM] * 5 + [ANY] * 3,
        [pltpu.VMEM((width, 3 * width), BF), pltpu.VMEM((seqs, 3 * width, rows), BF), pltpu.SemaphoreType.DMA((7,))],
        (meta, dj, tokens, steps, gains, h1g, own["joined"], near4, far4),
        6 * tall * width * width, 6 << 20,
    )

    if fast:
        whole_u = add_low(u_keep, over_x(u_send))
        whole_u = add_low(whole_u, over_ctx(whole_u, 8))
        pieces = [whole_u] + [over_ctx(whole_u, mask) for mask in (4, 2, 6)]
        pieces = pieces + [over_ctx(piece, 1) for piece in pieces]
        self_in_grad, extra = call(
            place_joined_kernel, "place_joined",
            [((width // 2, 3 * width), F32), ((extra_rows, width // 2), F32)],
            [SM] + [VM] * 8, [pltpu.VMEM((3 * width, width // 2), F32)], (meta, *pieces), 0, 4 << 20,
        )
        kv = over_ctx(kv_send, 1)
        wide = enc_rows // 4
        got = over_ctx(add_low(kv_keep[:, :, wide:], kv[:, :, wide:]), 2)
        kv = add_low(kv_keep[:, :, :wide], kv[:, :, :wide], got).transpose(0, 2, 1)
        kv = add_low(kv[:, : wide // 2], over_ctx(kv[:, wide // 2 :], 4))
        kv = add_low(kv[:, : wide // 4], over_ctx(kv[:, wide // 4 :], 8))
        f_pieces = gather_blocks(reduce_blocks(f_keep, f_send))
        c_pieces = gather_blocks(reduce_blocks(c_keep, c_send))
        up_grad, down_grad = call(
            place_ffn_kernel, "place_ffn", [((width // 2, ff), F32), ((ff // 2, width), F32)],
            [SM] + [VM] * 8, [], (meta, *f_pieces), 0, 8 << 20,
        )
        out_g, query_g, cross_g, keyval_g = call(
            place_cross_kernel, "place_cross",
            [((width // 2, width), F32)] * 3 + [((width // 2, 2 * width), F32)],
            [SM] + [VM] * 8, [], (meta, *c_pieces), 0, 6 << 20,
        )
        bias_row = extra_rows - 10
        up_bias_grad = extra[bias_row + 1 : bias_row + 5].reshape(-1)
        down_bias_grad = extra[bias_row]
    else:
        def scatter(g, axis=0):
            return lax.psum(lax.psum_scatter(g, "fsdp", scatter_dimension=axis, tiled=True), "ctx")

        f_all = jnp.stack([f_keep, f_send], axis=1)
        c_all = jnp.stack([c_keep, c_send], axis=1)
        down_g = scatter(f_all[..., 0:64, :].reshape(ff, width).astype(F32))
        up_g = f_all[..., 64:128, :].reshape(2, 2, 2, 4, 64, width).transpose(0, 3, 4, 1, 2, 5)
        up_grad, down_grad = scatter(up_g.reshape(width, ff).astype(F32)), down_g
        out_g, query_g, cross_g = (scatter(c_all[..., k : k + 16, :].reshape(width, width).astype(F32)) for k in (0, 16, 32))
        keyval_g = scatter(c_all[..., 48:80, :].transpose(0, 2, 3, 1, 4).reshape(width, 2 * width).astype(F32))
        kv = jnp.concatenate([kv_keep, kv_send], axis=2).transpose(0, 2, 1)
        kv = lax.psum_scatter(kv, "ctx", scatter_dimension=1, tiled=True)
        u = jnp.concatenate([u_keep, u_send.astype(F32)], axis=1)
        every_u = lax.all_gather(lax.psum(u[: 3 * hd], "fsdp"), "ctx", axis=0, tiled=False)
        by_head = every_u.reshape(seqs, H, rep, 3, hd, width).sum(axis=(0, 2))
        joined_g = by_head.transpose(3, 1, 0, 2).reshape(width, 3 * width) if False else by_head.transpose(3, 1, 0, 2).reshape(width, 3 * width)
        self_in_grad = lax.dynamic_slice_in_dim(joined_g, x * self_in.shape[0], self_in.shape[0], 0)
        sums = lax.psum(u[3 * hd :], ("ctx", "fsdp"))
        part = norm_gain.shape[1]
        extra = lax.dynamic_slice_in_dim(sums, x * part, part, 1)
        bias_row = extra_rows - 10
        down_bias_grad = extra[bias_row]
        up_all = sums[bias_row + 1 : bias_row + 5].reshape(4, 2, width // 2).transpose(1, 0, 2).reshape(-1)
        up_bias_grad = lax.dynamic_slice_in_dim(up_all, x * up_bias.shape[0], up_bias.shape[0], 0)

    enc_grad = jnp.einsum("sre,de->srd", kv, w_keyval, preferred_element_type=F32)
    gain_grad = jnp.stack([extra[0], extra[bias_row + 7], extra[bias_row + 5]])
    shift_grad = jnp.stack([extra[1], extra[bias_row + 8], extra[bias_row + 6]])
    hot = (jnp.arange(steps_count, dtype=jnp.int32).astype(F32)[:, None, None] == all_ids.astype(F32)[None, :, None]).astype(F32)
    table_grad = jnp.sum(hot * extra[None, 2 : 2 + slots, :], axis=1)
    return (
        mixed, tokens_grad, enc_grad, self_in_grad, out_g, query_g, keyval_g, cross_g, up_grad, up_bias_grad,
        down_grad, down_bias_grad, gain_grad, shift_grad, table_grad,
    )


def solution(mesh):
    tok = P("fsdp", "ctx", None)
    row, vec, col = P("fsdp", None), P("fsdp"), P(None, "fsdp")
    in_specs = (tok, tok, vec, tok, row, row, row, row, row, row, vec, row, vec, col, col, col)
    out_specs = (tok, tok, tok, row, row, row, row, row, row, vec, row, vec, col, col, col)
    return jax.shard_map(shards, mesh=mesh, in_specs=in_specs, out_specs=out_specs, check_vma=False)
```

time: 1190 us -> 318 us (0.27)
  waiting for transfers between devices: 535 us -> 103 us
  blocking collectives: 244 us -> 0 us
  matrix products: 169 us -> 1.34 us
  local copies, waits for them, and re-layouts: 162 us -> 45.6 us
  Pallas kernels: 0 us -> 80 us
  starting transfers between devices: 1.25 us -> 68.1 us
  other arithmetic: 55.3 us -> 16.6 us
  between operations: 17.3 us -> 1.49 us
    all_gather x16 -> x0, waiting for transfers between devices: 296 us -> none  [the longest x2 80.8 us: layer_pass(): lax.all_gather(keyval, 'ctx', axis=0, tiled=True)]
    all_gather x20 -> x0, blocking collectives: 177 us -> none  [the longest x2 46.3 us: layer_pass(): lax.all_gather(row_delta, 'ctx', axis=0, tiled=True)]
    dot_general x110 -> x2, matrix products: 167 us -> 1.34 us  [the longest x1 1.15 us: shards(): jnp.einsum('sre,de->srd', kv, w_keyval, preferred_element_type=F32)]
    reduce_scatter x8 -> x0, waiting for transfers between devices: 164 us -> none  [the longest x1 34.7 us: shards(): lax.psum_scatter(totals[5].astype(jnp.bfloat16), 'fsdp', scatter_dimensio...]
    ppermute x0 -> x59, waiting for transfers between devices: none -> 91.6 us  [the longest x52 78.2 us: over_ctx(): return lax.ppermute(value, 'ctx', [(i, i ^ mask) for i in range(16)])]
    pallas_call x0 -> x9, Pallas kernels: none -> 80 us  [call(): pl.pallas_call(kernel, name=name, out_shape=[jax.ShapeDtypeStruct(s, d) f...]
    while x502 -> x0, local copies, waits for them, and re-layouts: 64.4 us -> none
    psum x1 -> x0, blocking collectives: 62.2 us -> none  [shards(): lax.psum(owned[6].astype(jnp.bfloat16), 'ctx').astype(jnp.float32)]
  transfers between devices with their start and end apart: 29 -> 62, of which waited for: 22 -> 20; matrix products, arithmetic and copies ran while one was open for 20% -> 18% of each run, Pallas kernels for 0% -> 19%
where the time goes in v1:
time: 318 us; the launch traced here: 317 us
  waiting for transfers between devices  103 us (32%)
  Pallas kernels  80 us (25%)
  starting transfers between devices  68.1 us (21%)
  local copies, waits for them, and re-layouts  45.6 us (14%)
  other arithmetic  16.6 us (5%)
    pallas_call x9, Pallas kernels, call(): pl.pallas_call(kernel, name=name, out_shape=[jax.ShapeDtypeStruct(s, d) f...  80 us
    ppermute x52, waiting for transfers between devices, over_ctx(): return lax.ppermute(value, 'ctx', [(i, i ^ mask) for i in range(16)])  78.2 us
    ppermute x52, starting transfers between devices, over_ctx(): return lax.ppermute(value, 'ctx', [(i, i ^ mask) for i in range(16)])  47.4 us
    unnamed x111, local copies, waits for them, and re-layouts  29.8 us
    ppermute x7, waiting for transfers between devices, over_x(): return lax.ppermute(value, 'fsdp', [(0, 1), (1, 0)])  13.4 us
    convert_element_type x14, other arithmetic, add_low(): return sum((t.astype(F32) for t in terms)).astype(BF)  10.7 us
    all_to_all x1, waiting for transfers between devices, shards(): lax.all_to_all(jnp.broadcast_to(by_unit, (units, rep, hd, rows)).reshape(...  9.33 us
  transfers between devices with their start and end apart: 62, of which 20 were waited for; matrix products, arithmetic and copies ran while one was open for 18% of the time, Pallas kernels for 19%

profile of v1, /device:TPU:0, one launch (start us, length us, event | category | flops | bytes accessed | tf_op | source)
XLA Modules:
  0.0 316.6 jit_solution(7173957899546251854)
XLA Ops:
  0.7 1.8 dynamic-slice_bitcast_fusion
  2.5 3.0 collective-permute-start.1
  14.9 1.9 collective-permute-start.14
  16.8 2.6 collective-permute-start.9
  27.4 1.6 dynamic-slice_dynamic-update-slice_fusion.2
  31.1 1.9 dynamic-slice_dynamic-update-slice_fusion
  35.8 1.8 collective-permute-start.16
  43.5 2.3 collective-permute-done.5
  48.0 2.8 collective-permute-done.6
  50.8 3.7 %collective-permute-start.7 = (bf16[128,512]{1,0:T(8,128)(2,1)S(1)}, bf16[128,512]{1,0:T(8,128)(2,1)S(1)}, u32[]{:S(2)}, u32[]{:S(2)}) collective-permute-start(bf16[128,512]{1,0:T(8,128)(2,1)S(1)} %collective-permute-done.4), channel_id=1, source_target_pairs={{0,12},{2,14},{4,8},{6,10},{8,4},{10,6},{12,0},{14,2},{16,28},{18,... | collective-permute-start | bytes 393224 | tf_op jit(solution)/shard_map/ppermute | solution.py:444
  55.2 2.3 collective-permute-done.7
  59.2 2.6 collective-permute-start.12
  63.5 2.6 collective-permute-done.12
  70.7 14.9 %attend.1 = (bf16[2048,512]{1,0:T(8,128)(2,1)}, bf16[192,2048]{1,0:T(8,128)(2,1)}, bf16[16,64,128]{2,1,0:T(8,128)(2,1)}, f32[64,2048]{1,0:T(8,128)}, f32[8,2048]{1,0:T(8,128)}) custom-call(s32[8]{0:T(128)} %stack.86.meta, s32[16]{0:T(128)} %broadcast_xor_fusion.place, bf16[8,128,512]{2,1,0:T(8,128)(2,1)} %bitcast_dynamic-update-slice_fusion.even, ...), custom_call_target="tpu_custom_call" | custom-call | flops 1476395008 | bytes 8388608 | tf_op jit(solution)/shard_map/attend/pallas_call | solution.py:52
  85.6 6.2 %all-to-all-start = ((bf16[16,64,128]{2,1,0:T(8,128)(2,1)}), bf16[16,64,128]{2,1,0:T(8,128)(2,1)S(1)}, u32[]{:S(2)}, u32[]{:S(2)}) async-start(bf16[16,64,128]{2,1,0:T(8,128)(2,1)} %get-tuple-element.49), calls=%async_computation | async-start | bytes 524288 | tf_op jit(solution)/shard_map/all_to_all | solution.py:600
  94.1 5.1 %encoder_rows.1 = (bf16[2,1024,512]{2,1,0:T(8,128)(2,1)}, bf16[512,1024]{1,0:T(8,128)(2,1)}) custom-call(s32[8]{0:T(128)} %stack.86.meta, bf16[2,512,512]{2,1,0:T(8,128)(2,1)} %bitcast.92, bf16[256,1024]{1,0:T(8,128)(2,1)} %own.2, bf16[640,512]{1,0:T(8,128)(2,1)} %copy-done.8, bf16[640,512]{1,0:T(8,128)(2,1)} %collective-permute-done.15.far.far2), custom_call_target="tpu_custom_call" | custom-call | flops 1073741824 | bytes 4194304 | tf_op jit(solution)/shard_map/encoder_rows/pallas_call | solution.py:52
  99.3 2.4 all-to-all-done
  102.4 14.4 %forward.1 = (bf16[2,128,512]{2,1,0:T(8,128)(2,1)}, f32[256,512]{1,0:T(8,128)}, f32[256,512]{1,0:T(8,128)}, bf16[256,512]{1,0:T(8,128)(2,1)}, bf16[2,512,128]{2,...) custom-call(s32[8]{0:T(128)} %stack.86.meta, ...), custom_call_target="tpu_custom_call" | custom-call | flops 3758096384 | bytes 25165824 | tf_op jit(solution)/shard_map/forward/pallas_call | solution.py:52
  116.9 14.7 %backward.1 = (f32[256,512]{1,0:T(8,128)}, bf16[2,512,128]{2,1,0:T(8,128)(2,1)}, bf16[2,1024,256]{2,1,0:T(8,128)(2,1)}, bf16[2,1024,256]{2,1,0:T(8,128)(2,1)}, f...) custom-call(s32[8]{0:T(128)} %stack.86.meta, ...), custom_call_target="tpu_custom_call" | custom-call | flops 2415919104 | bytes 25165824 | tf_op jit(solution)/shard_map/backward/pallas_call | solution.py:52
  132.1 3.5 %all-to-all-start.1 = ((bf16[16,64,128]{2,1,0:T(8,128)(2,1)}), bf16[16,64,128]{2,1,0:T(8,128)(2,1)S(1)}, u32[]{:S(2)}, u32[]{:S(2)}) async-start(bf16[16,64,128]{2,1,0:T(8,128)(2,1)} %bitcast.104), calls=%async_computation.1 | async-start | bytes 524288 | tf_op jit(solution)/shard_map/all_to_all | solution.py:640
  136.3 9.3 %all-to-all-done.1.grads = bf16[16,64,128]{2,1,0:T(8,128)(2,1)S(1)} async-done(((bf16[16,64,128]{2,1,0:T(8,128)(2,1)}), bf16[16,64,128]{2,1,0:T(8,128)(2,1)S(1)}, u32[]{:S(2)}, u32[]{:S(2)}) %all-to-all-start.1) | async-done | bytes 262176 | tf_op jit(solution)/shard_map/all_to_all | solution.py:640
  146.4 16.2 %attend_back.1 = (bf16[16,192,128]{2,1,0:T(8,128)(2,1)}, f32[208,256]{1,0:T(8,128)}, bf16[208,256]{1,0:T(8,128)(2,1)}) custom-call(s32[8]{0:T(128)} %stack.86.meta, bf16[192,2048]{1,0:T(8,128)(2,1)} %get-tuple-element.52.joined, f32[64,2048]{1,0:T(8,128)} %get-tuple-element.53.full, f32[8,2048]{1,0:T(8,128)} %get-tuple-element.54.stats, ...), custom_call_target="tpu_custom_call" | custom-call | flops 3087007744 | bytes 8388608 | tf_op jit(solution)/shard_map/attend_back/pallas_call | solution.py:52
  163.1 4.4 %collective-permute-done.24 = bf16[208,256]{1,0:T(8,128)(2,1)S(1)} collective-permute-done((bf16[208,256]{1,0:T(8,128)(2,1)}, bf16[208,256]{1,0:T(8,128)(2,1)S(1)}, u32[]{:S(2)}, u32[]{:S(2)}) %collective-permute-start.24) | collective-permute-done | bytes 106528 | tf_op jit(solution)/shard_map/ppermute | solution.py:448
  171.4 4.4 %collective-permute-done.25 = bf16[208,256]{1,0:T(8,128)(2,1)S(1)} collective-permute-done((bf16[208,256]{1,0:T(8,128)(2,1)S(1)}, bf16[208,256]{1,0:T(8,128)(2,1)S(1)}, u32[]{:S(2)}, u32[]{:S(2)}) %collective-permute-start.25) | collective-permute-done | bytes 106528 | tf_op jit(solution)/shard_map/ppermute | solution.py:444
  176.6 2.5 fusion.2
  180.6 2.0 collective-permute-start.28
  182.8 5.7 %collective-permute-done.34 = bf16[8,80,512]{2,1,0:T(8,128)(2,1)S(1)} collective-permute-done((bf16[8,80,512]{2,1,0:T(8,128)(2,1)S(1)}, bf16[8,80,512]{2,1,0:T(8,128)(2,1)S(1)}, u32[]{:S(2)}, u32[]{:S(2)}) %collective-permute-start.34) | collective-permute-done | bytes 655392 | tf_op jit(solution)/shard_map/ppermute | solution.py:448
  192.3 4.8 %all-to-all-start.2 = ((bf16[16,192,128]{2,1,0:T(8,128)(2,1)}), bf16[16,192,128]{2,1,0:T(8,128)(2,1)S(1)}, u32[]{:S(2)}, u32[]{:S(2)}) async-start(bf16[16,192,128]{2,1,0:T(8,128)(2,1)} %get-tuple-element.64), calls=%async_computation.2 | async-start | bytes 1572864 | tf_op jit(solution)/shard_map/all_to_all | solution.py:650
  197.6 3.0 place_joined.1
  202.0 1.8 collective-permute-done.35
  204.9 3.3 %collective-permute-done.47 = bf16[8,128,512]{2,1,0:T(8,128)(2,1)} collective-permute-done((bf16[8,128,512]{2,1,0:T(8,128)(2,1)}, bf16[8,128,512]{2,1,0:T(8,128)(2,1)}, u32[]{:S(2)}, u32[]{:S(2)}) %collective-permute-start.47) | collective-permute-done | bytes 1048608 | tf_op jit(solution)/shard_map/ppermute | solution.py:448
  208.2 2.0 fusion
  213.6 2.8 collective-permute-done.36
  216.4 2.6 collective-permute-start.37
  219.0 7.9 %collective-permute-done.48 = bf16[4,128,512]{2,1,0:T(8,128)(2,1)S(1)} collective-permute-done((bf16[4,128,512]{2,1,0:T(8,128)(2,1)S(1)}, bf16[4,128,512]{2,1,0:T(8,128)(2,1)S(1)}, u32[]{:S(2)}, u32[]{:S(2)}) %collective-permute-start.48) | collective-permute-done | bytes 524320 | tf_op jit(solution)/shard_map/ppermute | solution.py:444
  228.5 7.1 %collective-permute-done.21 = bf16[2,1024,128]{2,1,0:T(8,128)(2,1)S(1)} collective-permute-done((bf16[2,1024,128]{2,1,0:T(8,128)(2,1)S(1)}, bf16[2,1024,128]{2,1,0:T(8,128)(2,1)S(1)}, u32[]{:S(2)}, u32[]{:S(2)}) %collective-permute-start.21) | collective-permute-done | bytes 524320 | tf_op jit(solution)/shard_map/ppermute | solution.py:444
  237.1 2.2 collective-permute-start.22
  239.3 2.1 collective-permute-start.38
  242.5 11.8 %collective-permute-done.22 = bf16[2,64,1024]{1,2,0:T(8,128)(2,1)S(1)} collective-permute-done((bf16[2,64,1024]{1,2,0:T(8,128)(2,1)S(1)}, bf16[2,64,1024]{1,2,0:T(8,128)(2,1)S(1)}, u32[]{:S(2)}, u32[]{:S(2)}) %collective-permute-start.22) | collective-permute-done | bytes 262176 | tf_op jit(solution)/shard_map/ppermute | solution.py:444
  256.1 2.5 collective-permute-start.39
  258.7 1.7 collective-permute-start.40
  261.4 23.6 %collective-permute-done.51 = bf16[128,512]{1,0:T(8,128)(2,1)S(1)} collective-permute-done((bf16[128,512]{1,0:T(8,128)(2,1)S(1)}, bf16[128,512]{1,0:T(8,128)(2,1)S(1)}, u32[]{:S(2)}, u32[]{:S(2)}) %collective-permute-start.51) | collective-permute-done | bytes 131104 | tf_op jit(solution)/shard_map/ppermute | solution.py:444
  285.3 2.1 collective-permute-start.53
  294.3 4.9 %collective-permute-done.53.refs_2_ = bf16[2,128,512]{2,1,0:T(8,128)(2,1)S(1)} collective-permute-done((bf16[2,128,512]{2,1,0:T(8,128)(2,1)S(1)}, bf16[2,128,512]{2,1,0:T(8,128)(2,1)S(1)}, u32[]{:S(2)}, u32[]{:S(2)}) %collective-permute-start.53) | collective-permute-done | bytes 262176 | tf_op jit(solution)/shard_map/ppermute | solution.py:444
  299.2 1.8 collective-permute-done.54.refs_3_
  303.0 4.9 %start_grad.1 = f32[2,128,512]{2,1,0:T(8,128)} custom-call(s32[8]{0:T(128)} %stack.86.meta, bf16[2,8,192,128]{3,2,1,0:T(8,128)(2,1)} %bitcast.94, bf16[2,128,512]{2,1,0:T(8,128)(2,1)} %tokens.3, f32[2,512]{1,0:T(2,128)} %copy-done.36, f32[3,512]{1,0:T(4,128)} %copy-done.33, f32[256,512]{1,0:T(8,128)} %get-tuple-element.65.h1g, bf16[256,1536]{1,0:T(8,128)(2,1)} %own.3, ...), custom_call_target="tpu_custom_call" | custom-call | flops 402653184 | bytes 6291456 | tf_op jit(solution)/shard_map/start_grad/pallas_call | solution.py:52
  308.0 3.1 place_cross.1
  312.7 3.9 %place_ffn.1 = (f32[256,2048]{1,0:T(8,128)}, f32[1024,512]{1,0:T(8,128)}) custom-call(s32[8]{0:T(128)} %stack.86.meta, bf16[2,128,512]{2,1,0:T(8,128)(2,1)} %copy-done.4, bf16[2,128,512]{2,1,0:T(8,128)(2,1)} %copy-done.14, bf16[2,128,512]{2,1,0:T(8,128)(2,1)} %copy-done.15, bf16[2,128,512]{2,1,0:T(8,128)(2,1)} %copy-done.16, ...), custom_call_target="tpu_custom_call" | custom-call | bytes 8388608 | tf_op jit(solution)/shard_map/place_ffn/pallas_call | solution.py:52
  (261 shorter events, 78.6 us)
Async XLA Ops:
  2.5 31.4 %collective-permute-start.1 = (bf16[128,512]{1,0:T(8,128)(2,1)}, bf16[128,512]{1,0:T(8,128)(2,1)}, u32[]{:S(2)}, u32[]{:S(2)}) collective-permute-start(bf16[128,512]{1,0:T(8,128)(2,1)} %get-tuple-element.88), channel_id=1, source_target_pairs={{0,8},{2,10},{4,12},{6,14},{8,0},{10,2},{12,4},{14,6},{16,24},{18,... | collective-permute-start | bytes 393224 | tf_op jit(solution)/shard_map/ppermute | solution.py:444
  5.6 30.3 %collective-permute-start.2 = (bf16[128,512]{1,0:T(8,128)(2,1)}, bf16[128,512]{1,0:T(8,128)(2,1)}, u32[]{:S(2)}, u32[]{:S(2)}) collective-permute-start(bf16[128,512]{1,0:T(8,128)(2,1)} %get-tuple-element.88), channel_id=1, source_target_pairs={{0,4},{2,6},{4,0},{6,2},{8,12},{10,14},{12,8},{14,10},{16,20},{18,... | collective-permute-start | bytes 393224 | tf_op jit(solution)/shard_map/ppermute | solution.py:444
  7.1 32.1 %collective-permute-start.3 = (bf16[128,512]{1,0:T(8,128)(2,1)}, bf16[128,512]{1,0:T(8,128)(2,1)}, u32[]{:S(2)}, u32[]{:S(2)}) collective-permute-start(bf16[128,512]{1,0:T(8,128)(2,1)} %get-tuple-element.88), channel_id=1, source_target_pairs={{0,12},{2,14},{4,8},{6,10},{8,4},{10,6},{12,0},{14,2},{16,28},{18,... | collective-permute-start | bytes 393224 | tf_op jit(solution)/shard_map/ppermute | solution.py:444
  14.9 51.9 %collective-permute-start.14 = (bf16[640,512]{1,0:T(8,128)(2,1)}, bf16[640,512]{1,0:T(8,128)(2,1)S(1)}, u32[]{:S(2)}, u32[]{:S(2)}) collective-permute-start(bf16[640,512]{1,0:T(8,128)(2,1)} %dynamic-slice_dynamic-update-slice_fusion.7), channel_id=1, source_target_pairs={{0,1},{1,0},{2,3},{3,2},{4,5},{5,4},{6,7},{7,6},{8,9},{9,8},{10,11... | collective-permute-start | bytes 1966088 | tf_op jit(solution)/shard_map/ppermute | solution.py:448
  16.8 16.2 %collective-permute-start.9 = (bf16[2,32,512]{2,1,0:T(8,128)(2,1)}, bf16[2,32,512]{2,1,0:T(8,128)(2,1)S(1)}, u32[]{:S(2)}, u32[]{:S(2)}) collective-permute-start(bf16[2,32,512]{2,1,0:T(8,128)(2,1)} %param.18), channel_id=1, source_target_pairs={{0,16},{2,18},{4,20},{6,22},{8,24},{10,26},{12,28},{14,30},{16,0},... | collective-permute-start | bytes 196616 | tf_op jit(solution)/shard_map/ppermute | solution.py:444
  33.0 7.9 %collective-permute-start.4 = (bf16[128,512]{1,0:T(8,128)(2,1)}, bf16[128,512]{1,0:T(8,128)(2,1)S(1)}, u32[]{:S(2)}, u32[]{:S(2)}) collective-permute-start(bf16[128,512]{1,0:T(8,128)(2,1)} %get-tuple-element.86), channel_id=1, source_target_pairs={{0,16},{2,18},{4,20},{6,22},{8,24},{10,26},{12,28},{14,30},{16,0},... | collective-permute-start | bytes 393224 | tf_op jit(solution)/shard_map/ppermute | solution.py:444
  34.0 25.0 %collective-permute-start = (bf16[256,256]{1,0:T(8,128)(2,1)S(1)}, bf16[256,256]{1,0:T(8,128)(2,1)S(1)}, u32[]{:S(2)}, u32[]{:S(2)}) collective-permute-start(bf16[256,256]{1,0:T(8,128)(2,1)S(1)} %concatenate.53), channel_id=1, source_target_pairs={{0,1},{1,0},{2,3},{3,2},{4,5},{5,4},{6,7},{7,6},{8,9},{9,8},{10,11... | collective-permute-start | bytes 393224 | tf_op jit(solution)/shard_map/ppermute | solution.py:448
  35.8 26.7 %collective-permute-start.16 = (bf16[1024,512]{1,0:T(8,128)(2,1)}, bf16[1024,512]{1,0:T(8,128)(2,1)}, u32[]{:S(2)}, u32[]{:S(2)}) collective-permute-start(bf16[1024,512]{1,0:T(8,128)(2,1)} %dynamic-slice_dynamic-update-slice_fusion), channel_id=1, source_target_pairs={{0,1},{1,0},{2,3},{3,2},{4,5},{5,4},{6,7},{7,6},{8,9},{9,8},{10,11... | collective-permute-start | bytes 3145736 | tf_op jit(solution)/shard_map/ppermute | solution.py:448
  39.2 20.0 %collective-permute-start.10 = (bf16[2,2,32,512]{3,2,1,0:T(8,128)(2,1)S(1)}, bf16[2,2,32,512]{3,2,1,0:T(8,128)(2,1)S(1)}, u32[]{:S(2)}, u32[]{:S(2)}) collective-permute-start(bf16[2,2,32,512]{3,2,1,0:T(8,128)(2,1)S(1)} %pad_maximum_fusion.3), channel_id=1, source_target_pairs={{0,8},{2,10},{4,12},{6,14},{8,0},{10,2},{12,4},{14,6},{16,24},{18,... | collective-permute-start | bytes 393224 | tf_op jit(solution)/shard_map/ppermute | solution.py:444
  59.0 10.7 %collective-permute-start.8 = (bf16[8,128,512]{2,1,0:T(8,128)(2,1)}, bf16[8,128,512]{2,1,0:T(8,128)(2,1)S(1)}, u32[]{:S(2)}, u32[]{:S(2)}) collective-permute-start(bf16[8,128,512]{2,1,0:T(8,128)(2,1)} %bitcast_dynamic-update-slice_fusion.even), channel_id=1, source_target_pairs={{0,2},{2,0},{4,6},{6,4},{8,10},{10,8},{12,14},{14,12},{16,18},{18,... | collective-permute-start | bytes 3145736 | tf_op jit(solution)/shard_map/ppermute | solution.py:444
  62.6 39.1 %collective-permute-start.17 = (bf16[1024,512]{1,0:T(8,128)(2,1)}, bf16[1024,512]{1,0:T(8,128)(2,1)}, u32[]{:S(2)}, u32[]{:S(2)}) collective-permute-start(bf16[1024,512]{1,0:T(8,128)(2,1)} %collective-permute-done.16.near3), channel_id=1, source_target_pairs={{0,2},{2,0},{4,6},{6,4},{8,10},{10,8},{12,14},{14,12},{16,18},{18,... | collective-permute-start | bytes 3145736 | tf_op jit(solution)/shard_map/ppermute | solution.py:444
  66.8 26.2 %collective-permute-start.13 = (bf16[8,2,32,512]{3,2,1,0:T(8,128)(2,1)}, bf16[8,2,32,512]{3,2,1,0:T(8,128)(2,1)S(1)}, u32[]{:S(2)}, u32[]{:S(2)}) collective-permute-start(bf16[8,2,32,512]{3,2,1,0:T(8,128)(2,1)} %get-tuple-element.91), channel_id=1, source_target_pairs={{0,2},{2,0},{4,6},{6,4},{8,10},{10,8},{12,14},{14,12},{16,18},{18,... | collective-permute-start | bytes 1572872 | tf_op jit(solution)/shard_map/ppermute | solution.py:444
  66.8 27.3 %collective-permute-start.15 = (bf16[640,512]{1,0:T(8,128)(2,1)S(1)}, bf16[640,512]{1,0:T(8,128)(2,1)}, u32[]{:S(2)}, u32[]{:S(2)}) collective-permute-start(bf16[640,512]{1,0:T(8,128)(2,1)S(1)} %collective-permute-done.14.near.near2), channel_id=1, source_target_pairs={{0,2},{2,0},{4,6},{6,4},{8,10},{10,8},{12,14},{14,12},{16,18},{18,... | collective-permute-start | bytes 1966088 | tf_op jit(solution)/shard_map/ppermute | solution.py:444
  85.6 16.1 %all-to-all-start = ((bf16[16,64,128]{2,1,0:T(8,128)(2,1)}), bf16[16,64,128]{2,1,0:T(8,128)(2,1)S(1)}, u32[]{:S(2)}, u32[]{:S(2)}) async-start(bf16[16,64,128]{2,1,0:T(8,128)(2,1)} %get-tuple-element.49), calls=%async_computation | async-start | bytes 524288 | tf_op jit(solution)/shard_map/all_to_all | solution.py:600
  116.8 59.8 %collective-permute-start.46 = (bf16[2,8,128,512]{3,2,1,0:T(8,128)(2,1)}, bf16[2,8,128,512]{3,2,1,0:T(8,128)(2,1)}, u32[]{:S(2)}, u32[]{:S(2)}) collective-permute-start(bf16[2,8,128,512]{3,2,1,0:T(8,128)(2,1)} %get-tuple-element.79), channel_id=1, source_target_pairs={{0,2},{2,0},{4,6},{6,4},{8,10},{10,8},{12,14},{14,12},{16,18},{18,... | collective-permute-start | bytes 6291464 | tf_op jit(solution)/shard_map/ppermute | solution.py:444
  131.6 37.9 %collective-permute-start.33 = (bf16[2,8,80,512]{3,2,1,0:T(8,128)(2,1)}, bf16[2,8,80,512]{3,2,1,0:T(8,128)(2,1)}, u32[]{:S(2)}, u32[]{:S(2)}) collective-permute-start(bf16[2,8,80,512]{3,2,1,0:T(8,128)(2,1)} %get-tuple-element.73), channel_id=1, source_target_pairs={{0,2},{2,0},{4,6},{6,4},{8,10},{10,8},{12,14},{14,12},{16,18},{18,... | collective-permute-start | bytes 3932168 | tf_op jit(solution)/shard_map/ppermute | solution.py:444
  132.1 13.5 %all-to-all-start.1 = ((bf16[16,64,128]{2,1,0:T(8,128)(2,1)}), bf16[16,64,128]{2,1,0:T(8,128)(2,1)S(1)}, u32[]{:S(2)}, u32[]{:S(2)}) async-start(bf16[16,64,128]{2,1,0:T(8,128)(2,1)} %bitcast.104), calls=%async_computation.1 | async-start | bytes 524288 | tf_op jit(solution)/shard_map/all_to_all | solution.py:640
  135.8 44.0 %collective-permute-start.18 = (bf16[384,512]{1,0:T(8,128)(2,1)S(1)}, bf16[384,512]{1,0:T(8,128)(2,1)S(1)}, u32[]{:S(2)}, u32[]{:S(2)}) collective-permute-start(bf16[384,512]{1,0:T(8,128)(2,1)S(1)} %pad_maximum_fusion), channel_id=1, source_target_pairs={{0,1},{1,0},{2,3},{3,2},{4,5},{5,4},{6,7},{7,6},{8,9},{9,8},{10,11... | collective-permute-start | bytes 1179656 | tf_op jit(solution)/shard_map/ppermute | solution.py:448
  168.4 7.4 %collective-permute-start.25 = (bf16[208,256]{1,0:T(8,128)(2,1)S(1)}, bf16[208,256]{1,0:T(8,128)(2,1)S(1)}, u32[]{:S(2)}, u32[]{:S(2)}) collective-permute-start(bf16[208,256]{1,0:T(8,128)(2,1)S(1)} %add_convert_fusion.12), channel_id=1, source_target_pairs={{0,16},{2,18},{4,20},{6,22},{8,24},{10,26},{12,28},{14,30},{16,0},... | collective-permute-start | bytes 319496 | tf_op jit(solution)/shard_map/ppermute | solution.py:444
  170.8 17.7 %collective-permute-start.34 = (bf16[8,80,512]{2,1,0:T(8,128)(2,1)S(1)}, bf16[8,80,512]{2,1,0:T(8,128)(2,1)S(1)}, u32[]{:S(2)}, u32[]{:S(2)}) collective-permute-start(bf16[8,80,512]{2,1,0:T(8,128)(2,1)S(1)} %fusion.5), channel_id=1, source_target_pairs={{0,1},{1,0},{2,3},{3,2},{4,5},{5,4},{6,7},{7,6},{8,9},{9,8},{10,11... | collective-permute-start | bytes 1966088 | tf_op jit(solution)/shard_map/ppermute | solution.py:448
  179.1 29.1 %collective-permute-start.47 = (bf16[8,128,512]{2,1,0:T(8,128)(2,1)}, bf16[8,128,512]{2,1,0:T(8,128)(2,1)}, u32[]{:S(2)}, u32[]{:S(2)}) collective-permute-start(bf16[8,128,512]{2,1,0:T(8,128)(2,1)} %fusion.2), channel_id=1, source_target_pairs={{0,1},{1,0},{2,3},{3,2},{4,5},{5,4},{6,7},{7,6},{8,9},{9,8},{10,11... | collective-permute-start | bytes 3145736 | tf_op jit(solution)/shard_map/ppermute | solution.py:448
  179.7 32.0 %collective-permute-start.20 = (bf16[2,1024,256]{2,1,0:T(8,128)(2,1)}, bf16[2,1024,256]{2,1,0:T(8,128)(2,1)}, u32[]{:S(2)}, u32[]{:S(2)}) collective-permute-start(bf16[2,1024,256]{2,1,0:T(8,128)(2,1)} %get-tuple-element.67), channel_id=1, source_target_pairs={{0,2},{2,0},{4,6},{6,4},{8,10},{10,8},{12,14},{14,12},{16,18},{18,... | collective-permute-start | bytes 3145736 | tf_op jit(solution)/shard_map/ppermute | solution.py:444
  180.6 10.0 %collective-permute-start.28 = (bf16[208,256]{1,0:T(8,128)(2,1)S(1)}, bf16[208,256]{1,0:T(8,128)(2,1)}, u32[]{:S(2)}, u32[]{:S(2)}) collective-permute-start(bf16[208,256]{1,0:T(8,128)(2,1)S(1)} %add_convert_fusion.11.refs_0_), channel_id=1, source_target_pairs={{0,12},{2,14},{4,8},{6,10},{8,4},{10,6},{12,0},{14,2},{16,28},{18,... | collective-permute-start | bytes 319496 | tf_op jit(solution)/shard_map/ppermute | solution.py:444
  182.6 8.5 %collective-permute-start.29 = (bf16[208,256]{1,0:T(8,128)(2,1)S(1)}, bf16[208,256]{1,0:T(8,128)(2,1)S(1)}, u32[]{:S(2)}, u32[]{:S(2)}) collective-permute-start(bf16[208,256]{1,0:T(8,128)(2,1)S(1)} %add_convert_fusion.11.refs_0_), channel_id=1, source_target_pairs={{0,2},{2,0},{4,6},{6,4},{8,10},{10,8},{12,14},{14,12},{16,18},{18,... | collective-permute-start | bytes 319496 | tf_op jit(solution)/shard_map/ppermute | solution.py:444
  191.2 12.5 %collective-permute-start.35 = (bf16[4,80,512]{2,1,0:T(8,128)(2,1)}, bf16[4,80,512]{2,1,0:T(8,128)(2,1)}, u32[]{:S(2)}, u32[]{:S(2)}) collective-permute-start(bf16[4,80,512]{2,1,0:T(8,128)(2,1)} %slice.255), channel_id=1, source_target_pairs={{0,4},{2,6},{4,0},{6,2},{8,12},{10,14},{12,8},{14,10},{16,20},{18,... | collective-permute-start | bytes 983048 | tf_op jit(solution)/shard_map/ppermute | solution.py:444
  192.3 109.8 %all-to-all-start.2 = ((bf16[16,192,128]{2,1,0:T(8,128)(2,1)}), bf16[16,192,128]{2,1,0:T(8,128)(2,1)S(1)}, u32[]{:S(2)}, u32[]{:S(2)}) async-start(bf16[16,192,128]{2,1,0:T(8,128)(2,1)} %get-tuple-element.64), calls=%async_computation.2 | async-start | bytes 1572864 | tf_op jit(solution)/shard_map/all_to_all | solution.py:650
  197.1 63.4 %collective-permute-start.19 = (bf16[384,512]{1,0:T(8,128)(2,1)}, bf16[384,512]{1,0:T(8,128)(2,1)S(1)}, u32[]{:S(2)}, u32[]{:S(2)}) collective-permute-start(bf16[384,512]{1,0:T(8,128)(2,1)} %copy-done.11), channel_id=1, source_target_pairs={{0,2},{2,0},{4,6},{6,4},{8,10},{10,8},{12,14},{14,12},{16,18},{18,... | collective-permute-start | bytes 1179656 | tf_op jit(solution)/shard_map/ppermute | solution.py:444
  204.8 11.5 %collective-permute-start.36 = (bf16[2,80,512]{2,1,0:T(8,128)(2,1)S(1)}, bf16[2,80,512]{2,1,0:T(8,128)(2,1)S(1)}, u32[]{:S(2)}, u32[]{:S(2)}) collective-permute-start(bf16[2,80,512]{2,1,0:T(8,128)(2,1)S(1)} %slice.257), channel_id=1, source_target_pairs={{0,8},{2,10},{4,12},{6,14},{8,0},{10,2},{12,4},{14,6},{16,24},{18,... | collective-permute-start | bytes 491528 | tf_op jit(solution)/shard_map/ppermute | solution.py:444
  210.2 16.7 %collective-permute-start.48 = (bf16[4,128,512]{2,1,0:T(8,128)(2,1)S(1)}, bf16[4,128,512]{2,1,0:T(8,128)(2,1)S(1)}, u32[]{:S(2)}, u32[]{:S(2)}) collective-permute-start(bf16[4,128,512]{2,1,0:T(8,128)(2,1)S(1)} %slice.263), channel_id=1, source_target_pairs={{0,4},{2,6},{4,0},{6,2},{8,12},{10,14},{12,8},{14,10},{16,20},{18,... | collective-permute-start | bytes 1572872 | tf_op jit(solution)/shard_map/ppermute | solution.py:444
  212.9 22.7 %collective-permute-start.21 = (bf16[2,1024,128]{2,1,0:T(8,128)(2,1)S(1)}, bf16[2,1024,128]{2,1,0:T(8,128)(2,1)S(1)}, u32[]{:S(2)}, u32[]{:S(2)}) collective-permute-start(bf16[2,1024,128]{2,1,0:T(8,128)(2,1)S(1)} %add_convert_fusion.6), channel_id=1, source_target_pairs={{0,4},{2,6},{4,0},{6,2},{8,12},{10,14},{12,8},{14,10},{16,20},{18,... | collective-permute-start | bytes 1572872 | tf_op jit(solution)/shard_map/ppermute | solution.py:444
  216.4 22.9 %collective-permute-start.37 = (bf16[80,512]{1,0:T(8,128)(2,1)S(1)}, bf16[80,512]{1,0:T(8,128)(2,1)S(1)}, u32[]{:S(2)}, u32[]{:S(2)}) collective-permute-start(bf16[80,512]{1,0:T(8,128)(2,1)S(1)} %slice_bitcast_fusion.2), channel_id=1, source_target_pairs={{0,16},{2,18},{4,20},{6,22},{8,24},{10,26},{12,28},{14,30},{16,0},... | collective-permute-start | bytes 245768 | tf_op jit(solution)/shard_map/ppermute | solution.py:444
  227.1 14.3 %collective-permute-start.49 = (bf16[2,128,512]{2,1,0:T(8,128)(2,1)S(1)}, bf16[2,128,512]{2,1,0:T(8,128)(2,1)S(1)}, u32[]{:S(2)}, u32[]{:S(2)}) collective-permute-start(bf16[2,128,512]{2,1,0:T(8,128)(2,1)S(1)} %slice.265), channel_id=1, source_target_pairs={{0,8},{2,10},{4,12},{6,14},{8,0},{10,2},{12,4},{14,6},{16,24},{18,... | collective-permute-start | bytes 786440 | tf_op jit(solution)/shard_map/ppermute | solution.py:444
  237.1 17.2 %collective-permute-start.22 = (bf16[2,64,1024]{1,2,0:T(8,128)(2,1)S(1)}, bf16[2,64,1024]{1,2,0:T(8,128)(2,1)S(1)}, u32[]{:S(2)}, u32[]{:S(2)}) collective-permute-start(bf16[2,64,1024]{1,2,0:T(8,128)(2,1)S(1)} %slice.249), channel_id=1, source_target_pairs={{0,8},{2,10},{4,12},{6,14},{8,0},{10,2},{12,4},{14,6},{16,24},{18,... | collective-permute-start | bytes 786440 | tf_op jit(solution)/shard_map/ppermute | solution.py:444
  239.3 16.7 %collective-permute-start.38 = (bf16[80,512]{1,0:T(8,128)(2,1)S(1)}, bf16[80,512]{1,0:T(8,128)(2,1)S(1)}, u32[]{:S(2)}, u32[]{:S(2)}) collective-permute-start(bf16[80,512]{1,0:T(8,128)(2,1)S(1)} %fusion.9), channel_id=1, source_target_pairs={{0,16},{2,18},{4,20},{6,22},{8,24},{10,26},{12,28},{14,30},{16,0},... | collective-permute-start | bytes 245768 | tf_op jit(solution)/shard_map/ppermute | solution.py:444
  241.5 18.9 %collective-permute-start.50 = (bf16[128,512]{1,0:T(8,128)(2,1)S(1)}, bf16[128,512]{1,0:T(8,128)(2,1)S(1)}, u32[]{:S(2)}, u32[]{:S(2)}) collective-permute-start(bf16[128,512]{1,0:T(8,128)(2,1)S(1)} %slice_bitcast_fusion), channel_id=1, source_target_pairs={{0,16},{2,18},{4,20},{6,22},{8,24},{10,26},{12,28},{14,30},{16,0},... | collective-permute-start | bytes 393224 | tf_op jit(solution)/shard_map/ppermute | solution.py:444
  254.7 30.5 %collective-permute-start.23 = (bf16[2,32,1024]{1,2,0:T(8,128)(2,1)S(1)}, bf16[2,32,1024]{1,2,0:T(8,128)(2,1)S(1)}, u32[]{:S(2)}, u32[]{:S(2)}) collective-permute-start(bf16[2,32,1024]{1,2,0:T(8,128)(2,1)S(1)} %slice.251), channel_id=1, source_target_pairs={{0,16},{2,18},{4,20},{6,22},{8,24},{10,26},{12,28},{14,30},{16,0},... | collective-permute-start | bytes 393224 | tf_op jit(solution)/shard_map/ppermute | solution.py:444
  256.1 29.1 %collective-permute-start.39 = (bf16[2,80,512]{2,1,0:T(8,128)(2,1)S(1)}, bf16[2,80,512]{2,1,0:T(8,128)(2,1)S(1)}, u32[]{:S(2)}, u32[]{:S(2)}) collective-permute-start(bf16[2,80,512]{2,1,0:T(8,128)(2,1)S(1)} %pad_maximum_fusion.2.refs_0_), channel_id=1, source_target_pairs={{0,8},{2,10},{4,12},{6,14},{8,0},{10,2},{12,4},{14,6},{16,24},{18,... | collective-permute-start | bytes 491528 | tf_op jit(solution)/shard_map/ppermute | solution.py:444
  258.7 28.7 %collective-permute-start.40 = (bf16[2,80,512]{2,1,0:T(8,128)(2,1)S(1)}, bf16[2,80,512]{2,1,0:T(8,128)(2,1)S(1)}, u32[]{:S(2)}, u32[]{:S(2)}) collective-permute-start(bf16[2,80,512]{2,1,0:T(8,128)(2,1)S(1)} %pad_maximum_fusion.2.refs_0_), channel_id=1, source_target_pairs={{0,4},{2,6},{4,0},{6,2},{8,12},{10,14},{12,8},{14,10},{16,20},{18,... | collective-permute-start | bytes 491528 | tf_op jit(solution)/shard_map/ppermute | solution.py:444
  260.4 24.7 %collective-permute-start.51 = (bf16[128,512]{1,0:T(8,128)(2,1)S(1)}, bf16[128,512]{1,0:T(8,128)(2,1)S(1)}, u32[]{:S(2)}, u32[]{:S(2)}) collective-permute-start(bf16[128,512]{1,0:T(8,128)(2,1)S(1)} %fusion.8), channel_id=1, source_target_pairs={{0,16},{2,18},{4,20},{6,22},{8,24},{10,26},{12,28},{14,30},{16,0},... | collective-permute-start | bytes 393224 | tf_op jit(solution)/shard_map/ppermute | solution.py:444
  260.5 28.9 %collective-permute-start.41 = (bf16[2,80,512]{2,1,0:T(8,128)(2,1)S(1)}, bf16[2,80,512]{2,1,0:T(8,128)(2,1)S(1)}, u32[]{:S(2)}, u32[]{:S(2)}) collective-permute-start(bf16[2,80,512]{2,1,0:T(8,128)(2,1)S(1)} %pad_maximum_fusion.2.refs_0_), channel_id=1, source_target_pairs={{0,12},{2,14},{4,8},{6,10},{8,4},{10,6},{12,0},{14,2},{16,28},{18,... | collective-permute-start | bytes 491528 | tf_op jit(solution)/shard_map/ppermute | solution.py:444
  285.2 9.2 %collective-permute-start.52 = (bf16[2,128,512]{2,1,0:T(8,128)(2,1)S(1)}, bf16[2,128,512]{2,1,0:T(8,128)(2,1)S(1)}, u32[]{:S(2)}, u32[]{:S(2)}) collective-permute-start(bf16[2,128,512]{2,1,0:T(8,128)(2,1)S(1)} %pad_maximum_fusion.1.refs_0_), channel_id=1, source_target_pairs={{0,8},{2,10},{4,12},{6,14},{8,0},{10,2},{12,4},{14,6},{16,24},{18,... | collective-permute-start | bytes 786440 | tf_op jit(solution)/shard_map/ppermute | solution.py:444
  285.3 13.9 %collective-permute-start.53 = (bf16[2,128,512]{2,1,0:T(8,128)(2,1)S(1)}, bf16[2,128,512]{2,1,0:T(8,128)(2,1)S(1)}, u32[]{:S(2)}, u32[]{:S(2)}) collective-permute-start(bf16[2,128,512]{2,1,0:T(8,128)(2,1)S(1)} %pad_maximum_fusion.1.refs_0_), channel_id=1, source_target_pairs={{0,4},{2,6},{4,0},{6,2},{8,12},{10,14},{12,8},{14,10},{16,20},{18,... | collective-permute-start | bytes 786440 | tf_op jit(solution)/shard_map/ppermute | solution.py:444
  287.3 13.7 %collective-permute-start.54 = (bf16[2,128,512]{2,1,0:T(8,128)(2,1)S(1)}, bf16[2,128,512]{2,1,0:T(8,128)(2,1)S(1)}, u32[]{:S(2)}, u32[]{:S(2)}) collective-permute-start(bf16[2,128,512]{2,1,0:T(8,128)(2,1)S(1)} %pad_maximum_fusion.1.refs_0_), channel_id=1, source_target_pairs={{0,12},{2,14},{4,8},{6,10},{8,4},{10,6},{12,0},{14,2},{16,28},{18,... | collective-permute-start | bytes 786440 | tf_op jit(solution)/shard_map/ppermute | solution.py:444
  291.9 16.1 %collective-permute-start.45 = (bf16[2,80,512]{2,1,0:T(8,128)(2,1)S(1)}, bf16[2,80,512]{2,1,0:T(8,128)(2,1)}, u32[]{:S(2)}, u32[]{:S(2)}) collective-permute-start(bf16[2,80,512]{2,1,0:T(8,128)(2,1)S(1)} %collective-permute-done.41.refs_3_), channel_id=1, source_target_pairs={{0,2},{2,0},{4,6},{6,4},{8,10},{10,8},{12,14},{14,12},{16,18},{18,... | collective-permute-start | bytes 491528 | tf_op jit(solution)/shard_map/ppermute | solution.py:444
  292.6 18.5 %collective-permute-start.55 = (bf16[2,128,512]{2,1,0:T(8,128)(2,1)S(1)}, bf16[2,128,512]{2,1,0:T(8,128)(2,1)S(1)}, u32[]{:S(2)}, u32[]{:S(2)}) collective-permute-start(bf16[2,128,512]{2,1,0:T(8,128)(2,1)S(1)} %pad_maximum_fusion.1.refs_0_), channel_id=1, source_target_pairs={{0,2},{2,0},{4,6},{6,4},{8,10},{10,8},{12,14},{14,12},{16,18},{18,... | collective-permute-start | bytes 786440 | tf_op jit(solution)/shard_map/ppermute | solution.py:444
  294.3 16.8 %collective-permute-start.56 = (bf16[2,128,512]{2,1,0:T(8,128)(2,1)S(1)}, bf16[2,128,512]{2,1,0:T(8,128)(2,1)S(1)}, u32[]{:S(2)}, u32[]{:S(2)}) collective-permute-start(bf16[2,128,512]{2,1,0:T(8,128)(2,1)S(1)} %collective-permute-done.52.refs_1_), channel_id=1, source_target_pairs={{0,2},{2,0},{4,6},{6,4},{8,10},{10,8},{12,14},{14,12},{16,18},{18,... | collective-permute-start | bytes 786440 | tf_op jit(solution)/shard_map/ppermute | solution.py:444
  299.2 11.9 %collective-permute-start.57 = (bf16[2,128,512]{2,1,0:T(8,128)(2,1)S(1)}, bf16[2,128,512]{2,1,0:T(8,128)(2,1)S(1)}, u32[]{:S(2)}, u32[]{:S(2)}) collective-permute-start(bf16[2,128,512]{2,1,0:T(8,128)(2,1)S(1)} %collective-permute-done.53.refs_2_), channel_id=1, source_target_pairs={{0,2},{2,0},{4,6},{6,4},{8,10},{10,8},{12,14},{14,12},{16,18},{18,... | collective-permute-start | bytes 786440 | tf_op jit(solution)/shard_map/ppermute | solution.py:444
  301.0 10.1 %collective-permute-start.58 = (bf16[2,128,512]{2,1,0:T(8,128)(2,1)S(1)}, bf16[2,128,512]{2,1,0:T(8,128)(2,1)S(1)}, u32[]{:S(2)}, u32[]{:S(2)}) collective-permute-start(bf16[2,128,512]{2,1,0:T(8,128)(2,1)S(1)} %collective-permute-done.54.refs_3_), channel_id=1, source_target_pairs={{0,2},{2,0},{4,6},{6,4},{8,10},{10,8},{12,14},{14,12},{16,18},{18,... | collective-permute-start | bytes 786440 | tf_op jit(solution)/shard_map/ppermute | solution.py:444
  (58 other events, 793.7 us)

commit v2 on v1

v2 whole, which is shorter than its diff:
```python
import functools
import math

import jax
import jax.numpy as jnp
from jax import lax
from jax.experimental import pallas as pl
from jax.experimental.pallas import tpu as pltpu
from jax.sharding import PartitionSpec as P

H = 8
EPS = 1e-05
F32 = jnp.float32
BF = jnp.bfloat16
LOG2E = 1.4426950408889634
VMEM_LIMIT = 56 * 1024 * 1024


def nn(a, b):
    return lax.dot_general(a, b, (((1,), (0,)), ((), ())), preferred_element_type=F32)


def nt(a, b):
    return lax.dot_general(a, b, (((1,), (1,)), ((), ())), preferred_element_type=F32)


def flip(v):
    return jnp.transpose(v)


def normalise(v):
    centred = v - jnp.mean(v, axis=-1, keepdims=True)
    r = lax.rsqrt(jnp.mean(centred * centred, axis=-1, keepdims=True) + EPS)
    return centred * r, r


def norm_back(grad, gain, xhat, r):
    u = grad * gain
    return r * (u - jnp.mean(u, axis=-1, keepdims=True) - xhat * jnp.mean(u * xhat, axis=-1, keepdims=True))


def aligned(index, size):
    return pl.ds(pl.multiple_of(index, size), size)


VM = pl.BlockSpec(memory_space=pltpu.VMEM)
SM = pl.BlockSpec(memory_space=pltpu.SMEM)
ANY = pl.BlockSpec(memory_space=pl.ANY)


TOOK = dict(
    split=1.7, prepare=2.0, pack=3.7, unpack=1.7, attend=15.0, encoder_rows=6.0, forward=15.0, cross_back=10.6, hidden_back=4.0,
    weights_back=7.2, attend_back_1=8.4, attend_back_2=10.3, start_grad=5.0, encoder_back=2.8, place=5.0, place_cross=3.1,
)
PER_MICROSECOND = 3_500_000


def cost_of(name):
    return pl.CostEstimate(flops=0, bytes_accessed=int(TOOK.get(name, 2.5) * PER_MICROSECOND), transcendentals=0)


def call(kernel, name, outs, in_specs, scratch, args, out_specs=None, after=(), grid=()):
    count = len(in_specs)

    def body(*refs):
        kernel(*refs[:count], *refs[count + len(after) :])

    return pl.pallas_call(
        body,
        name=name,
        grid=grid,
        out_shape=[jax.ShapeDtypeStruct(s, d) for s, d in outs],
        in_specs=list(in_specs) + [ANY] * len(after),
        out_specs=out_specs or [VM] * len(outs),
        scratch_shapes=scratch,
        compiler_params=pltpu.CompilerParams(vmem_limit_bytes=VMEM_LIMIT),
        cost_estimate=cost_of(name),
    )(*args, *after)


class Placer:
    def __init__(self, sems, x, c):
        self.sems, self.x, self.c, self.used = sems, x, c, 0

    def copy(self, src, dst):
        copy = pltpu.make_async_copy(src, dst, self.sems.at[self.used])
        self.used += 1
        copy.start()
        return copy

    def lay(self, own, near, far, dst, row0, blocks):
        rows = own.shape[0]
        half = rows // 2
        base = (1 - self.x) * rows
        copies = [self.copy(own, dst.at[aligned(self.x * rows, rows)])]
        for b in range(blocks):
            cols = pl.ds(b * 512, 512)
            part = pl.ds(row0 + b * half, half)
            copies.append(self.copy(near.at[part], dst.at[aligned(base + self.c * half, half), cols]))
            copies.append(self.copy(far.at[part], dst.at[aligned(base + (1 - self.c) * half, half), cols]))
        return copies


def wait(copies):
    for copy in copies:
        copy.wait()


def split_kernel(meta, tokens, encoder, mine, others):
    rows, span = tokens.shape[1], encoder.shape[1]
    for out, s in ((others, 1 - meta[9]), (mine, meta[9])):
        out[0:rows, :] = tokens[s]
        for k in range(encoder.shape[0]):
            out[rows + k * span : rows + (k + 1) * span, :] = encoder[k]


ORDER = (0, 4, 2, 6, 8, 12, 10, 14, 1, 5, 3, 7, 9, 13, 11, 15)


def attend_kernel(meta, step, gains, shifts, wh, *refs):
    blocks, (xhat_out, joined_out, heads_out, full_out, stats_out, normed, keys) = refs[:-7], refs[-7:]
    n, width = xhat_out.shape
    hd = joined_out.shape[0] // 3
    rows = heads_out.shape[2]
    stats_out[...] = jnp.zeros_like(stats_out)
    for k, block in enumerate(blocks):
        xhat, r = normalise(block[0:rows, :].astype(F32) + step[...])
        at = aligned((meta[7] ^ ORDER[k] if len(blocks) == 16 else k) * rows, rows)
        xhat_out[at, :] = xhat.astype(BF)
        normed[at, :] = (xhat * gains[0:1, :] + shifts[0:1, :]).astype(BF)
        stats_out[1:2, at] = flip(jnp.broadcast_to(r, (rows, 128)))[0:1, :]
    for b in range(n // 512):
        cols = pl.ds(b * 512, 512)
        joined_out[:, cols] = nt(wh[...], normed[cols, :]).astype(BF)
    keys[...] = flip(joined_out[hd : 2 * hd, :].astype(F32)).astype(BF)
    factor = LOG2E / math.sqrt(hd)
    wide = 256

    def query_block(b, carry):
        cols = aligned(b * wide, wide)
        scores = nn(keys[...], joined_out[0:hd, cols]) * factor
        peak = jnp.max(scores, axis=0, keepdims=True)
        shares = jnp.exp2(scores - peak)
        total = jnp.sum(shares, axis=0, keepdims=True)
        out = nn(joined_out[2 * hd : 3 * hd, :], shares.astype(BF)) / total
        full_out[:, cols] = out
        stats_out[0:1, cols] = peak + jnp.log2(total)
        for part in range(wide // rows):
            heads_out[b * (wide // rows) + part] = out[:, part * rows : (part + 1) * rows].astype(BF)
        return carry

    lax.fori_loop(0, n // wide, query_block, 0)


def key_blocks(first, joined, full, stats, grads, keys, values, gout, key_grads, query_acc):
    n = full.shape[1]
    hd = joined.shape[0] // 3
    rows = grads.shape[2]
    span = keys.shape[0]
    scale = 1.0 / math.sqrt(hd)
    factor = LOG2E * scale
    for j in range(grads.shape[0]):
        gout[:, j * rows : (j + 1) * rows] = grads[j]
    mine = pl.ds(first, span)
    keys[...] = flip(joined[hd : 2 * hd, mine].astype(F32)).astype(BF)
    values[...] = flip(joined[2 * hd : 3 * hd, mine].astype(F32)).astype(BF)
    delta = jnp.sum(gout[...].astype(F32) * full[...], axis=0, keepdims=True)
    lse = stats[0:1, :]
    wide = 256

    def key_block(b, carry):
        at = aligned(b * wide, wide)
        queries = joined[0:hd, :]
        shares = jnp.exp2(nn(keys[at, :], queries) * factor - lse)
        share_grad = nn(values[at, :], gout[...])
        score_grad = (shares * (share_grad - delta)).astype(BF)
        key_grads[0:hd, at] = (nt(queries, score_grad) * scale).astype(BF)
        key_grads[hd : 2 * hd, at] = nt(gout[...], shares.astype(BF)).astype(BF)
        query_acc[...] += nn(joined[hd : 2 * hd, aligned(first + b * wide, wide)], score_grad)
        return carry

    lax.fori_loop(0, span // wide, key_block, 0)


def attend_back_first(joined, full, stats, grads, query_out, key_out, keys, values, gout):
    query_out[...] = jnp.zeros_like(query_out)
    key_blocks(0, joined, full, stats, grads, keys, values, gout, key_out, query_out)


def attend_back_second(
    meta, joined, full, stats, grads, query_in, key_in, xhat, gains, shifts, wh, extra, joined_grad_out, keep_out, send_out,
    keys, values, gout, key_grads, query_acc, lhs, whole,
):
    x, active, slot = meta[0], meta[3], meta[4]
    n, width = xhat.shape
    hd = joined.shape[0] // 3
    half = width // 2
    rows = grads.shape[2]
    scale = 1.0 / math.sqrt(hd)
    query_acc[...] = query_in[...]
    key_blocks(n // 2, joined, full, stats, grads, keys, values, gout, key_grads, query_acc)
    lhs[0:hd, :] = (query_acc[...] * scale).astype(BF)
    lhs[hd : 3 * hd, 0 : n // 2] = key_in[...]
    lhs[hd : 3 * hd, n // 2 :] = key_grads[...]
    for j in range(joined_grad_out.shape[0]):
        joined_grad_out[j] = lhs[0 : 3 * hd, j * rows : (j + 1) * rows]

    gain, shift = gains[0:1, :], shifts[0:1, :]
    grad = lhs[0 : 3 * hd, :].astype(F32)
    r = stats[1:2, :]
    weight = wh[...].astype(F32)
    bias = jnp.sum(weight * shift, axis=1, keepdims=True)
    mixed_mean = jnp.sum(grad * (joined[...].astype(F32) - bias), axis=0, keepdims=True) * (1.0 / width)
    tail = lhs.shape[0] - 3 * hd
    first = lax.broadcasted_iota(jnp.int32, (tail, n), 0) == 0
    lhs[3 * hd :, :] = jnp.where(first, mixed_mean * r, 0.0).astype(BF)
    product = nn(lhs[...], xhat[...])
    m = product[0 : 3 * hd]
    sums = jnp.sum(grad, axis=1, keepdims=True)
    scaled_sums = jnp.sum(grad * r, axis=1, keepdims=True)
    lead = gain * jnp.sum(weight * scaled_sums, axis=0, keepdims=True)
    start_sum = lead - jnp.mean(lead, axis=1, keepdims=True) - product[3 * hd : 3 * hd + 1]
    on = active.astype(F32)
    whole[0 : 3 * hd, :] = (m * gain + sums * shift) * on
    gain_grad = jnp.sum(weight * m, axis=0, keepdims=True) * on
    shift_grad = jnp.sum(weight * sums, axis=0, keepdims=True) * on
    row = lax.broadcasted_iota(jnp.int32, extra.shape, 0)
    more = jnp.where(row == 0, gain_grad, 0.0) + jnp.where(row == 1, shift_grad, 0.0)
    more = more + jnp.where(row == 2 + slot, start_sum * on, 0.0)
    whole[3 * hd :, :] = extra[...] + more
    keep_out[...] = whole[:, aligned(x * half, half)]
    send_out[...] = whole[:, aligned((1 - x) * half, half)].astype(BF)


def prepare_kernel(meta, ids, weight, gain, shift, table, down_bias, up_bias, out, turned, small):
    width = weight.shape[1] // 3
    hd = width // H
    pair, odd = meta[8] // 2, meta[8] % 2
    for j in range(3):
        turned[...] = flip(weight[:, aligned(j * width + pair * 2 * hd, 2 * hd)])
        out[j * hd : (j + 1) * hd, :] = turned[aligned(odd * hd, hd), :]
    small[...] = jnp.zeros_like(small)
    at = 0
    for part in (gain, shift, table):
        small[at : at + part.shape[0], :] = part[...].astype(F32)
        at += part.shape[0]
    half = small.shape[1]
    for part in (down_bias, up_bias):
        for q in range(part.shape[0] // half):
            small[at : at + 1, :] = part[q * half : (q + 1) * half].astype(F32).reshape(1, half)
            at += 1
    lane = lax.broadcasted_iota(jnp.int32, (1, small.shape[1]), 1)
    line = jnp.zeros((1, small.shape[1]), F32)
    for s in range(2):
        line = line + jnp.where(lane == s, ids[s].astype(F32), 0.0)
    small[at : at + 1, :] = line
    out[3 * hd :, :] = small[...].astype(BF)


def unpack_kernel(
    meta, ids, mine, other, wh_out, gains_out, shifts_out, steps_out, step_out, up_out, down_out, ids_out, both,
):
    x = meta[0]
    rows, half = mine.shape
    head_rows = wh_out.shape[0]
    count = rows - head_rows
    for part, at in ((mine, x), (other, 1 - x)):
        lanes = aligned(at * half, half)
        wh_out[:, lanes] = part[0:head_rows, :]
        both[:, lanes] = part[head_rows:, :].astype(F32)
    gains_out[...] = both[0:3, :]
    shifts_out[...] = both[3:6, :]
    for s in range(2):
        steps_out[s : s + 1, :] = both[pl.ds(6 + ids[s], 1), :]
    step_out[...] = both[pl.ds(6 + ids[meta[9]], 1), :]
    last = count - 8
    down_out[...] = both[last : last + 1, :]
    for q in range(4):
        line = both[last + 1 + q : last + 2 + q, :]
        up_out[:, q * half : (q + 1) * half] = line[:, 0:half]
        up_out[:, (4 + q) * half : (5 + q) * half] = line[:, half:]
    ids_out[...] = both[last + 5 : last + 6, :]


def encoder_kernel(meta, own, near, far, *refs):
    blocks, (enc_out, kvt_out, weight_out, sems) = refs[:-4], refs[-4:]
    put = Placer(sems, meta[0], meta[1])
    copies = put.lay(own, near, far, weight_out, 0, 2)
    rows = enc_out.shape[1] // len(blocks)
    first = blocks[0].shape[0] - enc_out.shape[0] * rows
    for k, block in enumerate(blocks):
        at = aligned((meta[7] ^ ORDER[k] if len(blocks) == 16 else k) * rows, rows)
        for s in range(enc_out.shape[0]):
            enc_out[s, at, :] = block[first + s * rows : first + (s + 1) * rows, :]
    wait(copies)
    for s in range(enc_out.shape[0]):
        for b in range(2):
            kv = nn(enc_out[s], weight_out[:, b * 512 : (b + 1) * 512])
            kvt_out[s, b * 512 : (b + 1) * 512, :] = flip(kv).astype(BF)


def pack_kernel(counts, meta, *refs):
    total = sum(counts)
    weights, outs, sems = refs[:total], refs[total:-1], refs[-1]
    copies = []
    index = 0
    for out, count in zip(outs, counts):
        at = 0
        for weight in weights[index : index + count]:
            half = weight.shape[0] // 2
            for b in range(weight.shape[1] // 512):
                src = weight.at[aligned(meta[1] * half, half), pl.ds(b * 512, 512)]
                copies.append(pltpu.make_async_copy(src, out.at[pl.ds(at, half)], sems.at[len(copies)]))
                copies[-1].start()
                at += half
        index += count
    wait(copies)


GROUPS = (("keyval", "out", "query", "cross", "up", "down"), ("joined",))


def chunk_at(meta, k, xr):
    x, c = meta[0], meta[1]
    return x ^ xr, c ^ k


def forward_kernel(
    meta, tokens, steps, att, kvt, gains, shifts, own_out, own_query, own_cross, near2, far2,
    h2_out, h1_out, q_out, crossed_out, shares_out, w_out, w_query, w_cross, sems,
):
    seqs, rows, width = tokens.shape
    hd = width // H
    put = Placer(sems, meta[0], meta[1])
    half = own_out.shape[0] // 2
    c_out = put.lay(own_out, near2, far2, w_out, 2 * half, 1)
    c_query = put.lay(own_query, near2, far2, w_query, 3 * half, 1)
    c_cross = put.lay(own_cross, near2, far2, w_cross, 4 * half, 1)
    factor = LOG2E / math.sqrt(hd)

    wait(c_out)
    for s in range(seqs):
        at = pl.ds(s * rows, rows)
        start = tokens[s].astype(F32) + steps[s : s + 1, :]
        h1_out[at, :] = start + nn(flip(att[s]), w_out[...])
    hidden1 = h1_out[...]
    xhat1, unused = normalise(hidden1)
    wait(c_query)
    q_out[...] = nn((xhat1 * gains[1:2, :] + shifts[1:2, :]).astype(BF), w_query[...]).astype(BF)
    for s in range(seqs):
        for first in range(0, H, TOGETHER):
            heads = range(first, first + TOGETHER)
            scores = [
                nn(q_out[s * rows : (s + 1) * rows, h * hd : (h + 1) * hd], kvt[s, h * hd : (h + 1) * hd, :]) * factor for h in heads
            ]
            peaks = [jnp.max(score, axis=1, keepdims=True) for score in scores]
            shares = [jnp.exp2(score - peak) for score, peak in zip(scores, peaks)]
            totals = [jnp.sum(share, axis=1, keepdims=True) for share in shares]
            lows = [(share * (1.0 / total)).astype(BF) for share, total in zip(shares, totals)]
            got = [nt(kvt[s, width + h * hd : width + (h + 1) * hd, :], low) for h, low in zip(heads, lows)]
            for k, h in enumerate(heads):
                shares_out[s * H + h] = lows[k]
                crossed_out[s, h * hd : (h + 1) * hd, :] = got[k].astype(BF)
    wait(c_cross)
    for s in range(seqs):
        at = pl.ds(s * rows, rows)
        h2_out[at, :] = h1_out[at, :] + nn(flip(crossed_out[s]), w_cross[...])


TOGETHER = 4


def feed_kernel(
    meta, hidden2_in, gains, shifts, up_bias, down_bias, out_grad, own_up, own_down, near2, far2,
    mixed_out, h2g_out, extra_out, down_keep, down_send, up_keep, up_send, w_up, w_down, act_t, n2_t, pre_low, sems,
):
    seqs, rows, width = out_grad.shape
    ff = w_down.shape[0]
    slots = extra_out.shape[0]
    put = Placer(sems, meta[0], meta[1])
    c_up = put.lay(own_up, near2, far2, w_up, 5 * (own_up.shape[0] // 2), 4)
    c_down = put.lay(own_down, near2, far2, w_down, 9 * (own_up.shape[0] // 2), 1)
    hidden2 = hidden2_in[...]
    xhat2, r2 = normalise(hidden2)
    n2 = (xhat2 * gains[2:3, :] + shifts[2:3, :]).astype(BF)
    n2_t[...] = flip(n2)
    grad = jnp.concatenate([out_grad[s] for s in range(seqs)], axis=0)
    top = grad.astype(F32)
    wait(c_up)
    wait(c_down)
    mixed = hidden2 + down_bias[...]
    n2_grad = jnp.zeros_like(hidden2)
    extra_out[...] = jnp.zeros_like(extra_out)
    root = math.sqrt(2.0 / math.pi)
    bias_row = slots - 10
    for b in range(ff // 512):
        cols = pl.ds(b * 512, 512)
        pre = nn(n2, w_up[:, cols]) + up_bias[:, cols]
        square = pre * pre
        bent = jnp.tanh(root * pre * (1.0 + 0.044715 * square))
        act = (0.5 * pre * (1.0 + bent)).astype(BF)
        slope = 0.5 * (1.0 + bent) + 0.5 * root * pre * (1.0 - bent * bent) * (1.0 + 3.0 * 0.044715 * square)
        mixed = mixed + nn(act, w_down[cols, :])
        act_t[cols, :] = flip(act)
        low = (nt(grad, w_down[cols, :]) * slope).astype(BF)
        pre_low[:, cols] = low
        n2_grad = n2_grad + nt(low, w_up[:, cols])
        sums = jnp.sum(low.astype(F32), axis=0, keepdims=True)
        per_half = ff // 512 // 2
        lanes = pl.ds((b // per_half) * 256, 256)
        for piece in range(2):
            row = bias_row + 1 + (b % per_half) * 2 + piece
            extra_out[row : row + 1, lanes] = sums[:, piece * 256 : (piece + 1) * 256]
    for s in range(seqs):
        mixed_out[s] = mixed[s * rows : (s + 1) * rows].astype(BF)
    h2g_out[...] = top + norm_back(n2_grad, gains[2:3, :], xhat2, r2)
    extra_out[bias_row : bias_row + 1, :] = jnp.sum(top, axis=0, keepdims=True)
    extra_out[bias_row + 5 : bias_row + 6, :] = jnp.sum(n2_grad * xhat2, axis=0, keepdims=True)
    extra_out[bias_row + 6 : bias_row + 7, :] = jnp.sum(n2_grad, axis=0, keepdims=True)

    me = meta[2]
    for k in (1, 0):
        down_out, up_out = (down_send, up_send) if k else (down_keep, up_keep)
        for xr in (1, 0):
            xa, ca = chunk_at(meta, k, xr)
            down = nn(act_t[aligned(xa * (ff // 2) + ca * (ff // 4), ff // 4), :], grad).astype(BF)
            up = nn(n2_t[aligned(xa * (width // 2), width // 2), :], pre_low[:, aligned(ca * (ff // 2), ff // 2)])
            up = up.astype(BF)
            for a in range(8):
                at = a ^ me
                down_out[xr * 8 + at] = down[a * 64 : (a + 1) * 64]
                up_out[(at // 4) * 8 + xr * 4 + at % 4] = up[(a % 4) * 64 : (a % 4 + 1) * 64, (a // 4) * 512 : (a // 4 + 1) * 512]


def cross_back_kernel(meta, h2g, q, shares, kvt, own_cross, near2, far2, dq_out, part_out, w_cross, dc, sems):
    width = h2g.shape[1]
    seqs, unused, enc_rows = kvt.shape
    rows = h2g.shape[0] // seqs
    hd = width // H
    scale = 1.0 / math.sqrt(hd)
    put = Placer(sems, meta[0], meta[1])
    half = own_cross.shape[0] // 2
    wait(put.lay(own_cross, near2, far2, w_cross, 4 * half, 1))
    dc[...] = nt(h2g[...].astype(BF), w_cross[...]).astype(BF)
    for s in range(seqs):
        at = slice(s * rows, (s + 1) * rows)
        q_t = flip(q[at, :])
        dc_t = flip(dc[at, :])
        for first in range(0, H, TOGETHER):
            heads = range(first, first + TOGETHER)
            lows = [shares[s * H + h] for h in heads]
            wides = [low.astype(F32) for low in lows]
            share_grads = [nn(dc[at, h * hd : (h + 1) * hd], kvt[s, width + h * hd : width + (h + 1) * hd, :]) for h in heads]
            means = [jnp.sum(wide * grad, axis=1, keepdims=True) for wide, grad in zip(wides, share_grads)]
            score_grads = [(wide * (grad - mean)).astype(BF) for wide, grad, mean in zip(wides, share_grads, means)]
            q_grads = [nt(grad, kvt[s, h * hd : (h + 1) * hd, :]) for h, grad in zip(heads, score_grads)]
            k_grads = [nn(q_t[h * hd : (h + 1) * hd], grad) for h, grad in zip(heads, score_grads)]
            v_grads = [nn(dc_t[h * hd : (h + 1) * hd], low) for h, low in zip(heads, lows)]
            for k, h in enumerate(heads):
                head = slice(h * hd, (h + 1) * hd)
                dq_out[at, head] = (q_grads[k] * scale).astype(BF)
                part_out[s, head, :] = (k_grads[k] * scale).astype(BF)
                part_out[s, width + h * hd : width + (h + 1) * hd, :] = v_grads[k].astype(BF)


def hidden_back_kernel(
    meta, h2g, hidden1, dq, gains, extra_in, own_out, own_query, near2, far2, h1g_out, att_grad_out, extra_out,
    w_out, w_query, sems,
):
    width = h2g.shape[1]
    seqs, unused, rows = att_grad_out.shape
    put = Placer(sems, meta[0], meta[1])
    half = own_out.shape[0] // 2
    c_query = put.lay(own_query, near2, far2, w_query, 3 * half, 1)
    c_out = put.lay(own_out, near2, far2, w_out, 2 * half, 1)
    xhat1, r1 = normalise(hidden1[...])
    wait(c_query)
    n1_grad = nt(dq[...], w_query[...])
    grad1 = h2g[...] + norm_back(n1_grad, gains[1:2, :], xhat1, r1)
    h1g_out[...] = grad1
    low1 = grad1.astype(BF)
    wait(c_out)
    for s in range(seqs):
        att_grad_out[s] = nt(w_out[...], low1[s * rows : (s + 1) * rows]).astype(BF)
    last = extra_out.shape[0] - 10
    row = lax.broadcasted_iota(jnp.int32, extra_out.shape, 0)
    more = jnp.where(row == last + 7, jnp.sum(n1_grad * xhat1, axis=0, keepdims=True), 0.0)
    more = more + jnp.where(row == last + 8, jnp.sum(n1_grad, axis=0, keepdims=True), 0.0)
    for s in range(seqs):
        token_sum = jnp.sum(grad1[s * rows : (s + 1) * rows], axis=0, keepdims=True)
        more = more + jnp.where(row == 2 + meta[5] + s, token_sum, 0.0)
    extra_out[...] = extra_in[...] + more


def weights_back_kernel(
    meta, h2g, h1g, hidden1, crossed, att, dq, part, enc, gains, shifts, keep1, send1, keep0, send0, kv_keep, kv_send,
    n1_t, enc_t, part_t,
):
    width = h2g.shape[1]
    seqs, unused, rows = att.shape
    xhat1, unused = normalise(hidden1[...])
    n1_t[...] = flip((xhat1 * gains[1:2, :] + shifts[1:2, :]).astype(BF))
    low2, low1 = h2g[...].astype(BF), h1g[...].astype(BF)
    enc_rows = enc.shape[1]
    span = enc_rows // 16
    for s in range(seqs):
        enc_t[s] = flip(enc[s])
        part_t[s] = flip(part[s])
    for k in (1, 0):
        out = kv_send if k else kv_keep
        for at in range(8):
            a = at ^ meta[2]
            first = aligned(((a & 1) * 8 + (a & 2) * 2 + (a & 4) // 2 + (meta[1] ^ k)) * span, span)
            for s in range(seqs):
                for j in range(2):
                    row = (s * 2 + j) * span
                    out[at, row : row + span, :] = part_t[s, first, j * width : (j + 1) * width]
    me = meta[2]
    for k in (1, 0):
        for xr in (1, 0):
            out = ((keep0, keep1), (send0, send1))[k][xr]
            xa, ca = chunk_at(meta, k, xr)
            at = aligned(xa * (width // 2) + ca * (width // 4), width // 4)
            outer = jnp.zeros((width // 4, width), F32)
            cross = jnp.zeros((width // 4, width), F32)
            keyval = jnp.zeros((width // 2, width), F32)
            for s in range(seqs):
                mine = slice(s * rows, (s + 1) * rows)
                outer = outer + nn(att[s, at, :], low1[mine])
                cross = cross + nn(crossed[s, at, :], low2[mine])
                keyval = keyval + nt(enc_t[s, aligned(xa * (width // 2), width // 2), :], part[s, aligned(ca * width, width), :])
            query = nn(n1_t[at, :], dq[...]).astype(BF)
            outer, cross, keyval = outer.astype(BF), cross.astype(BF), keyval.astype(BF)
            for a in range(8):
                out[a ^ me, 0:16, :] = outer[a * 16 : (a + 1) * 16]
                out[a ^ me, 16:32, :] = query[a * 16 : (a + 1) * 16]
                out[a ^ me, 32:48, :] = cross[a * 16 : (a + 1) * 16]
                out[a ^ me, 48:80, :] = keyval[a * 32 : (a + 1) * 32]


def start_kernel(meta, grads, tokens, steps, gains, h1g, own, near, far, grad_out, weight, turned, sems):
    seqs, rows, width = tokens.shape
    hd = width // H
    put = Placer(sems, meta[0], meta[1])
    copies = put.lay(own, near, far, weight, 0, 3)
    for s in range(seqs):
        for h in range(H):
            for j in range(3):
                turned[s, j * width + h * hd : j * width + (h + 1) * hd, :] = grads[s, h, j * hd : (j + 1) * hd, :]
    wait(copies)
    for s in range(seqs):
        xhat, r = normalise(tokens[s].astype(F32) + steps[s : s + 1, :])
        grad = nt(flip(turned[s]), weight[...])
        grad_out[s] = h1g[s * rows : (s + 1) * rows, :] + norm_back(grad, gains[0:1, :], xhat, r)


PIECES = [(core, mask + far, far) for core in (0, 1) for mask in (0, 2, 4, 6) for far in (0, 1)]


def place_cross_kernel(meta, *refs):
    pieces, (out_out, query_out, cross_out, keyval_out) = refs[:-4], refs[-4:]
    c, me = meta[1], meta[2]
    for k, (core, mask, index) in enumerate(PIECES):
        block = pieces[k // 2][index].astype(F32)
        a = me ^ mask
        ca = c ^ core
        at = aligned(ca * 128 + a * 16, 16)
        out_out[at, :] = block[0:16]
        query_out[at, :] = block[16:32]
        cross_out[at, :] = block[32:48]
        keyval_out[aligned(a * 32, 32), aligned(ca * 512, 512)] = block[48:80]


def encoder_back_kernel(kv, got, weight, out):
    seqs, span, width = out.shape
    total = (kv[0].astype(F32) + got[0].astype(F32)).astype(BF)
    for s in range(seqs):
        first = s * 2 * span
        keys = nt(total[first : first + span], weight[:, 0:width])
        out[s] = keys + nt(total[first + span : first + 2 * span], weight[:, width:])


def merge_kernel(feed, feed_got, heads, heads_got, out):
    rows = feed.shape[1]
    for k in range(2):
        total = feed[k].astype(F32) + feed_got[1 - k].astype(F32)
        out[0, k * rows : (k + 1) * rows, :] = total.astype(BF)
    total = heads[0].astype(F32) + heads_got[0].astype(F32)
    count, half = total.shape
    split = out.shape[1] - 2 * rows
    out[0, 2 * rows :, 0:half] = total[0:split].astype(BF)
    rest = jnp.concatenate([total[split:], jnp.zeros((2 * split - count, half), F32)], axis=0)
    out[0, 2 * rows :, half:] = rest.astype(BF)


def place_kernel(meta, ids, *refs):
    pieces = refs[:8]
    feed_up, feed_down, grad_out, gain_out, shift_out, table_out, down_out, up_out, stacked = refs[8:]
    c, me, low = meta[1], meta[2], meta[6]
    for k, (core, mask, index) in enumerate(PIECES):
        block = pieces[k // 2][0, index * 128 : (index + 1) * 128, :].astype(F32)
        a = me ^ mask
        ca = c ^ core
        feed_down[aligned(ca * 512 + a * 64, 64), :] = block[0:64]
        feed_up[aligned((a % 4) * 64, 64), aligned(ca * 1024 + (a // 4) * 512, 512)] = block[64:128]
    hd = 64
    half = grad_out.shape[0]
    total = jnp.zeros((16, half), F32)
    for k, mask in enumerate((0, 4, 2, 6, 1, 5, 3, 7)):
        wide = pieces[k][0, 256:368, :].astype(F32)
        block = jnp.concatenate([wide[:, 0:half], wide[0:96, half:]], axis=0)
        head = low ^ mask
        for j in range(3):
            stacked[aligned(j * H * hd + head * hd, hd), :] = block[j * hd : (j + 1) * hd]
        total = total + block[3 * hd :]
    for b in range(3):
        grad_out[:, b * 512 : (b + 1) * 512] = flip(stacked[b * 512 : (b + 1) * 512, :])
    last = total.shape[0] - 10
    for row, (g, b) in enumerate(((0, 1), (last + 7, last + 8), (last + 5, last + 6))):
        gain_out[row : row + 1, :] = total[g : g + 1]
        shift_out[row : row + 1, :] = total[b : b + 1]
    down_out[...] = total[last : last + 1]
    up_out[...] = total[last + 1 : last + 5]
    step = lax.broadcasted_iota(jnp.int32, table_out.shape, 0).astype(F32)
    table = jnp.zeros(table_out.shape, F32)
    for k in range(4):
        lane = (k // 2) * half + k % 2
        table = table + jnp.where(step == ids[:, lane : lane + 1], total[2 + k : 3 + k], 0.0)
    table_out[...] = table


def sums(name, outs, after=()):
    arrays, specs, plan, shapes = [], [], [], []
    for groups in outs:
        rows = 0
        steps = []
        for terms in groups:
            spans = []
            for array, size, index, span, swap in terms:
                spans.append((len(arrays), span or (0, array.shape[1]), swap))
                arrays.append(array)
                specs.append(pl.BlockSpec((size,) + array.shape[1:], lambda g, index=index: (index, 0, 0)))
            high = spans[0][1][1] - spans[0][1][0]
            steps.append((rows, rows + high, spans))
            rows += high
        plan.append(steps)
        shapes.append((terms[0][1], rows, array.shape[2]))
    count = len(arrays)

    def kernel(*refs):
        results = refs[count + len(after) :]
        for out, steps in zip(results, plan):
            for low, high, spans in steps:
                total = None
                for k, (first, last), swap in spans:
                    value = refs[k][:, first:last, :].astype(F32)
                    if swap:
                        value = jnp.concatenate([value[1:2], value[0:1]], axis=0)
                    total = value if total is None else total + value
                out[:, low:high, :] = total.astype(BF)

    return pl.pallas_call(
        kernel,
        name=name,
        grid=(1,),
        out_shape=[jax.ShapeDtypeStruct(shape, BF) for shape in shapes],
        in_specs=specs + [ANY] * len(after),
        out_specs=[pl.BlockSpec(shape, lambda g: (0, 0, 0)) for shape in shapes],
        compiler_params=pltpu.CompilerParams(vmem_limit_bytes=VMEM_LIMIT),
        cost_estimate=cost_of(name),
    )(*arrays, *after)


def term(array, size, index, span=None, swap=False):
    return array, size, index, span, swap


def tie(value, *others):
    return lax.optimization_barrier((value,) + others)[0]


def over_ctx(value, mask):
    return lax.ppermute(value, "ctx", [(i, i ^ mask) for i in range(16)])


def over_x(value):
    return lax.ppermute(value, "fsdp", [(0, 1), (1, 0)])


def spread(piece, first=()):
    pieces = [piece] + [over_ctx(piece, mask) for mask in (4, 2, 6)]
    pieces = [tie(p, *first) for p in pieces]
    return pieces + [over_ctx(p, 1) for p in pieces]


def shards(
    tokens, encoder, step_ids, out_grad, self_in, self_out, cross_query, cross_keyval, cross_out,
    ffn_up, up_bias, ffn_down, down_bias, norm_gain, norm_shift, step_table,
):
    nctx, nx = lax.axis_size("ctx"), lax.axis_size("fsdp")
    i, x = lax.axis_index("ctx"), lax.axis_index("fsdp")
    seqs, rows, width = tokens.shape
    hd = width // H
    units = seqs * H
    rep = nctx // units
    unit = i // rep
    s_mine, head = unit // H, unit % H
    n = rows * nctx
    ff = 2048
    fast = nctx == 16 and nx == 2
    steps_count = step_table.shape[0]
    slots = seqs * nx
    extra_rows = -(-(slots + 12) // 16) * 16
    zero = jnp.int32(0)

    xk, c, me = zero, zero, zero
    if fast:
        xk, c, me = x, i & 1, ((i >> 1) & 1) * 4 + ((i >> 2) & 1) * 2 + ((i >> 3) & 1)
    active = (i % rep == 0).astype(jnp.int32)
    meta = jnp.stack([xk, c, me, active, seqs * x + s_mine, seqs * x, i & 7, i, head, s_mine]).astype(jnp.int32)

    if fast:
        mine, others = call(
            split_kernel, "split", [((rows + seqs * encoder.shape[1], width), BF)] * 2, [SM, VM, VM], [], (meta, tokens, encoder),
        )
        got = over_ctx(others, 8)
        blocks = [mine] + [over_ctx(mine, mask) for mask in (4, 2, 6)]
        blocks += [got] + [over_ctx(got, mask) for mask in (4, 2, 6)]
        blocks += [over_ctx(block, 1) for block in blocks]

        (small,) = call(
            prepare_kernel, "prepare", [((256, width // 2), BF)], [SM, SM] + [VM] * 6,
            [pltpu.VMEM((2 * hd, width // 2), BF), pltpu.VMEM((64, width // 2), F32)],
            (meta, step_ids, self_in, norm_gain, norm_shift, step_table, down_bias, up_bias),
            after=[mine],
        )
        own = dict(keyval=cross_keyval, out=self_out, query=cross_query, cross=cross_out, up=ffn_up, down=ffn_down, joined=self_in)

        weights = [own[name] for group in GROUPS for name in group]
        sizes = [sum(own[name].size for name in group) // 1024 for group in GROUPS]
        packed = call(
            functools.partial(pack_kernel, [len(group) for group in GROUPS]), "pack", [((size, 512), BF) for size in sizes],
            [SM] + [ANY] * len(weights), [pltpu.SemaphoreType.DMA((13,))], (meta, *weights), after=[small],
        )
        other_small = over_x(tie(small, packed[0], *blocks[1:5]))
        near2 = over_x(tie(packed[0], other_small))
        wh, gains, shifts, steps, step_mine, bias_u, bias_d, all_ids = call(
            unpack_kernel, "unpack",
            [((3 * hd, width), BF), ((3, width), F32), ((3, width), F32), ((seqs, width), F32), ((1, width), F32),
             ((1, ff), F32), ((1, width), F32), ((1, width), F32)],
            [SM, SM, VM, VM], [pltpu.VMEM((64, width), F32)], (meta, step_ids, small, other_small), after=[packed[0]],
        )
    else:
        def gather(w, axis=0):
            return lax.all_gather(w, "fsdp", axis=axis, tiled=True)

        gains, shifts = gather(norm_gain, 1).astype(F32), gather(norm_shift, 1).astype(F32)
        table = gather(step_table, 1)
        bias_d, bias_u = gather(down_bias)[None, :].astype(F32), gather(up_bias)[None, :].astype(F32)
        all_ids = gather(step_ids.astype(BF)).astype(F32)
        full = dict(keyval=gather(cross_keyval), out=gather(self_out), query=gather(cross_query), cross=gather(cross_out),
                    up=gather(ffn_up), down=gather(ffn_down), joined=gather(self_in))
        half_of = {name: w.shape[0] // 2 for name, w in full.items()}
        own = {name: w[: half_of[name]] for name, w in full.items()}

        def group(names, which):
            parts = []
            for name in names:
                rest = full[name][half_of[name] :]
                quarter = half_of[name] // 2
                part = rest[which * quarter : (which + 1) * quarter]
                parts += [part[:, b : b + 512] for b in range(0, part.shape[1], 512)]
            return jnp.concatenate(parts, axis=0)

        (near2, far2), (near4, far4) = ([group(names, w) for w in (0, 1)] for names in GROUPS)
        by_head = full["joined"].reshape(width, 3, H, hd)
        wh = lax.dynamic_index_in_dim(by_head, head, 2, False).reshape(width, 3 * hd).T
        onehot = (jnp.arange(steps_count, dtype=jnp.int32)[None, :] == step_ids[:, None]).astype(BF)
        steps = jnp.dot(onehot, table, preferred_element_type=F32)
        step_mine = lax.dynamic_index_in_dim(steps, s_mine, 0, True)
        every = lax.all_gather(tokens, "ctx", axis=0, tiled=False)
        chosen = lax.dynamic_index_in_dim(every, s_mine, 1, False)
        encs = lax.all_gather(encoder, "ctx", axis=0, tiled=False)
        blocks = [jnp.concatenate([chosen[j], encs[j].reshape(-1, width)], axis=0) for j in range(nctx)]
    xhat0, joined, heads, attended_full, stats = call(
        attend_kernel, "attend",
        [((n, width), BF), ((3 * hd, n), BF), ((nctx, hd, rows), BF), ((hd, n), F32), ((8, n), F32)],
        [SM] + [VM] * (4 + nctx),
        [pltpu.VMEM((n, width), BF), pltpu.VMEM((n, hd), BF)],
        (meta, step_mine, gains, shifts, wh, *blocks),
    )
    hold = []
    back = lax.all_to_all(heads, "ctx", 0, 0, tiled=True)
    if fast:
        far2 = over_ctx(tie(near2, heads), 1)
    att = back.reshape(units, rep, hd, rows)[:, 0].reshape(seqs, width, rows)

    enc_rows = nctx * encoder.shape[1]
    enc_all, kvt, w_keyval = call(
        encoder_kernel, "encoder_rows",
        [((seqs, enc_rows, width), BF), ((seqs, 2 * width, enc_rows), BF), ((width, 2 * width), BF)],
        [SM, ANY, ANY, ANY] + [VM] * nctx,
        [pltpu.SemaphoreType.DMA((5,))],
        (meta, own["keyval"], near2, far2, *blocks),
    )
    if fast:
        near4 = over_x(tie(packed[1], kvt))
        hold = [near4]

    tall = seqs * rows
    square = pltpu.VMEM((width, width), BF)
    hidden2, hidden1, q, crossed, shares = call(
        forward_kernel, "forward",
        [((tall, width), F32), ((tall, width), F32), ((tall, width), BF), ((seqs, width, rows), BF), ((units, rows, enc_rows), BF)],
        [SM] + [VM] * 6 + [ANY] * 5,
        [square] * 3 + [pltpu.SemaphoreType.DMA((9,))],
        (meta, tokens, steps, att, kvt, gains, shifts, own["out"], own["query"], own["cross"], near2, far2),
    )
    mixed, h2g, extra1, down_keep, down_send, up_keep, up_send = call(
        feed_kernel, "feed",
        [((seqs, rows, width), BF), ((tall, width), F32), ((extra_rows, width), F32)] + [((16, 64, width), BF)] * 4,
        [SM] + [VM] * 6 + [ANY] * 4,
        [pltpu.VMEM((width, ff), BF), pltpu.VMEM((ff, width), BF), pltpu.VMEM((ff, tall), BF),
         pltpu.VMEM((width, tall), BF), pltpu.VMEM((tall, ff), BF), pltpu.SemaphoreType.DMA((12,))],
        (meta, hidden2, gains, shifts, bias_u, bias_d, out_grad, own["up"], own["down"], near2, far2),
        after=hold,
    )
    hold = []
    if fast:
        far4 = over_ctx(tie(near4, h2g), 1)
        hold = [far4]
        down_got, up_got = over_ctx(down_send, 1), over_ctx(up_send, 1)
    dq, part = call(
        cross_back_kernel, "cross_back",
        [((tall, width), BF), ((seqs, 2 * width, enc_rows), BF)],
        [SM] + [VM] * 4 + [ANY] * 3,
        [square, pltpu.VMEM((tall, width), BF), pltpu.SemaphoreType.DMA((3,))],
        (meta, h2g, q, shares, kvt, own["cross"], near2, far2), after=hold,
    )
    hold = []
    if fast:
        down_x, up_y = sums(
            "reduce_1", [[[term(down_keep, 8, 1), term(down_got, 8, 1)]], [[term(up_keep, 8, 1), term(up_got, 8, 1)]]], [dq])
        down_x1, up_y1 = over_x(down_x), over_ctx(up_y, 2)
        hold = [down_x]
    h1g, att_grad, extra2 = call(
        hidden_back_kernel, "hidden_back",
        [((tall, width), F32), ((seqs, width, rows), BF), ((extra_rows, width), F32)],
        [SM] + [VM] * 5 + [ANY] * 4,
        [square, square, pltpu.SemaphoreType.DMA((6,))],
        (meta, h2g, hidden1, dq, gains, extra1, own["out"], own["query"], near2, far2),
        after=hold,
    )
    by_unit = att_grad.reshape(units, 1, hd, rows)
    grads = lax.all_to_all(jnp.broadcast_to(by_unit, (units, rep, hd, rows)).reshape(nctx, hd, rows), "ctx", 0, 0, tiled=True)
    keep1, send1, keep0, send0, kv_keep, kv_send = call(
        weights_back_kernel, "weights_back",
        [((8, 80, width), BF)] * 4 + [((8, enc_rows // 4, width), BF)] * 2,
        [SM] + [VM] * 10,
        [pltpu.VMEM((width, tall), BF), pltpu.VMEM((seqs, width, enc_rows), BF), pltpu.VMEM((seqs, enc_rows, 2 * width), BF)],
        (meta, h2g, h1g, hidden1, crossed, att, dq, part, enc_all, gains, shifts),
    )
    hold = []
    if fast:
        got1, got0, kv_0 = (over_ctx(tie(part, grads, down_x1, up_y1), 1) for part in (send1, send0, kv_send))

        def terms(arrays, size, index, whole=()):
            found = [term(array, size, index) for array in arrays]
            return found + [term(array, size, index, rows) for array, rows in whole]

        down_y, up_x = sums(
            "reduce_2", [[terms([down_keep, down_got, down_x1], 4, 1)], [terms([up_keep, up_got, up_y1], 4, 1)]], [grads, keep1],
        )
        down_y1, up_x1 = over_ctx(down_y, 2), over_x(up_x)
        hold = [down_y]

    head_scratch = [pltpu.VMEM((n // 2, hd), BF), pltpu.VMEM((n // 2, hd), BF), pltpu.VMEM((hd, n), BF)]
    query_acc, key_half = call(
        attend_back_first, "attend_back_1", [((hd, n), F32), ((2 * hd, n // 2), BF)], [VM] * 4, head_scratch,
        (joined, attended_full, stats, grads), after=hold,
    )
    hold = []
    if fast:
        downs, ups, kvs = [down_keep, down_got, down_x1, down_y1], [up_keep, up_got, up_y1, up_x1], [kv_keep, kv_0]
        feed_z, cross_x, kv_y = sums(
            "reduce_3", [[terms(downs, 2, 1), terms(ups, 2, 1)], [terms([keep1, got1], 8, 0)], [terms(kvs, 4, 1)]], [query_acc],
        )
        feed_z1, cross_x1, kv_1 = over_ctx(feed_z, 4), over_x(cross_x), over_ctx(kv_y, 2)
        kvs = kvs + [kv_1]
        hold = [feed_z]
    joined_grad, u_keep, u_send = call(
        attend_back_second, "attend_back_2",
        [((nctx, 3 * hd, rows), BF), ((3 * hd + extra_rows, width // 2), F32), ((3 * hd + extra_rows, width // 2), BF)],
        [SM] + [VM] * 11,
        head_scratch
        + [pltpu.VMEM((2 * hd, n // 2), BF), pltpu.VMEM((hd, n), F32), pltpu.VMEM((3 * hd + 16, n), BF),
           pltpu.VMEM((3 * hd + extra_rows, width), F32)],
        (meta, joined, attended_full, stats, grads, query_acc, key_half, xhat0, gains, shifts, wh, extra2),
        after=hold,
    )
    if fast:
        joined_grad, u_send = tie(joined_grad, feed_z1, kv_1), tie(u_send, feed_z1, kv_1)
        u_x1 = over_x(u_send)[None]
        u_keep = u_keep[None]
        crosses = [keep0, got0, cross_x1]
        feed_w, u_sum, kv_z, cross_y = sums(
            "reduce_4",
            [[terms(downs, 2, 0, [(feed_z1, (0, 64))]), terms(ups, 2, 0, [(feed_z1, (64, 128))])],
             [terms([u_keep, u_x1], 1, 0)], [terms(kvs, 2, 1)], [terms(crosses, 4, 1)]],
        )
        feed_w1, u_8, kv_2, cross_y1 = over_ctx(feed_w, 8), over_ctx(u_sum, 8), over_ctx(kv_z, 4), over_ctx(cross_y, 2)
        kvs, crosses = kvs + [kv_2], crosses + [cross_y1]
        (cross_z,) = sums("reduce_5", [[terms(crosses, 2, 1)]])
        cross_z1 = over_ctx(cross_z, 4)
        crosses = crosses + [cross_z1]
        (merged,) = call(
            merge_kernel, "reduce_6", [((1, 368, width), BF)], [VM] * 4, [], (feed_w, feed_w1, u_sum, u_8), after=[cross_z1, kv_2],
        )
        cross_w, kv_far, kv_near = sums(
            "reduce_7", [[terms(crosses, 2, 0)], [terms(kvs, 1, 1)], [terms(kvs, 1, 0)]], [merged],
        )
        cross_w1, kv_got = over_ctx(cross_w, 8), over_ctx(kv_far, 8)
        merged = tie(merged, cross_w)
        spread_out = [over_ctx(merged, mask) for mask in (4, 2, 6)]
        hold = [cross_w]
    dj = lax.all_to_all(joined_grad, "ctx", 0, 0, tiled=True)
    dj = dj.reshape(units, rep, 3 * hd, rows)[:, 0].reshape(seqs, H, 3 * hd, rows)
    (tokens_grad,) = call(
        start_kernel, "start_grad",
        [((seqs, rows, width), F32)],
        [SM] + [VM] * 5 + [ANY] * 3,
        [pltpu.VMEM((width, 3 * width), BF), pltpu.VMEM((seqs, 3 * width, rows), BF), pltpu.SemaphoreType.DMA((7,))],
        (meta, dj, tokens, steps, gains, h1g, own["joined"], near4, far4),
        after=hold,
    )

    if fast:
        (cross_pair,) = sums("reduce_8", [[[term(cross_w, 2, 0), term(cross_w1, 2, 0, None, True)]]], [kv_got, tokens_grad])
        pieces = [tie(piece, cross_pair) for piece in [merged] + spread_out]
        pieces = pieces + [over_ctx(piece, 1) for piece in pieces]
        (enc_grad,) = call(
            encoder_back_kernel, "encoder_back", [(encoder.shape, F32)], [VM] * 3, [], (kv_near, kv_got, w_keyval), after=[cross_pair],
        )
        up_grad, down_grad, self_in_grad, gain_grad, shift_grad, table_grad, down_bias_grad, up_bias_grad = call(
            place_kernel, "place",
            [((width // 2, ff), F32), ((ff // 2, width), F32), ((width // 2, 3 * width), F32), ((3, width // 2), F32),
             ((3, width // 2), F32), ((steps_count, width // 2), F32), ((1, width // 2), F32), ((4, width // 2), F32)],
            [SM] + [VM] * 9, [pltpu.VMEM((3 * width, width // 2), F32)], (meta, all_ids, *pieces), after=[enc_grad],
        )
        down_bias_grad, up_bias_grad = down_bias_grad.reshape(-1), up_bias_grad.reshape(-1)
        cross_pieces = spread(cross_pair, [up_grad])
        out_g, query_g, cross_g, keyval_g = call(
            place_cross_kernel, "place_cross",
            [((width // 2, width), F32)] * 3 + [((width // 2, 2 * width), F32)],
            [SM] + [VM] * 8, [], (meta, *cross_pieces),
        )
    else:
        def scatter(g, axis=0):
            return lax.psum(lax.psum_scatter(g, "fsdp", scatter_dimension=axis, tiled=True), "ctx")

        down_all = jnp.stack([down_keep, down_send]).reshape(2, 2, 8, 64, width).transpose(1, 0, 2, 3, 4)
        up_all = jnp.stack([up_keep, up_send]).reshape(2, 2, 2, 4, 64, width).transpose(2, 3, 4, 0, 1, 5)
        down_grad, up_grad = scatter(down_all.reshape(ff, width).astype(F32)), scatter(up_all.reshape(width, ff).astype(F32))
        c_all = jnp.stack([jnp.stack([keep0, send0]), jnp.stack([keep1, send1])])
        out_g, query_g, cross_g = (scatter(c_all[:, :, :, k : k + 16].reshape(width, width).astype(F32)) for k in (0, 16, 32))
        keyval_g = scatter(c_all[:, :, :, 48:80].transpose(0, 2, 3, 1, 4).reshape(width, 2 * width).astype(F32))
        kv = jnp.stack([kv_keep, kv_send]).reshape(2, 2, 2, 2, seqs, 2, enc_rows // 16, width).transpose(4, 3, 2, 1, 0, 6, 5, 7)
        kv = lax.psum_scatter(kv.reshape(seqs, enc_rows, 2 * width), "ctx", scatter_dimension=1, tiled=True)
        enc_grad = jnp.einsum("sre,de->srd", kv, w_keyval, preferred_element_type=F32)
        u = jnp.concatenate([u_keep, u_send.astype(F32)], axis=1)
        every_u = lax.all_gather(lax.psum(u[: 3 * hd], "fsdp"), "ctx", axis=0, tiled=False)
        by_head = every_u.reshape(seqs, H, rep, 3, hd, width).sum(axis=(0, 2))
        joined_g = by_head.transpose(3, 1, 0, 2).reshape(width, 3 * width)
        self_in_grad = lax.dynamic_slice_in_dim(joined_g, x * self_in.shape[0], self_in.shape[0], 0)
        total = lax.psum(u[3 * hd :], ("ctx", "fsdp"))
        wide = norm_gain.shape[1]
        extra = lax.dynamic_slice_in_dim(total, x * wide, wide, 1)
        last = extra_rows - 10
        down_bias_grad = extra[last]
        up_bias_all = total[last + 1 : last + 5].reshape(4, 2, width // 2).transpose(1, 0, 2).reshape(-1)
        up_bias_grad = lax.dynamic_slice_in_dim(up_bias_all, x * up_bias.shape[0], up_bias.shape[0], 0)
        gain_grad = jnp.stack([extra[0], extra[last + 7], extra[last + 5]])
        shift_grad = jnp.stack([extra[1], extra[last + 8], extra[last + 6]])
        hot = (jnp.arange(steps_count, dtype=jnp.int32).astype(F32)[:, None, None] == all_ids[None, :, None]).astype(F32)
        table_grad = jnp.sum(hot * extra[None, 2 : 2 + slots, :], axis=1)

    return (
        mixed, tokens_grad, enc_grad, self_in_grad, out_g, query_g, keyval_g, cross_g, up_grad, up_bias_grad,
        down_grad, down_bias_grad, gain_grad, shift_grad, table_grad,
    )


def solution(mesh):
    tok = P("fsdp", "ctx", None)
    row, vec, col = P("fsdp", None), P("fsdp"), P(None, "fsdp")
    in_specs = (tok, tok, vec, tok, row, row, row, row, row, row, vec, row, vec, col, col, col)
    out_specs = (tok, tok, tok, row, row, row, row, row, row, vec, row, vec, col, col, col)
    return jax.shard_map(shards, mesh=mesh, in_specs=in_specs, out_specs=out_specs, check_vma=False)
```

time: 318 us -> 263 us (0.83)
  waiting for transfers between devices: 103 us -> 60.6 us
  Pallas kernels: 80 us -> 122 us
  local copies, waits for them, and re-layouts: 45.6 us -> 15.8 us
  other arithmetic: 16.6 us -> 0 us
  starting transfers between devices: 68.1 us -> 62.1 us
    pallas_call x9 -> x25, Pallas kernels: 80 us -> 122 us  [the longest x18 104 us: call(): pl.pallas_call(body, name=name, grid=grid, out_shape=[jax.ShapeDtypeStruc...]
    ppermute x52 -> x47, waiting for transfers between devices: 78.2 us -> 44.5 us  [over_ctx(): return lax.ppermute(value, 'ctx', [(i, i ^ mask) for i in range(16)])]
    unnamed x111 -> x125, local copies, waits for them, and re-layouts: 29.8 us -> 15.3 us
    convert_element_type x20 -> x0, other arithmetic: 12.1 us -> none  [the longest x14 10.7 us: add_low(): return sum((t.astype(F32) for t in terms)).astype(BF)]
    ppermute x52 -> x47, starting transfers between devices: 47.4 us -> 39.2 us  [over_ctx(): return lax.ppermute(value, 'ctx', [(i, i ^ mask) for i in range(16)])]
    all_to_all x1, waiting for transfers between devices: 9.33 us -> 2.9 us  [shards(): lax.all_to_all(jnp.broadcast_to(by_unit, (units, rep, hd, rows)).reshape(...]
    concatenate x7 -> x0, local copies, waits for them, and re-layouts: 5.92 us -> none  [the longest x2 3.43 us: fetch_group(): jnp.concatenate([p for w in weights for p in half_rows(w, c)], axis=0)]
    slice x12 -> x0, local copies, waits for them, and re-layouts: 4.49 us -> none  [the longest x1 1.41 us: shards(): shift_grad = jnp.stack([extra[1], extra[bias_row + 8], extra[bias_row + 6]])]
  transfers between devices with their start and end apart: 62 -> 57, of which waited for: 20 -> 16; matrix products, arithmetic and copies ran while one was open for 18% -> 0% of each run, Pallas kernels for 19% -> 38%
where the time goes in v2:
time: 263 us; the launch traced here: 262 us
  Pallas kernels  122 us (46%)
  starting transfers between devices  62.1 us (24%)
  waiting for transfers between devices  60.6 us (23%)
  local copies, waits for them, and re-layouts  15.8 us (6%)
    pallas_call x18, Pallas kernels, call(): pl.pallas_call(body, name=name, grid=grid, out_shape=[jax.ShapeDtypeStruc...  104 us
    ppermute x47, waiting for transfers between devices, over_ctx(): return lax.ppermute(value, 'ctx', [(i, i ^ mask) for i in range(16)])  44.5 us
    ppermute x47, starting transfers between devices, over_ctx(): return lax.ppermute(value, 'ctx', [(i, i ^ mask) for i in range(16)])  39.2 us
    pallas_call x7, Pallas kernels, sums(): pl.pallas_call(kernel, name=name, grid=(1,), out_shape=[jax.ShapeDtypeStr...  17.7 us
    unnamed x125, local copies, waits for them, and re-layouts  15.3 us
    ppermute x7, waiting for transfers between devices, over_x(): return lax.ppermute(value, 'fsdp', [(0, 1), (1, 0)])  12.3 us
    ppermute x7, starting transfers between devices, over_x(): return lax.ppermute(value, 'fsdp', [(0, 1), (1, 0)])  9.85 us
  transfers between devices with their start and end apart: 57, of which 16 were waited for; matrix products, arithmetic and copies ran while one was open for 0% of the time, Pallas kernels for 38%

profile of v2, /device:TPU:0, one launch (start us, length us, event | category | flops | bytes accessed | tf_op | source)
XLA Modules:
  0.0 261.9 jit_solution(354067308074792948)
XLA Ops:
  1.3 1.7 split.1
  3.0 4.0 %collective-permute-start.3 = (bf16[192,512]{1,0:T(8,128)(2,1)}, bf16[192,512]{1,0:T(8,128)(2,1)S(1)}, u32[]{:S(2)}, u32[]{:S(2)}) collective-permute-start(bf16[192,512]{1,0:T(8,128)(2,1)} %get-tuple-element.110), channel_id=1, source_target_pairs={{0,16},{2,18},{4,20},{6,22},{8,24},{10,26},{12,28},{14,30},{16,0},... | collective-permute-start | bytes 589832 | tf_op jit(solution)/shard_map/ppermute | solution.py:683
  7.0 2.5 collective-permute-start.2
  10.5 2.0 prepare.1.refs_8_.refs_2_
  12.5 3.8 %pack.1 = (bf16[1664,512]{1,0:T(8,128)(2,1)}, bf16[384,512]{1,0:T(8,128)(2,1)}) custom-call(s32[10]{0:T(128)} %stack.40.refs_0_, bf16[256,1024]{1,0:T(8,128)(2,1)} %refs_1_.10, bf16[256,512]{1,0:T(8,128)(2,1)} %refs_6_.8, bf16[256,512]{1,0:T(8,128)(2,1)} %refs_7_.9, bf16[256,512]{1,0:T(8,128)(2,1)} %refs_5_.5, bf16[256,2048]{1,0:T(8,128)(2,1)} %refs_7_.8, ...), custom_call_target="tpu_custom_call" | custom-call | bytes 12950000 | tf_op jit(solution)/shard_map/pack/pallas_call | solution.py:68
  16.4 2.6 collective-permute-done.2.refs_8_.refs_7_
  19.1 2.8 %collective-permute-done.refs_6_.refs_5_ = bf16[192,512]{1,0:T(8,128)(2,1)S(1)} collective-permute-done((bf16[192,512]{1,0:T(8,128)(2,1)}, bf16[192,512]{1,0:T(8,128)(2,1)S(1)}, u32[]{:S(2)}, u32[]{:S(2)}) %collective-permute-start) | collective-permute-done | bytes 196640 | tf_op jit(solution)/shard_map/ppermute | solution.py:683
  23.4 3.4 %collective-permute-done.4.refs_3_ = bf16[256,256]{1,0:T(8,128)(2,1)S(1)} collective-permute-done((bf16[256,256]{1,0:T(8,128)(2,1)S(1)}, bf16[256,256]{1,0:T(8,128)(2,1)S(1)}, u32[]{:S(2)}, u32[]{:S(2)}) %collective-permute-start.4) | collective-permute-done | bytes 131104 | tf_op jit(solution)/shard_map/ppermute | solution.py:687
  32.4 5.2 %collective-permute-done.7.refs_12_.refs_11_ = bf16[192,512]{1,0:T(8,128)(2,1)S(1)} collective-permute-done((bf16[192,512]{1,0:T(8,128)(2,1)S(1)}, bf16[192,512]{1,0:T(8,128)(2,1)S(1)}, u32[]{:S(2)}, u32[]{:S(2)}) %collective-permute-start.7) | collective-permute-done | bytes 196640 | tf_op jit(solution)/shard_map/ppermute | solution.py:683
  37.6 3.2 %collective-permute-done.6.refs_11_.refs_10_ = bf16[192,512]{1,0:T(8,128)(2,1)S(1)} collective-permute-done((bf16[192,512]{1,0:T(8,128)(2,1)S(1)}, bf16[192,512]{1,0:T(8,128)(2,1)S(1)}, u32[]{:S(2)}, u32[]{:S(2)}) %collective-permute-start.6) | collective-permute-done | bytes 196640 | tf_op jit(solution)/shard_map/ppermute | solution.py:683
  44.4 15.3 %attend.1 = (bf16[2048,512]{1,0:T(8,128)(2,1)}, bf16[192,2048]{1,0:T(8,128)(2,1)}, bf16[16,64,128]{2,1,0:T(8,128)(2,1)}, f32[64,2048]{1,0:T(8,128)}, f32[8,2048]{1,0:T(8,128)}) custom-call(s32[10]{0:T(128)} %stack.40.refs_0_, f32[1,512]{1,0:T(1,128)} %get-tuple-element.113.refs_1_, f32[3,512]{1,0:T(4,128)} %get-tuple-element.114.refs_2_.refs_5_.refs_4_.refs_9_.refs_8_, ...), custom_call_target="tpu_custom_call" | custom-call | bytes 52500000 | tf_op jit(solution)/shard_map/attend/pallas_call | solution.py:68
  59.7 3.9 %collective-permute-done.16.refs_2_.refs_10_.refs_9_.refs_6_.refs_8_ = bf16[1664,512]{1,0:T(8,128)(2,1)S(1)} collective-permute-done((bf16[1664,512]{1,0:T(8,128)(2,1)}, bf16[1664,512]{1,0:T(8,128)(2,1)S(1)}, u32[]{:S(2)}, u32[]{:S(2)}) %collective-permute-start.16) | collective-permute-done | bytes 1703968 | tf_op jit(solution)/shard_map/ppermute | solution.py:687
  63.6 4.4 %all-to-all-start = ((bf16[16,64,128]{2,1,0:T(8,128)(2,1)}), bf16[16,64,128]{2,1,0:T(8,128)(2,1)}, u32[]{:S(2)}, u32[]{:S(2)}) async-start(bf16[16,64,128]{2,1,0:T(8,128)(2,1)} %get-tuple-element.117), calls=%async_computation | async-start | bytes 524288 | tf_op jit(solution)/shard_map/all_to_all | solution.py:793
  69.2 6.2 %encoder_rows.1 = (bf16[2,512,512]{2,1,0:T(8,128)(2,1)}, bf16[2,1024,512]{2,1,0:T(8,128)(2,1)}, bf16[512,1024]{1,0:T(8,128)(2,1)}) custom-call(s32[10]{0:T(128)} %stack.40.refs_0_, bf16[256,1024]{1,0:T(8,128)(2,1)} %refs_1_.10, bf16[1664,512]{1,0:T(8,128)(2,1)} %copy-done, bf16[1664,512]{1,0:T(8,128)(2,1)} %copy-done.1, ...), custom_call_target="tpu_custom_call" | custom-call | bytes 21000000 | tf_op jit(solution)/shard_map/encoder_rows/pallas_call | solution.py:68
  77.9 8.1 %forward.1 = (f32[256,512]{1,0:T(8,128)}, f32[256,512]{1,0:T(8,128)}, bf16[256,512]{1,0:T(8,128)(2,1)}, bf16[2,512,128]{2,1,0:T(8,128)(2,1)}, bf16[16,128,512]{2,1,0:T(8,128)(2,1)}) custom-call(s32[10]{0:T(128)} %stack.40.refs_0_, bf16[2,128,512]{2,1,0:T(8,128)(2,1)} %refs_2_.7, f32[2,512]{1,0:T(2,128)} %get-tuple-element.112.refs_2_.refs_3_, ...), custom_call_target="tpu_custom_call" | custom-call | bytes 52500000 | tf_op jit(solution)/shard_map/forward/pallas_call | solution.py:68
  87.9 10.6 %feed.1 = (bf16[2,128,512]{2,1,0:T(8,128)(2,1)}, f32[256,512]{1,0:T(8,128)}, f32[16,512]{1,0:T(8,128)}, bf16[16,64,512]{2,1,0:T(8,128)(2,1)}, bf16[16,64,512]{2,...) custom-call(s32[10]{0:T(128)} %stack.40.refs_0_, f32[256,512]{1,0:T(8,128)} %get-tuple-element.121.refs_1_, ...), custom_call_target="tpu_custom_call" | custom-call | bytes 8750000 | tf_op jit(solution)/shard_map/feed/pallas_call | solution.py:68
  99.1 4.3 %collective-permute-done.19.refs_8_ = bf16[384,512]{1,0:T(8,128)(2,1)S(1)} collective-permute-done((bf16[384,512]{1,0:T(8,128)(2,1)}, bf16[384,512]{1,0:T(8,128)(2,1)S(1)}, u32[]{:S(2)}, u32[]{:S(2)}) %collective-permute-start.19) | collective-permute-done | bytes 393248 | tf_op jit(solution)/shard_map/ppermute | solution.py:683
  104.2 7.6 %cross_back.1 = (bf16[256,512]{1,0:T(8,128)(2,1)}, bf16[2,1024,512]{2,1,0:T(8,128)(2,1)}) custom-call(s32[10]{0:T(128)} %stack.40.refs_0_, f32[256,512]{1,0:T(8,128)} %get-tuple-element.130.refs_1_, bf16[256,512]{1,0:T(8,128)(2,1)} %get-tuple-element.132.refs_2_, bf16[16,128,512]{2,1,0:T(8,128)(2,1)} %get-tuple-element.133.refs_3_, ...), custom_call_target="tpu_custom_call" | custom-call | bytes 37100000 | tf_op jit(solution)/shard_map/cross_back/pallas_call | solution.py:68
  113.1 2.8 %reduce_1.1 = (bf16[8,64,512]{2,1,0:T(8,128)(2,1)}, bf16[8,64,512]{2,1,0:T(8,128)(2,1)}) custom-call(bf16[16,64,512]{2,1,0:T(8,128)(2,1)} %get-tuple-element.137.refs_0_, bf16[16,64,512]{2,1,0:T(8,128)(2,1)} %copy-done.2, bf16[16,64,512]{2,1,0:T(8,128)(2,1)} %get-tuple-element.139.refs_2_.refs_3_.refs_4_.refs_5_, bf16[16,64,512]{2,1,0:T(8,128)(2,1)} %copy-done.3, ...), custom_call_target="tpu_custom_call" | custom-call | bytes 8750000 | tf_op jit(solution)/shard_map/reduce_1/pallas_call | solution.py:662
  118.8 4.0 %hidden_back.1 = (f32[256,512]{1,0:T(8,128)}, bf16[2,512,128]{2,1,0:T(8,128)(2,1)}, f32[16,512]{1,0:T(8,128)}) custom-call(s32[10]{0:T(128)} %stack.40.refs_0_, f32[256,512]{1,0:T(8,128)} %get-tuple-element.130.refs_1_, f32[256,512]{1,0:T(8,128)} %get-tuple-element.131.refs_2_.refs_3_, bf16[256,512]{1,0:T(8,128)(2,1)} %get-tuple-element.135.refs_4_.refs_3_.refs_6_, ...), custom_call_target="tpu_custom_call" | custom-call | bytes 14000000 | tf_op jit(solution)/shard_map/hidden_back/pallas_call | solution.py:68
  122.8 4.7 %all-to-all-start.1 = ((bf16[16,64,128]{2,1,0:T(8,128)(2,1)}), bf16[16,64,128]{2,1,0:T(8,128)(2,1)S(1)}, u32[]{:S(2)}, u32[]{:S(2)}) async-start(bf16[16,64,128]{2,1,0:T(8,128)(2,1)} %bitcast.18), calls=%async_computation.1 | async-start | bytes 524288 | tf_op jit(solution)/shard_map/all_to_all | solution.py:855
  127.5 7.1 %weights_back.1 = (bf16[8,80,512]{2,1,0:T(8,128)(2,1)}, bf16[8,80,512]{2,1,0:T(8,128)(2,1)}, bf16[8,80,512]{2,1,0:T(8,128)(2,1)}, bf16[8,80,512]{2,1,0:T(8,128)(...) custom-call(s32[10]{0:T(128)} %stack.40.refs_0_, f32[256,512]{1,0:T(8,128)} %get-tuple-element.130.refs_1_, ...), custom_call_target="tpu_custom_call" | custom-call | bytes 25200000 | tf_op jit(solution)/shard_map/weights_back/pallas_call | solution.py:68
  134.7 2.9 %all-to-all-done.1.refs_6_.refs_3_.refs_4_ = bf16[16,64,128]{2,1,0:T(8,128)(2,1)S(1)} async-done(((bf16[16,64,128]{2,1,0:T(8,128)(2,1)}), bf16[16,64,128]{2,1,0:T(8,128)(2,1)S(1)}, u32[]{:S(2)}, u32[]{:S(2)}) %all-to-all-start.1) | async-done | bytes 262176 | tf_op jit(solution)/shard_map/all_to_all | solution.py:855
  138.6 2.2 reduce_2.1
  141.3 8.3 %attend_back_1.1 = (f32[64,2048]{1,0:T(8,128)}, bf16[128,1024]{1,0:T(8,128)(2,1)}) custom-call(bf16[192,2048]{1,0:T(8,128)(2,1)} %get-tuple-element.127.refs_0_.refs_1_, f32[64,2048]{1,0:T(8,128)} %get-tuple-element.128.refs_1_.refs_2_, f32[8,2048]{1,0:T(8,128)} %get-tuple-element.129.refs_2_.refs_3_, bf16[16,64,128]{2,1,0:T(8,128)(2,1)} %copy-done.10, ...), custom_call_target="tpu_custom_call" | custom-call | bytes 29400000 | tf_op jit(solution)/shard_map/attend_back_1/pallas_call | solution.py:68
  151.0 3.4 %reduce_3.1 = (bf16[2,128,512]{2,1,0:T(8,128)(2,1)}, bf16[8,80,512]{2,1,0:T(8,128)(2,1)}, bf16[4,128,512]{2,1,0:T(8,128)(2,1)}) custom-call(bf16[16,64,512]{2,1,0:T(8,128)(2,1)} %get-tuple-element.137.refs_0_, bf16[16,64,512]{2,1,0:T(8,128)(2,1)} %copy-done.2, bf16[8,64,512]{2,1,0:T(8,128)(2,1)} %copy-done.8, bf16[4,64,512]{2,1,0:T(8,128)(2,1)} %copy-done.21, ...), custom_call_target="tpu_custom_call" | custom-call | bytes 8750000 | tf_op jit(solution)/shard_map/reduce_3/pallas_call | solution.py:662
  154.4 2.0 collective-permute-start.29
  158.0 10.3 %attend_back_2.1 = (bf16[16,192,128]{2,1,0:T(8,128)(2,1)}, f32[208,256]{1,0:T(8,128)}, bf16[208,256]{1,0:T(8,128)(2,1)}) custom-call(s32[10]{0:T(128)} %stack.40.refs_0_, bf16[192,2048]{1,0:T(8,128)(2,1)} %get-tuple-element.127.refs_0_.refs_1_, f32[64,2048]{1,0:T(8,128)} %get-tuple-element.128.refs_1_.refs_2_, f32[8,2048]{1,0:T(8,128)} %get-tuple-element.129.refs_2_.refs_3_, ...), custom_call_target="tpu_custom_call" | custom-call | bytes 36050000 | tf_op jit(solution)/shard_map/attend_back_2/pallas_call | solution.py:68
  168.4 3.9 %all-to-all-start.2 = ((bf16[16,192,128]{2,1,0:T(8,128)(2,1)}), bf16[16,192,128]{2,1,0:T(8,128)(2,1)S(1)}, u32[]{:S(2)}, u32[]{:S(2)}) async-start(bf16[16,192,128]{2,1,0:T(8,128)(2,1)} %get-tuple-element.163), calls=%async_computation.2 | async-start | bytes 1572864 | tf_op jit(solution)/shard_map/all_to_all | solution.py:926
  173.9 3.8 %collective-permute-done.32 = bf16[208,256]{1,0:T(8,128)(2,1)S(1)} collective-permute-done((bf16[208,256]{1,0:T(8,128)(2,1)}, bf16[208,256]{1,0:T(8,128)(2,1)S(1)}, u32[]{:S(2)}, u32[]{:S(2)}) %collective-permute-start.32) | collective-permute-done | bytes 106528 | tf_op jit(solution)/shard_map/ppermute | solution.py:687
  178.6 3.2 %reduce_4.1 = (bf16[2,128,512]{2,1,0:T(8,128)(2,1)}, bf16[1,208,256]{2,1,0:T(8,128)(2,1)}, bf16[2,128,512]{2,1,0:T(8,128)(2,1)}, bf16[4,80,512]{2,1,0:T(8,128)(2,1)}) custom-call(bf16[16,64,512]{2,1,0:T(8,128)(2,1)} %get-tuple-element.137.refs_0_, bf16[16,64,512]{2,1,0:T(8,128)(2,1)} %copy-done.2, bf16[8,64,512]{2,1,0:T(8,128)(2,1)} %copy-done.8, ...), custom_call_target="tpu_custom_call" | custom-call | bytes 8750000 | tf_op jit(solution)/shard_map/reduce_4/pallas_call | solution.py:662
  181.8 1.7 collective-permute-start.33
  185.0 2.4 collective-permute-start.36
  187.4 6.3 %collective-permute-done.33.refs_3_ = bf16[4,80,512]{2,1,0:T(8,128)(2,1)S(1)} collective-permute-done((bf16[4,80,512]{2,1,0:T(8,128)(2,1)}, bf16[4,80,512]{2,1,0:T(8,128)(2,1)S(1)}, u32[]{:S(2)}, u32[]{:S(2)}) %collective-permute-start.33) | collective-permute-done | bytes 327712 | tf_op jit(solution)/shard_map/ppermute | solution.py:683
  194.4 1.9 reduce_5.1
  196.3 2.4 collective-permute-start.34
  199.8 9.3 %collective-permute-done.37.refs_3_ = bf16[1,208,256]{2,1,0:T(8,128)(2,1)S(1)} collective-permute-done((bf16[1,208,256]{2,1,0:T(8,128)(2,1)S(1)}, bf16[1,208,256]{2,1,0:T(8,128)(2,1)S(1)}, u32[]{:S(2)}, u32[]{:S(2)}) %collective-permute-start.37) | collective-permute-done | bytes 106528 | tf_op jit(solution)/shard_map/ppermute | solution.py:683
  210.5 1.9 reduce_6.1.refs_13_.refs_2_
  212.4 2.5 reduce_7.1
  216.5 1.9 collective-permute-start.40
  218.6 2.7 %collective-permute-start.38 = (bf16[1,128,512]{2,1,0:T(8,128)(2,1)}, bf16[1,128,512]{2,1,0:T(8,128)(2,1)S(1)}, u32[]{:S(2)}, u32[]{:S(2)}) collective-permute-start(bf16[1,128,512]{2,1,0:T(8,128)(2,1)} %get-tuple-element.177), channel_id=1, source_target_pairs={{0,16},{2,18},{4,20},{6,22},{8,24},{10,26},{12,28},{14,30},{16,0},... | collective-permute-start | bytes 393224 | tf_op jit(solution)/shard_map/ppermute | solution.py:683
  222.3 4.9 %start_grad.1.refs_3_ = f32[2,128,512]{2,1,0:T(8,128)} custom-call(s32[10]{0:T(128)} %stack.40.refs_0_, bf16[2,8,192,128]{3,2,1,0:T(8,128)(2,1)} %bitcast.17, bf16[2,128,512]{2,1,0:T(8,128)(2,1)} %refs_2_.7, f32[2,512]{1,0:T(2,128)} %get-tuple-element.112.refs_2_.refs_3_, f32[3,512]{1,0:T(4,128)} %get-tuple-element.114.refs_2_.refs_5_.refs_4_.refs_9_.refs_8_, ...), custom_call_target="tpu_custom_call" | custom-call | bytes 17500000 | tf_op jit(solution)/shard_map/start_grad/pallas_call | solution.py:68
  227.1 10.5 %collective-permute-done.38.refs_2_.refs_1_ = bf16[1,128,512]{2,1,0:T(8,128)(2,1)S(1)} collective-permute-done((bf16[1,128,512]{2,1,0:T(8,128)(2,1)}, bf16[1,128,512]{2,1,0:T(8,128)(2,1)S(1)}, u32[]{:S(2)}, u32[]{:S(2)}) %collective-permute-start.38) | collective-permute-done | bytes 131104 | tf_op jit(solution)/shard_map/ppermute | solution.py:683
  238.9 1.7 reduce_8.1.refs_3_.refs_1_
  241.7 3.3 %collective-permute-start.49 = (bf16[2,80,512]{2,1,0:T(8,128)(2,1)}, bf16[2,80,512]{2,1,0:T(8,128)(2,1)S(1)}, u32[]{:S(2)}, u32[]{:S(2)}) collective-permute-start(bf16[2,80,512]{2,1,0:T(8,128)(2,1)} %reduce_8.1.refs_3_.refs_1_), channel_id=1, source_target_pairs={{0,12},{2,14},{4,8},{6,10},{8,4},{10,6},{12,0},{14,2},{16,28},{18,... | collective-permute-start | bytes 491528 | tf_op jit(solution)/shard_map/ppermute | solution.py:683
  246.2 2.8 %encoder_back.1.refs_10_ = f32[2,32,512]{2,1,0:T(8,128)} custom-call(bf16[1,128,512]{2,1,0:T(8,128)(2,1)} %get-tuple-element.176.refs_0_, bf16[1,128,512]{2,1,0:T(8,128)(2,1)} %copy-done.40, bf16[512,1024]{1,0:T(8,128)(2,1)} %get-tuple-element.178.refs_2_, bf16[2,80,512]{2,1,0:T(8,128)(2,1)} %reduce_8.1.refs_3_.refs_1_), custom_call_target="tpu_custom_call" | custom-call | bytes 9800000 | tf_op jit(solution)/shard_map/encoder_back/pallas_call | solution.py:68
  249.9 5.0 %place.1 = (f32[256,2048]{1,0:T(8,128)}, f32[1024,512]{1,0:T(8,128)}, f32[256,1536]{1,0:T(8,128)}, f32[3,256]{1,0:T(4,128)}, f32[3,256]{1,0:T(4,128)}, /*index=5...) custom-call(s32[10]{0:T(128)} %stack.40.refs_0_, f32[1,512]{1,0:T(1,128)} %get-tuple-element.179.refs_1_, ...), custom_call_target="tpu_custom_call" | custom-call | bytes 17500000 | tf_op jit(solution)/shard_map/place/pallas_call | solution.py:68
  258.8 3.1 %place_cross.1 = (f32[256,512]{1,0:T(8,128)}, f32[256,512]{1,0:T(8,128)}, f32[256,512]{1,0:T(8,128)}, f32[256,1024]{1,0:T(8,128)}) custom-call(s32[10]{0:T(128)} %stack.40.refs_0_, bf16[2,80,512]{2,1,0:T(8,128)(2,1)} %reduce_8.1.refs_3_.refs_1_, bf16[2,80,512]{2,1,0:T(8,128)(2,1)} %copy-done.51, bf16[2,80,512]{2,1,0:T(8,128)(2,1)} %copy-done.50, ...), custom_call_target="tpu_custom_call" | custom-call | bytes 10850000 | tf_op jit(solution)/shard_map/place_cross/pallas_call | solution.py:68
  (217 shorter events, 45.8 us)
Async XLA Ops:
  3.0 13.5 %collective-permute-start.3 = (bf16[192,512]{1,0:T(8,128)(2,1)}, bf16[192,512]{1,0:T(8,128)(2,1)S(1)}, u32[]{:S(2)}, u32[]{:S(2)}) collective-permute-start(bf16[192,512]{1,0:T(8,128)(2,1)} %get-tuple-element.110), channel_id=1, source_target_pairs={{0,16},{2,18},{4,20},{6,22},{8,24},{10,26},{12,28},{14,30},{16,0},... | collective-permute-start | bytes 589832 | tf_op jit(solution)/shard_map/ppermute | solution.py:683
  7.0 12.0 %collective-permute-start.2 = (bf16[192,512]{1,0:T(8,128)(2,1)}, bf16[192,512]{1,0:T(8,128)(2,1)S(1)}, u32[]{:S(2)}, u32[]{:S(2)}) collective-permute-start(bf16[192,512]{1,0:T(8,128)(2,1)} %get-tuple-element.108.refs_8_.refs_5_.refs_4_), channel_id=1, source_target_pairs={{0,12},{2,14},{4,8},{6,10},{8,4},{10,6},{12,0},{14,2},{16,28},{18,... | collective-permute-start | bytes 589832 | tf_op jit(solution)/shard_map/ppermute | solution.py:683
  9.5 9.5 %collective-permute-start.1 = (bf16[192,512]{1,0:T(8,128)(2,1)}, bf16[192,512]{1,0:T(8,128)(2,1)S(1)}, u32[]{:S(2)}, u32[]{:S(2)}) collective-permute-start(bf16[192,512]{1,0:T(8,128)(2,1)} %get-tuple-element.108.refs_8_.refs_5_.refs_4_), channel_id=1, source_target_pairs={{0,4},{2,6},{4,0},{6,2},{8,12},{10,14},{12,8},{14,10},{16,20},{18,... | collective-permute-start | bytes 589832 | tf_op jit(solution)/shard_map/ppermute | solution.py:683
  10.1 11.8 %collective-permute-start = (bf16[192,512]{1,0:T(8,128)(2,1)}, bf16[192,512]{1,0:T(8,128)(2,1)S(1)}, u32[]{:S(2)}, u32[]{:S(2)}) collective-permute-start(bf16[192,512]{1,0:T(8,128)(2,1)} %get-tuple-element.108.refs_8_.refs_5_.refs_4_), channel_id=1, source_target_pairs={{0,8},{2,10},{4,12},{6,14},{8,0},{10,2},{12,4},{14,6},{16,24},{18,... | collective-permute-start | bytes 589832 | tf_op jit(solution)/shard_map/ppermute | solution.py:683
  21.8 5.0 %collective-permute-start.4 = (bf16[256,256]{1,0:T(8,128)(2,1)S(1)}, bf16[256,256]{1,0:T(8,128)(2,1)S(1)}, u32[]{:S(2)}, u32[]{:S(2)}) collective-permute-start(bf16[256,256]{1,0:T(8,128)(2,1)S(1)} %copy-done.19), channel_id=1, source_target_pairs={{0,1},{1,0},{2,3},{3,2},{4,5},{5,4},{6,7},{7,6},{8,9},{9,8},{10,11... | collective-permute-start | bytes 393224 | tf_op jit(solution)/shard_map/ppermute | solution.py:687
  26.8 36.8 %collective-permute-start.16 = (bf16[1664,512]{1,0:T(8,128)(2,1)}, bf16[1664,512]{1,0:T(8,128)(2,1)S(1)}, u32[]{:S(2)}, u32[]{:S(2)}) collective-permute-start(bf16[1664,512]{1,0:T(8,128)(2,1)} %get-tuple-element.118.refs_4_), channel_id=1, source_target_pairs={{0,1},{1,0},{2,3},{3,2},{4,5},{5,4},{6,7},{7,6},{8,9},{9,8},{10,11... | collective-permute-start | bytes 5111816 | tf_op jit(solution)/shard_map/ppermute | solution.py:687
  28.3 4.0 %collective-permute-start.12 = (bf16[192,512]{1,0:T(8,128)(2,1)S(1)}, bf16[192,512]{1,0:T(8,128)(2,1)S(1)}, u32[]{:S(2)}, u32[]{:S(2)}) collective-permute-start(bf16[192,512]{1,0:T(8,128)(2,1)S(1)} %collective-permute-done.3.refs_9_.refs_8_), channel_id=1, source_target_pairs={{0,2},{2,0},{4,6},{6,4},{8,10},{10,8},{12,14},{14,12},{16,18},{18,... | collective-permute-start | bytes 589832 | tf_op jit(solution)/shard_map/ppermute | solution.py:683
  28.8 8.7 %collective-permute-start.7 = (bf16[192,512]{1,0:T(8,128)(2,1)S(1)}, bf16[192,512]{1,0:T(8,128)(2,1)S(1)}, u32[]{:S(2)}, u32[]{:S(2)}) collective-permute-start(bf16[192,512]{1,0:T(8,128)(2,1)S(1)} %collective-permute-done.3.refs_9_.refs_8_), channel_id=1, source_target_pairs={{0,12},{2,14},{4,8},{6,10},{8,4},{10,6},{12,0},{14,2},{16,28},{18,... | collective-permute-start | bytes 589832 | tf_op jit(solution)/shard_map/ppermute | solution.py:683
  30.3 10.5 %collective-permute-start.6 = (bf16[192,512]{1,0:T(8,128)(2,1)S(1)}, bf16[192,512]{1,0:T(8,128)(2,1)S(1)}, u32[]{:S(2)}, u32[]{:S(2)}) collective-permute-start(bf16[192,512]{1,0:T(8,128)(2,1)S(1)} %collective-permute-done.3.refs_9_.refs_8_), channel_id=1, source_target_pairs={{0,4},{2,6},{4,0},{6,2},{8,12},{10,14},{12,8},{14,10},{16,20},{18,... | collective-permute-start | bytes 589832 | tf_op jit(solution)/shard_map/ppermute | solution.py:683
  30.8 10.0 %collective-permute-start.5 = (bf16[192,512]{1,0:T(8,128)(2,1)S(1)}, bf16[192,512]{1,0:T(8,128)(2,1)S(1)}, u32[]{:S(2)}, u32[]{:S(2)}) collective-permute-start(bf16[192,512]{1,0:T(8,128)(2,1)S(1)} %collective-permute-done.3.refs_9_.refs_8_), channel_id=1, source_target_pairs={{0,8},{2,10},{4,12},{6,14},{8,0},{10,2},{12,4},{14,6},{16,24},{18,... | collective-permute-start | bytes 589832 | tf_op jit(solution)/shard_map/ppermute | solution.py:683
  32.3 8.9 %collective-permute-start.11 = (bf16[192,512]{1,0:T(8,128)(2,1)S(1)}, bf16[192,512]{1,0:T(8,128)(2,1)S(1)}, u32[]{:S(2)}, u32[]{:S(2)}) collective-permute-start(bf16[192,512]{1,0:T(8,128)(2,1)S(1)} %collective-permute-done.2.refs_8_.refs_7_), channel_id=1, source_target_pairs={{0,2},{2,0},{4,6},{6,4},{8,10},{10,8},{12,14},{14,12},{16,18},{18,... | collective-permute-start | bytes 589832 | tf_op jit(solution)/shard_map/ppermute | solution.py:683
  37.6 3.8 %collective-permute-start.10 = (bf16[192,512]{1,0:T(8,128)(2,1)S(1)}, bf16[192,512]{1,0:T(8,128)(2,1)S(1)}, u32[]{:S(2)}, u32[]{:S(2)}) collective-permute-start(bf16[192,512]{1,0:T(8,128)(2,1)S(1)} %collective-permute-done.1.refs_7_.refs_6_), channel_id=1, source_target_pairs={{0,2},{2,0},{4,6},{6,4},{8,10},{10,8},{12,14},{14,12},{16,18},{18,... | collective-permute-start | bytes 589832 | tf_op jit(solution)/shard_map/ppermute | solution.py:683
  63.6 4.4 %collective-permute-start.17 = (bf16[1664,512]{1,0:T(8,128)(2,1)S(1)}, bf16[1664,512]{1,0:T(8,128)(2,1)S(1)}, u32[]{:S(2)}, u32[]{:S(2)}) collective-permute-start(bf16[1664,512]{1,0:T(8,128)(2,1)S(1)} %collective-permute-done.16.refs_2_.refs_10_.refs_9_.refs_6_.refs_8_), channel_id=1, source_target_pairs={{0,2},{2,0},{4,6},{6,4},{8,10},{10,8},{12,14},{14,12},{16,18},{18,... | collective-permute-start | bytes 5111816 | tf_op jit(solution)/shard_map/ppermute | solution.py:683
  63.6 14.2 %all-to-all-start = ((bf16[16,64,128]{2,1,0:T(8,128)(2,1)}), bf16[16,64,128]{2,1,0:T(8,128)(2,1)}, u32[]{:S(2)}, u32[]{:S(2)}) async-start(bf16[16,64,128]{2,1,0:T(8,128)(2,1)} %get-tuple-element.117), calls=%async_computation | async-start | bytes 524288 | tf_op jit(solution)/shard_map/all_to_all | solution.py:793
  75.4 11.7 %collective-permute-start.18 = (bf16[384,512]{1,0:T(8,128)(2,1)}, bf16[384,512]{1,0:T(8,128)(2,1)S(1)}, u32[]{:S(2)}, u32[]{:S(2)}) collective-permute-start(bf16[384,512]{1,0:T(8,128)(2,1)} %get-tuple-element.125), channel_id=1, source_target_pairs={{0,1},{1,0},{2,3},{3,2},{4,5},{5,4},{6,7},{7,6},{8,9},{9,8},{10,11... | collective-permute-start | bytes 1179656 | tf_op jit(solution)/shard_map/ppermute | solution.py:687
  98.4 13.4 %collective-permute-start.20 = (bf16[16,64,512]{2,1,0:T(8,128)(2,1)}, bf16[16,64,512]{2,1,0:T(8,128)(2,1)S(1)}, u32[]{:S(2)}, u32[]{:S(2)}) collective-permute-start(bf16[16,64,512]{2,1,0:T(8,128)(2,1)} %get-tuple-element.138), channel_id=1, source_target_pairs={{0,2},{2,0},{4,6},{6,4},{8,10},{10,8},{12,14},{14,12},{16,18},{18,... | collective-permute-start | bytes 3145736 | tf_op jit(solution)/shard_map/ppermute | solution.py:683
  98.5 13.3 %collective-permute-start.21 = (bf16[16,64,512]{2,1,0:T(8,128)(2,1)}, bf16[16,64,512]{2,1,0:T(8,128)(2,1)S(1)}, u32[]{:S(2)}, u32[]{:S(2)}) collective-permute-start(bf16[16,64,512]{2,1,0:T(8,128)(2,1)} %get-tuple-element.140), channel_id=1, source_target_pairs={{0,2},{2,0},{4,6},{6,4},{8,10},{10,8},{12,14},{14,12},{16,18},{18,... | collective-permute-start | bytes 3145736 | tf_op jit(solution)/shard_map/ppermute | solution.py:683
  99.0 4.4 %collective-permute-start.19 = (bf16[384,512]{1,0:T(8,128)(2,1)}, bf16[384,512]{1,0:T(8,128)(2,1)S(1)}, u32[]{:S(2)}, u32[]{:S(2)}) collective-permute-start(bf16[384,512]{1,0:T(8,128)(2,1)} %copy-done.16), channel_id=1, source_target_pairs={{0,2},{2,0},{4,6},{6,4},{8,10},{10,8},{12,14},{14,12},{16,18},{18,... | collective-permute-start | bytes 1179656 | tf_op jit(solution)/shard_map/ppermute | solution.py:683
  115.9 21.7 %collective-permute-start.23 = (bf16[8,64,512]{2,1,0:T(8,128)(2,1)}, bf16[8,64,512]{2,1,0:T(8,128)(2,1)S(1)}, u32[]{:S(2)}, u32[]{:S(2)}) collective-permute-start(bf16[8,64,512]{2,1,0:T(8,128)(2,1)} %get-tuple-element.143), channel_id=1, source_target_pairs={{0,4},{2,6},{4,0},{6,2},{8,12},{10,14},{12,8},{14,10},{16,20},{18,... | collective-permute-start | bytes 1572872 | tf_op jit(solution)/shard_map/ppermute | solution.py:683
  117.3 20.3 %collective-permute-start.22 = (bf16[8,64,512]{2,1,0:T(8,128)(2,1)}, bf16[8,64,512]{2,1,0:T(8,128)(2,1)S(1)}, u32[]{:S(2)}, u32[]{:S(2)}) collective-permute-start(bf16[8,64,512]{2,1,0:T(8,128)(2,1)} %get-tuple-element.141.refs_10_), channel_id=1, source_target_pairs={{0,1},{1,0},{2,3},{3,2},{4,5},{5,4},{6,7},{7,6},{8,9},{9,8},{10,11... | collective-permute-start | bytes 1572872 | tf_op jit(solution)/shard_map/ppermute | solution.py:687
  122.8 14.8 %all-to-all-start.1 = ((bf16[16,64,128]{2,1,0:T(8,128)(2,1)}), bf16[16,64,128]{2,1,0:T(8,128)(2,1)S(1)}, u32[]{:S(2)}, u32[]{:S(2)}) async-start(bf16[16,64,128]{2,1,0:T(8,128)(2,1)} %bitcast.18), calls=%async_computation.1 | async-start | bytes 524288 | tf_op jit(solution)/shard_map/all_to_all | solution.py:855
  137.6 12.1 %collective-permute-start.27 = (bf16[8,128,512]{2,1,0:T(8,128)(2,1)}, bf16[8,128,512]{2,1,0:T(8,128)(2,1)S(1)}, u32[]{:S(2)}, u32[]{:S(2)}) collective-permute-start(bf16[8,128,512]{2,1,0:T(8,128)(2,1)} %get-tuple-element.159), channel_id=1, source_target_pairs={{0,2},{2,0},{4,6},{6,4},{8,10},{10,8},{12,14},{14,12},{16,18},{18,... | collective-permute-start | bytes 3145736 | tf_op jit(solution)/shard_map/ppermute | solution.py:683
  137.7 12.0 %collective-permute-start.26 = (bf16[8,80,512]{2,1,0:T(8,128)(2,1)}, bf16[8,80,512]{2,1,0:T(8,128)(2,1)S(1)}, u32[]{:S(2)}, u32[]{:S(2)}) collective-permute-start(bf16[8,80,512]{2,1,0:T(8,128)(2,1)} %get-tuple-element.156), channel_id=1, source_target_pairs={{0,2},{2,0},{4,6},{6,4},{8,10},{10,8},{12,14},{14,12},{16,18},{18,... | collective-permute-start | bytes 1966088 | tf_op jit(solution)/shard_map/ppermute | solution.py:683
  140.9 8.8 %collective-permute-start.25 = (bf16[4,64,512]{2,1,0:T(8,128)(2,1)}, bf16[4,64,512]{2,1,0:T(8,128)(2,1)S(1)}, u32[]{:S(2)}, u32[]{:S(2)}) collective-permute-start(bf16[4,64,512]{2,1,0:T(8,128)(2,1)} %get-tuple-element.154), channel_id=1, source_target_pairs={{0,1},{1,0},{2,3},{3,2},{4,5},{5,4},{6,7},{7,6},{8,9},{9,8},{10,11... | collective-permute-start | bytes 786440 | tf_op jit(solution)/shard_map/ppermute | solution.py:687
  141.3 8.3 %collective-permute-start.24 = (bf16[4,64,512]{2,1,0:T(8,128)(2,1)}, bf16[4,64,512]{2,1,0:T(8,128)(2,1)S(1)}, u32[]{:S(2)}, u32[]{:S(2)}) collective-permute-start(bf16[4,64,512]{2,1,0:T(8,128)(2,1)} %get-tuple-element.149.refs_4_), channel_id=1, source_target_pairs={{0,4},{2,6},{4,0},{6,2},{8,12},{10,14},{12,8},{14,10},{16,20},{18,... | collective-permute-start | bytes 786440 | tf_op jit(solution)/shard_map/ppermute | solution.py:683
  154.4 14.0 %collective-permute-start.29 = (bf16[4,128,512]{2,1,0:T(8,128)(2,1)}, bf16[4,128,512]{2,1,0:T(8,128)(2,1)S(1)}, u32[]{:S(2)}, u32[]{:S(2)}) collective-permute-start(bf16[4,128,512]{2,1,0:T(8,128)(2,1)} %get-tuple-element.162), channel_id=1, source_target_pairs={{0,4},{2,6},{4,0},{6,2},{8,12},{10,14},{12,8},{14,10},{16,20},{18,... | collective-permute-start | bytes 1572872 | tf_op jit(solution)/shard_map/ppermute | solution.py:683
  156.4 11.9 %collective-permute-start.28 = (bf16[2,128,512]{2,1,0:T(8,128)(2,1)}, bf16[2,128,512]{2,1,0:T(8,128)(2,1)S(1)}, u32[]{:S(2)}, u32[]{:S(2)}) collective-permute-start(bf16[2,128,512]{2,1,0:T(8,128)(2,1)} %get-tuple-element.160.refs_12_), channel_id=1, source_target_pairs={{0,8},{2,10},{4,12},{6,14},{8,0},{10,2},{12,4},{14,6},{16,24},{18,... | collective-permute-start | bytes 786440 | tf_op jit(solution)/shard_map/ppermute | solution.py:683
  156.4 17.5 %collective-permute-start.30 = (bf16[8,80,512]{2,1,0:T(8,128)(2,1)S(1)}, bf16[8,80,512]{2,1,0:T(8,128)(2,1)S(1)}, u32[]{:S(2)}, u32[]{:S(2)}) collective-permute-start(bf16[8,80,512]{2,1,0:T(8,128)(2,1)S(1)} %copy-done.61), channel_id=1, source_target_pairs={{0,2},{2,0},{4,6},{6,4},{8,10},{10,8},{12,14},{14,12},{16,18},{18,... | collective-permute-start | bytes 1966088 | tf_op jit(solution)/shard_map/ppermute | solution.py:683
  156.4 21.3 %collective-permute-start.31 = (bf16[8,80,512]{2,1,0:T(8,128)(2,1)}, bf16[8,80,512]{2,1,0:T(8,128)(2,1)S(1)}, u32[]{:S(2)}, u32[]{:S(2)}) collective-permute-start(bf16[8,80,512]{2,1,0:T(8,128)(2,1)} %get-tuple-element.167), channel_id=1, source_target_pairs={{0,1},{1,0},{2,3},{3,2},{4,5},{5,4},{6,7},{7,6},{8,9},{9,8},{10,11... | collective-permute-start | bytes 1966088 | tf_op jit(solution)/shard_map/ppermute | solution.py:687
  168.4 53.0 %all-to-all-start.2 = ((bf16[16,192,128]{2,1,0:T(8,128)(2,1)}), bf16[16,192,128]{2,1,0:T(8,128)(2,1)S(1)}, u32[]{:S(2)}, u32[]{:S(2)}) async-start(bf16[16,192,128]{2,1,0:T(8,128)(2,1)} %get-tuple-element.163), calls=%async_computation.2 | async-start | bytes 1572864 | tf_op jit(solution)/shard_map/all_to_all | solution.py:926
  172.3 5.4 %collective-permute-start.32 = (bf16[208,256]{1,0:T(8,128)(2,1)}, bf16[208,256]{1,0:T(8,128)(2,1)S(1)}, u32[]{:S(2)}, u32[]{:S(2)}) collective-permute-start(bf16[208,256]{1,0:T(8,128)(2,1)} %get-tuple-element.170), channel_id=1, source_target_pairs={{0,1},{1,0},{2,3},{3,2},{4,5},{5,4},{6,7},{7,6},{8,9},{9,8},{10,11... | collective-permute-start | bytes 319496 | tf_op jit(solution)/shard_map/ppermute | solution.py:687
  181.8 11.9 %collective-permute-start.33 = (bf16[4,80,512]{2,1,0:T(8,128)(2,1)}, bf16[4,80,512]{2,1,0:T(8,128)(2,1)S(1)}, u32[]{:S(2)}, u32[]{:S(2)}) collective-permute-start(bf16[4,80,512]{2,1,0:T(8,128)(2,1)} %get-tuple-element.171), channel_id=1, source_target_pairs={{0,4},{2,6},{4,0},{6,2},{8,12},{10,14},{12,8},{14,10},{16,20},{18,... | collective-permute-start | bytes 983048 | tf_op jit(solution)/shard_map/ppermute | solution.py:683
  183.5 25.5 %collective-permute-start.35 = (bf16[2,128,512]{2,1,0:T(8,128)(2,1)}, bf16[2,128,512]{2,1,0:T(8,128)(2,1)S(1)}, u32[]{:S(2)}, u32[]{:S(2)}) collective-permute-start(bf16[2,128,512]{2,1,0:T(8,128)(2,1)} %get-tuple-element.172), channel_id=1, source_target_pairs={{0,8},{2,10},{4,12},{6,14},{8,0},{10,2},{12,4},{14,6},{16,24},{18,... | collective-permute-start | bytes 786440 | tf_op jit(solution)/shard_map/ppermute | solution.py:683
  185.0 24.0 %collective-permute-start.36 = (bf16[2,128,512]{2,1,0:T(8,128)(2,1)}, bf16[2,128,512]{2,1,0:T(8,128)(2,1)S(1)}, u32[]{:S(2)}, u32[]{:S(2)}) collective-permute-start(bf16[2,128,512]{2,1,0:T(8,128)(2,1)} %get-tuple-element.173.refs_0_), channel_id=1, source_target_pairs={{0,16},{2,18},{4,20},{6,22},{8,24},{10,26},{12,28},{14,30},{16,0},... | collective-permute-start | bytes 786440 | tf_op jit(solution)/shard_map/ppermute | solution.py:683
  196.3 12.7 %collective-permute-start.34 = (bf16[2,80,512]{2,1,0:T(8,128)(2,1)}, bf16[2,80,512]{2,1,0:T(8,128)(2,1)S(1)}, u32[]{:S(2)}, u32[]{:S(2)}) collective-permute-start(bf16[2,80,512]{2,1,0:T(8,128)(2,1)} %reduce_5.1), channel_id=1, source_target_pairs={{0,8},{2,10},{4,12},{6,14},{8,0},{10,2},{12,4},{14,6},{16,24},{18,... | collective-permute-start | bytes 491528 | tf_op jit(solution)/shard_map/ppermute | solution.py:683
  198.8 10.3 %collective-permute-start.37 = (bf16[1,208,256]{2,1,0:T(8,128)(2,1)S(1)}, bf16[1,208,256]{2,1,0:T(8,128)(2,1)S(1)}, u32[]{:S(2)}, u32[]{:S(2)}) collective-permute-start(bf16[1,208,256]{2,1,0:T(8,128)(2,1)S(1)} %copy-done.59), channel_id=1, source_target_pairs={{0,16},{2,18},{4,20},{6,22},{8,24},{10,26},{12,28},{14,30},{16,0},... | collective-permute-start | bytes 319496 | tf_op jit(solution)/shard_map/ppermute | solution.py:683
  214.9 25.7 %collective-permute-start.42 = (bf16[1,368,512]{2,1,0:T(8,128)(2,1)S(1)}, bf16[1,368,512]{2,1,0:T(8,128)(2,1)S(1)}, u32[]{:S(2)}, u32[]{:S(2)}) collective-permute-start(bf16[1,368,512]{2,1,0:T(8,128)(2,1)S(1)} %copy-done.11), channel_id=1, source_target_pairs={{0,12},{2,14},{4,8},{6,10},{8,4},{10,6},{12,0},{14,2},{16,28},{18,... | collective-permute-start | bytes 1130504 | tf_op jit(solution)/shard_map/ppermute | solution.py:683
  215.0 26.2 %collective-permute-start.41 = (bf16[1,368,512]{2,1,0:T(8,128)(2,1)S(1)}, bf16[1,368,512]{2,1,0:T(8,128)(2,1)S(1)}, u32[]{:S(2)}, u32[]{:S(2)}) collective-permute-start(bf16[1,368,512]{2,1,0:T(8,128)(2,1)S(1)} %copy-done.11), channel_id=1, source_target_pairs={{0,4},{2,6},{4,0},{6,2},{8,12},{10,14},{12,8},{14,10},{16,20},{18,... | collective-permute-start | bytes 1130504 | tf_op jit(solution)/shard_map/ppermute | solution.py:683
  216.5 24.7 %collective-permute-start.40 = (bf16[1,368,512]{2,1,0:T(8,128)(2,1)S(1)}, bf16[1,368,512]{2,1,0:T(8,128)(2,1)S(1)}, u32[]{:S(2)}, u32[]{:S(2)}) collective-permute-start(bf16[1,368,512]{2,1,0:T(8,128)(2,1)S(1)} %copy-done.11), channel_id=1, source_target_pairs={{0,8},{2,10},{4,12},{6,14},{8,0},{10,2},{12,4},{14,6},{16,24},{18,... | collective-permute-start | bytes 1130504 | tf_op jit(solution)/shard_map/ppermute | solution.py:683
  218.4 19.2 %collective-permute-start.39 = (bf16[2,80,512]{2,1,0:T(8,128)(2,1)}, bf16[2,80,512]{2,1,0:T(8,128)(2,1)S(1)}, u32[]{:S(2)}, u32[]{:S(2)}) collective-permute-start(bf16[2,80,512]{2,1,0:T(8,128)(2,1)} %get-tuple-element.175.refs_9_.refs_0_), channel_id=1, source_target_pairs={{0,16},{2,18},{4,20},{6,22},{8,24},{10,26},{12,28},{14,30},{16,0},... | collective-permute-start | bytes 491528 | tf_op jit(solution)/shard_map/ppermute | solution.py:683
  218.6 19.0 %collective-permute-start.38 = (bf16[1,128,512]{2,1,0:T(8,128)(2,1)}, bf16[1,128,512]{2,1,0:T(8,128)(2,1)S(1)}, u32[]{:S(2)}, u32[]{:S(2)}) collective-permute-start(bf16[1,128,512]{2,1,0:T(8,128)(2,1)} %get-tuple-element.177), channel_id=1, source_target_pairs={{0,16},{2,18},{4,20},{6,22},{8,24},{10,26},{12,28},{14,30},{16,0},... | collective-permute-start | bytes 393224 | tf_op jit(solution)/shard_map/ppermute | solution.py:683
  240.6 4.4 %collective-permute-start.43 = (bf16[1,368,512]{2,1,0:T(8,128)(2,1)S(1)}, bf16[1,368,512]{2,1,0:T(8,128)(2,1)S(1)}, u32[]{:S(2)}, u32[]{:S(2)}) collective-permute-start(bf16[1,368,512]{2,1,0:T(8,128)(2,1)S(1)} %copy-done.11), channel_id=1, source_target_pairs={{0,2},{2,0},{4,6},{6,4},{8,10},{10,8},{12,14},{14,12},{16,18},{18,... | collective-permute-start | bytes 1130504 | tf_op jit(solution)/shard_map/ppermute | solution.py:683
  240.7 5.0 %collective-permute-start.46 = (bf16[1,368,512]{2,1,0:T(8,128)(2,1)S(1)}, bf16[1,368,512]{2,1,0:T(8,128)(2,1)S(1)}, u32[]{:S(2)}, u32[]{:S(2)}) collective-permute-start(bf16[1,368,512]{2,1,0:T(8,128)(2,1)S(1)} %collective-permute-done.42.refs_5_), channel_id=1, source_target_pairs={{0,2},{2,0},{4,6},{6,4},{8,10},{10,8},{12,14},{14,12},{16,18},{18,... | collective-permute-start | bytes 1130504 | tf_op jit(solution)/shard_map/ppermute | solution.py:683
  241.2 7.9 %collective-permute-start.45 = (bf16[1,368,512]{2,1,0:T(8,128)(2,1)S(1)}, bf16[1,368,512]{2,1,0:T(8,128)(2,1)S(1)}, u32[]{:S(2)}, u32[]{:S(2)}) collective-permute-start(bf16[1,368,512]{2,1,0:T(8,128)(2,1)S(1)} %collective-permute-done.41.refs_4_), channel_id=1, source_target_pairs={{0,2},{2,0},{4,6},{6,4},{8,10},{10,8},{12,14},{14,12},{16,18},{18,... | collective-permute-start | bytes 1130504 | tf_op jit(solution)/shard_map/ppermute | solution.py:683
  241.3 7.8 %collective-permute-start.44 = (bf16[1,368,512]{2,1,0:T(8,128)(2,1)S(1)}, bf16[1,368,512]{2,1,0:T(8,128)(2,1)S(1)}, u32[]{:S(2)}, u32[]{:S(2)}) collective-permute-start(bf16[1,368,512]{2,1,0:T(8,128)(2,1)S(1)} %collective-permute-done.40.refs_3_), channel_id=1, source_target_pairs={{0,2},{2,0},{4,6},{6,4},{8,10},{10,8},{12,14},{14,12},{16,18},{18,... | collective-permute-start | bytes 1130504 | tf_op jit(solution)/shard_map/ppermute | solution.py:683
  241.7 13.2 %collective-permute-start.49 = (bf16[2,80,512]{2,1,0:T(8,128)(2,1)}, bf16[2,80,512]{2,1,0:T(8,128)(2,1)S(1)}, u32[]{:S(2)}, u32[]{:S(2)}) collective-permute-start(bf16[2,80,512]{2,1,0:T(8,128)(2,1)} %reduce_8.1.refs_3_.refs_1_), channel_id=1, source_target_pairs={{0,12},{2,14},{4,8},{6,10},{8,4},{10,6},{12,0},{14,2},{16,28},{18,... | collective-permute-start | bytes 491528 | tf_op jit(solution)/shard_map/ppermute | solution.py:683
  245.0 9.9 %collective-permute-start.48 = (bf16[2,80,512]{2,1,0:T(8,128)(2,1)}, bf16[2,80,512]{2,1,0:T(8,128)(2,1)S(1)}, u32[]{:S(2)}, u32[]{:S(2)}) collective-permute-start(bf16[2,80,512]{2,1,0:T(8,128)(2,1)} %reduce_8.1.refs_3_.refs_1_), channel_id=1, source_target_pairs={{0,4},{2,6},{4,0},{6,2},{8,12},{10,14},{12,8},{14,10},{16,20},{18,... | collective-permute-start | bytes 491528 | tf_op jit(solution)/shard_map/ppermute | solution.py:683
  245.7 9.3 %collective-permute-start.47 = (bf16[2,80,512]{2,1,0:T(8,128)(2,1)}, bf16[2,80,512]{2,1,0:T(8,128)(2,1)S(1)}, u32[]{:S(2)}, u32[]{:S(2)}) collective-permute-start(bf16[2,80,512]{2,1,0:T(8,128)(2,1)} %reduce_8.1.refs_3_.refs_1_), channel_id=1, source_target_pairs={{0,8},{2,10},{4,12},{6,14},{8,0},{10,2},{12,4},{14,6},{16,24},{18,... | collective-permute-start | bytes 491528 | tf_op jit(solution)/shard_map/ppermute | solution.py:683
  (71 other events, 325.3 us)

commit v3 on v2

--- a/solution.py
+++ b/solution.py
@@ -13,7 +13,12 @@
 F32 = jnp.float32
 BF = jnp.bfloat16
 LOG2E = 1.4426950408889634
-VMEM_LIMIT = 56 * 1024 * 1024
+LARGE, SMALL = 62, 16
+ROOMY = ("split", "prepare", "pack", "unpack", "attend", "encoder_rows", "weights_back", "start_grad")
+
+
+def limit_of(name):
+    return (LARGE if name in ROOMY else SMALL) * 1024 * 1024
 
 
 def nn(a, b):
@@ -46,17 +51,6 @@
 VM = pl.BlockSpec(memory_space=pltpu.VMEM)
 SM = pl.BlockSpec(memory_space=pltpu.SMEM)
 ANY = pl.BlockSpec(memory_space=pl.ANY)
-
-
-TOOK = dict(
-    split=1.7, prepare=2.0, pack=3.7, unpack=1.7, attend=15.0, encoder_rows=6.0, forward=15.0, cross_back=10.6, hidden_back=4.0,
-    weights_back=7.2, attend_back_1=8.4, attend_back_2=10.3, start_grad=5.0, encoder_back=2.8, place=5.0, place_cross=3.1,
-)
-PER_MICROSECOND = 3_500_000
-
-
-def cost_of(name):
-    return pl.CostEstimate(flops=0, bytes_accessed=int(TOOK.get(name, 2.5) * PER_MICROSECOND), transcendentals=0)
 
 
 def call(kernel, name, outs, in_specs, scratch, args, out_specs=None, after=(), grid=()):
@@ -73,8 +67,8 @@
         in_specs=list(in_specs) + [ANY] * len(after),
         out_specs=out_specs or [VM] * len(outs),
         scratch_shapes=scratch,
-        compiler_params=pltpu.CompilerParams(vmem_limit_bytes=VMEM_LIMIT),
-        cost_estimate=cost_of(name),
+        compiler_params=pltpu.CompilerParams(vmem_limit_bytes=limit_of(name)),
+        cost_estimate=pl.CostEstimate(flops=1000, bytes_accessed=1000, transcendentals=0),
     )(*args, *after)
 
 
@@ -629,50 +623,40 @@
     table_out[...] = table
 
 
-def sums(name, outs, after=()):
-    arrays, specs, plan, shapes = [], [], [], []
-    for groups in outs:
-        rows = 0
-        steps = []
-        for terms in groups:
-            spans = []
-            for array, size, index, span, swap in terms:
-                spans.append((len(arrays), span or (0, array.shape[1]), swap))
-                arrays.append(array)
-                specs.append(pl.BlockSpec((size,) + array.shape[1:], lambda g, index=index: (index, 0, 0)))
-            high = spans[0][1][1] - spans[0][1][0]
-            steps.append((rows, rows + high, spans))
-            rows += high
-        plan.append(steps)
-        shapes.append((terms[0][1], rows, array.shape[2]))
+def sums(name, jobs, after=()):
+    arrays, plan, outs = [], [], []
+    for groups, split in jobs:
+        steps, row = [], 0
+        for group in groups:
+            steps.append((row, range(len(arrays), len(arrays) + len(group))))
+            row += group[0].shape[1]
+            arrays += group
+        blocks, width = groups[0][0].shape[0], groups[0][0].shape[2]
+        plan.append((len(outs), blocks, split, steps))
+        outs += [((blocks // 2, row, width), BF)] * 2 if split else [((blocks, row, width), BF)]
     count = len(arrays)
 
     def kernel(*refs):
-        results = refs[count + len(after) :]
-        for out, steps in zip(results, plan):
-            for low, high, spans in steps:
-                total = None
-                for k, (first, last), swap in spans:
-                    value = refs[k][:, first:last, :].astype(F32)
-                    if swap:
-                        value = jnp.concatenate([value[1:2], value[0:1]], axis=0)
-                    total = value if total is None else total + value
-                out[:, low:high, :] = total.astype(BF)
-
-    return pl.pallas_call(
-        kernel,
-        name=name,
-        grid=(1,),
-        out_shape=[jax.ShapeDtypeStruct(shape, BF) for shape in shapes],
-        in_specs=specs + [ANY] * len(after),
-        out_specs=[pl.BlockSpec(shape, lambda g: (0, 0, 0)) for shape in shapes],
-        compiler_params=pltpu.CompilerParams(vmem_limit_bytes=VMEM_LIMIT),
-        cost_estimate=cost_of(name),
-    )(*arrays, *after)
-
-
-def term(array, size, index, span=None, swap=False):
-    return array, size, index, span, swap
+        results = refs[count:]
+        for first, blocks, split, steps in plan:
+            for row, which in steps:
+                total = refs[which[0]][...].astype(F32)
+                for k in which[1:]:
+                    total = total + refs[k][...].astype(F32)
+                total = total.astype(BF)
+                rows = pl.ds(row, total.shape[1])
+                if split:
+                    results[first][:, rows, :] = total[blocks // 2 :]
+                    results[first + 1][:, rows, :] = total[: blocks // 2]
+                else:
+                    results[first][:, rows, :] = total
+
+    return call(kernel, name, outs, [VM] * count, [], arrays, after=after)
+
+
+def pair_kernel(mine, got, out):
+    for k in range(2):
+        out[k] = (mine[k].astype(F32) + got[1 - k].astype(F32)).astype(BF)
 
 
 def tie(value, *others):
@@ -742,8 +726,8 @@
             functools.partial(pack_kernel, [len(group) for group in GROUPS]), "pack", [((size, 512), BF) for size in sizes],
             [SM] + [ANY] * len(weights), [pltpu.SemaphoreType.DMA((13,))], (meta, *weights), after=[small],
         )
-        other_small = over_x(tie(small, packed[0], *blocks[1:5]))
-        near2 = over_x(tie(packed[0], other_small))
+        other_small = over_x(small)
+        near2 = over_x(tie(packed[0], other_small, *blocks[1:5]))
         wh, gains, shifts, steps, step_mine, bias_u, bias_d, all_ids = call(
             unpack_kernel, "unpack",
             [((3 * hd, width), BF), ((3, width), F32), ((3, width), F32), ((seqs, width), F32), ((1, width), F32),
@@ -825,10 +809,10 @@
         (meta, hidden2, gains, shifts, bias_u, bias_d, out_grad, own["up"], own["down"], near2, far2),
         after=hold,
     )
-    hold = []
+    hold, hold_far = [], []
     if fast:
         far4 = over_ctx(tie(near4, h2g), 1)
-        hold = [far4]
+        hold_far = [far4]
         down_got, up_got = over_ctx(down_send, 1), over_ctx(up_send, 1)
     dq, part = call(
         cross_back_kernel, "cross_back",
@@ -839,8 +823,8 @@
     )
     hold = []
     if fast:
-        down_x, up_y = sums(
-            "reduce_1", [[[term(down_keep, 8, 1), term(down_got, 8, 1)]], [[term(up_keep, 8, 1), term(up_got, 8, 1)]]], [dq])
+        down_x, down_kept, up_y, up_kept = sums(
+            "reduce_1", [([[down_keep, down_got]], True), ([[up_keep, up_got]], True)], [dq])
         down_x1, up_y1 = over_x(down_x), over_ctx(up_y, 2)
         hold = [down_x]
     h1g, att_grad, extra2 = call(
@@ -858,18 +842,14 @@
         [((8, 80, width), BF)] * 4 + [((8, enc_rows // 4, width), BF)] * 2,
         [SM] + [VM] * 10,
         [pltpu.VMEM((width, tall), BF), pltpu.VMEM((seqs, width, enc_rows), BF), pltpu.VMEM((seqs, enc_rows, 2 * width), BF)],
-        (meta, h2g, h1g, hidden1, crossed, att, dq, part, enc_all, gains, shifts),
+        (meta, h2g, h1g, hidden1, crossed, att, dq, part, enc_all, gains, shifts), after=hold_far,
     )
     hold = []
     if fast:
         got1, got0, kv_0 = (over_ctx(tie(part, grads, down_x1, up_y1), 1) for part in (send1, send0, kv_send))
 
-        def terms(arrays, size, index, whole=()):
-            found = [term(array, size, index) for array in arrays]
-            return found + [term(array, size, index, rows) for array, rows in whole]
-
-        down_y, up_x = sums(
-            "reduce_2", [[terms([down_keep, down_got, down_x1], 4, 1)], [terms([up_keep, up_got, up_y1], 4, 1)]], [grads, keep1],
+        down_y, down_kept, up_x, up_kept = sums(
+            "reduce_2", [([[down_kept, down_x1]], True), ([[up_kept, up_y1]], True)], [grads, keep1],
         )
         down_y1, up_x1 = over_ctx(down_y, 2), over_x(up_x)
         hold = [down_y]
@@ -881,12 +861,12 @@
     )
     hold = []
     if fast:
-        downs, ups, kvs = [down_keep, down_got, down_x1, down_y1], [up_keep, up_got, up_y1, up_x1], [kv_keep, kv_0]
-        feed_z, cross_x, kv_y = sums(
-            "reduce_3", [[terms(downs, 2, 1), terms(ups, 2, 1)], [terms([keep1, got1], 8, 0)], [terms(kvs, 4, 1)]], [query_acc],
+        feed_z, feed_kept, cross_x, cross_kept, kv_y, kv_kept = sums(
+            "reduce_3",
+            [([[down_kept, down_y1], [up_kept, up_x1]], True), ([[keep1, got1]], False), ([[keep0, got0]], False), ([[kv_keep, kv_0]], True)],
+            [query_acc],
         )
         feed_z1, cross_x1, kv_1 = over_ctx(feed_z, 4), over_x(cross_x), over_ctx(kv_y, 2)
-        kvs = kvs + [kv_1]
         hold = [feed_z]
     joined_grad, u_keep, u_send = call(
         attend_back_second, "attend_back_2",
@@ -901,24 +881,16 @@
     if fast:
         joined_grad, u_send = tie(joined_grad, feed_z1, kv_1), tie(u_send, feed_z1, kv_1)
         u_x1 = over_x(u_send)[None]
-        u_keep = u_keep[None]
-        crosses = [keep0, got0, cross_x1]
-        feed_w, u_sum, kv_z, cross_y = sums(
-            "reduce_4",
-            [[terms(downs, 2, 0, [(feed_z1, (0, 64))]), terms(ups, 2, 0, [(feed_z1, (64, 128))])],
-             [terms([u_keep, u_x1], 1, 0)], [terms(kvs, 2, 1)], [terms(crosses, 4, 1)]],
-        )
-        feed_w1, u_8, kv_2, cross_y1 = over_ctx(feed_w, 8), over_ctx(u_sum, 8), over_ctx(kv_z, 4), over_ctx(cross_y, 2)
-        kvs, crosses = kvs + [kv_2], crosses + [cross_y1]
-        (cross_z,) = sums("reduce_5", [[terms(crosses, 2, 1)]])
-        cross_z1 = over_ctx(cross_z, 4)
-        crosses = crosses + [cross_z1]
+        feed_w, kv_z, kv_kept, cross_y, cross_kept = sums(
+            "reduce_4", [([[feed_kept, feed_z1]], False), ([[kv_kept, kv_1]], True), ([[cross_kept, cross_x1]], True)], [u_send],
+        )
+        feed_w1, kv_2, cross_y1 = over_ctx(feed_w, 8), over_ctx(kv_z, 4), over_ctx(cross_y, 2)
+        cross_z, cross_kept, u_sum = sums("reduce_5", [([[cross_kept, cross_y1]], True), ([[u_keep[None], u_x1]], False)])
+        cross_z1, u_8 = over_ctx(cross_z, 4), over_ctx(u_sum, 8)
         (merged,) = call(
             merge_kernel, "reduce_6", [((1, 368, width), BF)], [VM] * 4, [], (feed_w, feed_w1, u_sum, u_8), after=[cross_z1, kv_2],
         )
-        cross_w, kv_far, kv_near = sums(
-            "reduce_7", [[terms(crosses, 2, 0)], [terms(kvs, 1, 1)], [terms(kvs, 1, 0)]], [merged],
-        )
+        cross_w, kv_far, kv_near = sums("reduce_7", [([[cross_kept, cross_z1]], False), ([[kv_kept, kv_2]], True)], [merged])
         cross_w1, kv_got = over_ctx(cross_w, 8), over_ctx(kv_far, 8)
         merged = tie(merged, cross_w)
         spread_out = [over_ctx(merged, mask) for mask in (4, 2, 6)]
@@ -935,7 +907,9 @@
     )
 
     if fast:
-        (cross_pair,) = sums("reduce_8", [[[term(cross_w, 2, 0), term(cross_w1, 2, 0, None, True)]]], [kv_got, tokens_grad])
+        (cross_pair,) = call(
+            pair_kernel, "reduce_8", [((2, 80, width), BF)], [VM] * 2, [], (cross_w, cross_w1), after=[kv_got, tokens_grad],
+        )
         pieces = [tie(piece, cross_pair) for piece in [merged] + spread_out]
         pieces = pieces + [over_ctx(piece, 1) for piece in pieces]
         (enc_grad,) = call(

time: 263 us -> 239 us (0.909)
  Pallas kernels: 122 us -> 92.4 us
  local copies, waits for them, and re-layouts: 15.8 us -> 25.6 us
  waiting for transfers between devices: 60.6 us -> 54.4 us
    pallas_call x7 -> x0, Pallas kernels: 17.7 us -> none  [sums(): pl.pallas_call(kernel, name=name, grid=(1,), out_shape=[jax.ShapeDtypeStr...]
    pallas_call x18 -> x25, Pallas kernels: 104 us -> 92.4 us  [call(): pl.pallas_call(body, name=name, grid=grid, out_shape=[jax.ShapeDtypeStruc...]
    unnamed x125 -> x149, local copies, waits for them, and re-layouts: 15.3 us -> 25 us
    ppermute x7, waiting for transfers between devices: 12.3 us -> 4.65 us  [over_x(): return lax.ppermute(value, 'fsdp', [(0, 1), (1, 0)])]
    ppermute x47, waiting for transfers between devices: 44.5 us -> 47.5 us  [over_ctx(): return lax.ppermute(value, 'ctx', [(i, i ^ mask) for i in range(16)])]
  transfers between devices with their start and end apart: 57 -> 57, of which waited for: 16 -> 17; matrix products, arithmetic and copies ran while one was open for 0% -> 0% of each run, Pallas kernels for 38% -> 33%
where the time goes in v3:
time: 239 us; the launch traced here: 238 us
  Pallas kernels  92.4 us (39%)
  starting transfers between devices  63.8 us (27%)
  waiting for transfers between devices  54.4 us (23%)
  local copies, waits for them, and re-layouts  25.6 us (11%)
    pallas_call x25, Pallas kernels, call(): pl.pallas_call(body, name=name, grid=grid, out_shape=[jax.ShapeDtypeStruc...  92.4 us
    ppermute x47, waiting for transfers between devices, over_ctx(): return lax.ppermute(value, 'ctx', [(i, i ^ mask) for i in range(16)])  47.5 us
    ppermute x47, starting transfers between devices, over_ctx(): return lax.ppermute(value, 'ctx', [(i, i ^ mask) for i in range(16)])  41.6 us
    unnamed x149, local copies, waits for them, and re-layouts  25 us
    ppermute x7, starting transfers between devices, over_x(): return lax.ppermute(value, 'fsdp', [(0, 1), (1, 0)])  9.31 us
  transfers between devices with their start and end apart: 57, of which 17 were waited for; matrix products, arithmetic and copies ran while one was open for 0% of the time, Pallas kernels for 33%

profile of v3, /device:TPU:0, one launch (start us, length us, event | category | flops | bytes accessed | tf_op | source)
XLA Modules:
  0.0 237.7 jit_solution(3834220990425822779)
XLA Ops:
  1.3 1.7 split.1
  3.0 4.0 %collective-permute-start.4 = (bf16[192,512]{1,0:T(8,128)(2,1)}, bf16[192,512]{1,0:T(8,128)(2,1)S(1)}, u32[]{:S(2)}, u32[]{:S(2)}) collective-permute-start(bf16[192,512]{1,0:T(8,128)(2,1)} %get-tuple-element.125), channel_id=1, source_target_pairs={{0,16},{2,18},{4,20},{6,22},{8,24},{10,26},{12,28},{14,30},{16,0},... | collective-permute-start | bytes 589832 | tf_op jit(solution)/shard_map/ppermute | solution.py:667
  7.1 2.5 %collective-permute-start.3 = (bf16[192,512]{1,0:T(8,128)(2,1)}, bf16[192,512]{1,0:T(8,128)(2,1)S(1)}, u32[]{:S(2)}, u32[]{:S(2)}) collective-permute-start(bf16[192,512]{1,0:T(8,128)(2,1)} %get-tuple-element.118.refs_8_.refs_5_.refs_4_), channel_id=1, source_target_pairs={{0,12},{2,14},{4,8},{6,10},{8,4},{10,6},{12,0},{14,2},{16,28},{18,... | collective-permute-start | bytes 589832 | tf_op jit(solution)/shard_map/ppermute | solution.py:667
  10.6 2.0 prepare.1.refs_8_.refs_2_
  12.5 1.5 collective-permute-start
  14.0 3.7 %pack.1 = (bf16[1664,512]{1,0:T(8,128)(2,1)}, bf16[384,512]{1,0:T(8,128)(2,1)}) custom-call(s32[10]{0:T(128)} %stack.40.refs_0_, bf16[256,1024]{1,0:T(8,128)(2,1)} %refs_1_.10, bf16[256,512]{1,0:T(8,128)(2,1)} %refs_6_.8, bf16[256,512]{1,0:T(8,128)(2,1)} %refs_7_.9, bf16[256,512]{1,0:T(8,128)(2,1)} %refs_5_.5, bf16[256,2048]{1,0:T(8,128)(2,1)} %refs_7_.8, ...), custom_call_target="tpu_custom_call" | custom-call | flops 1000 | bytes 1000 | tf_op jit(solution)/shard_map/pack/pallas_call | solution.py:62
  19.1 2.8 %collective-permute-done.1.refs_6_.refs_5_ = bf16[192,512]{1,0:T(8,128)(2,1)S(1)} collective-permute-done((bf16[192,512]{1,0:T(8,128)(2,1)}, bf16[192,512]{1,0:T(8,128)(2,1)S(1)}, u32[]{:S(2)}, u32[]{:S(2)}) %collective-permute-start.1) | collective-permute-done | bytes 196640 | tf_op jit(solution)/shard_map/ppermute | solution.py:667
  22.6 1.5 collective-permute-start.16
  24.6 1.5 collective-permute-start.7
  27.3 1.5 collective-permute-start.5
  28.8 4.8 %collective-permute-done.7.refs_12_.refs_11_ = bf16[192,512]{1,0:T(8,128)(2,1)} collective-permute-done((bf16[192,512]{1,0:T(8,128)(2,1)}, bf16[192,512]{1,0:T(8,128)(2,1)}, u32[]{:S(2)}, u32[]{:S(2)}) %collective-permute-start.7) | collective-permute-done | bytes 196640 | tf_op jit(solution)/shard_map/ppermute | solution.py:667
  33.6 3.2 %collective-permute-done.6.refs_11_.refs_10_ = bf16[192,512]{1,0:T(8,128)(2,1)} collective-permute-done((bf16[192,512]{1,0:T(8,128)(2,1)}, bf16[192,512]{1,0:T(8,128)(2,1)}, u32[]{:S(2)}, u32[]{:S(2)}) %collective-permute-start.6) | collective-permute-done | bytes 196640 | tf_op jit(solution)/shard_map/ppermute | solution.py:667
  38.8 1.7 unpack.1
  40.6 15.3 %attend.1 = (bf16[2048,512]{1,0:T(8,128)(2,1)}, bf16[192,2048]{1,0:T(8,128)(2,1)}, bf16[16,64,128]{2,1,0:T(8,128)(2,1)}, f32[64,2048]{1,0:T(8,128)}, f32[8,2048]{1,0:T(8,128)}) custom-call(s32[10]{0:T(128)} %stack.40.refs_0_, f32[1,512]{1,0:T(1,128)} %get-tuple-element.121.refs_1_, f32[3,512]{1,0:T(4,128)} %get-tuple-element.122.refs_2_.refs_5_.refs_4_.refs_9_.refs_8_, ...), custom_call_target="tpu_custom_call" | custom-call | flops 1000 | bytes 1000 | tf_op jit(solution)/shard_map/attend/pallas_call | solution.py:62
  55.9 4.6 %collective-permute-done.16.refs_2_.refs_10_.refs_9_.refs_6_.refs_8_ = bf16[1664,512]{1,0:T(8,128)(2,1)S(1)} collective-permute-done((bf16[1664,512]{1,0:T(8,128)(2,1)}, bf16[1664,512]{1,0:T(8,128)(2,1)S(1)}, u32[]{:S(2)}, u32[]{:S(2)}) %collective-permute-start.16) | collective-permute-done | bytes 1703968 | tf_op jit(solution)/shard_map/ppermute | solution.py:671
  60.5 4.4 %all-to-all-start = ((bf16[16,64,128]{2,1,0:T(8,128)(2,1)}), bf16[16,64,128]{2,1,0:T(8,128)(2,1)}, u32[]{:S(2)}, u32[]{:S(2)}) async-start(bf16[16,64,128]{2,1,0:T(8,128)(2,1)} %get-tuple-element.126), calls=%async_computation | async-start | bytes 524288 | tf_op jit(solution)/shard_map/all_to_all | solution.py:777
  65.0 6.2 %encoder_rows.1 = (bf16[2,512,512]{2,1,0:T(8,128)(2,1)}, bf16[2,1024,512]{2,1,0:T(8,128)(2,1)}, bf16[512,1024]{1,0:T(8,128)(2,1)}) custom-call(s32[10]{0:T(128)} %stack.40.refs_0_, bf16[256,1024]{1,0:T(8,128)(2,1)} %refs_1_.10, bf16[1664,512]{1,0:T(8,128)(2,1)} %copy-done, ...), custom_call_target="tpu_custom_call" | custom-call | flops 1000 | bytes 1000 | tf_op jit(solution)/shard_map/encoder_rows/pallas_call | solution.py:62
  71.2 1.6 collective-permute-start.18
  72.8 1.9 all-to-all-done
  76.3 1.6 copy-done.3
  80.7 6.1 %forward.1 = (f32[256,512]{1,0:T(8,128)S(1)}, f32[256,512]{1,0:T(8,128)S(1)}, bf16[256,512]{1,0:T(8,128)(2,1)S(1)}, bf16[2,512,128]{2,1,0:T(8,128)(2,1)S(1)}, bf16[16,128,512]{2,1,0:T(8,128)(2,1)S(1)}) custom-call(s32[10]{0:T(128)S(1)} %copy-done.52, bf16[2,128,512]{2,1,0:T(8,128)(2,1)S(1)} %copy-done.16, f32[2,512]{1,0:T(2,128)S(1)} %copy-done.59, ...), custom_call_target="tpu_custom_call" | custom-call | flops 1000 | bytes 1000 | tf_op jit(solution)/shard_map/forward/pallas_call | solution.py:62
  86.9 7.9 %feed.1 = (bf16[2,128,512]{2,1,0:T(8,128)(2,1)}, f32[256,512]{1,0:T(8,128)S(1)}, f32[16,512]{1,0:T(8,128)S(1)}, bf16[16,64,512]{2,1,0:T(8,128)(2,1)S(1)}, bf16[1...) custom-call(s32[10]{0:T(128)S(1)} %copy-done.52, ...), custom_call_target="tpu_custom_call" | custom-call | flops 1000 | bytes 1000 | tf_op jit(solution)/shard_map/feed/pallas_call | solution.py:62
  95.4 4.6 %cross_back.1 = (bf16[256,512]{1,0:T(8,128)(2,1)S(1)}, bf16[2,1024,512]{2,1,0:T(8,128)(2,1)S(1)}) custom-call(s32[10]{0:T(128)S(1)} %copy-done.52, f32[256,512]{1,0:T(8,128)S(1)} %get-tuple-element.139.refs_1_, bf16[256,512]{1,0:T(8,128)(2,1)S(1)} %get-tuple-element.141.refs_2_, bf16[16,128,512]{2,1,0:T(8,128)(2,1)S(1)} %get-tuple-element.142.refs_3_, ...), custom_call_target="tpu_custom_call" | custom-call | flops 1000 | bytes 1000 | tf_op jit(solution)/shard_map/cross_back/pallas_call | solution.py:62
  104.4 1.5 collective-permute-start.21
  105.9 3.4 %hidden_back.1 = (f32[256,512]{1,0:T(8,128)S(1)}, bf16[2,512,128]{2,1,0:T(8,128)(2,1)}, f32[16,512]{1,0:T(8,128)S(1)}) custom-call(s32[10]{0:T(128)S(1)} %copy-done.52, f32[256,512]{1,0:T(8,128)S(1)} %get-tuple-element.139.refs_1_, f32[256,512]{1,0:T(8,128)S(1)} %get-tuple-element.140.refs_2_.refs_3_, ...), custom_call_target="tpu_custom_call" | custom-call | flops 1000 | bytes 1000 | tf_op jit(solution)/shard_map/hidden_back/pallas_call | solution.py:62
  110.8 3.8 %all-to-all-start.1 = ((bf16[16,64,128]{2,1,0:T(8,128)(2,1)}), bf16[16,64,128]{2,1,0:T(8,128)(2,1)S(1)}, u32[]{:S(2)}, u32[]{:S(2)}) async-start(bf16[16,64,128]{2,1,0:T(8,128)(2,1)} %bitcast.10), calls=%async_computation.1 | async-start | bytes 524288 | tf_op jit(solution)/shard_map/all_to_all | solution.py:839
  117.1 7.2 %weights_back.1 = (bf16[8,80,512]{2,1,0:T(8,128)(2,1)}, bf16[8,80,512]{2,1,0:T(8,128)(2,1)}, bf16[8,80,512]{2,1,0:T(8,128)(2,1)}, bf16[8,80,512]{2,1,0:T(8,128)(...) custom-call(s32[10]{0:T(128)} %stack.40.refs_0_, f32[256,512]{1,0:T(8,128)} %copy-done.5, ...), custom_call_target="tpu_custom_call" | custom-call | flops 1000 | bytes 1000 | tf_op jit(solution)/shard_map/weights_back/pallas_call | solution.py:62
  126.4 1.6 reduce_2.1
  129.1 1.7 collective-permute-start.24
  130.7 6.1 %attend_back_1.1 = (f32[64,2048]{1,0:T(8,128)S(1)}, bf16[128,1024]{1,0:T(8,128)(2,1)S(1)}) custom-call(bf16[192,2048]{1,0:T(8,128)(2,1)S(1)} %copy-done.8, f32[64,2048]{1,0:T(8,128)S(1)} %copy-done.23, f32[8,2048]{1,0:T(8,128)S(1)} %copy-done.46, bf16[16,64,128]{2,1,0:T(8,128)(2,1)S(1)} %all-to-all-done.1.refs_4_.refs_3_, ...), custom_call_target="tpu_custom_call" | custom-call | flops 1000 | bytes 1000 | tf_op jit(solution)/shard_map/attend_back_1/pallas_call | solution.py:62
  138.9 1.7 collective-permute-start.30
  143.1 8.1 %attend_back_2.1 = (bf16[16,192,128]{2,1,0:T(8,128)(2,1)}, f32[208,256]{1,0:T(8,128)S(1)}, bf16[208,256]{1,0:T(8,128)(2,1)S(1)}) custom-call(s32[10]{0:T(128)S(1)} %copy-done.53, bf16[192,2048]{1,0:T(8,128)(2,1)S(1)} %copy-done.8, f32[64,2048]{1,0:T(8,128)S(1)} %copy-done.23, f32[8,2048]{1,0:T(8,128)S(1)} %copy-done.47, ...), custom_call_target="tpu_custom_call" | custom-call | flops 1000 | bytes 1000 | tf_op jit(solution)/shard_map/attend_back_2/pallas_call | solution.py:62
  154.0 4.7 %all-to-all-start.2 = ((bf16[16,192,128]{2,1,0:T(8,128)(2,1)}), bf16[16,192,128]{2,1,0:T(8,128)(2,1)}, u32[]{:S(2)}, u32[]{:S(2)}) async-start(bf16[16,192,128]{2,1,0:T(8,128)(2,1)} %get-tuple-element.179), calls=%async_computation.2 | async-start | bytes 1572864 | tf_op jit(solution)/shard_map/all_to_all | solution.py:898
  163.0 1.8 collective-permute-start.32
  167.3 2.4 collective-permute-start.36
  169.7 7.0 %collective-permute-done.32.refs_1_ = bf16[4,80,512]{2,1,0:T(8,128)(2,1)S(1)} collective-permute-done((bf16[4,80,512]{2,1,0:T(8,128)(2,1)S(1)}, bf16[4,80,512]{2,1,0:T(8,128)(2,1)S(1)}, u32[]{:S(2)}, u32[]{:S(2)}) %collective-permute-start.32) | collective-permute-done | bytes 327712 | tf_op jit(solution)/shard_map/ppermute | solution.py:667
  176.8 2.7 %collective-permute-start.34 = (bf16[2,80,512]{2,1,0:T(8,128)(2,1)S(1)}, bf16[2,80,512]{2,1,0:T(8,128)(2,1)S(1)}, u32[]{:S(2)}, u32[]{:S(2)}) collective-permute-start(bf16[2,80,512]{2,1,0:T(8,128)(2,1)S(1)} %get-tuple-element.190), channel_id=1, source_target_pairs={{0,8},{2,10},{4,12},{6,14},{8,0},{10,2},{12,4},{14,6},{16,24},{18,... | collective-permute-start | bytes 491528 | tf_op jit(solution)/shard_map/ppermute | solution.py:667
  179.4 1.8 collective-permute-start.37
  181.2 1.7 collective-permute-done.35.refs_5_.refs_3_
  182.9 10.7 %collective-permute-done.36.refs_1_ = bf16[2,128,512]{2,1,0:T(8,128)(2,1)S(1)} collective-permute-done((bf16[2,128,512]{2,1,0:T(8,128)(2,1)S(1)}, bf16[2,128,512]{2,1,0:T(8,128)(2,1)S(1)}, u32[]{:S(2)}, u32[]{:S(2)}) %collective-permute-start.36) | collective-permute-done | bytes 262176 | tf_op jit(solution)/shard_map/ppermute | solution.py:667
  193.6 1.8 collective-permute-done.37.refs_3_
  197.7 2.0 collective-permute-start.40
  199.7 2.9 %collective-permute-start.38 = (bf16[1,128,512]{2,1,0:T(8,128)(2,1)}, bf16[1,128,512]{2,1,0:T(8,128)(2,1)S(1)}, u32[]{:S(2)}, u32[]{:S(2)}) collective-permute-start(bf16[1,128,512]{2,1,0:T(8,128)(2,1)} %get-tuple-element.197), channel_id=1, source_target_pairs={{0,16},{2,18},{4,20},{6,22},{8,24},{10,26},{12,28},{14,30},{16,0},... | collective-permute-start | bytes 393224 | tf_op jit(solution)/shard_map/ppermute | solution.py:667
  202.7 4.9 %start_grad.1.refs_3_ = f32[2,128,512]{2,1,0:T(8,128)} custom-call(s32[10]{0:T(128)} %stack.40.refs_0_, bf16[2,8,192,128]{3,2,1,0:T(8,128)(2,1)} %bitcast.11.refs_1_, bf16[2,128,512]{2,1,0:T(8,128)(2,1)} %refs_2_.7, f32[2,512]{1,0:T(2,128)} %get-tuple-element.120.refs_2_.refs_3_, f32[3,512]{1,0:T(4,128)} %get-tuple-element.122.refs_2_.refs_5_.refs_4_.refs_9_.refs_8_, ...), custom_call_target="tpu_custom_call" | custom-call | flops 1000 | bytes 1000 | tf_op jit(solution)/shard_map/start_grad/pallas_call | solution.py:62
  207.6 11.3 %collective-permute-done.38.refs_2_.refs_1_ = bf16[1,128,512]{2,1,0:T(8,128)(2,1)S(1)} collective-permute-done((bf16[1,128,512]{2,1,0:T(8,128)(2,1)}, bf16[1,128,512]{2,1,0:T(8,128)(2,1)S(1)}, u32[]{:S(2)}, u32[]{:S(2)}) %collective-permute-start.38) | collective-permute-done | bytes 131104 | tf_op jit(solution)/shard_map/ppermute | solution.py:667
  222.0 3.2 %collective-permute-start.49 = (bf16[2,80,512]{2,1,0:T(8,128)(2,1)S(1)}, bf16[2,80,512]{2,1,0:T(8,128)(2,1)S(1)}, u32[]{:S(2)}, u32[]{:S(2)}) collective-permute-start(bf16[2,80,512]{2,1,0:T(8,128)(2,1)S(1)} %reduce_8.1.refs_3_.refs_1_), channel_id=1, source_target_pairs={{0,12},{2,14},{4,8},{6,10},{8,4},{10,6},{12,0},{14,2},{16,28},{18,... | collective-permute-start | bytes 491528 | tf_op jit(solution)/shard_map/ppermute | solution.py:667
  228.8 4.4 %place.1 = (f32[256,2048]{1,0:T(8,128)}, f32[1024,512]{1,0:T(8,128)}, f32[256,1536]{1,0:T(8,128)}, f32[3,256]{1,0:T(4,128)}, f32[3,256]{1,0:T(4,128)}, /*index=5...) custom-call(s32[10]{0:T(128)S(1)} %copy-done.54, f32[1,512]{1,0:T(1,128)S(1)} %copy-done.62, ...), custom_call_target="tpu_custom_call" | custom-call | flops 1000 | bytes 1000 | tf_op jit(solution)/shard_map/place/pallas_call | solution.py:62
  235.5 2.2 place_cross.1
  (241 shorter events, 49.0 us)
Async XLA Ops:
  3.0 14.7 %collective-permute-start.4 = (bf16[192,512]{1,0:T(8,128)(2,1)}, bf16[192,512]{1,0:T(8,128)(2,1)S(1)}, u32[]{:S(2)}, u32[]{:S(2)}) collective-permute-start(bf16[192,512]{1,0:T(8,128)(2,1)} %get-tuple-element.125), channel_id=1, source_target_pairs={{0,16},{2,18},{4,20},{6,22},{8,24},{10,26},{12,28},{14,30},{16,0},... | collective-permute-start | bytes 589832 | tf_op jit(solution)/shard_map/ppermute | solution.py:667
  7.1 12.0 %collective-permute-start.3 = (bf16[192,512]{1,0:T(8,128)(2,1)}, bf16[192,512]{1,0:T(8,128)(2,1)S(1)}, u32[]{:S(2)}, u32[]{:S(2)}) collective-permute-start(bf16[192,512]{1,0:T(8,128)(2,1)} %get-tuple-element.118.refs_8_.refs_5_.refs_4_), channel_id=1, source_target_pairs={{0,12},{2,14},{4,8},{6,10},{8,4},{10,6},{12,0},{14,2},{16,28},{18,... | collective-permute-start | bytes 589832 | tf_op jit(solution)/shard_map/ppermute | solution.py:667
  9.6 9.5 %collective-permute-start.2 = (bf16[192,512]{1,0:T(8,128)(2,1)}, bf16[192,512]{1,0:T(8,128)(2,1)S(1)}, u32[]{:S(2)}, u32[]{:S(2)}) collective-permute-start(bf16[192,512]{1,0:T(8,128)(2,1)} %get-tuple-element.118.refs_8_.refs_5_.refs_4_), channel_id=1, source_target_pairs={{0,4},{2,6},{4,0},{6,2},{8,12},{10,14},{12,8},{14,10},{16,20},{18,... | collective-permute-start | bytes 589832 | tf_op jit(solution)/shard_map/ppermute | solution.py:667
  10.1 11.8 %collective-permute-start.1 = (bf16[192,512]{1,0:T(8,128)(2,1)}, bf16[192,512]{1,0:T(8,128)(2,1)S(1)}, u32[]{:S(2)}, u32[]{:S(2)}) collective-permute-start(bf16[192,512]{1,0:T(8,128)(2,1)} %get-tuple-element.118.refs_8_.refs_5_.refs_4_), channel_id=1, source_target_pairs={{0,8},{2,10},{4,12},{6,14},{8,0},{10,2},{12,4},{14,6},{16,24},{18,... | collective-permute-start | bytes 589832 | tf_op jit(solution)/shard_map/ppermute | solution.py:667
  12.5 5.2 %collective-permute-start = (bf16[256,256]{1,0:T(8,128)(2,1)}, bf16[256,256]{1,0:T(8,128)(2,1)S(1)}, u32[]{:S(2)}, u32[]{:S(2)}) collective-permute-start(bf16[256,256]{1,0:T(8,128)(2,1)} %prepare.1.refs_8_.refs_2_), channel_id=1, source_target_pairs={{0,1},{1,0},{2,3},{3,2},{4,5},{5,4},{6,7},{7,6},{8,9},{9,8},{10,11... | collective-permute-start | bytes 393224 | tf_op jit(solution)/shard_map/ppermute | solution.py:671
  22.6 38.0 %collective-permute-start.16 = (bf16[1664,512]{1,0:T(8,128)(2,1)}, bf16[1664,512]{1,0:T(8,128)(2,1)S(1)}, u32[]{:S(2)}, u32[]{:S(2)}) collective-permute-start(bf16[1664,512]{1,0:T(8,128)(2,1)} %get-tuple-element.127.refs_4_), channel_id=1, source_target_pairs={{0,1},{1,0},{2,3},{3,2},{4,5},{5,4},{6,7},{7,6},{8,9},{9,8},{10,11... | collective-permute-start | bytes 5111816 | tf_op jit(solution)/shard_map/ppermute | solution.py:671
  24.1 4.7 %collective-permute-start.12 = (bf16[192,512]{1,0:T(8,128)(2,1)}, bf16[192,512]{1,0:T(8,128)(2,1)}, u32[]{:S(2)}, u32[]{:S(2)}) collective-permute-start(bf16[192,512]{1,0:T(8,128)(2,1)} %copy-done.65), channel_id=1, source_target_pairs={{0,2},{2,0},{4,6},{6,4},{8,10},{10,8},{12,14},{14,12},{16,18},{18,... | collective-permute-start | bytes 589832 | tf_op jit(solution)/shard_map/ppermute | solution.py:667
  24.6 9.0 %collective-permute-start.7 = (bf16[192,512]{1,0:T(8,128)(2,1)}, bf16[192,512]{1,0:T(8,128)(2,1)}, u32[]{:S(2)}, u32[]{:S(2)}) collective-permute-start(bf16[192,512]{1,0:T(8,128)(2,1)} %copy-done.65), channel_id=1, source_target_pairs={{0,12},{2,14},{4,8},{6,10},{8,4},{10,6},{12,0},{14,2},{16,28},{18,... | collective-permute-start | bytes 589832 | tf_op jit(solution)/shard_map/ppermute | solution.py:667
  26.1 10.8 %collective-permute-start.6 = (bf16[192,512]{1,0:T(8,128)(2,1)}, bf16[192,512]{1,0:T(8,128)(2,1)}, u32[]{:S(2)}, u32[]{:S(2)}) collective-permute-start(bf16[192,512]{1,0:T(8,128)(2,1)} %copy-done.65), channel_id=1, source_target_pairs={{0,4},{2,6},{4,0},{6,2},{8,12},{10,14},{12,8},{14,10},{16,20},{18,... | collective-permute-start | bytes 589832 | tf_op jit(solution)/shard_map/ppermute | solution.py:667
  27.3 9.6 %collective-permute-start.5 = (bf16[192,512]{1,0:T(8,128)(2,1)}, bf16[192,512]{1,0:T(8,128)(2,1)S(1)}, u32[]{:S(2)}, u32[]{:S(2)}) collective-permute-start(bf16[192,512]{1,0:T(8,128)(2,1)} %copy-done.65), channel_id=1, source_target_pairs={{0,8},{2,10},{4,12},{6,14},{8,0},{10,2},{12,4},{14,6},{16,24},{18,... | collective-permute-start | bytes 589832 | tf_op jit(solution)/shard_map/ppermute | solution.py:667
  28.8 8.6 %collective-permute-start.11 = (bf16[192,512]{1,0:T(8,128)(2,1)}, bf16[192,512]{1,0:T(8,128)(2,1)S(1)}, u32[]{:S(2)}, u32[]{:S(2)}) collective-permute-start(bf16[192,512]{1,0:T(8,128)(2,1)} %copy-done.66), channel_id=1, source_target_pairs={{0,2},{2,0},{4,6},{6,4},{8,10},{10,8},{12,14},{14,12},{16,18},{18,... | collective-permute-start | bytes 589832 | tf_op jit(solution)/shard_map/ppermute | solution.py:667
  33.6 4.4 %collective-permute-start.10 = (bf16[192,512]{1,0:T(8,128)(2,1)}, bf16[192,512]{1,0:T(8,128)(2,1)S(1)}, u32[]{:S(2)}, u32[]{:S(2)}) collective-permute-start(bf16[192,512]{1,0:T(8,128)(2,1)} %copy-done.67), channel_id=1, source_target_pairs={{0,2},{2,0},{4,6},{6,4},{8,10},{10,8},{12,14},{14,12},{16,18},{18,... | collective-permute-start | bytes 589832 | tf_op jit(solution)/shard_map/ppermute | solution.py:667
  36.9 3.7 %collective-permute-start.9 = (bf16[192,512]{1,0:T(8,128)(2,1)}, bf16[192,512]{1,0:T(8,128)(2,1)}, u32[]{:S(2)}, u32[]{:S(2)}) collective-permute-start(bf16[192,512]{1,0:T(8,128)(2,1)} %copy-done.68), channel_id=1, source_target_pairs={{0,2},{2,0},{4,6},{6,4},{8,10},{10,8},{12,14},{14,12},{16,18},{18,... | collective-permute-start | bytes 589832 | tf_op jit(solution)/shard_map/ppermute | solution.py:667
  60.5 4.4 %collective-permute-start.17 = (bf16[1664,512]{1,0:T(8,128)(2,1)S(1)}, bf16[1664,512]{1,0:T(8,128)(2,1)}, u32[]{:S(2)}, u32[]{:S(2)}) collective-permute-start(bf16[1664,512]{1,0:T(8,128)(2,1)S(1)} %collective-permute-done.16.refs_2_.refs_10_.refs_9_.refs_6_.refs_8_), channel_id=1, source_target_pairs={{0,2},{2,0},{4,6},{6,4},{8,10},{10,8},{12,14},{14,12},{16,18},{18,... | collective-permute-start | bytes 5111816 | tf_op jit(solution)/shard_map/ppermute | solution.py:667
  60.5 14.3 %all-to-all-start = ((bf16[16,64,128]{2,1,0:T(8,128)(2,1)}), bf16[16,64,128]{2,1,0:T(8,128)(2,1)}, u32[]{:S(2)}, u32[]{:S(2)}) async-start(bf16[16,64,128]{2,1,0:T(8,128)(2,1)} %get-tuple-element.126), calls=%async_computation | async-start | bytes 524288 | tf_op jit(solution)/shard_map/all_to_all | solution.py:777
  71.2 15.6 %collective-permute-start.18 = (bf16[384,512]{1,0:T(8,128)(2,1)}, bf16[384,512]{1,0:T(8,128)(2,1)S(1)}, u32[]{:S(2)}, u32[]{:S(2)}) collective-permute-start(bf16[384,512]{1,0:T(8,128)(2,1)} %get-tuple-element.134), channel_id=1, source_target_pairs={{0,1},{1,0},{2,3},{3,2},{4,5},{5,4},{6,7},{7,6},{8,9},{9,8},{10,11... | collective-permute-start | bytes 1179656 | tf_op jit(solution)/shard_map/ppermute | solution.py:671
  94.8 6.5 %collective-permute-start.19 = (bf16[16,64,512]{2,1,0:T(8,128)(2,1)S(1)}, bf16[16,64,512]{2,1,0:T(8,128)(2,1)S(1)}, u32[]{:S(2)}, u32[]{:S(2)}) collective-permute-start(bf16[16,64,512]{2,1,0:T(8,128)(2,1)S(1)} %get-tuple-element.146), channel_id=1, source_target_pairs={{0,2},{2,0},{4,6},{6,4},{8,10},{10,8},{12,14},{14,12},{16,18},{18,... | collective-permute-start | bytes 3145736 | tf_op jit(solution)/shard_map/ppermute | solution.py:667
  94.9 6.4 %collective-permute-start.20 = (bf16[16,64,512]{2,1,0:T(8,128)(2,1)S(1)}, bf16[16,64,512]{2,1,0:T(8,128)(2,1)S(1)}, u32[]{:S(2)}, u32[]{:S(2)}) collective-permute-start(bf16[16,64,512]{2,1,0:T(8,128)(2,1)S(1)} %get-tuple-element.148), channel_id=1, source_target_pairs={{0,2},{2,0},{4,6},{6,4},{8,10},{10,8},{12,14},{14,12},{16,18},{18,... | collective-permute-start | bytes 3145736 | tf_op jit(solution)/shard_map/ppermute | solution.py:667
  104.3 20.3 %collective-permute-start.22 = (bf16[8,64,512]{2,1,0:T(8,128)(2,1)}, bf16[8,64,512]{2,1,0:T(8,128)(2,1)}, u32[]{:S(2)}, u32[]{:S(2)}) collective-permute-start(bf16[8,64,512]{2,1,0:T(8,128)(2,1)} %get-tuple-element.153), channel_id=1, source_target_pairs={{0,4},{2,6},{4,0},{6,2},{8,12},{10,14},{12,8},{14,10},{16,20},{18,... | collective-permute-start | bytes 1572872 | tf_op jit(solution)/shard_map/ppermute | solution.py:667
  104.4 20.2 %collective-permute-start.21 = (bf16[8,64,512]{2,1,0:T(8,128)(2,1)}, bf16[8,64,512]{2,1,0:T(8,128)(2,1)}, u32[]{:S(2)}, u32[]{:S(2)}) collective-permute-start(bf16[8,64,512]{2,1,0:T(8,128)(2,1)} %get-tuple-element.149.refs_10_), channel_id=1, source_target_pairs={{0,1},{1,0},{2,3},{3,2},{4,5},{5,4},{6,7},{7,6},{8,9},{9,8},{10,11... | collective-permute-start | bytes 1572872 | tf_op jit(solution)/shard_map/ppermute | solution.py:671
  110.8 13.8 %all-to-all-start.1 = ((bf16[16,64,128]{2,1,0:T(8,128)(2,1)}), bf16[16,64,128]{2,1,0:T(8,128)(2,1)S(1)}, u32[]{:S(2)}, u32[]{:S(2)}) async-start(bf16[16,64,128]{2,1,0:T(8,128)(2,1)} %bitcast.10), calls=%async_computation.1 | async-start | bytes 524288 | tf_op jit(solution)/shard_map/all_to_all | solution.py:839
  124.6 12.7 %collective-permute-start.28 = (bf16[8,128,512]{2,1,0:T(8,128)(2,1)}, bf16[8,128,512]{2,1,0:T(8,128)(2,1)S(1)}, u32[]{:S(2)}, u32[]{:S(2)}) collective-permute-start(bf16[8,128,512]{2,1,0:T(8,128)(2,1)} %get-tuple-element.175), channel_id=1, source_target_pairs={{0,2},{2,0},{4,6},{6,4},{8,10},{10,8},{12,14},{14,12},{16,18},{18,... | collective-permute-start | bytes 3145736 | tf_op jit(solution)/shard_map/ppermute | solution.py:667
  124.8 12.5 %collective-permute-start.26 = (bf16[8,80,512]{2,1,0:T(8,128)(2,1)}, bf16[8,80,512]{2,1,0:T(8,128)(2,1)S(1)}, u32[]{:S(2)}, u32[]{:S(2)}) collective-permute-start(bf16[8,80,512]{2,1,0:T(8,128)(2,1)} %get-tuple-element.169), channel_id=1, source_target_pairs={{0,2},{2,0},{4,6},{6,4},{8,10},{10,8},{12,14},{14,12},{16,18},{18,... | collective-permute-start | bytes 1966088 | tf_op jit(solution)/shard_map/ppermute | solution.py:667
  125.1 12.2 %collective-permute-start.27 = (bf16[8,80,512]{2,1,0:T(8,128)(2,1)}, bf16[8,80,512]{2,1,0:T(8,128)(2,1)S(1)}, u32[]{:S(2)}, u32[]{:S(2)}) collective-permute-start(bf16[8,80,512]{2,1,0:T(8,128)(2,1)} %get-tuple-element.172), channel_id=1, source_target_pairs={{0,2},{2,0},{4,6},{6,4},{8,10},{10,8},{12,14},{14,12},{16,18},{18,... | collective-permute-start | bytes 1966088 | tf_op jit(solution)/shard_map/ppermute | solution.py:667
  128.0 8.8 %collective-permute-start.25 = (bf16[4,64,512]{2,1,0:T(8,128)(2,1)S(1)}, bf16[4,64,512]{2,1,0:T(8,128)(2,1)S(1)}, u32[]{:S(2)}, u32[]{:S(2)}) collective-permute-start(bf16[4,64,512]{2,1,0:T(8,128)(2,1)S(1)} %get-tuple-element.167), channel_id=1, source_target_pairs={{0,1},{1,0},{2,3},{3,2},{4,5},{5,4},{6,7},{7,6},{8,9},{9,8},{10,11... | collective-permute-start | bytes 786440 | tf_op jit(solution)/shard_map/ppermute | solution.py:671
  129.1 8.3 %collective-permute-start.24 = (bf16[4,64,512]{2,1,0:T(8,128)(2,1)S(1)}, bf16[4,64,512]{2,1,0:T(8,128)(2,1)S(1)}, u32[]{:S(2)}, u32[]{:S(2)}) collective-permute-start(bf16[4,64,512]{2,1,0:T(8,128)(2,1)S(1)} %get-tuple-element.160.refs_4_), channel_id=1, source_target_pairs={{0,4},{2,6},{4,0},{6,2},{8,12},{10,14},{12,8},{14,10},{16,20},{18,... | collective-permute-start | bytes 786440 | tf_op jit(solution)/shard_map/ppermute | solution.py:667
  138.9 14.4 %collective-permute-start.30 = (bf16[4,128,512]{2,1,0:T(8,128)(2,1)S(1)}, bf16[4,128,512]{2,1,0:T(8,128)(2,1)S(1)}, u32[]{:S(2)}, u32[]{:S(2)}) collective-permute-start(bf16[4,128,512]{2,1,0:T(8,128)(2,1)S(1)} %get-tuple-element.178), channel_id=1, source_target_pairs={{0,4},{2,6},{4,0},{6,2},{8,12},{10,14},{12,8},{14,10},{16,20},{18,... | collective-permute-start | bytes 1572872 | tf_op jit(solution)/shard_map/ppermute | solution.py:667
  140.6 12.0 %collective-permute-start.29 = (bf16[2,128,512]{2,1,0:T(8,128)(2,1)S(1)}, bf16[2,128,512]{2,1,0:T(8,128)(2,1)S(1)}, u32[]{:S(2)}, u32[]{:S(2)}) collective-permute-start(bf16[2,128,512]{2,1,0:T(8,128)(2,1)S(1)} %get-tuple-element.176.refs_12_), channel_id=1, source_target_pairs={{0,8},{2,10},{4,12},{6,14},{8,0},{10,2},{12,4},{14,6},{16,24},{18,... | collective-permute-start | bytes 786440 | tf_op jit(solution)/shard_map/ppermute | solution.py:667
  142.0 16.8 %collective-permute-start.31 = (bf16[8,80,512]{2,1,0:T(8,128)(2,1)}, bf16[8,80,512]{2,1,0:T(8,128)(2,1)S(1)}, u32[]{:S(2)}, u32[]{:S(2)}) collective-permute-start(bf16[8,80,512]{2,1,0:T(8,128)(2,1)} %get-tuple-element.183), channel_id=1, source_target_pairs={{0,1},{1,0},{2,3},{3,2},{4,5},{5,4},{6,7},{7,6},{8,9},{9,8},{10,11... | collective-permute-start | bytes 1966088 | tf_op jit(solution)/shard_map/ppermute | solution.py:671
  154.0 48.6 %all-to-all-start.2 = ((bf16[16,192,128]{2,1,0:T(8,128)(2,1)}), bf16[16,192,128]{2,1,0:T(8,128)(2,1)}, u32[]{:S(2)}, u32[]{:S(2)}) async-start(bf16[16,192,128]{2,1,0:T(8,128)(2,1)} %get-tuple-element.179), calls=%async_computation.2 | async-start | bytes 1572864 | tf_op jit(solution)/shard_map/all_to_all | solution.py:898
  163.0 13.7 %collective-permute-start.32 = (bf16[4,80,512]{2,1,0:T(8,128)(2,1)S(1)}, bf16[4,80,512]{2,1,0:T(8,128)(2,1)S(1)}, u32[]{:S(2)}, u32[]{:S(2)}) collective-permute-start(bf16[4,80,512]{2,1,0:T(8,128)(2,1)S(1)} %get-tuple-element.187), channel_id=1, source_target_pairs={{0,4},{2,6},{4,0},{6,2},{8,12},{10,14},{12,8},{14,10},{16,20},{18,... | collective-permute-start | bytes 983048 | tf_op jit(solution)/shard_map/ppermute | solution.py:667
  164.8 4.9 %collective-permute-start.33 = (bf16[208,256]{1,0:T(8,128)(2,1)S(1)}, bf16[208,256]{1,0:T(8,128)(2,1)S(1)}, u32[]{:S(2)}, u32[]{:S(2)}) collective-permute-start(bf16[208,256]{1,0:T(8,128)(2,1)S(1)} %copy-done.56), channel_id=1, source_target_pairs={{0,1},{1,0},{2,3},{3,2},{4,5},{5,4},{6,7},{7,6},{8,9},{9,8},{10,11... | collective-permute-start | bytes 319496 | tf_op jit(solution)/shard_map/ppermute | solution.py:671
  165.8 17.1 %collective-permute-start.35 = (bf16[2,128,512]{2,1,0:T(8,128)(2,1)S(1)}, bf16[2,128,512]{2,1,0:T(8,128)(2,1)S(1)}, u32[]{:S(2)}, u32[]{:S(2)}) collective-permute-start(bf16[2,128,512]{2,1,0:T(8,128)(2,1)S(1)} %get-tuple-element.192), channel_id=1, source_target_pairs={{0,8},{2,10},{4,12},{6,14},{8,0},{10,2},{12,4},{14,6},{16,24},{18,... | collective-permute-start | bytes 786440 | tf_op jit(solution)/shard_map/ppermute | solution.py:667
  167.3 26.3 %collective-permute-start.36 = (bf16[2,128,512]{2,1,0:T(8,128)(2,1)S(1)}, bf16[2,128,512]{2,1,0:T(8,128)(2,1)S(1)}, u32[]{:S(2)}, u32[]{:S(2)}) collective-permute-start(bf16[2,128,512]{2,1,0:T(8,128)(2,1)S(1)} %get-tuple-element.193.refs_0_), channel_id=1, source_target_pairs={{0,16},{2,18},{4,20},{6,22},{8,24},{10,26},{12,28},{14,30},{16,0},... | collective-permute-start | bytes 786440 | tf_op jit(solution)/shard_map/ppermute | solution.py:667
  176.8 18.7 %collective-permute-start.34 = (bf16[2,80,512]{2,1,0:T(8,128)(2,1)S(1)}, bf16[2,80,512]{2,1,0:T(8,128)(2,1)S(1)}, u32[]{:S(2)}, u32[]{:S(2)}) collective-permute-start(bf16[2,80,512]{2,1,0:T(8,128)(2,1)S(1)} %get-tuple-element.190), channel_id=1, source_target_pairs={{0,8},{2,10},{4,12},{6,14},{8,0},{10,2},{12,4},{14,6},{16,24},{18,... | collective-permute-start | bytes 491528 | tf_op jit(solution)/shard_map/ppermute | solution.py:667
  179.4 16.0 %collective-permute-start.37 = (bf16[1,208,256]{2,1,0:T(8,128)(2,1)S(1)}, bf16[1,208,256]{2,1,0:T(8,128)(2,1)S(1)}, u32[]{:S(2)}, u32[]{:S(2)}) collective-permute-start(bf16[1,208,256]{2,1,0:T(8,128)(2,1)S(1)} %get-tuple-element.194.refs_2_), channel_id=1, source_target_pairs={{0,16},{2,18},{4,20},{6,22},{8,24},{10,26},{12,28},{14,30},{16,0},... | collective-permute-start | bytes 319496 | tf_op jit(solution)/shard_map/ppermute | solution.py:667
  196.2 24.7 %collective-permute-start.42 = (bf16[1,368,512]{2,1,0:T(8,128)(2,1)S(1)}, bf16[1,368,512]{2,1,0:T(8,128)(2,1)}, u32[]{:S(2)}, u32[]{:S(2)}) collective-permute-start(bf16[1,368,512]{2,1,0:T(8,128)(2,1)S(1)} %reduce_6.1.refs_4_.refs_2_), channel_id=1, source_target_pairs={{0,12},{2,14},{4,8},{6,10},{8,4},{10,6},{12,0},{14,2},{16,28},{18,... | collective-permute-start | bytes 1130504 | tf_op jit(solution)/shard_map/ppermute | solution.py:667
  196.2 25.2 %collective-permute-start.41 = (bf16[1,368,512]{2,1,0:T(8,128)(2,1)S(1)}, bf16[1,368,512]{2,1,0:T(8,128)(2,1)}, u32[]{:S(2)}, u32[]{:S(2)}) collective-permute-start(bf16[1,368,512]{2,1,0:T(8,128)(2,1)S(1)} %reduce_6.1.refs_4_.refs_2_), channel_id=1, source_target_pairs={{0,4},{2,6},{4,0},{6,2},{8,12},{10,14},{12,8},{14,10},{16,20},{18,... | collective-permute-start | bytes 1130504 | tf_op jit(solution)/shard_map/ppermute | solution.py:667
  197.7 24.3 %collective-permute-start.40 = (bf16[1,368,512]{2,1,0:T(8,128)(2,1)S(1)}, bf16[1,368,512]{2,1,0:T(8,128)(2,1)}, u32[]{:S(2)}, u32[]{:S(2)}) collective-permute-start(bf16[1,368,512]{2,1,0:T(8,128)(2,1)S(1)} %reduce_6.1.refs_4_.refs_2_), channel_id=1, source_target_pairs={{0,8},{2,10},{4,12},{6,14},{8,0},{10,2},{12,4},{14,6},{16,24},{18,... | collective-permute-start | bytes 1130504 | tf_op jit(solution)/shard_map/ppermute | solution.py:667
  199.7 19.2 %collective-permute-start.39 = (bf16[2,80,512]{2,1,0:T(8,128)(2,1)S(1)}, bf16[2,80,512]{2,1,0:T(8,128)(2,1)S(1)}, u32[]{:S(2)}, u32[]{:S(2)}) collective-permute-start(bf16[2,80,512]{2,1,0:T(8,128)(2,1)S(1)} %get-tuple-element.195.refs_9_.refs_0_), channel_id=1, source_target_pairs={{0,16},{2,18},{4,20},{6,22},{8,24},{10,26},{12,28},{14,30},{16,0},... | collective-permute-start | bytes 491528 | tf_op jit(solution)/shard_map/ppermute | solution.py:667
  199.7 19.2 %collective-permute-start.38 = (bf16[1,128,512]{2,1,0:T(8,128)(2,1)}, bf16[1,128,512]{2,1,0:T(8,128)(2,1)S(1)}, u32[]{:S(2)}, u32[]{:S(2)}) collective-permute-start(bf16[1,128,512]{2,1,0:T(8,128)(2,1)} %get-tuple-element.197), channel_id=1, source_target_pairs={{0,16},{2,18},{4,20},{6,22},{8,24},{10,26},{12,28},{14,30},{16,0},... | collective-permute-start | bytes 393224 | tf_op jit(solution)/shard_map/ppermute | solution.py:667
  220.9 4.4 %collective-permute-start.43 = (bf16[1,368,512]{2,1,0:T(8,128)(2,1)S(1)}, bf16[1,368,512]{2,1,0:T(8,128)(2,1)S(1)}, u32[]{:S(2)}, u32[]{:S(2)}) collective-permute-start(bf16[1,368,512]{2,1,0:T(8,128)(2,1)S(1)} %reduce_6.1.refs_4_.refs_2_), channel_id=1, source_target_pairs={{0,2},{2,0},{4,6},{6,4},{8,10},{10,8},{12,14},{14,12},{16,18},{18,... | collective-permute-start | bytes 1130504 | tf_op jit(solution)/shard_map/ppermute | solution.py:667
  221.0 5.0 %collective-permute-start.46 = (bf16[1,368,512]{2,1,0:T(8,128)(2,1)}, bf16[1,368,512]{2,1,0:T(8,128)(2,1)S(1)}, u32[]{:S(2)}, u32[]{:S(2)}) collective-permute-start(bf16[1,368,512]{2,1,0:T(8,128)(2,1)} %collective-permute-done.42.refs_5_), channel_id=1, source_target_pairs={{0,2},{2,0},{4,6},{6,4},{8,10},{10,8},{12,14},{14,12},{16,18},{18,... | collective-permute-start | bytes 1130504 | tf_op jit(solution)/shard_map/ppermute | solution.py:667
  221.5 6.4 %collective-permute-start.45 = (bf16[1,368,512]{2,1,0:T(8,128)(2,1)}, bf16[1,368,512]{2,1,0:T(8,128)(2,1)S(1)}, u32[]{:S(2)}, u32[]{:S(2)}) collective-permute-start(bf16[1,368,512]{2,1,0:T(8,128)(2,1)} %collective-permute-done.41.refs_4_), channel_id=1, source_target_pairs={{0,2},{2,0},{4,6},{6,4},{8,10},{10,8},{12,14},{14,12},{16,18},{18,... | collective-permute-start | bytes 1130504 | tf_op jit(solution)/shard_map/ppermute | solution.py:667
  222.0 5.9 %collective-permute-start.44 = (bf16[1,368,512]{2,1,0:T(8,128)(2,1)}, bf16[1,368,512]{2,1,0:T(8,128)(2,1)S(1)}, u32[]{:S(2)}, u32[]{:S(2)}) collective-permute-start(bf16[1,368,512]{2,1,0:T(8,128)(2,1)} %collective-permute-done.40.refs_3_), channel_id=1, source_target_pairs={{0,2},{2,0},{4,6},{6,4},{8,10},{10,8},{12,14},{14,12},{16,18},{18,... | collective-permute-start | bytes 1130504 | tf_op jit(solution)/shard_map/ppermute | solution.py:667
  222.0 11.2 %collective-permute-start.49 = (bf16[2,80,512]{2,1,0:T(8,128)(2,1)S(1)}, bf16[2,80,512]{2,1,0:T(8,128)(2,1)S(1)}, u32[]{:S(2)}, u32[]{:S(2)}) collective-permute-start(bf16[2,80,512]{2,1,0:T(8,128)(2,1)S(1)} %reduce_8.1.refs_3_.refs_1_), channel_id=1, source_target_pairs={{0,12},{2,14},{4,8},{6,10},{8,4},{10,6},{12,0},{14,2},{16,28},{18,... | collective-permute-start | bytes 491528 | tf_op jit(solution)/shard_map/ppermute | solution.py:667
  225.3 8.0 %collective-permute-start.48 = (bf16[2,80,512]{2,1,0:T(8,128)(2,1)S(1)}, bf16[2,80,512]{2,1,0:T(8,128)(2,1)S(1)}, u32[]{:S(2)}, u32[]{:S(2)}) collective-permute-start(bf16[2,80,512]{2,1,0:T(8,128)(2,1)S(1)} %reduce_8.1.refs_3_.refs_1_), channel_id=1, source_target_pairs={{0,4},{2,6},{4,0},{6,2},{8,12},{10,14},{12,8},{14,10},{16,20},{18,... | collective-permute-start | bytes 491528 | tf_op jit(solution)/shard_map/ppermute | solution.py:667
  226.0 7.3 %collective-permute-start.47 = (bf16[2,80,512]{2,1,0:T(8,128)(2,1)S(1)}, bf16[2,80,512]{2,1,0:T(8,128)(2,1)S(1)}, u32[]{:S(2)}, u32[]{:S(2)}) collective-permute-start(bf16[2,80,512]{2,1,0:T(8,128)(2,1)S(1)} %reduce_8.1.refs_3_.refs_1_), channel_id=1, source_target_pairs={{0,8},{2,10},{4,12},{6,14},{8,0},{10,2},{12,4},{14,6},{16,24},{18,... | collective-permute-start | bytes 491528 | tf_op jit(solution)/shard_map/ppermute | solution.py:667
  (83 other events, 506.9 us)

commit v4 on v3

--- a/solution.py
+++ b/solution.py
@@ -53,23 +53,20 @@
 ANY = pl.BlockSpec(memory_space=pl.ANY)
 
 
-def call(kernel, name, outs, in_specs, scratch, args, out_specs=None, after=(), grid=()):
-    count = len(in_specs)
-
-    def body(*refs):
-        kernel(*refs[:count], *refs[count + len(after) :])
-
+def call(kernel, name, outs, in_specs, scratch, args, out_specs=None, after=()):
+    args = list(args)
+    if after:
+        args[0] = tie(args[0], *after)
     return pl.pallas_call(
-        body,
+        kernel,
         name=name,
-        grid=grid,
         out_shape=[jax.ShapeDtypeStruct(s, d) for s, d in outs],
-        in_specs=list(in_specs) + [ANY] * len(after),
+        in_specs=in_specs,
         out_specs=out_specs or [VM] * len(outs),
         scratch_shapes=scratch,
         compiler_params=pltpu.CompilerParams(vmem_limit_bytes=limit_of(name)),
         cost_estimate=pl.CostEstimate(flops=1000, bytes_accessed=1000, transcendentals=0),
-    )(*args, *after)
+    )(*args)
 
 
 class Placer:
@@ -128,7 +125,7 @@
         joined_out[:, cols] = nt(wh[...], normed[cols, :]).astype(BF)
     keys[...] = flip(joined_out[hd : 2 * hd, :].astype(F32)).astype(BF)
     factor = LOG2E / math.sqrt(hd)
-    wide = 256
+    wide = 1024
 
     def query_block(b, carry):
         cols = aligned(b * wide, wide)
@@ -136,7 +133,7 @@
         peak = jnp.max(scores, axis=0, keepdims=True)
         shares = jnp.exp2(scores - peak)
         total = jnp.sum(shares, axis=0, keepdims=True)
-        out = nn(joined_out[2 * hd : 3 * hd, :], shares.astype(BF)) / total
+        out = nn(joined_out[2 * hd : 3 * hd, :], shares.astype(BF)) * (1.0 / total)
         full_out[:, cols] = out
         stats_out[0:1, cols] = peak + jnp.log2(total)
         for part in range(wide // rows):
@@ -311,7 +308,7 @@
     wait(copies)
 
 
-GROUPS = (("keyval", "out", "query", "cross", "up", "down"), ("joined",))
+GROUPS = (("keyval", "out", "query", "cross", "up"), ("down",), ("joined",))
 
 
 def chunk_at(meta, k, xr):
@@ -361,11 +358,11 @@
         h2_out[at, :] = h1_out[at, :] + nn(flip(crossed_out[s]), w_cross[...])
 
 
-TOGETHER = 4
+TOGETHER = 8
 
 
 def feed_kernel(
-    meta, hidden2_in, gains, shifts, up_bias, down_bias, out_grad, own_up, own_down, near2, far2,
+    meta, hidden2_in, gains, shifts, up_bias, down_bias, out_grad, own_up, own_down, near2, far2, near3, far3,
     mixed_out, h2g_out, extra_out, down_keep, down_send, up_keep, up_send, w_up, w_down, act_t, n2_t, pre_low, sems,
 ):
     seqs, rows, width = out_grad.shape
@@ -373,7 +370,7 @@
     slots = extra_out.shape[0]
     put = Placer(sems, meta[0], meta[1])
     c_up = put.lay(own_up, near2, far2, w_up, 5 * (own_up.shape[0] // 2), 4)
-    c_down = put.lay(own_down, near2, far2, w_down, 9 * (own_up.shape[0] // 2), 1)
+    c_down = put.lay(own_down, near3, far3, w_down, 0, 1)
     hidden2 = hidden2_in[...]
     xhat2, r2 = normalise(hidden2)
     n2 = (xhat2 * gains[2:3, :] + shifts[2:3, :]).astype(BF)
@@ -727,7 +724,7 @@
             [SM] + [ANY] * len(weights), [pltpu.SemaphoreType.DMA((13,))], (meta, *weights), after=[small],
         )
         other_small = over_x(small)
-        near2 = over_x(tie(packed[0], other_small, *blocks[1:5]))
+        near2, near3 = (over_x(tie(p, other_small, *blocks[1:5])) for p in packed[:2])
         wh, gains, shifts, steps, step_mine, bias_u, bias_d, all_ids = call(
             unpack_kernel, "unpack",
             [((3 * hd, width), BF), ((3, width), F32), ((3, width), F32), ((seqs, width), F32), ((1, width), F32),
@@ -756,7 +753,7 @@
                 parts += [part[:, b : b + 512] for b in range(0, part.shape[1], 512)]
             return jnp.concatenate(parts, axis=0)
 
-        (near2, far2), (near4, far4) = ([group(names, w) for w in (0, 1)] for names in GROUPS)
+        (near2, far2), (near3, far3), (near4, far4) = ([group(names, w) for w in (0, 1)] for names in GROUPS)
         by_head = full["joined"].reshape(width, 3, H, hd)
         wh = lax.dynamic_index_in_dim(by_head, head, 2, False).reshape(width, 3 * hd).T
         onehot = (jnp.arange(steps_count, dtype=jnp.int32)[None, :] == step_ids[:, None]).astype(BF)
@@ -788,7 +785,7 @@
         (meta, own["keyval"], near2, far2, *blocks),
     )
     if fast:
-        near4 = over_x(tie(packed[1], kvt))
+        near4 = over_x(tie(packed[2], kvt))
         hold = [near4]
 
     tall = seqs * rows
@@ -800,16 +797,17 @@
         [square] * 3 + [pltpu.SemaphoreType.DMA((9,))],
         (meta, tokens, steps, att, kvt, gains, shifts, own["out"], own["query"], own["cross"], near2, far2),
     )
+    if fast:
+        far3 = over_ctx(tie(near3, hidden2), 1)
     mixed, h2g, extra1, down_keep, down_send, up_keep, up_send = call(
         feed_kernel, "feed",
         [((seqs, rows, width), BF), ((tall, width), F32), ((extra_rows, width), F32)] + [((16, 64, width), BF)] * 4,
-        [SM] + [VM] * 6 + [ANY] * 4,
+        [SM] + [VM] * 6 + [ANY] * 6,
         [pltpu.VMEM((width, ff), BF), pltpu.VMEM((ff, width), BF), pltpu.VMEM((ff, tall), BF),
          pltpu.VMEM((width, tall), BF), pltpu.VMEM((tall, ff), BF), pltpu.SemaphoreType.DMA((12,))],
-        (meta, hidden2, gains, shifts, bias_u, bias_d, out_grad, own["up"], own["down"], near2, far2),
-        after=hold,
-    )
-    hold, hold_far = [], []
+        (meta, hidden2, gains, shifts, bias_u, bias_d, out_grad, own["up"], own["down"], near2, far2, near3, far3),
+    )
+    hold_far = []
     if fast:
         far4 = over_ctx(tie(near4, h2g), 1)
         hold_far = [far4]
@@ -819,7 +817,7 @@
         [((tall, width), BF), ((seqs, 2 * width, enc_rows), BF)],
         [SM] + [VM] * 4 + [ANY] * 3,
         [square, pltpu.VMEM((tall, width), BF), pltpu.SemaphoreType.DMA((3,))],
-        (meta, h2g, q, shares, kvt, own["cross"], near2, far2), after=hold,
+        (meta, h2g, q, shares, kvt, own["cross"], near2, far2),
     )
     hold = []
     if fast:

time: 239 us -> 231 us (0.967)
  local copies, waits for them, and re-layouts: 25.6 us -> 22 us
  Pallas kernels: 92.4 us -> 89.8 us
    ppermute x7 -> x8, waiting for transfers between devices: 4.65 us -> 0.32 us  [over_x(): return lax.ppermute(value, 'fsdp', [(0, 1), (1, 0)])]
    unnamed x149 -> x143, local copies, waits for them, and re-layouts: 25 us -> 21.3 us
    ppermute x47 -> x48, waiting for transfers between devices: 47.5 us -> 50.3 us  [over_ctx(): return lax.ppermute(value, 'ctx', [(i, i ^ mask) for i in range(16)])]
    pallas_call x25, Pallas kernels: 92.4 us -> 89.8 us  [call(): pl.pallas_call(kernel, name=name, out_shape=[jax.ShapeDtypeStruct(s, d) f...]
    ppermute x7 -> x8, starting transfers between devices: 9.31 us -> 8.26 us  [over_x(): return lax.ppermute(value, 'fsdp', [(0, 1), (1, 0)])]
    ppermute x47 -> x48, starting transfers between devices: 41.6 us -> 41.5 us  [over_ctx(): return lax.ppermute(value, 'ctx', [(i, i ^ mask) for i in range(16)])]
  transfers between devices with their start and end apart: 57 -> 59, of which waited for: 17 -> 19; matrix products, arithmetic and copies ran while one was open for 0% -> 0% of each run, Pallas kernels for 33% -> 33%
where the time goes in v4:
time: 231 us; the launch traced here: 230 us
  Pallas kernels  89.8 us (39%)
  starting transfers between devices  62.7 us (27%)
  waiting for transfers between devices  54.4 us (24%)
  local copies, waits for them, and re-layouts  22 us (10%)
    pallas_call x25, Pallas kernels, call(): pl.pallas_call(kernel, name=name, out_shape=[jax.ShapeDtypeStruct(s, d) f...  89.8 us
    ppermute x48, waiting for transfers between devices, over_ctx(): return lax.ppermute(value, 'ctx', [(i, i ^ mask) for i in range(16)])  50.3 us
    ppermute x48, starting transfers between devices, over_ctx(): return lax.ppermute(value, 'ctx', [(i, i ^ mask) for i in range(16)])  41.5 us
    unnamed x143, local copies, waits for them, and re-layouts  21.3 us
    ppermute x8, starting transfers between devices, over_x(): return lax.ppermute(value, 'fsdp', [(0, 1), (1, 0)])  8.26 us
    all_to_all x1, starting transfers between devices, shards(): dj = lax.all_to_all(joined_grad, 'ctx', 0, 0, tiled=True)  4.94 us
  transfers between devices with their start and end apart: 59, of which 19 were waited for; matrix products, arithmetic and copies ran while one was open for 0% of the time, Pallas kernels for 33%

profile of v4, /device:TPU:0, one launch (start us, length us, event | category | flops | bytes accessed | tf_op | source)
XLA Modules:
  0.0 230.3 jit_solution(12198727724057059154)
XLA Ops:
  1.4 1.7 split.1
  3.1 4.0 %collective-permute-start.4 = (bf16[192,512]{1,0:T(8,128)(2,1)}, bf16[192,512]{1,0:T(8,128)(2,1)S(1)}, u32[]{:S(2)}, u32[]{:S(2)}) collective-permute-start(bf16[192,512]{1,0:T(8,128)(2,1)} %get-tuple-element.148), channel_id=1, source_target_pairs={{0,16},{2,18},{4,20},{6,22},{8,24},{10,26},{12,28},{14,30},{16,0},... | collective-permute-start | bytes 589832 | tf_op jit(solution)/shard_map/ppermute | solution.py:664
  7.1 2.5 %collective-permute-start.3 = (bf16[192,512]{1,0:T(8,128)(2,1)}, bf16[192,512]{1,0:T(8,128)(2,1)S(1)}, u32[]{:S(2)}, u32[]{:S(2)}) collective-permute-start(bf16[192,512]{1,0:T(8,128)(2,1)} %get-tuple-element.138.refs_0_), channel_id=1, source_target_pairs={{0,12},{2,14},{4,8},{6,10},{8,4},{10,6},{12,0},{14,2},{16,28},{18,... | collective-permute-start | bytes 589832 | tf_op jit(solution)/shard_map/ppermute | solution.py:664
  10.6 2.0 prepare.1.mine
  14.1 3.7 %pack.1 = (bf16[1152,512]{1,0:T(8,128)(2,1)}, bf16[512,512]{1,0:T(8,128)(2,1)}, bf16[384,512]{1,0:T(8,128)(2,1)}) custom-call(s32[10]{0:T(128)} %stack.40.meta, bf16[256,1024]{1,0:T(8,128)(2,1)} %own.2, bf16[256,512]{1,0:T(8,128)(2,1)} %own_out.3, bf16[256,512]{1,0:T(8,128)(2,1)} %own_query.3, bf16[256,512]{1,0:T(8,128)(2,1)} %own_cross.3, ...), custom_call_target="tpu_custom_call" | custom-call | flops 1000 | bytes 1000 | tf_op jit(solution)/shard_map/pack/pallas_call | solution.py:60
  19.2 2.8 %collective-permute-done.1.refs_1_ = bf16[192,512]{1,0:T(8,128)(2,1)S(1)} collective-permute-done((bf16[192,512]{1,0:T(8,128)(2,1)}, bf16[192,512]{1,0:T(8,128)(2,1)S(1)}, u32[]{:S(2)}, u32[]{:S(2)}) %collective-permute-start.1) | collective-permute-done | bytes 196640 | tf_op jit(solution)/shard_map/ppermute | solution.py:664
  22.6 1.5 collective-permute-start.16
  26.6 1.5 collective-permute-start.5
  28.2 5.3 %collective-permute-done.7.refs_7_ = bf16[192,512]{1,0:T(8,128)(2,1)} collective-permute-done((bf16[192,512]{1,0:T(8,128)(2,1)S(1)}, bf16[192,512]{1,0:T(8,128)(2,1)}, u32[]{:S(2)}, u32[]{:S(2)}) %collective-permute-start.7) | collective-permute-done | bytes 196640 | tf_op jit(solution)/shard_map/ppermute | solution.py:664
  33.5 3.2 %collective-permute-done.6.refs_6_ = bf16[192,512]{1,0:T(8,128)(2,1)} collective-permute-done((bf16[192,512]{1,0:T(8,128)(2,1)S(1)}, bf16[192,512]{1,0:T(8,128)(2,1)}, u32[]{:S(2)}, u32[]{:S(2)}) %collective-permute-start.6) | collective-permute-done | bytes 196640 | tf_op jit(solution)/shard_map/ppermute | solution.py:664
  38.7 1.7 unpack.1
  40.4 12.2 %attend.1 = (bf16[2048,512]{1,0:T(8,128)(2,1)}, bf16[192,2048]{1,0:T(8,128)(2,1)}, bf16[16,64,128]{2,1,0:T(8,128)(2,1)}, f32[64,2048]{1,0:T(8,128)}, f32[8,2048]{1,0:T(8,128)}) custom-call(s32[10]{0:T(128)} %stack.40.meta, f32[1,512]{1,0:T(1,128)} %get-tuple-element.144.step, f32[3,512]{1,0:T(4,128)} %get-tuple-element.145.gains, ...), custom_call_target="tpu_custom_call" | custom-call | flops 1000 | bytes 1000 | tf_op jit(solution)/shard_map/attend/pallas_call | solution.py:60
  53.6 4.4 %all-to-all-start = ((bf16[16,64,128]{2,1,0:T(8,128)(2,1)}), bf16[16,64,128]{2,1,0:T(8,128)(2,1)}, u32[]{:S(2)}, u32[]{:S(2)}) async-start(bf16[16,64,128]{2,1,0:T(8,128)(2,1)} %get-tuple-element.149), calls=%async_computation | async-start | bytes 524288 | tf_op jit(solution)/shard_map/all_to_all | solution.py:774
  58.1 6.2 %encoder_rows.1 = (bf16[2,512,512]{2,1,0:T(8,128)(2,1)}, bf16[2,1024,512]{2,1,0:T(8,128)(2,1)}, bf16[512,1024]{1,0:T(8,128)(2,1)}) custom-call(s32[10]{0:T(128)} %stack.40.meta, bf16[256,1024]{1,0:T(8,128)(2,1)} %own.2, bf16[1152,512]{1,0:T(8,128)(2,1)} %copy-done, bf16[1152,512]{1,0:T(8,128)(2,1)} %collective-permute-done.17.far.far2, ...), custom_call_target="tpu_custom_call" | custom-call | flops 1000 | bytes 1000 | tf_op jit(solution)/shard_map/encoder_rows/pallas_call | solution.py:60
  64.4 3.5 %all-to-all-done = bf16[16,64,128]{2,1,0:T(8,128)(2,1)} async-done(((bf16[16,64,128]{2,1,0:T(8,128)(2,1)}), bf16[16,64,128]{2,1,0:T(8,128)(2,1)}, u32[]{:S(2)}, u32[]{:S(2)}) %all-to-all-start) | async-done | bytes 262176 | tf_op jit(solution)/shard_map/all_to_all | solution.py:774
  69.2 1.6 copy-done.3
  71.8 5.4 %forward.1 = (f32[256,512]{1,0:T(8,128)S(1)}, f32[256,512]{1,0:T(8,128)S(1)}, bf16[256,512]{1,0:T(8,128)(2,1)S(1)}, bf16[2,512,128]{2,1,0:T(8,128)(2,1)S(1)}, bf16[16,128,512]{2,1,0:T(8,128)(2,1)S(1)}) custom-call(s32[10]{0:T(128)S(1)} %copy-done.48, bf16[2,128,512]{2,1,0:T(8,128)(2,1)S(1)} %copy-done.12, f32[2,512]{1,0:T(2,128)S(1)} %copy-done.51, ...), custom_call_target="tpu_custom_call" | custom-call | flops 1000 | bytes 1000 | tf_op jit(solution)/shard_map/forward/pallas_call | solution.py:60
  78.0 2.1 collective-permute-done.19.far3
  80.1 7.6 %feed.1 = (bf16[2,128,512]{2,1,0:T(8,128)(2,1)}, f32[256,512]{1,0:T(8,128)S(1)}, f32[16,512]{1,0:T(8,128)S(1)}, bf16[16,64,512]{2,1,0:T(8,128)(2,1)S(1)}, bf16[1...) custom-call(s32[10]{0:T(128)S(1)} %copy-done.48, ...), custom_call_target="tpu_custom_call" | custom-call | flops 1000 | bytes 1000 | tf_op jit(solution)/shard_map/feed/pallas_call | solution.py:60
  88.3 1.5 collective-permute-start.22
  89.8 4.4 %cross_back.1 = (bf16[256,512]{1,0:T(8,128)(2,1)S(1)}, bf16[2,1024,512]{2,1,0:T(8,128)(2,1)S(1)}) custom-call(s32[10]{0:T(128)S(1)} %copy-done.48, f32[256,512]{1,0:T(8,128)S(1)} %get-tuple-element.161.h2g, bf16[256,512]{1,0:T(8,128)(2,1)S(1)} %get-tuple-element.162.q, bf16[16,128,512]{2,1,0:T(8,128)(2,1)S(1)} %get-tuple-element.163.shares, ...), custom_call_target="tpu_custom_call" | custom-call | flops 1000 | bytes 1000 | tf_op jit(solution)/shard_map/cross_back/pallas_call | solution.py:60
  98.4 3.4 %hidden_back.1 = (f32[256,512]{1,0:T(8,128)S(1)}, bf16[2,512,128]{2,1,0:T(8,128)(2,1)}, f32[16,512]{1,0:T(8,128)S(1)}) custom-call(s32[10]{0:T(128)S(1)} %copy-done.48, f32[256,512]{1,0:T(8,128)S(1)} %get-tuple-element.161.h2g, f32[256,512]{1,0:T(8,128)S(1)} %get-tuple-element.172.hidden1, bf16[256,512]{1,0:T(8,128)(2,1)S(1)} %get-tuple-element.164.dq, ...), custom_call_target="tpu_custom_call" | custom-call | flops 1000 | bytes 1000 | tf_op jit(solution)/shard_map/hidden_back/pallas_call | solution.py:60
  102.6 3.7 %all-to-all-start.1 = ((bf16[16,64,128]{2,1,0:T(8,128)(2,1)}), bf16[16,64,128]{2,1,0:T(8,128)(2,1)S(1)}, u32[]{:S(2)}, u32[]{:S(2)}) async-start(bf16[16,64,128]{2,1,0:T(8,128)(2,1)} %bitcast.10), calls=%async_computation.1 | async-start | bytes 524288 | tf_op jit(solution)/shard_map/all_to_all | solution.py:837
  108.9 7.2 %weights_back.1 = (bf16[8,80,512]{2,1,0:T(8,128)(2,1)}, bf16[8,80,512]{2,1,0:T(8,128)(2,1)}, bf16[8,80,512]{2,1,0:T(8,128)(2,1)}, bf16[8,80,512]{2,1,0:T(8,128)(...) custom-call(s32[10]{0:T(128)} %stack.40.meta, f32[256,512]{1,0:T(8,128)} %copy-done.5, ...), custom_call_target="tpu_custom_call" | custom-call | flops 1000 | bytes 1000 | tf_op jit(solution)/shard_map/weights_back/pallas_call | solution.py:60
  119.7 1.6 collective-permute-start.27
  121.3 1.9 collective-permute-start.26
  123.2 6.1 %attend_back_1.1 = (f32[64,2048]{1,0:T(8,128)S(1)}, bf16[128,1024]{1,0:T(8,128)(2,1)S(1)}) custom-call(bf16[192,2048]{1,0:T(8,128)(2,1)S(1)} %copy-done.8, f32[64,2048]{1,0:T(8,128)S(1)} %copy-done.13, f32[8,2048]{1,0:T(8,128)S(1)} %copy-done.34, bf16[16,64,128]{2,1,0:T(8,128)(2,1)S(1)} %all-to-all-done.1.grads), custom_call_target="tpu_custom_call" | custom-call | flops 1000 | bytes 1000 | tf_op jit(solution)/shard_map/attend_back_1/pallas_call | solution.py:60
  131.2 1.7 collective-permute-start.32
  134.8 8.1 %attend_back_2.1 = (bf16[16,192,128]{2,1,0:T(8,128)(2,1)}, f32[208,256]{1,0:T(8,128)S(1)}, bf16[208,256]{1,0:T(8,128)(2,1)S(1)}) custom-call(s32[10]{0:T(128)S(1)} %copy-done.49, bf16[192,2048]{1,0:T(8,128)(2,1)S(1)} %copy-done.8, f32[64,2048]{1,0:T(8,128)S(1)} %copy-done.13, f32[8,2048]{1,0:T(8,128)S(1)} %copy-done.35, ...), custom_call_target="tpu_custom_call" | custom-call | flops 1000 | bytes 1000 | tf_op jit(solution)/shard_map/attend_back_2/pallas_call | solution.py:60
  145.8 4.9 %all-to-all-start.2 = ((bf16[16,192,128]{2,1,0:T(8,128)(2,1)}), bf16[16,192,128]{2,1,0:T(8,128)(2,1)S(1)}, u32[]{:S(2)}, u32[]{:S(2)}) async-start(bf16[16,192,128]{2,1,0:T(8,128)(2,1)} %get-tuple-element.232), calls=%async_computation.2 | async-start | bytes 1572864 | tf_op jit(solution)/shard_map/all_to_all | solution.py:896
  155.0 2.0 collective-permute-start.34
  159.1 2.4 %collective-permute-start.38 = (bf16[2,128,512]{2,1,0:T(8,128)(2,1)S(1)}, bf16[2,128,512]{2,1,0:T(8,128)(2,1)S(1)}, u32[]{:S(2)}, u32[]{:S(2)}) collective-permute-start(bf16[2,128,512]{2,1,0:T(8,128)(2,1)S(1)} %get-tuple-element.225.feed), channel_id=1, source_target_pairs={{0,16},{2,18},{4,20},{6,22},{8,24},{10,26},{12,28},{14,30},{16,0},... | collective-permute-start | bytes 786440 | tf_op jit(solution)/shard_map/ppermute | solution.py:664
  161.8 7.1 %collective-permute-done.34.refs_1_ = bf16[4,80,512]{2,1,0:T(8,128)(2,1)S(1)} collective-permute-done((bf16[4,80,512]{2,1,0:T(8,128)(2,1)S(1)}, bf16[4,80,512]{2,1,0:T(8,128)(2,1)S(1)}, u32[]{:S(2)}, u32[]{:S(2)}) %collective-permute-start.34) | collective-permute-done | bytes 327712 | tf_op jit(solution)/shard_map/ppermute | solution.py:664
  169.0 2.7 %collective-permute-start.36 = (bf16[2,80,512]{2,1,0:T(8,128)(2,1)S(1)}, bf16[2,80,512]{2,1,0:T(8,128)(2,1)S(1)}, u32[]{:S(2)}, u32[]{:S(2)}) collective-permute-start(bf16[2,80,512]{2,1,0:T(8,128)(2,1)S(1)} %get-tuple-element.223), channel_id=1, source_target_pairs={{0,8},{2,10},{4,12},{6,14},{8,0},{10,2},{12,4},{14,6},{16,24},{18,... | collective-permute-start | bytes 491528 | tf_op jit(solution)/shard_map/ppermute | solution.py:664
  171.7 1.6 collective-permute-start.39
  173.3 1.7 collective-permute-done.37.refs_3_
  175.0 4.4 %collective-permute-done.36.refs_1_ = bf16[2,80,512]{2,1,0:T(8,128)(2,1)S(1)} collective-permute-done((bf16[2,80,512]{2,1,0:T(8,128)(2,1)S(1)}, bf16[2,80,512]{2,1,0:T(8,128)(2,1)S(1)}, u32[]{:S(2)}, u32[]{:S(2)}) %collective-permute-start.36) | collective-permute-done | bytes 163872 | tf_op jit(solution)/shard_map/ppermute | solution.py:664
  179.4 6.3 %collective-permute-done.38.feed_got = bf16[2,128,512]{2,1,0:T(8,128)(2,1)S(1)} collective-permute-done((bf16[2,128,512]{2,1,0:T(8,128)(2,1)S(1)}, bf16[2,128,512]{2,1,0:T(8,128)(2,1)S(1)}, u32[]{:S(2)}, u32[]{:S(2)}) %collective-permute-start.38) | collective-permute-done | bytes 262176 | tf_op jit(solution)/shard_map/ppermute | solution.py:664
  185.7 1.8 collective-permute-done.39.heads_got
  190.4 2.0 collective-permute-start.42
  192.5 2.9 %collective-permute-start.40 = (bf16[1,128,512]{2,1,0:T(8,128)(2,1)}, bf16[1,128,512]{2,1,0:T(8,128)(2,1)}, u32[]{:S(2)}, u32[]{:S(2)}) collective-permute-start(bf16[1,128,512]{2,1,0:T(8,128)(2,1)} %get-tuple-element.234), channel_id=1, source_target_pairs={{0,16},{2,18},{4,20},{6,22},{8,24},{10,26},{12,28},{14,30},{16,0},... | collective-permute-start | bytes 393224 | tf_op jit(solution)/shard_map/ppermute | solution.py:664
  196.3 4.9 %start_grad.1 = f32[2,128,512]{2,1,0:T(8,128)} custom-call(s32[10]{0:T(128)} %stack.40.meta, bf16[2,8,192,128]{3,2,1,0:T(8,128)(2,1)} %bitcast.20, bf16[2,128,512]{2,1,0:T(8,128)(2,1)} %tokens.5, f32[2,512]{1,0:T(2,128)} %get-tuple-element.143.steps, f32[3,512]{1,0:T(4,128)} %get-tuple-element.145.gains, f32[256,512]{1,0:T(8,128)} %copy-done.16, ...), custom_call_target="tpu_custom_call" | custom-call | flops 1000 | bytes 1000 | tf_op jit(solution)/shard_map/start_grad/pallas_call | solution.py:60
  201.1 10.5 %collective-permute-done.40.got = bf16[1,128,512]{2,1,0:T(8,128)(2,1)} collective-permute-done((bf16[1,128,512]{2,1,0:T(8,128)(2,1)}, bf16[1,128,512]{2,1,0:T(8,128)(2,1)}, u32[]{:S(2)}, u32[]{:S(2)}) %collective-permute-start.40) | collective-permute-done | bytes 131104 | tf_op jit(solution)/shard_map/ppermute | solution.py:664
  213.3 1.5 collective-permute-done.42.refs_1_
  214.8 2.3 collective-permute-start.51
  219.2 2.3 encoder_back.1
  221.5 4.3 %place.1 = (f32[256,2048]{1,0:T(8,128)}, f32[1024,512]{1,0:T(8,128)}, f32[256,1536]{1,0:T(8,128)}, f32[3,256]{1,0:T(4,128)}, f32[3,256]{1,0:T(4,128)}, /*index=5...) custom-call(s32[10]{0:T(128)S(1)} %copy-done.50, f32[1,512]{1,0:T(1,128)S(1)} %copy-done.54, ...), custom_call_target="tpu_custom_call" | custom-call | flops 1000 | bytes 1000 | tf_op jit(solution)/shard_map/place/pallas_call | solution.py:60
  228.1 2.2 place_cross.1
  (239 shorter events, 48.4 us)
Async XLA Ops:
  3.1 14.7 %collective-permute-start.4 = (bf16[192,512]{1,0:T(8,128)(2,1)}, bf16[192,512]{1,0:T(8,128)(2,1)S(1)}, u32[]{:S(2)}, u32[]{:S(2)}) collective-permute-start(bf16[192,512]{1,0:T(8,128)(2,1)} %get-tuple-element.148), channel_id=1, source_target_pairs={{0,16},{2,18},{4,20},{6,22},{8,24},{10,26},{12,28},{14,30},{16,0},... | collective-permute-start | bytes 589832 | tf_op jit(solution)/shard_map/ppermute | solution.py:664
  7.1 12.0 %collective-permute-start.3 = (bf16[192,512]{1,0:T(8,128)(2,1)}, bf16[192,512]{1,0:T(8,128)(2,1)S(1)}, u32[]{:S(2)}, u32[]{:S(2)}) collective-permute-start(bf16[192,512]{1,0:T(8,128)(2,1)} %get-tuple-element.138.refs_0_), channel_id=1, source_target_pairs={{0,12},{2,14},{4,8},{6,10},{8,4},{10,6},{12,0},{14,2},{16,28},{18,... | collective-permute-start | bytes 589832 | tf_op jit(solution)/shard_map/ppermute | solution.py:664
  9.7 9.5 %collective-permute-start.2 = (bf16[192,512]{1,0:T(8,128)(2,1)}, bf16[192,512]{1,0:T(8,128)(2,1)S(1)}, u32[]{:S(2)}, u32[]{:S(2)}) collective-permute-start(bf16[192,512]{1,0:T(8,128)(2,1)} %get-tuple-element.138.refs_0_), channel_id=1, source_target_pairs={{0,4},{2,6},{4,0},{6,2},{8,12},{10,14},{12,8},{14,10},{16,20},{18,... | collective-permute-start | bytes 589832 | tf_op jit(solution)/shard_map/ppermute | solution.py:664
  10.2 11.8 %collective-permute-start.1 = (bf16[192,512]{1,0:T(8,128)(2,1)}, bf16[192,512]{1,0:T(8,128)(2,1)S(1)}, u32[]{:S(2)}, u32[]{:S(2)}) collective-permute-start(bf16[192,512]{1,0:T(8,128)(2,1)} %get-tuple-element.138.refs_0_), channel_id=1, source_target_pairs={{0,8},{2,10},{4,12},{6,14},{8,0},{10,2},{12,4},{14,6},{16,24},{18,... | collective-permute-start | bytes 589832 | tf_op jit(solution)/shard_map/ppermute | solution.py:664
  12.6 5.2 %collective-permute-start = (bf16[256,256]{1,0:T(8,128)(2,1)}, bf16[256,256]{1,0:T(8,128)(2,1)S(1)}, u32[]{:S(2)}, u32[]{:S(2)}) collective-permute-start(bf16[256,256]{1,0:T(8,128)(2,1)} %prepare.1.mine), channel_id=1, source_target_pairs={{0,1},{1,0},{2,3},{3,2},{4,5},{5,4},{6,7},{7,6},{8,9},{9,8},{10,11... | collective-permute-start | bytes 393224 | tf_op jit(solution)/shard_map/ppermute | solution.py:668
  22.6 30.1 %collective-permute-start.16 = (bf16[1152,512]{1,0:T(8,128)(2,1)}, bf16[1152,512]{1,0:T(8,128)(2,1)S(1)}, u32[]{:S(2)}, u32[]{:S(2)}) collective-permute-start(bf16[1152,512]{1,0:T(8,128)(2,1)} %get-tuple-element.150), channel_id=1, source_target_pairs={{0,1},{1,0},{2,3},{3,2},{4,5},{5,4},{6,7},{7,6},{8,9},{9,8},{10,11... | collective-permute-start | bytes 3538952 | tf_op jit(solution)/shard_map/ppermute | solution.py:668
  24.2 4.0 %collective-permute-start.12 = (bf16[192,512]{1,0:T(8,128)(2,1)S(1)}, bf16[192,512]{1,0:T(8,128)(2,1)S(1)}, u32[]{:S(2)}, u32[]{:S(2)}) collective-permute-start(bf16[192,512]{1,0:T(8,128)(2,1)S(1)} %collective-permute-done.4.refs_4_), channel_id=1, source_target_pairs={{0,2},{2,0},{4,6},{6,4},{8,10},{10,8},{12,14},{14,12},{16,18},{18,... | collective-permute-start | bytes 589832 | tf_op jit(solution)/shard_map/ppermute | solution.py:664
  24.7 8.8 %collective-permute-start.7 = (bf16[192,512]{1,0:T(8,128)(2,1)S(1)}, bf16[192,512]{1,0:T(8,128)(2,1)}, u32[]{:S(2)}, u32[]{:S(2)}) collective-permute-start(bf16[192,512]{1,0:T(8,128)(2,1)S(1)} %collective-permute-done.4.refs_4_), channel_id=1, source_target_pairs={{0,12},{2,14},{4,8},{6,10},{8,4},{10,6},{12,0},{14,2},{16,28},{18,... | collective-permute-start | bytes 589832 | tf_op jit(solution)/shard_map/ppermute | solution.py:664
  26.1 10.6 %collective-permute-start.6 = (bf16[192,512]{1,0:T(8,128)(2,1)S(1)}, bf16[192,512]{1,0:T(8,128)(2,1)}, u32[]{:S(2)}, u32[]{:S(2)}) collective-permute-start(bf16[192,512]{1,0:T(8,128)(2,1)S(1)} %collective-permute-done.4.refs_4_), channel_id=1, source_target_pairs={{0,4},{2,6},{4,0},{6,2},{8,12},{10,14},{12,8},{14,10},{16,20},{18,... | collective-permute-start | bytes 589832 | tf_op jit(solution)/shard_map/ppermute | solution.py:664
  26.6 10.1 %collective-permute-start.5 = (bf16[192,512]{1,0:T(8,128)(2,1)S(1)}, bf16[192,512]{1,0:T(8,128)(2,1)S(1)}, u32[]{:S(2)}, u32[]{:S(2)}) collective-permute-start(bf16[192,512]{1,0:T(8,128)(2,1)S(1)} %collective-permute-done.4.refs_4_), channel_id=1, source_target_pairs={{0,8},{2,10},{4,12},{6,14},{8,0},{10,2},{12,4},{14,6},{16,24},{18,... | collective-permute-start | bytes 589832 | tf_op jit(solution)/shard_map/ppermute | solution.py:664
  28.2 9.0 %collective-permute-start.11 = (bf16[192,512]{1,0:T(8,128)(2,1)S(1)}, bf16[192,512]{1,0:T(8,128)(2,1)S(1)}, u32[]{:S(2)}, u32[]{:S(2)}) collective-permute-start(bf16[192,512]{1,0:T(8,128)(2,1)S(1)} %collective-permute-done.3.refs_3_), channel_id=1, source_target_pairs={{0,2},{2,0},{4,6},{6,4},{8,10},{10,8},{12,14},{14,12},{16,18},{18,... | collective-permute-start | bytes 589832 | tf_op jit(solution)/shard_map/ppermute | solution.py:664
  33.5 3.8 %collective-permute-start.10 = (bf16[192,512]{1,0:T(8,128)(2,1)S(1)}, bf16[192,512]{1,0:T(8,128)(2,1)S(1)}, u32[]{:S(2)}, u32[]{:S(2)}) collective-permute-start(bf16[192,512]{1,0:T(8,128)(2,1)S(1)} %collective-permute-done.2.refs_2_), channel_id=1, source_target_pairs={{0,2},{2,0},{4,6},{6,4},{8,10},{10,8},{12,14},{14,12},{16,18},{18,... | collective-permute-start | bytes 589832 | tf_op jit(solution)/shard_map/ppermute | solution.py:664
  52.7 5.4 %collective-permute-start.17 = (bf16[1152,512]{1,0:T(8,128)(2,1)S(1)}, bf16[1152,512]{1,0:T(8,128)(2,1)}, u32[]{:S(2)}, u32[]{:S(2)}) collective-permute-start(bf16[1152,512]{1,0:T(8,128)(2,1)S(1)} %collective-permute-done.16.near.near2), channel_id=1, source_target_pairs={{0,2},{2,0},{4,6},{6,4},{8,10},{10,8},{12,14},{14,12},{16,18},{18,... | collective-permute-start | bytes 3538952 | tf_op jit(solution)/shard_map/ppermute | solution.py:664
  53.2 24.8 %collective-permute-start.18 = (bf16[512,512]{1,0:T(8,128)(2,1)}, bf16[512,512]{1,0:T(8,128)(2,1)}, u32[]{:S(2)}, u32[]{:S(2)}) collective-permute-start(bf16[512,512]{1,0:T(8,128)(2,1)} %get-tuple-element.157), channel_id=1, source_target_pairs={{0,1},{1,0},{2,3},{3,2},{4,5},{5,4},{6,7},{7,6},{8,9},{9,8},{10,11... | collective-permute-start | bytes 1572872 | tf_op jit(solution)/shard_map/ppermute | solution.py:668
  53.6 14.2 %all-to-all-start = ((bf16[16,64,128]{2,1,0:T(8,128)(2,1)}), bf16[16,64,128]{2,1,0:T(8,128)(2,1)}, u32[]{:S(2)}, u32[]{:S(2)}) async-start(bf16[16,64,128]{2,1,0:T(8,128)(2,1)} %get-tuple-element.149), calls=%async_computation | async-start | bytes 524288 | tf_op jit(solution)/shard_map/all_to_all | solution.py:774
  87.7 7.8 %collective-permute-start.20 = (bf16[16,64,512]{2,1,0:T(8,128)(2,1)S(1)}, bf16[16,64,512]{2,1,0:T(8,128)(2,1)S(1)}, u32[]{:S(2)}, u32[]{:S(2)}) collective-permute-start(bf16[16,64,512]{2,1,0:T(8,128)(2,1)S(1)} %get-tuple-element.166), channel_id=1, source_target_pairs={{0,2},{2,0},{4,6},{6,4},{8,10},{10,8},{12,14},{14,12},{16,18},{18,... | collective-permute-start | bytes 3145736 | tf_op jit(solution)/shard_map/ppermute | solution.py:664
  87.9 7.6 %collective-permute-start.21 = (bf16[16,64,512]{2,1,0:T(8,128)(2,1)S(1)}, bf16[16,64,512]{2,1,0:T(8,128)(2,1)S(1)}, u32[]{:S(2)}, u32[]{:S(2)}) collective-permute-start(bf16[16,64,512]{2,1,0:T(8,128)(2,1)S(1)} %get-tuple-element.168), channel_id=1, source_target_pairs={{0,2},{2,0},{4,6},{6,4},{8,10},{10,8},{12,14},{14,12},{16,18},{18,... | collective-permute-start | bytes 3145736 | tf_op jit(solution)/shard_map/ppermute | solution.py:664
  88.3 18.0 %collective-permute-start.22 = (bf16[384,512]{1,0:T(8,128)(2,1)}, bf16[384,512]{1,0:T(8,128)(2,1)S(1)}, u32[]{:S(2)}, u32[]{:S(2)}) collective-permute-start(bf16[384,512]{1,0:T(8,128)(2,1)} %get-tuple-element.176), channel_id=1, source_target_pairs={{0,1},{1,0},{2,3},{3,2},{4,5},{5,4},{6,7},{7,6},{8,9},{9,8},{10,11... | collective-permute-start | bytes 1179656 | tf_op jit(solution)/shard_map/ppermute | solution.py:668
  97.8 18.6 %collective-permute-start.25 = (bf16[8,64,512]{2,1,0:T(8,128)(2,1)}, bf16[8,64,512]{2,1,0:T(8,128)(2,1)}, u32[]{:S(2)}, u32[]{:S(2)}) collective-permute-start(bf16[8,64,512]{2,1,0:T(8,128)(2,1)} %get-tuple-element.186), channel_id=1, source_target_pairs={{0,4},{2,6},{4,0},{6,2},{8,12},{10,14},{12,8},{14,10},{16,20},{18,... | collective-permute-start | bytes 1572872 | tf_op jit(solution)/shard_map/ppermute | solution.py:664
  97.9 18.4 %collective-permute-start.24 = (bf16[8,64,512]{2,1,0:T(8,128)(2,1)}, bf16[8,64,512]{2,1,0:T(8,128)(2,1)}, u32[]{:S(2)}, u32[]{:S(2)}) collective-permute-start(bf16[8,64,512]{2,1,0:T(8,128)(2,1)} %get-tuple-element.170), channel_id=1, source_target_pairs={{0,1},{1,0},{2,3},{3,2},{4,5},{5,4},{6,7},{7,6},{8,9},{9,8},{10,11... | collective-permute-start | bytes 1572872 | tf_op jit(solution)/shard_map/ppermute | solution.py:668
  102.6 13.7 %all-to-all-start.1 = ((bf16[16,64,128]{2,1,0:T(8,128)(2,1)}), bf16[16,64,128]{2,1,0:T(8,128)(2,1)S(1)}, u32[]{:S(2)}, u32[]{:S(2)}) async-start(bf16[16,64,128]{2,1,0:T(8,128)(2,1)} %bitcast.10), calls=%async_computation.1 | async-start | bytes 524288 | tf_op jit(solution)/shard_map/all_to_all | solution.py:837
  116.4 13.2 %collective-permute-start.30 = (bf16[8,128,512]{2,1,0:T(8,128)(2,1)}, bf16[8,128,512]{2,1,0:T(8,128)(2,1)S(1)}, u32[]{:S(2)}, u32[]{:S(2)}) collective-permute-start(bf16[8,128,512]{2,1,0:T(8,128)(2,1)} %get-tuple-element.204), channel_id=1, source_target_pairs={{0,2},{2,0},{4,6},{6,4},{8,10},{10,8},{12,14},{14,12},{16,18},{18,... | collective-permute-start | bytes 3145736 | tf_op jit(solution)/shard_map/ppermute | solution.py:664
  116.6 13.0 %collective-permute-start.28 = (bf16[8,80,512]{2,1,0:T(8,128)(2,1)}, bf16[8,80,512]{2,1,0:T(8,128)(2,1)S(1)}, u32[]{:S(2)}, u32[]{:S(2)}) collective-permute-start(bf16[8,80,512]{2,1,0:T(8,128)(2,1)} %get-tuple-element.198), channel_id=1, source_target_pairs={{0,2},{2,0},{4,6},{6,4},{8,10},{10,8},{12,14},{14,12},{16,18},{18,... | collective-permute-start | bytes 1966088 | tf_op jit(solution)/shard_map/ppermute | solution.py:664
  117.0 12.7 %collective-permute-start.29 = (bf16[8,80,512]{2,1,0:T(8,128)(2,1)}, bf16[8,80,512]{2,1,0:T(8,128)(2,1)S(1)}, u32[]{:S(2)}, u32[]{:S(2)}) collective-permute-start(bf16[8,80,512]{2,1,0:T(8,128)(2,1)} %get-tuple-element.201), channel_id=1, source_target_pairs={{0,2},{2,0},{4,6},{6,4},{8,10},{10,8},{12,14},{14,12},{16,18},{18,... | collective-permute-start | bytes 1966088 | tf_op jit(solution)/shard_map/ppermute | solution.py:664
  119.7 9.6 %collective-permute-start.27 = (bf16[4,64,512]{2,1,0:T(8,128)(2,1)S(1)}, bf16[4,64,512]{2,1,0:T(8,128)(2,1)S(1)}, u32[]{:S(2)}, u32[]{:S(2)}) collective-permute-start(bf16[4,64,512]{2,1,0:T(8,128)(2,1)S(1)} %get-tuple-element.196), channel_id=1, source_target_pairs={{0,1},{1,0},{2,3},{3,2},{4,5},{5,4},{6,7},{7,6},{8,9},{9,8},{10,11... | collective-permute-start | bytes 786440 | tf_op jit(solution)/shard_map/ppermute | solution.py:668
  121.3 8.3 %collective-permute-start.26 = (bf16[4,64,512]{2,1,0:T(8,128)(2,1)S(1)}, bf16[4,64,512]{2,1,0:T(8,128)(2,1)S(1)}, u32[]{:S(2)}, u32[]{:S(2)}) collective-permute-start(bf16[4,64,512]{2,1,0:T(8,128)(2,1)S(1)} %get-tuple-element.189), channel_id=1, source_target_pairs={{0,4},{2,6},{4,0},{6,2},{8,12},{10,14},{12,8},{14,10},{16,20},{18,... | collective-permute-start | bytes 786440 | tf_op jit(solution)/shard_map/ppermute | solution.py:664
  131.2 13.8 %collective-permute-start.32 = (bf16[4,128,512]{2,1,0:T(8,128)(2,1)S(1)}, bf16[4,128,512]{2,1,0:T(8,128)(2,1)S(1)}, u32[]{:S(2)}, u32[]{:S(2)}) collective-permute-start(bf16[4,128,512]{2,1,0:T(8,128)(2,1)S(1)} %get-tuple-element.212), channel_id=1, source_target_pairs={{0,4},{2,6},{4,0},{6,2},{8,12},{10,14},{12,8},{14,10},{16,20},{18,... | collective-permute-start | bytes 1572872 | tf_op jit(solution)/shard_map/ppermute | solution.py:664
  132.8 11.4 %collective-permute-start.31 = (bf16[2,128,512]{2,1,0:T(8,128)(2,1)S(1)}, bf16[2,128,512]{2,1,0:T(8,128)(2,1)S(1)}, u32[]{:S(2)}, u32[]{:S(2)}) collective-permute-start(bf16[2,128,512]{2,1,0:T(8,128)(2,1)S(1)} %get-tuple-element.206), channel_id=1, source_target_pairs={{0,8},{2,10},{4,12},{6,14},{8,0},{10,2},{12,4},{14,6},{16,24},{18,... | collective-permute-start | bytes 786440 | tf_op jit(solution)/shard_map/ppermute | solution.py:664
  134.3 16.4 %collective-permute-start.33 = (bf16[8,80,512]{2,1,0:T(8,128)(2,1)}, bf16[8,80,512]{2,1,0:T(8,128)(2,1)S(1)}, u32[]{:S(2)}, u32[]{:S(2)}) collective-permute-start(bf16[8,80,512]{2,1,0:T(8,128)(2,1)} %get-tuple-element.217), channel_id=1, source_target_pairs={{0,1},{1,0},{2,3},{3,2},{4,5},{5,4},{6,7},{7,6},{8,9},{9,8},{10,11... | collective-permute-start | bytes 1966088 | tf_op jit(solution)/shard_map/ppermute | solution.py:668
  145.8 49.6 %all-to-all-start.2 = ((bf16[16,192,128]{2,1,0:T(8,128)(2,1)}), bf16[16,192,128]{2,1,0:T(8,128)(2,1)S(1)}, u32[]{:S(2)}, u32[]{:S(2)}) async-start(bf16[16,192,128]{2,1,0:T(8,128)(2,1)} %get-tuple-element.232), calls=%async_computation.2 | async-start | bytes 1572864 | tf_op jit(solution)/shard_map/all_to_all | solution.py:896
  155.0 13.8 %collective-permute-start.34 = (bf16[4,80,512]{2,1,0:T(8,128)(2,1)S(1)}, bf16[4,80,512]{2,1,0:T(8,128)(2,1)S(1)}, u32[]{:S(2)}, u32[]{:S(2)}) collective-permute-start(bf16[4,80,512]{2,1,0:T(8,128)(2,1)S(1)} %get-tuple-element.219), channel_id=1, source_target_pairs={{0,4},{2,6},{4,0},{6,2},{8,12},{10,14},{12,8},{14,10},{16,20},{18,... | collective-permute-start | bytes 983048 | tf_op jit(solution)/shard_map/ppermute | solution.py:664
  157.0 4.7 %collective-permute-start.35 = (bf16[208,256]{1,0:T(8,128)(2,1)S(1)}, bf16[208,256]{1,0:T(8,128)(2,1)S(1)}, u32[]{:S(2)}, u32[]{:S(2)}) collective-permute-start(bf16[208,256]{1,0:T(8,128)(2,1)S(1)} %copy-done.56), channel_id=1, source_target_pairs={{0,1},{1,0},{2,3},{3,2},{4,5},{5,4},{6,7},{7,6},{8,9},{9,8},{10,11... | collective-permute-start | bytes 319496 | tf_op jit(solution)/shard_map/ppermute | solution.py:668
  157.6 17.3 %collective-permute-start.37 = (bf16[2,128,512]{2,1,0:T(8,128)(2,1)S(1)}, bf16[2,128,512]{2,1,0:T(8,128)(2,1)S(1)}, u32[]{:S(2)}, u32[]{:S(2)}) collective-permute-start(bf16[2,128,512]{2,1,0:T(8,128)(2,1)S(1)} %get-tuple-element.224), channel_id=1, source_target_pairs={{0,8},{2,10},{4,12},{6,14},{8,0},{10,2},{12,4},{14,6},{16,24},{18,... | collective-permute-start | bytes 786440 | tf_op jit(solution)/shard_map/ppermute | solution.py:664
  159.1 26.6 %collective-permute-start.38 = (bf16[2,128,512]{2,1,0:T(8,128)(2,1)S(1)}, bf16[2,128,512]{2,1,0:T(8,128)(2,1)S(1)}, u32[]{:S(2)}, u32[]{:S(2)}) collective-permute-start(bf16[2,128,512]{2,1,0:T(8,128)(2,1)S(1)} %get-tuple-element.225.feed), channel_id=1, source_target_pairs={{0,16},{2,18},{4,20},{6,22},{8,24},{10,26},{12,28},{14,30},{16,0},... | collective-permute-start | bytes 786440 | tf_op jit(solution)/shard_map/ppermute | solution.py:664
  169.0 10.5 %collective-permute-start.36 = (bf16[2,80,512]{2,1,0:T(8,128)(2,1)S(1)}, bf16[2,80,512]{2,1,0:T(8,128)(2,1)S(1)}, u32[]{:S(2)}, u32[]{:S(2)}) collective-permute-start(bf16[2,80,512]{2,1,0:T(8,128)(2,1)S(1)} %get-tuple-element.223), channel_id=1, source_target_pairs={{0,8},{2,10},{4,12},{6,14},{8,0},{10,2},{12,4},{14,6},{16,24},{18,... | collective-permute-start | bytes 491528 | tf_op jit(solution)/shard_map/ppermute | solution.py:664
  171.7 15.9 %collective-permute-start.39 = (bf16[1,208,256]{2,1,0:T(8,128)(2,1)S(1)}, bf16[1,208,256]{2,1,0:T(8,128)(2,1)S(1)}, u32[]{:S(2)}, u32[]{:S(2)}) collective-permute-start(bf16[1,208,256]{2,1,0:T(8,128)(2,1)S(1)} %get-tuple-element.226.heads), channel_id=1, source_target_pairs={{0,16},{2,18},{4,20},{6,22},{8,24},{10,26},{12,28},{14,30},{16,0},... | collective-permute-start | bytes 319496 | tf_op jit(solution)/shard_map/ppermute | solution.py:664
  189.0 23.7 %collective-permute-start.44 = (bf16[1,368,512]{2,1,0:T(8,128)(2,1)S(1)}, bf16[1,368,512]{2,1,0:T(8,128)(2,1)S(1)}, u32[]{:S(2)}, u32[]{:S(2)}) collective-permute-start(bf16[1,368,512]{2,1,0:T(8,128)(2,1)S(1)} %reduce_6.1.refs_0_), channel_id=1, source_target_pairs={{0,12},{2,14},{4,8},{6,10},{8,4},{10,6},{12,0},{14,2},{16,28},{18,... | collective-permute-start | bytes 1130504 | tf_op jit(solution)/shard_map/ppermute | solution.py:664
  189.0 24.2 %collective-permute-start.43 = (bf16[1,368,512]{2,1,0:T(8,128)(2,1)S(1)}, bf16[1,368,512]{2,1,0:T(8,128)(2,1)}, u32[]{:S(2)}, u32[]{:S(2)}) collective-permute-start(bf16[1,368,512]{2,1,0:T(8,128)(2,1)S(1)} %reduce_6.1.refs_0_), channel_id=1, source_target_pairs={{0,4},{2,6},{4,0},{6,2},{8,12},{10,14},{12,8},{14,10},{16,20},{18,... | collective-permute-start | bytes 1130504 | tf_op jit(solution)/shard_map/ppermute | solution.py:664
  190.4 24.3 %collective-permute-start.42 = (bf16[1,368,512]{2,1,0:T(8,128)(2,1)S(1)}, bf16[1,368,512]{2,1,0:T(8,128)(2,1)}, u32[]{:S(2)}, u32[]{:S(2)}) collective-permute-start(bf16[1,368,512]{2,1,0:T(8,128)(2,1)S(1)} %reduce_6.1.refs_0_), channel_id=1, source_target_pairs={{0,8},{2,10},{4,12},{6,14},{8,0},{10,2},{12,4},{14,6},{16,24},{18,... | collective-permute-start | bytes 1130504 | tf_op jit(solution)/shard_map/ppermute | solution.py:664
  192.5 19.2 %collective-permute-start.41 = (bf16[2,80,512]{2,1,0:T(8,128)(2,1)S(1)}, bf16[2,80,512]{2,1,0:T(8,128)(2,1)}, u32[]{:S(2)}, u32[]{:S(2)}) collective-permute-start(bf16[2,80,512]{2,1,0:T(8,128)(2,1)S(1)} %get-tuple-element.235.mine), channel_id=1, source_target_pairs={{0,16},{2,18},{4,20},{6,22},{8,24},{10,26},{12,28},{14,30},{16,0},... | collective-permute-start | bytes 491528 | tf_op jit(solution)/shard_map/ppermute | solution.py:664
  192.5 19.2 %collective-permute-start.40 = (bf16[1,128,512]{2,1,0:T(8,128)(2,1)}, bf16[1,128,512]{2,1,0:T(8,128)(2,1)}, u32[]{:S(2)}, u32[]{:S(2)}) collective-permute-start(bf16[1,128,512]{2,1,0:T(8,128)(2,1)} %get-tuple-element.234), channel_id=1, source_target_pairs={{0,16},{2,18},{4,20},{6,22},{8,24},{10,26},{12,28},{14,30},{16,0},... | collective-permute-start | bytes 393224 | tf_op jit(solution)/shard_map/ppermute | solution.py:664
  212.6 4.5 %collective-permute-start.45 = (bf16[1,368,512]{2,1,0:T(8,128)(2,1)S(1)}, bf16[1,368,512]{2,1,0:T(8,128)(2,1)S(1)}, u32[]{:S(2)}, u32[]{:S(2)}) collective-permute-start(bf16[1,368,512]{2,1,0:T(8,128)(2,1)S(1)} %reduce_6.1.refs_0_), channel_id=1, source_target_pairs={{0,2},{2,0},{4,6},{6,4},{8,10},{10,8},{12,14},{14,12},{16,18},{18,... | collective-permute-start | bytes 1130504 | tf_op jit(solution)/shard_map/ppermute | solution.py:664
  212.7 5.1 %collective-permute-start.48 = (bf16[1,368,512]{2,1,0:T(8,128)(2,1)S(1)}, bf16[1,368,512]{2,1,0:T(8,128)(2,1)S(1)}, u32[]{:S(2)}, u32[]{:S(2)}) collective-permute-start(bf16[1,368,512]{2,1,0:T(8,128)(2,1)S(1)} %collective-permute-done.44.refs_3_), channel_id=1, source_target_pairs={{0,2},{2,0},{4,6},{6,4},{8,10},{10,8},{12,14},{14,12},{16,18},{18,... | collective-permute-start | bytes 1130504 | tf_op jit(solution)/shard_map/ppermute | solution.py:664
  213.2 8.3 %collective-permute-start.47 = (bf16[1,368,512]{2,1,0:T(8,128)(2,1)}, bf16[1,368,512]{2,1,0:T(8,128)(2,1)S(1)}, u32[]{:S(2)}, u32[]{:S(2)}) collective-permute-start(bf16[1,368,512]{2,1,0:T(8,128)(2,1)} %collective-permute-done.43.refs_2_), channel_id=1, source_target_pairs={{0,2},{2,0},{4,6},{6,4},{8,10},{10,8},{12,14},{14,12},{16,18},{18,... | collective-permute-start | bytes 1130504 | tf_op jit(solution)/shard_map/ppermute | solution.py:664
  214.8 6.7 %collective-permute-start.46 = (bf16[1,368,512]{2,1,0:T(8,128)(2,1)}, bf16[1,368,512]{2,1,0:T(8,128)(2,1)S(1)}, u32[]{:S(2)}, u32[]{:S(2)}) collective-permute-start(bf16[1,368,512]{2,1,0:T(8,128)(2,1)} %collective-permute-done.42.refs_1_), channel_id=1, source_target_pairs={{0,2},{2,0},{4,6},{6,4},{8,10},{10,8},{12,14},{14,12},{16,18},{18,... | collective-permute-start | bytes 1130504 | tf_op jit(solution)/shard_map/ppermute | solution.py:664
  214.8 11.1 %collective-permute-start.51 = (bf16[2,80,512]{2,1,0:T(8,128)(2,1)S(1)}, bf16[2,80,512]{2,1,0:T(8,128)(2,1)S(1)}, u32[]{:S(2)}, u32[]{:S(2)}) collective-permute-start(bf16[2,80,512]{2,1,0:T(8,128)(2,1)S(1)} %reduce_8.1.refs_0_), channel_id=1, source_target_pairs={{0,12},{2,14},{4,8},{6,10},{8,4},{10,6},{12,0},{14,2},{16,28},{18,... | collective-permute-start | bytes 491528 | tf_op jit(solution)/shard_map/ppermute | solution.py:664
  217.1 8.8 %collective-permute-start.50 = (bf16[2,80,512]{2,1,0:T(8,128)(2,1)S(1)}, bf16[2,80,512]{2,1,0:T(8,128)(2,1)S(1)}, u32[]{:S(2)}, u32[]{:S(2)}) collective-permute-start(bf16[2,80,512]{2,1,0:T(8,128)(2,1)S(1)} %reduce_8.1.refs_0_), channel_id=1, source_target_pairs={{0,4},{2,6},{4,0},{6,2},{8,12},{10,14},{12,8},{14,10},{16,20},{18,... | collective-permute-start | bytes 491528 | tf_op jit(solution)/shard_map/ppermute | solution.py:664
  217.8 8.1 %collective-permute-start.49 = (bf16[2,80,512]{2,1,0:T(8,128)(2,1)S(1)}, bf16[2,80,512]{2,1,0:T(8,128)(2,1)S(1)}, u32[]{:S(2)}, u32[]{:S(2)}) collective-permute-start(bf16[2,80,512]{2,1,0:T(8,128)(2,1)S(1)} %reduce_8.1.refs_0_), channel_id=1, source_target_pairs={{0,8},{2,10},{4,12},{6,14},{8,0},{10,2},{12,4},{14,6},{16,24},{18,... | collective-permute-start | bytes 491528 | tf_op jit(solution)/shard_map/ppermute | solution.py:664
  (82 other events, 569.1 us)

commit v5 on v4

--- a/solution.py
+++ b/solution.py
@@ -13,8 +13,8 @@
 F32 = jnp.float32
 BF = jnp.bfloat16
 LOG2E = 1.4426950408889634
-LARGE, SMALL = 62, 16
-ROOMY = ("split", "prepare", "pack", "unpack", "attend", "encoder_rows", "weights_back", "start_grad")
+LARGE, SMALL = 62, 32
+ROOMY = ("split", "prepare", "pack", "unpack", "attend", "encoder_rows", "weights_back")
 
 
 def limit_of(name):
@@ -707,7 +707,6 @@
         got = over_ctx(others, 8)
         blocks = [mine] + [over_ctx(mine, mask) for mask in (4, 2, 6)]
         blocks += [got] + [over_ctx(got, mask) for mask in (4, 2, 6)]
-        blocks += [over_ctx(block, 1) for block in blocks]
 
         (small,) = call(
             prepare_kernel, "prepare", [((256, width // 2), BF)], [SM, SM] + [VM] * 6,
@@ -731,6 +730,7 @@
              ((1, ff), F32), ((1, width), F32), ((1, width), F32)],
             [SM, SM, VM, VM], [pltpu.VMEM((64, width), F32)], (meta, step_ids, small, other_small), after=[packed[0]],
         )
+        blocks += [over_ctx(tie(block, wh), 1) for block in blocks]
     else:
         def gather(w, axis=0):
             return lax.all_gather(w, "fsdp", axis=axis, tiled=True)

time: 231 us -> 228 us (0.987)
  Pallas kernels: 89.8 us -> 87 us
    pallas_call x25, Pallas kernels: 89.8 us -> 87 us  [call(): pl.pallas_call(kernel, name=name, out_shape=[jax.ShapeDtypeStruct(s, d) f...]
    unnamed x143 -> x153, local copies, waits for them, and re-layouts: 21.3 us -> 20.4 us
  transfers between devices with their start and end apart: 59 -> 59, of which waited for: 19 -> 25; matrix products, arithmetic and copies ran while one was open for 0% -> 0% of each run, Pallas kernels for 33% -> 33%
where the time goes in v5:
time: 228 us; the launch traced here: 227 us
  Pallas kernels  87 us (38%)
  starting transfers between devices  63 us (28%)
  waiting for transfers between devices  54.7 us (24%)
  local copies, waits for them, and re-layouts  21.1 us (9%)
    pallas_call x25, Pallas kernels, call(): pl.pallas_call(kernel, name=name, out_shape=[jax.ShapeDtypeStruct(s, d) f...  87 us
    ppermute x48, waiting for transfers between devices, over_ctx(): return lax.ppermute(value, 'ctx', [(i, i ^ mask) for i in range(16)])  50.6 us
    ppermute x48, starting transfers between devices, over_ctx(): return lax.ppermute(value, 'ctx', [(i, i ^ mask) for i in range(16)])  41.3 us
    unnamed x153, local copies, waits for them, and re-layouts  20.4 us
    ppermute x8, starting transfers between devices, over_x(): return lax.ppermute(value, 'fsdp', [(0, 1), (1, 0)])  8.28 us
    all_to_all x1, starting transfers between devices, shards(): dj = lax.all_to_all(joined_grad, 'ctx', 0, 0, tiled=True)  5.38 us
  transfers between devices with their start and end apart: 59, of which 25 were waited for; matrix products, arithmetic and copies ran while one was open for 0% of the time, Pallas kernels for 33%

profile of v5, /device:TPU:0, one launch (start us, length us, event | category | flops | bytes accessed | tf_op | source)
XLA Modules:
  0.0 227.2 jit_solution(10904376700029069544)
XLA Ops:
  1.3 1.7 split.1
  3.0 4.0 %collective-permute-start.4 = (bf16[192,512]{1,0:T(8,128)(2,1)}, bf16[192,512]{1,0:T(8,128)(2,1)S(1)}, u32[]{:S(2)}, u32[]{:S(2)}) collective-permute-start(bf16[192,512]{1,0:T(8,128)(2,1)} %get-tuple-element.156), channel_id=1, source_target_pairs={{0,16},{2,18},{4,20},{6,22},{8,24},{10,26},{12,28},{14,30},{16,0},... | collective-permute-start | bytes 589832 | tf_op jit(solution)/shard_map/ppermute | solution.py:664
  7.1 2.5 %collective-permute-start.3 = (bf16[192,512]{1,0:T(8,128)(2,1)}, bf16[192,512]{1,0:T(8,128)(2,1)S(1)}, u32[]{:S(2)}, u32[]{:S(2)}) collective-permute-start(bf16[192,512]{1,0:T(8,128)(2,1)} %get-tuple-element.157.refs_0_), channel_id=1, source_target_pairs={{0,12},{2,14},{4,8},{6,10},{8,4},{10,6},{12,0},{14,2},{16,28},{18,... | collective-permute-start | bytes 589832 | tf_op jit(solution)/shard_map/ppermute | solution.py:664
  10.6 2.0 prepare.1.mine
  12.5 1.5 collective-permute-start
  14.0 3.7 %pack.1 = (bf16[1152,512]{1,0:T(8,128)(2,1)}, bf16[512,512]{1,0:T(8,128)(2,1)}, bf16[384,512]{1,0:T(8,128)(2,1)}) custom-call(s32[10]{0:T(128)} %stack.40.meta, bf16[256,1024]{1,0:T(8,128)(2,1)} %own.2, bf16[256,512]{1,0:T(8,128)(2,1)} %own_out.3, bf16[256,512]{1,0:T(8,128)(2,1)} %own_query.3, bf16[256,512]{1,0:T(8,128)(2,1)} %own_cross.3, ...), custom_call_target="tpu_custom_call" | custom-call | flops 1000 | bytes 1000 | tf_op jit(solution)/shard_map/pack/pallas_call | solution.py:60
  19.1 2.9 %collective-permute-done.1.refs_1_ = bf16[192,512]{1,0:T(8,128)(2,1)} collective-permute-done((bf16[192,512]{1,0:T(8,128)(2,1)}, bf16[192,512]{1,0:T(8,128)(2,1)}, u32[]{:S(2)}, u32[]{:S(2)}) %collective-permute-start.1) | collective-permute-done | bytes 196640 | tf_op jit(solution)/shard_map/ppermute | solution.py:664
  22.0 1.5 collective-permute-start.16
  23.5 1.5 collective-permute-start.7
  25.5 1.5 collective-permute-start.5
  27.0 1.7 unpack.1
  28.8 3.1 %collective-permute-done.7.refs_7_ = bf16[192,512]{1,0:T(8,128)(2,1)} collective-permute-done((bf16[192,512]{1,0:T(8,128)(2,1)S(1)}, bf16[192,512]{1,0:T(8,128)(2,1)}, u32[]{:S(2)}, u32[]{:S(2)}) %collective-permute-start.7) | collective-permute-done | bytes 196640 | tf_op jit(solution)/shard_map/ppermute | solution.py:664
  31.9 2.0 collective-permute-done.6.refs_6_
  38.0 12.2 %attend.1 = (bf16[2048,512]{1,0:T(8,128)(2,1)}, bf16[192,2048]{1,0:T(8,128)(2,1)}, bf16[16,64,128]{2,1,0:T(8,128)(2,1)}, f32[64,2048]{1,0:T(8,128)}, f32[8,2048]{1,0:T(8,128)}) custom-call(s32[10]{0:T(128)} %stack.40.meta, f32[1,512]{1,0:T(1,128)} %get-tuple-element.152.step, f32[3,512]{1,0:T(4,128)} %get-tuple-element.153.gains, ...), custom_call_target="tpu_custom_call" | custom-call | flops 1000 | bytes 1000 | tf_op jit(solution)/shard_map/attend/pallas_call | solution.py:60
  51.1 4.4 %all-to-all-start = ((bf16[16,64,128]{2,1,0:T(8,128)(2,1)}), bf16[16,64,128]{2,1,0:T(8,128)(2,1)}, u32[]{:S(2)}, u32[]{:S(2)}) async-start(bf16[16,64,128]{2,1,0:T(8,128)(2,1)} %get-tuple-element.165), calls=%async_computation | async-start | bytes 524288 | tf_op jit(solution)/shard_map/all_to_all | solution.py:774
  55.6 6.3 %encoder_rows.1 = (bf16[2,512,512]{2,1,0:T(8,128)(2,1)}, bf16[2,1024,512]{2,1,0:T(8,128)(2,1)}, bf16[512,1024]{1,0:T(8,128)(2,1)}) custom-call(s32[10]{0:T(128)} %stack.40.meta, bf16[256,1024]{1,0:T(8,128)(2,1)} %own.2, bf16[1152,512]{1,0:T(8,128)(2,1)} %copy-done, bf16[1152,512]{1,0:T(8,128)(2,1)} %collective-permute-done.17.far.far2, ...), custom_call_target="tpu_custom_call" | custom-call | flops 1000 | bytes 1000 | tf_op jit(solution)/shard_map/encoder_rows/pallas_call | solution.py:60
  61.8 3.5 %all-to-all-done = bf16[16,64,128]{2,1,0:T(8,128)(2,1)} async-done(((bf16[16,64,128]{2,1,0:T(8,128)(2,1)}), bf16[16,64,128]{2,1,0:T(8,128)(2,1)}, u32[]{:S(2)}, u32[]{:S(2)}) %all-to-all-start) | async-done | bytes 262176 | tf_op jit(solution)/shard_map/all_to_all | solution.py:774
  66.7 1.6 copy-done.3
  69.2 5.4 %forward.1 = (f32[256,512]{1,0:T(8,128)S(1)}, f32[256,512]{1,0:T(8,128)S(1)}, bf16[256,512]{1,0:T(8,128)(2,1)S(1)}, bf16[2,512,128]{2,1,0:T(8,128)(2,1)S(1)}, bf16[16,128,512]{2,1,0:T(8,128)(2,1)S(1)}) custom-call(s32[10]{0:T(128)S(1)} %copy-done.55, bf16[2,128,512]{2,1,0:T(8,128)(2,1)S(1)} %copy-done.13, f32[2,512]{1,0:T(2,128)S(1)} %copy-done.57, ...), custom_call_target="tpu_custom_call" | custom-call | flops 1000 | bytes 1000 | tf_op jit(solution)/shard_map/forward/pallas_call | solution.py:60
  75.4 2.1 collective-permute-done.19.far3
  77.6 7.5 %feed.1 = (bf16[2,128,512]{2,1,0:T(8,128)(2,1)}, f32[256,512]{1,0:T(8,128)S(1)}, f32[16,512]{1,0:T(8,128)S(1)}, bf16[16,64,512]{2,1,0:T(8,128)(2,1)S(1)}, bf16[1...) custom-call(s32[10]{0:T(128)S(1)} %copy-done.55, ...), custom_call_target="tpu_custom_call" | custom-call | flops 1000 | bytes 1000 | tf_op jit(solution)/shard_map/feed/pallas_call | solution.py:60
  85.7 1.5 collective-permute-start.22
  87.2 4.3 %cross_back.1 = (bf16[256,512]{1,0:T(8,128)(2,1)S(1)}, bf16[2,1024,512]{2,1,0:T(8,128)(2,1)S(1)}) custom-call(s32[10]{0:T(128)S(1)} %copy-done.55, f32[256,512]{1,0:T(8,128)S(1)} %get-tuple-element.177.h2g, bf16[256,512]{1,0:T(8,128)(2,1)S(1)} %get-tuple-element.178.q, bf16[16,128,512]{2,1,0:T(8,128)(2,1)S(1)} %get-tuple-element.179.shares, ...), custom_call_target="tpu_custom_call" | custom-call | flops 1000 | bytes 1000 | tf_op jit(solution)/shard_map/cross_back/pallas_call | solution.py:60
  95.8 3.4 %hidden_back.1 = (f32[256,512]{1,0:T(8,128)S(1)}, bf16[2,512,128]{2,1,0:T(8,128)(2,1)}, f32[16,512]{1,0:T(8,128)S(1)}) custom-call(s32[10]{0:T(128)S(1)} %copy-done.55, f32[256,512]{1,0:T(8,128)S(1)} %get-tuple-element.177.h2g, f32[256,512]{1,0:T(8,128)S(1)} %get-tuple-element.188.hidden1, bf16[256,512]{1,0:T(8,128)(2,1)S(1)} %get-tuple-element.180.dq, ...), custom_call_target="tpu_custom_call" | custom-call | flops 1000 | bytes 1000 | tf_op jit(solution)/shard_map/hidden_back/pallas_call | solution.py:60
  100.1 3.7 %all-to-all-start.1 = ((bf16[16,64,128]{2,1,0:T(8,128)(2,1)}), bf16[16,64,128]{2,1,0:T(8,128)(2,1)S(1)}, u32[]{:S(2)}, u32[]{:S(2)}) async-start(bf16[16,64,128]{2,1,0:T(8,128)(2,1)} %bitcast.10), calls=%async_computation.1 | async-start | bytes 524288 | tf_op jit(solution)/shard_map/all_to_all | solution.py:837
  106.3 7.2 %weights_back.1 = (bf16[8,80,512]{2,1,0:T(8,128)(2,1)}, bf16[8,80,512]{2,1,0:T(8,128)(2,1)}, bf16[8,80,512]{2,1,0:T(8,128)(2,1)}, bf16[8,80,512]{2,1,0:T(8,128)(...) custom-call(s32[10]{0:T(128)} %stack.40.meta, f32[256,512]{1,0:T(8,128)} %copy-done.6, ...), custom_call_target="tpu_custom_call" | custom-call | flops 1000 | bytes 1000 | tf_op jit(solution)/shard_map/weights_back/pallas_call | solution.py:60
  117.1 1.6 collective-permute-start.27
  118.7 1.9 collective-permute-start.26
  120.6 6.1 %attend_back_1.1 = (f32[64,2048]{1,0:T(8,128)S(1)}, bf16[128,1024]{1,0:T(8,128)(2,1)S(1)}) custom-call(bf16[192,2048]{1,0:T(8,128)(2,1)S(1)} %copy-done.9, f32[64,2048]{1,0:T(8,128)S(1)} %copy-done.15, f32[8,2048]{1,0:T(8,128)S(1)} %copy-done.41, bf16[16,64,128]{2,1,0:T(8,128)(2,1)S(1)} %all-to-all-done.1.grads), custom_call_target="tpu_custom_call" | custom-call | flops 1000 | bytes 1000 | tf_op jit(solution)/shard_map/attend_back_1/pallas_call | solution.py:60
  128.5 1.7 collective-permute-start.32
  132.2 8.1 %attend_back_2.1 = (bf16[16,192,128]{2,1,0:T(8,128)(2,1)}, f32[208,256]{1,0:T(8,128)S(1)}, bf16[208,256]{1,0:T(8,128)(2,1)S(1)}) custom-call(s32[10]{0:T(128)S(1)} %copy-done.56, bf16[192,2048]{1,0:T(8,128)(2,1)S(1)} %copy-done.9, f32[64,2048]{1,0:T(8,128)S(1)} %copy-done.15, f32[8,2048]{1,0:T(8,128)S(1)} %copy-done.42, ...), custom_call_target="tpu_custom_call" | custom-call | flops 1000 | bytes 1000 | tf_op jit(solution)/shard_map/attend_back_2/pallas_call | solution.py:60
  142.5 5.4 %all-to-all-start.2 = ((bf16[16,192,128]{2,1,0:T(8,128)(2,1)}), bf16[16,192,128]{2,1,0:T(8,128)(2,1)S(1)}, u32[]{:S(2)}, u32[]{:S(2)}) async-start(bf16[16,192,128]{2,1,0:T(8,128)(2,1)} %get-tuple-element.248), calls=%async_computation.2 | async-start | bytes 1572864 | tf_op jit(solution)/shard_map/all_to_all | solution.py:896
  152.3 2.0 collective-permute-start.34
  156.4 2.4 %collective-permute-start.38 = (bf16[2,128,512]{2,1,0:T(8,128)(2,1)S(1)}, bf16[2,128,512]{2,1,0:T(8,128)(2,1)S(1)}, u32[]{:S(2)}, u32[]{:S(2)}) collective-permute-start(bf16[2,128,512]{2,1,0:T(8,128)(2,1)S(1)} %get-tuple-element.241.feed), channel_id=1, source_target_pairs={{0,16},{2,18},{4,20},{6,22},{8,24},{10,26},{12,28},{14,30},{16,0},... | collective-permute-start | bytes 786440 | tf_op jit(solution)/shard_map/ppermute | solution.py:664
  159.0 7.2 %collective-permute-done.34.refs_1_ = bf16[4,80,512]{2,1,0:T(8,128)(2,1)S(1)} collective-permute-done((bf16[4,80,512]{2,1,0:T(8,128)(2,1)S(1)}, bf16[4,80,512]{2,1,0:T(8,128)(2,1)S(1)}, u32[]{:S(2)}, u32[]{:S(2)}) %collective-permute-start.34) | collective-permute-done | bytes 327712 | tf_op jit(solution)/shard_map/ppermute | solution.py:664
  167.3 2.6 %collective-permute-start.36 = (bf16[2,80,512]{2,1,0:T(8,128)(2,1)S(1)}, bf16[2,80,512]{2,1,0:T(8,128)(2,1)S(1)}, u32[]{:S(2)}, u32[]{:S(2)}) collective-permute-start(bf16[2,80,512]{2,1,0:T(8,128)(2,1)S(1)} %get-tuple-element.239), channel_id=1, source_target_pairs={{0,8},{2,10},{4,12},{6,14},{8,0},{10,2},{12,4},{14,6},{16,24},{18,... | collective-permute-start | bytes 491528 | tf_op jit(solution)/shard_map/ppermute | solution.py:664
  169.9 1.6 collective-permute-start.39
  172.0 4.7 %collective-permute-done.36.refs_1_ = bf16[2,80,512]{2,1,0:T(8,128)(2,1)S(1)} collective-permute-done((bf16[2,80,512]{2,1,0:T(8,128)(2,1)S(1)}, bf16[2,80,512]{2,1,0:T(8,128)(2,1)S(1)}, u32[]{:S(2)}, u32[]{:S(2)}) %collective-permute-start.36) | collective-permute-done | bytes 163872 | tf_op jit(solution)/shard_map/ppermute | solution.py:664
  176.6 6.3 %collective-permute-done.38.feed_got = bf16[2,128,512]{2,1,0:T(8,128)(2,1)S(1)} collective-permute-done((bf16[2,128,512]{2,1,0:T(8,128)(2,1)S(1)}, bf16[2,128,512]{2,1,0:T(8,128)(2,1)S(1)}, u32[]{:S(2)}, u32[]{:S(2)}) %collective-permute-start.38) | collective-permute-done | bytes 262176 | tf_op jit(solution)/shard_map/ppermute | solution.py:664
  182.9 1.8 collective-permute-done.39.heads_got
  187.6 2.0 collective-permute-start.42
  189.7 2.9 %collective-permute-start.40 = (bf16[1,128,512]{2,1,0:T(8,128)(2,1)}, bf16[1,128,512]{2,1,0:T(8,128)(2,1)}, u32[]{:S(2)}, u32[]{:S(2)}) collective-permute-start(bf16[1,128,512]{2,1,0:T(8,128)(2,1)} %get-tuple-element.250), channel_id=1, source_target_pairs={{0,16},{2,18},{4,20},{6,22},{8,24},{10,26},{12,28},{14,30},{16,0},... | collective-permute-start | bytes 393224 | tf_op jit(solution)/shard_map/ppermute | solution.py:664
  193.7 2.9 %start_grad.1 = f32[2,128,512]{2,1,0:T(8,128)} custom-call(s32[10]{0:T(128)S(1)} %copy-done.56, bf16[2,8,192,128]{3,2,1,0:T(8,128)(2,1)S(1)} %bitcast.17, bf16[2,128,512]{2,1,0:T(8,128)(2,1)S(1)} %copy-done.14, f32[2,512]{1,0:T(2,128)S(1)} %copy-done.57, f32[3,512]{1,0:T(4,128)S(1)} %copy-done.36, f32[256,512]{1,0:T(8,128)S(1)} %copy-done.19, ...), custom_call_target="tpu_custom_call" | custom-call | flops 1000 | bytes 1000 | tf_op jit(solution)/shard_map/start_grad/pallas_call | solution.py:60
  196.6 12.2 %collective-permute-done.40.got = bf16[1,128,512]{2,1,0:T(8,128)(2,1)} collective-permute-done((bf16[1,128,512]{2,1,0:T(8,128)(2,1)}, bf16[1,128,512]{2,1,0:T(8,128)(2,1)}, u32[]{:S(2)}, u32[]{:S(2)}) %collective-permute-start.40) | collective-permute-done | bytes 131104 | tf_op jit(solution)/shard_map/ppermute | solution.py:664
  209.5 2.4 %collective-permute-done.42.refs_1_ = bf16[1,368,512]{2,1,0:T(8,128)(2,1)} collective-permute-done((bf16[1,368,512]{2,1,0:T(8,128)(2,1)S(1)}, bf16[1,368,512]{2,1,0:T(8,128)(2,1)}, u32[]{:S(2)}, u32[]{:S(2)}) %collective-permute-start.42) | collective-permute-done | bytes 376864 | tf_op jit(solution)/shard_map/ppermute | solution.py:664
  215.5 2.3 %encoder_back.1 = f32[2,32,512]{2,1,0:T(8,128)} custom-call(bf16[1,128,512]{2,1,0:T(8,128)(2,1)S(1)} %copy-done.54, bf16[1,128,512]{2,1,0:T(8,128)(2,1)} %collective-permute-done.40.got, bf16[512,1024]{1,0:T(8,128)(2,1)S(1)} %copy-done.22), custom_call_target="tpu_custom_call" | custom-call | flops 1000 | bytes 1000 | tf_op jit(solution)/shard_map/encoder_back/pallas_call | solution.py:60
  217.8 4.4 %place.1 = (f32[256,2048]{1,0:T(8,128)}, f32[1024,512]{1,0:T(8,128)}, f32[256,1536]{1,0:T(8,128)}, f32[3,256]{1,0:T(4,128)}, f32[3,256]{1,0:T(4,128)}, /*index=5...) custom-call(s32[10]{0:T(128)S(1)} %copy-done.56, f32[1,512]{1,0:T(1,128)S(1)} %copy-done.60, ...), custom_call_target="tpu_custom_call" | custom-call | flops 1000 | bytes 1000 | tf_op jit(solution)/shard_map/place/pallas_call | solution.py:60
  224.9 2.2 place_cross.1
  (249 shorter events, 48.3 us)
Async XLA Ops:
  3.0 14.7 %collective-permute-start.4 = (bf16[192,512]{1,0:T(8,128)(2,1)}, bf16[192,512]{1,0:T(8,128)(2,1)S(1)}, u32[]{:S(2)}, u32[]{:S(2)}) collective-permute-start(bf16[192,512]{1,0:T(8,128)(2,1)} %get-tuple-element.156), channel_id=1, source_target_pairs={{0,16},{2,18},{4,20},{6,22},{8,24},{10,26},{12,28},{14,30},{16,0},... | collective-permute-start | bytes 589832 | tf_op jit(solution)/shard_map/ppermute | solution.py:664
  7.1 12.0 %collective-permute-start.3 = (bf16[192,512]{1,0:T(8,128)(2,1)}, bf16[192,512]{1,0:T(8,128)(2,1)S(1)}, u32[]{:S(2)}, u32[]{:S(2)}) collective-permute-start(bf16[192,512]{1,0:T(8,128)(2,1)} %get-tuple-element.157.refs_0_), channel_id=1, source_target_pairs={{0,12},{2,14},{4,8},{6,10},{8,4},{10,6},{12,0},{14,2},{16,28},{18,... | collective-permute-start | bytes 589832 | tf_op jit(solution)/shard_map/ppermute | solution.py:664
  9.6 9.5 %collective-permute-start.2 = (bf16[192,512]{1,0:T(8,128)(2,1)}, bf16[192,512]{1,0:T(8,128)(2,1)S(1)}, u32[]{:S(2)}, u32[]{:S(2)}) collective-permute-start(bf16[192,512]{1,0:T(8,128)(2,1)} %get-tuple-element.157.refs_0_), channel_id=1, source_target_pairs={{0,4},{2,6},{4,0},{6,2},{8,12},{10,14},{12,8},{14,10},{16,20},{18,... | collective-permute-start | bytes 589832 | tf_op jit(solution)/shard_map/ppermute | solution.py:664
  10.1 11.9 %collective-permute-start.1 = (bf16[192,512]{1,0:T(8,128)(2,1)}, bf16[192,512]{1,0:T(8,128)(2,1)}, u32[]{:S(2)}, u32[]{:S(2)}) collective-permute-start(bf16[192,512]{1,0:T(8,128)(2,1)} %get-tuple-element.157.refs_0_), channel_id=1, source_target_pairs={{0,8},{2,10},{4,12},{6,14},{8,0},{10,2},{12,4},{14,6},{16,24},{18,... | collective-permute-start | bytes 589832 | tf_op jit(solution)/shard_map/ppermute | solution.py:664
  12.5 5.2 %collective-permute-start = (bf16[256,256]{1,0:T(8,128)(2,1)}, bf16[256,256]{1,0:T(8,128)(2,1)S(1)}, u32[]{:S(2)}, u32[]{:S(2)}) collective-permute-start(bf16[256,256]{1,0:T(8,128)(2,1)} %prepare.1.mine), channel_id=1, source_target_pairs={{0,1},{1,0},{2,3},{3,2},{4,5},{5,4},{6,7},{7,6},{8,9},{9,8},{10,11... | collective-permute-start | bytes 393224 | tf_op jit(solution)/shard_map/ppermute | solution.py:668
  22.0 28.3 %collective-permute-start.16 = (bf16[1152,512]{1,0:T(8,128)(2,1)}, bf16[1152,512]{1,0:T(8,128)(2,1)S(1)}, u32[]{:S(2)}, u32[]{:S(2)}) collective-permute-start(bf16[1152,512]{1,0:T(8,128)(2,1)} %get-tuple-element.166), channel_id=1, source_target_pairs={{0,1},{1,0},{2,3},{3,2},{4,5},{5,4},{6,7},{7,6},{8,9},{9,8},{10,11... | collective-permute-start | bytes 3538952 | tf_op jit(solution)/shard_map/ppermute | solution.py:668
  23.5 8.4 %collective-permute-start.7 = (bf16[192,512]{1,0:T(8,128)(2,1)S(1)}, bf16[192,512]{1,0:T(8,128)(2,1)}, u32[]{:S(2)}, u32[]{:S(2)}) collective-permute-start(bf16[192,512]{1,0:T(8,128)(2,1)S(1)} %collective-permute-done.4.refs_4_), channel_id=1, source_target_pairs={{0,12},{2,14},{4,8},{6,10},{8,4},{10,6},{12,0},{14,2},{16,28},{18,... | collective-permute-start | bytes 589832 | tf_op jit(solution)/shard_map/ppermute | solution.py:664
  25.0 8.9 %collective-permute-start.6 = (bf16[192,512]{1,0:T(8,128)(2,1)S(1)}, bf16[192,512]{1,0:T(8,128)(2,1)}, u32[]{:S(2)}, u32[]{:S(2)}) collective-permute-start(bf16[192,512]{1,0:T(8,128)(2,1)S(1)} %collective-permute-done.4.refs_4_), channel_id=1, source_target_pairs={{0,4},{2,6},{4,0},{6,2},{8,12},{10,14},{12,8},{14,10},{16,20},{18,... | collective-permute-start | bytes 589832 | tf_op jit(solution)/shard_map/ppermute | solution.py:664
  25.5 8.4 %collective-permute-start.5 = (bf16[192,512]{1,0:T(8,128)(2,1)S(1)}, bf16[192,512]{1,0:T(8,128)(2,1)}, u32[]{:S(2)}, u32[]{:S(2)}) collective-permute-start(bf16[192,512]{1,0:T(8,128)(2,1)S(1)} %collective-permute-done.4.refs_4_), channel_id=1, source_target_pairs={{0,8},{2,10},{4,12},{6,14},{8,0},{10,2},{12,4},{14,6},{16,24},{18,... | collective-permute-start | bytes 589832 | tf_op jit(solution)/shard_map/ppermute | solution.py:664
  28.7 5.7 %collective-permute-start.8 = (bf16[192,512]{1,0:T(8,128)(2,1)S(1)}, bf16[192,512]{1,0:T(8,128)(2,1)S(1)}, u32[]{:S(2)}, u32[]{:S(2)}) collective-permute-start(bf16[192,512]{1,0:T(8,128)(2,1)S(1)} %copy-done.63), channel_id=1, source_target_pairs={{0,2},{2,0},{4,6},{6,4},{8,10},{10,8},{12,14},{14,12},{16,18},{18,... | collective-permute-start | bytes 589832 | tf_op jit(solution)/shard_map/ppermute | solution.py:664
  31.9 2.6 %collective-permute-start.9 = (bf16[192,512]{1,0:T(8,128)(2,1)}, bf16[192,512]{1,0:T(8,128)(2,1)S(1)}, u32[]{:S(2)}, u32[]{:S(2)}) collective-permute-start(bf16[192,512]{1,0:T(8,128)(2,1)} %collective-permute-done.1.refs_1_), channel_id=1, source_target_pairs={{0,2},{2,0},{4,6},{6,4},{8,10},{10,8},{12,14},{14,12},{16,18},{18,... | collective-permute-start | bytes 589832 | tf_op jit(solution)/shard_map/ppermute | solution.py:664
  50.3 5.3 %collective-permute-start.17 = (bf16[1152,512]{1,0:T(8,128)(2,1)S(1)}, bf16[1152,512]{1,0:T(8,128)(2,1)}, u32[]{:S(2)}, u32[]{:S(2)}) collective-permute-start(bf16[1152,512]{1,0:T(8,128)(2,1)S(1)} %collective-permute-done.16.near.near2), channel_id=1, source_target_pairs={{0,2},{2,0},{4,6},{6,4},{8,10},{10,8},{12,14},{14,12},{16,18},{18,... | collective-permute-start | bytes 3538952 | tf_op jit(solution)/shard_map/ppermute | solution.py:664
  50.6 24.8 %collective-permute-start.18 = (bf16[512,512]{1,0:T(8,128)(2,1)}, bf16[512,512]{1,0:T(8,128)(2,1)}, u32[]{:S(2)}, u32[]{:S(2)}) collective-permute-start(bf16[512,512]{1,0:T(8,128)(2,1)} %get-tuple-element.173), channel_id=1, source_target_pairs={{0,1},{1,0},{2,3},{3,2},{4,5},{5,4},{6,7},{7,6},{8,9},{9,8},{10,11... | collective-permute-start | bytes 1572872 | tf_op jit(solution)/shard_map/ppermute | solution.py:668
  51.1 14.3 %all-to-all-start = ((bf16[16,64,128]{2,1,0:T(8,128)(2,1)}), bf16[16,64,128]{2,1,0:T(8,128)(2,1)}, u32[]{:S(2)}, u32[]{:S(2)}) async-start(bf16[16,64,128]{2,1,0:T(8,128)(2,1)} %get-tuple-element.165), calls=%async_computation | async-start | bytes 524288 | tf_op jit(solution)/shard_map/all_to_all | solution.py:774
  75.4 2.1 collective-permute-start.19
  85.1 7.8 %collective-permute-start.20 = (bf16[16,64,512]{2,1,0:T(8,128)(2,1)S(1)}, bf16[16,64,512]{2,1,0:T(8,128)(2,1)S(1)}, u32[]{:S(2)}, u32[]{:S(2)}) collective-permute-start(bf16[16,64,512]{2,1,0:T(8,128)(2,1)S(1)} %get-tuple-element.182), channel_id=1, source_target_pairs={{0,2},{2,0},{4,6},{6,4},{8,10},{10,8},{12,14},{14,12},{16,18},{18,... | collective-permute-start | bytes 3145736 | tf_op jit(solution)/shard_map/ppermute | solution.py:664
  85.3 7.6 %collective-permute-start.21 = (bf16[16,64,512]{2,1,0:T(8,128)(2,1)S(1)}, bf16[16,64,512]{2,1,0:T(8,128)(2,1)S(1)}, u32[]{:S(2)}, u32[]{:S(2)}) collective-permute-start(bf16[16,64,512]{2,1,0:T(8,128)(2,1)S(1)} %get-tuple-element.184), channel_id=1, source_target_pairs={{0,2},{2,0},{4,6},{6,4},{8,10},{10,8},{12,14},{14,12},{16,18},{18,... | collective-permute-start | bytes 3145736 | tf_op jit(solution)/shard_map/ppermute | solution.py:664
  85.7 18.1 %collective-permute-start.22 = (bf16[384,512]{1,0:T(8,128)(2,1)}, bf16[384,512]{1,0:T(8,128)(2,1)S(1)}, u32[]{:S(2)}, u32[]{:S(2)}) collective-permute-start(bf16[384,512]{1,0:T(8,128)(2,1)} %get-tuple-element.192), channel_id=1, source_target_pairs={{0,1},{1,0},{2,3},{3,2},{4,5},{5,4},{6,7},{7,6},{8,9},{9,8},{10,11... | collective-permute-start | bytes 1179656 | tf_op jit(solution)/shard_map/ppermute | solution.py:668
  95.2 18.6 %collective-permute-start.25 = (bf16[8,64,512]{2,1,0:T(8,128)(2,1)}, bf16[8,64,512]{2,1,0:T(8,128)(2,1)}, u32[]{:S(2)}, u32[]{:S(2)}) collective-permute-start(bf16[8,64,512]{2,1,0:T(8,128)(2,1)} %get-tuple-element.202), channel_id=1, source_target_pairs={{0,4},{2,6},{4,0},{6,2},{8,12},{10,14},{12,8},{14,10},{16,20},{18,... | collective-permute-start | bytes 1572872 | tf_op jit(solution)/shard_map/ppermute | solution.py:664
  95.3 18.5 %collective-permute-start.24 = (bf16[8,64,512]{2,1,0:T(8,128)(2,1)}, bf16[8,64,512]{2,1,0:T(8,128)(2,1)}, u32[]{:S(2)}, u32[]{:S(2)}) collective-permute-start(bf16[8,64,512]{2,1,0:T(8,128)(2,1)} %get-tuple-element.186), channel_id=1, source_target_pairs={{0,1},{1,0},{2,3},{3,2},{4,5},{5,4},{6,7},{7,6},{8,9},{9,8},{10,11... | collective-permute-start | bytes 1572872 | tf_op jit(solution)/shard_map/ppermute | solution.py:668
  100.1 13.8 %all-to-all-start.1 = ((bf16[16,64,128]{2,1,0:T(8,128)(2,1)}), bf16[16,64,128]{2,1,0:T(8,128)(2,1)S(1)}, u32[]{:S(2)}, u32[]{:S(2)}) async-start(bf16[16,64,128]{2,1,0:T(8,128)(2,1)} %bitcast.10), calls=%async_computation.1 | async-start | bytes 524288 | tf_op jit(solution)/shard_map/all_to_all | solution.py:837
  113.8 13.2 %collective-permute-start.30 = (bf16[8,128,512]{2,1,0:T(8,128)(2,1)}, bf16[8,128,512]{2,1,0:T(8,128)(2,1)S(1)}, u32[]{:S(2)}, u32[]{:S(2)}) collective-permute-start(bf16[8,128,512]{2,1,0:T(8,128)(2,1)} %get-tuple-element.220), channel_id=1, source_target_pairs={{0,2},{2,0},{4,6},{6,4},{8,10},{10,8},{12,14},{14,12},{16,18},{18,... | collective-permute-start | bytes 3145736 | tf_op jit(solution)/shard_map/ppermute | solution.py:664
  114.0 13.0 %collective-permute-start.28 = (bf16[8,80,512]{2,1,0:T(8,128)(2,1)}, bf16[8,80,512]{2,1,0:T(8,128)(2,1)S(1)}, u32[]{:S(2)}, u32[]{:S(2)}) collective-permute-start(bf16[8,80,512]{2,1,0:T(8,128)(2,1)} %get-tuple-element.214), channel_id=1, source_target_pairs={{0,2},{2,0},{4,6},{6,4},{8,10},{10,8},{12,14},{14,12},{16,18},{18,... | collective-permute-start | bytes 1966088 | tf_op jit(solution)/shard_map/ppermute | solution.py:664
  114.4 12.6 %collective-permute-start.29 = (bf16[8,80,512]{2,1,0:T(8,128)(2,1)}, bf16[8,80,512]{2,1,0:T(8,128)(2,1)S(1)}, u32[]{:S(2)}, u32[]{:S(2)}) collective-permute-start(bf16[8,80,512]{2,1,0:T(8,128)(2,1)} %get-tuple-element.217), channel_id=1, source_target_pairs={{0,2},{2,0},{4,6},{6,4},{8,10},{10,8},{12,14},{14,12},{16,18},{18,... | collective-permute-start | bytes 1966088 | tf_op jit(solution)/shard_map/ppermute | solution.py:664
  117.1 9.6 %collective-permute-start.27 = (bf16[4,64,512]{2,1,0:T(8,128)(2,1)S(1)}, bf16[4,64,512]{2,1,0:T(8,128)(2,1)S(1)}, u32[]{:S(2)}, u32[]{:S(2)}) collective-permute-start(bf16[4,64,512]{2,1,0:T(8,128)(2,1)S(1)} %get-tuple-element.212), channel_id=1, source_target_pairs={{0,1},{1,0},{2,3},{3,2},{4,5},{5,4},{6,7},{7,6},{8,9},{9,8},{10,11... | collective-permute-start | bytes 786440 | tf_op jit(solution)/shard_map/ppermute | solution.py:668
  118.7 8.3 %collective-permute-start.26 = (bf16[4,64,512]{2,1,0:T(8,128)(2,1)S(1)}, bf16[4,64,512]{2,1,0:T(8,128)(2,1)S(1)}, u32[]{:S(2)}, u32[]{:S(2)}) collective-permute-start(bf16[4,64,512]{2,1,0:T(8,128)(2,1)S(1)} %get-tuple-element.205), channel_id=1, source_target_pairs={{0,4},{2,6},{4,0},{6,2},{8,12},{10,14},{12,8},{14,10},{16,20},{18,... | collective-permute-start | bytes 786440 | tf_op jit(solution)/shard_map/ppermute | solution.py:664
  128.5 13.2 %collective-permute-start.32 = (bf16[4,128,512]{2,1,0:T(8,128)(2,1)S(1)}, bf16[4,128,512]{2,1,0:T(8,128)(2,1)S(1)}, u32[]{:S(2)}, u32[]{:S(2)}) collective-permute-start(bf16[4,128,512]{2,1,0:T(8,128)(2,1)S(1)} %get-tuple-element.228), channel_id=1, source_target_pairs={{0,4},{2,6},{4,0},{6,2},{8,12},{10,14},{12,8},{14,10},{16,20},{18,... | collective-permute-start | bytes 1572872 | tf_op jit(solution)/shard_map/ppermute | solution.py:664
  130.2 10.8 %collective-permute-start.31 = (bf16[2,128,512]{2,1,0:T(8,128)(2,1)S(1)}, bf16[2,128,512]{2,1,0:T(8,128)(2,1)S(1)}, u32[]{:S(2)}, u32[]{:S(2)}) collective-permute-start(bf16[2,128,512]{2,1,0:T(8,128)(2,1)S(1)} %get-tuple-element.222), channel_id=1, source_target_pairs={{0,8},{2,10},{4,12},{6,14},{8,0},{10,2},{12,4},{14,6},{16,24},{18,... | collective-permute-start | bytes 786440 | tf_op jit(solution)/shard_map/ppermute | solution.py:664
  131.7 16.3 %collective-permute-start.33 = (bf16[8,80,512]{2,1,0:T(8,128)(2,1)}, bf16[8,80,512]{2,1,0:T(8,128)(2,1)S(1)}, u32[]{:S(2)}, u32[]{:S(2)}) collective-permute-start(bf16[8,80,512]{2,1,0:T(8,128)(2,1)} %get-tuple-element.233), channel_id=1, source_target_pairs={{0,1},{1,0},{2,3},{3,2},{4,5},{5,4},{6,7},{7,6},{8,9},{9,8},{10,11... | collective-permute-start | bytes 1966088 | tf_op jit(solution)/shard_map/ppermute | solution.py:668
  142.5 50.1 %all-to-all-start.2 = ((bf16[16,192,128]{2,1,0:T(8,128)(2,1)}), bf16[16,192,128]{2,1,0:T(8,128)(2,1)S(1)}, u32[]{:S(2)}, u32[]{:S(2)}) async-start(bf16[16,192,128]{2,1,0:T(8,128)(2,1)} %get-tuple-element.248), calls=%async_computation.2 | async-start | bytes 1572864 | tf_op jit(solution)/shard_map/all_to_all | solution.py:896
  152.3 13.9 %collective-permute-start.34 = (bf16[4,80,512]{2,1,0:T(8,128)(2,1)S(1)}, bf16[4,80,512]{2,1,0:T(8,128)(2,1)S(1)}, u32[]{:S(2)}, u32[]{:S(2)}) collective-permute-start(bf16[4,80,512]{2,1,0:T(8,128)(2,1)S(1)} %get-tuple-element.235), channel_id=1, source_target_pairs={{0,4},{2,6},{4,0},{6,2},{8,12},{10,14},{12,8},{14,10},{16,20},{18,... | collective-permute-start | bytes 983048 | tf_op jit(solution)/shard_map/ppermute | solution.py:664
  154.3 4.7 %collective-permute-start.35 = (bf16[208,256]{1,0:T(8,128)(2,1)S(1)}, bf16[208,256]{1,0:T(8,128)(2,1)S(1)}, u32[]{:S(2)}, u32[]{:S(2)}) collective-permute-start(bf16[208,256]{1,0:T(8,128)(2,1)S(1)} %copy-done.62), channel_id=1, source_target_pairs={{0,1},{1,0},{2,3},{3,2},{4,5},{5,4},{6,7},{7,6},{8,9},{9,8},{10,11... | collective-permute-start | bytes 319496 | tf_op jit(solution)/shard_map/ppermute | solution.py:668
  154.9 17.1 %collective-permute-start.37 = (bf16[2,128,512]{2,1,0:T(8,128)(2,1)S(1)}, bf16[2,128,512]{2,1,0:T(8,128)(2,1)S(1)}, u32[]{:S(2)}, u32[]{:S(2)}) collective-permute-start(bf16[2,128,512]{2,1,0:T(8,128)(2,1)S(1)} %get-tuple-element.240), channel_id=1, source_target_pairs={{0,8},{2,10},{4,12},{6,14},{8,0},{10,2},{12,4},{14,6},{16,24},{18,... | collective-permute-start | bytes 786440 | tf_op jit(solution)/shard_map/ppermute | solution.py:664
  156.4 26.6 %collective-permute-start.38 = (bf16[2,128,512]{2,1,0:T(8,128)(2,1)S(1)}, bf16[2,128,512]{2,1,0:T(8,128)(2,1)S(1)}, u32[]{:S(2)}, u32[]{:S(2)}) collective-permute-start(bf16[2,128,512]{2,1,0:T(8,128)(2,1)S(1)} %get-tuple-element.241.feed), channel_id=1, source_target_pairs={{0,16},{2,18},{4,20},{6,22},{8,24},{10,26},{12,28},{14,30},{16,0},... | collective-permute-start | bytes 786440 | tf_op jit(solution)/shard_map/ppermute | solution.py:664
  167.3 9.4 %collective-permute-start.36 = (bf16[2,80,512]{2,1,0:T(8,128)(2,1)S(1)}, bf16[2,80,512]{2,1,0:T(8,128)(2,1)S(1)}, u32[]{:S(2)}, u32[]{:S(2)}) collective-permute-start(bf16[2,80,512]{2,1,0:T(8,128)(2,1)S(1)} %get-tuple-element.239), channel_id=1, source_target_pairs={{0,8},{2,10},{4,12},{6,14},{8,0},{10,2},{12,4},{14,6},{16,24},{18,... | collective-permute-start | bytes 491528 | tf_op jit(solution)/shard_map/ppermute | solution.py:664
  169.9 14.9 %collective-permute-start.39 = (bf16[1,208,256]{2,1,0:T(8,128)(2,1)S(1)}, bf16[1,208,256]{2,1,0:T(8,128)(2,1)S(1)}, u32[]{:S(2)}, u32[]{:S(2)}) collective-permute-start(bf16[1,208,256]{2,1,0:T(8,128)(2,1)S(1)} %get-tuple-element.242.heads), channel_id=1, source_target_pairs={{0,16},{2,18},{4,20},{6,22},{8,24},{10,26},{12,28},{14,30},{16,0},... | collective-permute-start | bytes 319496 | tf_op jit(solution)/shard_map/ppermute | solution.py:664
  186.2 22.8 %collective-permute-start.44 = (bf16[1,368,512]{2,1,0:T(8,128)(2,1)S(1)}, bf16[1,368,512]{2,1,0:T(8,128)(2,1)}, u32[]{:S(2)}, u32[]{:S(2)}) collective-permute-start(bf16[1,368,512]{2,1,0:T(8,128)(2,1)S(1)} %reduce_6.1.refs_0_), channel_id=1, source_target_pairs={{0,12},{2,14},{4,8},{6,10},{8,4},{10,6},{12,0},{14,2},{16,28},{18,... | collective-permute-start | bytes 1130504 | tf_op jit(solution)/shard_map/ppermute | solution.py:664
  186.2 23.3 %collective-permute-start.43 = (bf16[1,368,512]{2,1,0:T(8,128)(2,1)S(1)}, bf16[1,368,512]{2,1,0:T(8,128)(2,1)}, u32[]{:S(2)}, u32[]{:S(2)}) collective-permute-start(bf16[1,368,512]{2,1,0:T(8,128)(2,1)S(1)} %reduce_6.1.refs_0_), channel_id=1, source_target_pairs={{0,4},{2,6},{4,0},{6,2},{8,12},{10,14},{12,8},{14,10},{16,20},{18,... | collective-permute-start | bytes 1130504 | tf_op jit(solution)/shard_map/ppermute | solution.py:664
  187.6 24.3 %collective-permute-start.42 = (bf16[1,368,512]{2,1,0:T(8,128)(2,1)S(1)}, bf16[1,368,512]{2,1,0:T(8,128)(2,1)}, u32[]{:S(2)}, u32[]{:S(2)}) collective-permute-start(bf16[1,368,512]{2,1,0:T(8,128)(2,1)S(1)} %reduce_6.1.refs_0_), channel_id=1, source_target_pairs={{0,8},{2,10},{4,12},{6,14},{8,0},{10,2},{12,4},{14,6},{16,24},{18,... | collective-permute-start | bytes 1130504 | tf_op jit(solution)/shard_map/ppermute | solution.py:664
  189.7 19.2 %collective-permute-start.41 = (bf16[2,80,512]{2,1,0:T(8,128)(2,1)S(1)}, bf16[2,80,512]{2,1,0:T(8,128)(2,1)S(1)}, u32[]{:S(2)}, u32[]{:S(2)}) collective-permute-start(bf16[2,80,512]{2,1,0:T(8,128)(2,1)S(1)} %get-tuple-element.251.mine), channel_id=1, source_target_pairs={{0,16},{2,18},{4,20},{6,22},{8,24},{10,26},{12,28},{14,30},{16,0},... | collective-permute-start | bytes 491528 | tf_op jit(solution)/shard_map/ppermute | solution.py:664
  189.7 19.2 %collective-permute-start.40 = (bf16[1,128,512]{2,1,0:T(8,128)(2,1)}, bf16[1,128,512]{2,1,0:T(8,128)(2,1)}, u32[]{:S(2)}, u32[]{:S(2)}) collective-permute-start(bf16[1,128,512]{2,1,0:T(8,128)(2,1)} %get-tuple-element.250), channel_id=1, source_target_pairs={{0,16},{2,18},{4,20},{6,22},{8,24},{10,26},{12,28},{14,30},{16,0},... | collective-permute-start | bytes 393224 | tf_op jit(solution)/shard_map/ppermute | solution.py:664
  208.9 4.5 %collective-permute-start.45 = (bf16[1,368,512]{2,1,0:T(8,128)(2,1)S(1)}, bf16[1,368,512]{2,1,0:T(8,128)(2,1)S(1)}, u32[]{:S(2)}, u32[]{:S(2)}) collective-permute-start(bf16[1,368,512]{2,1,0:T(8,128)(2,1)S(1)} %reduce_6.1.refs_0_), channel_id=1, source_target_pairs={{0,2},{2,0},{4,6},{6,4},{8,10},{10,8},{12,14},{14,12},{16,18},{18,... | collective-permute-start | bytes 1130504 | tf_op jit(solution)/shard_map/ppermute | solution.py:664
  209.0 5.1 %collective-permute-start.48 = (bf16[1,368,512]{2,1,0:T(8,128)(2,1)}, bf16[1,368,512]{2,1,0:T(8,128)(2,1)S(1)}, u32[]{:S(2)}, u32[]{:S(2)}) collective-permute-start(bf16[1,368,512]{2,1,0:T(8,128)(2,1)} %collective-permute-done.44.refs_3_), channel_id=1, source_target_pairs={{0,2},{2,0},{4,6},{6,4},{8,10},{10,8},{12,14},{14,12},{16,18},{18,... | collective-permute-start | bytes 1130504 | tf_op jit(solution)/shard_map/ppermute | solution.py:664
  209.5 8.3 %collective-permute-start.47 = (bf16[1,368,512]{2,1,0:T(8,128)(2,1)}, bf16[1,368,512]{2,1,0:T(8,128)(2,1)S(1)}, u32[]{:S(2)}, u32[]{:S(2)}) collective-permute-start(bf16[1,368,512]{2,1,0:T(8,128)(2,1)} %collective-permute-done.43.refs_2_), channel_id=1, source_target_pairs={{0,2},{2,0},{4,6},{6,4},{8,10},{10,8},{12,14},{14,12},{16,18},{18,... | collective-permute-start | bytes 1130504 | tf_op jit(solution)/shard_map/ppermute | solution.py:664
  212.0 5.8 %collective-permute-start.46 = (bf16[1,368,512]{2,1,0:T(8,128)(2,1)}, bf16[1,368,512]{2,1,0:T(8,128)(2,1)S(1)}, u32[]{:S(2)}, u32[]{:S(2)}) collective-permute-start(bf16[1,368,512]{2,1,0:T(8,128)(2,1)} %collective-permute-done.42.refs_1_), channel_id=1, source_target_pairs={{0,2},{2,0},{4,6},{6,4},{8,10},{10,8},{12,14},{14,12},{16,18},{18,... | collective-permute-start | bytes 1130504 | tf_op jit(solution)/shard_map/ppermute | solution.py:664
  212.0 10.2 %collective-permute-start.51 = (bf16[2,80,512]{2,1,0:T(8,128)(2,1)S(1)}, bf16[2,80,512]{2,1,0:T(8,128)(2,1)S(1)}, u32[]{:S(2)}, u32[]{:S(2)}) collective-permute-start(bf16[2,80,512]{2,1,0:T(8,128)(2,1)S(1)} %reduce_8.1.refs_0_), channel_id=1, source_target_pairs={{0,12},{2,14},{4,8},{6,10},{8,4},{10,6},{12,0},{14,2},{16,28},{18,... | collective-permute-start | bytes 491528 | tf_op jit(solution)/shard_map/ppermute | solution.py:664
  213.4 9.4 %collective-permute-start.50 = (bf16[2,80,512]{2,1,0:T(8,128)(2,1)S(1)}, bf16[2,80,512]{2,1,0:T(8,128)(2,1)S(1)}, u32[]{:S(2)}, u32[]{:S(2)}) collective-permute-start(bf16[2,80,512]{2,1,0:T(8,128)(2,1)S(1)} %reduce_8.1.refs_0_), channel_id=1, source_target_pairs={{0,4},{2,6},{4,0},{6,2},{8,12},{10,14},{12,8},{14,10},{16,20},{18,... | collective-permute-start | bytes 491528 | tf_op jit(solution)/shard_map/ppermute | solution.py:664
  214.1 8.7 %collective-permute-start.49 = (bf16[2,80,512]{2,1,0:T(8,128)(2,1)S(1)}, bf16[2,80,512]{2,1,0:T(8,128)(2,1)S(1)}, u32[]{:S(2)}, u32[]{:S(2)}) collective-permute-start(bf16[2,80,512]{2,1,0:T(8,128)(2,1)S(1)} %reduce_8.1.refs_0_), channel_id=1, source_target_pairs={{0,8},{2,10},{4,12},{6,14},{8,0},{10,2},{12,4},{14,6},{16,24},{18,... | collective-permute-start | bytes 491528 | tf_op jit(solution)/shard_map/ppermute | solution.py:664
  (87 other events, 662.4 us)

commit v6 on v5

--- a/solution.py
+++ b/solution.py
@@ -810,7 +810,7 @@
     hold_far = []
     if fast:
         far4 = over_ctx(tie(near4, h2g), 1)
-        hold_far = [far4]
+        late = [far4]
         down_got, up_got = over_ctx(down_send, 1), over_ctx(up_send, 1)
     dq, part = call(
         cross_back_kernel, "cross_back",
@@ -888,7 +888,7 @@
         (merged,) = call(
             merge_kernel, "reduce_6", [((1, 368, width), BF)], [VM] * 4, [], (feed_w, feed_w1, u_sum, u_8), after=[cross_z1, kv_2],
         )
-        cross_w, kv_far, kv_near = sums("reduce_7", [([[cross_kept, cross_z1]], False), ([[kv_kept, kv_2]], True)], [merged])
+        cross_w, kv_far, kv_near = sums("reduce_7", [([[cross_kept, cross_z1]], False), ([[kv_kept, kv_2]], True)], [merged] + late)
         cross_w1, kv_got = over_ctx(cross_w, 8), over_ctx(kv_far, 8)
         merged = tie(merged, cross_w)
         spread_out = [over_ctx(merged, mask) for mask in (4, 2, 6)]

time: 228 us -> 225 us (0.987)
  starting transfers between devices: 63 us -> 58.7 us
  waiting for transfers between devices: 54.7 us -> 57.2 us
    ppermute x48, waiting for transfers between devices: 50.6 us -> 45.4 us  [over_ctx(): return lax.ppermute(value, 'ctx', [(i, i ^ mask) for i in range(16)])]
    ppermute x8, waiting for transfers between devices: 0.32 us -> 5.52 us  [over_x(): return lax.ppermute(value, 'fsdp', [(0, 1), (1, 0)])]
    ppermute x48, starting transfers between devices: 41.3 us -> 36.9 us  [over_ctx(): return lax.ppermute(value, 'ctx', [(i, i ^ mask) for i in range(16)])]
    all_to_all x1, waiting for transfers between devices: 0.27 us -> 2.8 us  [shards(): lax.all_to_all(jnp.broadcast_to(by_unit, (units, rep, hd, rows)).reshape(...]
    unnamed x153 -> x149, local copies, waits for them, and re-layouts: 20.4 us -> 18.9 us
  transfers between devices with their start and end apart: 59 -> 59, of which waited for: 25 -> 26; matrix products, arithmetic and copies ran while one was open for 0% -> 0% of each run, Pallas kernels for 33% -> 32%
where the time goes in v6:
time: 225 us; the launch traced here: 224 us
  Pallas kernels  86.9 us (39%)
  starting transfers between devices  58.7 us (26%)
  waiting for transfers between devices  57.2 us (25%)
  local copies, waits for them, and re-layouts  19.5 us (9%)
    pallas_call x25, Pallas kernels, call(): pl.pallas_call(kernel, name=name, out_shape=[jax.ShapeDtypeStruct(s, d) f...  86.9 us
    ppermute x48, waiting for transfers between devices, over_ctx(): return lax.ppermute(value, 'ctx', [(i, i ^ mask) for i in range(16)])  45.4 us
    ppermute x48, starting transfers between devices, over_ctx(): return lax.ppermute(value, 'ctx', [(i, i ^ mask) for i in range(16)])  36.9 us
    unnamed x149, local copies, waits for them, and re-layouts  18.9 us
    ppermute x8, starting transfers between devices, over_x(): return lax.ppermute(value, 'fsdp', [(0, 1), (1, 0)])  10.1 us
    ppermute x8, waiting for transfers between devices, over_x(): return lax.ppermute(value, 'fsdp', [(0, 1), (1, 0)])  5.52 us
  transfers between devices with their start and end apart: 59, of which 26 were waited for; matrix products, arithmetic and copies ran while one was open for 0% of the time, Pallas kernels for 32%

profile of v6, /device:TPU:0, one launch (start us, length us, event | category | flops | bytes accessed | tf_op | source)
XLA Modules:
  0.0 223.7 jit_solution(16019937347359316395)
XLA Ops:
  1.3 1.7 split.1
  3.0 4.0 %collective-permute-start.4 = (bf16[192,512]{1,0:T(8,128)(2,1)}, bf16[192,512]{1,0:T(8,128)(2,1)S(1)}, u32[]{:S(2)}, u32[]{:S(2)}) collective-permute-start(bf16[192,512]{1,0:T(8,128)(2,1)} %get-tuple-element.155), channel_id=1, source_target_pairs={{0,16},{2,18},{4,20},{6,22},{8,24},{10,26},{12,28},{14,30},{16,0},... | collective-permute-start | bytes 589832 | tf_op jit(solution)/shard_map/ppermute | solution.py:664
  7.0 2.5 %collective-permute-start.3 = (bf16[192,512]{1,0:T(8,128)(2,1)}, bf16[192,512]{1,0:T(8,128)(2,1)S(1)}, u32[]{:S(2)}, u32[]{:S(2)}) collective-permute-start(bf16[192,512]{1,0:T(8,128)(2,1)} %get-tuple-element.156.refs_0_), channel_id=1, source_target_pairs={{0,12},{2,14},{4,8},{6,10},{8,4},{10,6},{12,0},{14,2},{16,28},{18,... | collective-permute-start | bytes 589832 | tf_op jit(solution)/shard_map/ppermute | solution.py:664
  10.5 2.0 prepare.1.mine
  12.5 1.5 collective-permute-start
  14.0 3.7 %pack.1 = (bf16[1152,512]{1,0:T(8,128)(2,1)}, bf16[512,512]{1,0:T(8,128)(2,1)}, bf16[384,512]{1,0:T(8,128)(2,1)}) custom-call(s32[10]{0:T(128)} %stack.40.meta, bf16[256,1024]{1,0:T(8,128)(2,1)} %own.2, bf16[256,512]{1,0:T(8,128)(2,1)} %own_out.3, bf16[256,512]{1,0:T(8,128)(2,1)} %own_query.3, bf16[256,512]{1,0:T(8,128)(2,1)} %own_cross.3, ...), custom_call_target="tpu_custom_call" | custom-call | flops 1000 | bytes 1000 | tf_op jit(solution)/shard_map/pack/pallas_call | solution.py:60
  19.1 2.9 %collective-permute-done.1.refs_1_ = bf16[192,512]{1,0:T(8,128)(2,1)} collective-permute-done((bf16[192,512]{1,0:T(8,128)(2,1)}, bf16[192,512]{1,0:T(8,128)(2,1)}, u32[]{:S(2)}, u32[]{:S(2)}) %collective-permute-start.1) | collective-permute-done | bytes 196640 | tf_op jit(solution)/shard_map/ppermute | solution.py:664
  21.9 1.5 collective-permute-start.16
  25.5 1.5 collective-permute-start.5
  27.0 1.7 unpack.1
  28.8 3.1 %collective-permute-done.7.refs_7_ = bf16[192,512]{1,0:T(8,128)(2,1)} collective-permute-done((bf16[192,512]{1,0:T(8,128)(2,1)S(1)}, bf16[192,512]{1,0:T(8,128)(2,1)}, u32[]{:S(2)}, u32[]{:S(2)}) %collective-permute-start.7) | collective-permute-done | bytes 196640 | tf_op jit(solution)/shard_map/ppermute | solution.py:664
  31.9 2.0 collective-permute-done.6.refs_6_
  37.9 12.2 %attend.1 = (bf16[2048,512]{1,0:T(8,128)(2,1)}, bf16[192,2048]{1,0:T(8,128)(2,1)}, bf16[16,64,128]{2,1,0:T(8,128)(2,1)}, f32[64,2048]{1,0:T(8,128)}, f32[8,2048]{1,0:T(8,128)}) custom-call(s32[10]{0:T(128)} %stack.40.meta, f32[1,512]{1,0:T(1,128)} %get-tuple-element.151.step, f32[3,512]{1,0:T(4,128)} %get-tuple-element.152.gains, ...), custom_call_target="tpu_custom_call" | custom-call | flops 1000 | bytes 1000 | tf_op jit(solution)/shard_map/attend/pallas_call | solution.py:60
  51.0 4.4 %all-to-all-start = ((bf16[16,64,128]{2,1,0:T(8,128)(2,1)}), bf16[16,64,128]{2,1,0:T(8,128)(2,1)}, u32[]{:S(2)}, u32[]{:S(2)}) async-start(bf16[16,64,128]{2,1,0:T(8,128)(2,1)} %get-tuple-element.164), calls=%async_computation | async-start | bytes 524288 | tf_op jit(solution)/shard_map/all_to_all | solution.py:774
  55.5 6.3 %encoder_rows.1 = (bf16[2,512,512]{2,1,0:T(8,128)(2,1)}, bf16[2,1024,512]{2,1,0:T(8,128)(2,1)}, bf16[512,1024]{1,0:T(8,128)(2,1)}) custom-call(s32[10]{0:T(128)} %stack.40.meta, bf16[256,1024]{1,0:T(8,128)(2,1)} %own.2, bf16[1152,512]{1,0:T(8,128)(2,1)} %copy-done, bf16[1152,512]{1,0:T(8,128)(2,1)} %collective-permute-done.17.far.far2, ...), custom_call_target="tpu_custom_call" | custom-call | flops 1000 | bytes 1000 | tf_op jit(solution)/shard_map/encoder_rows/pallas_call | solution.py:60
  61.7 3.5 %all-to-all-done = bf16[16,64,128]{2,1,0:T(8,128)(2,1)} async-done(((bf16[16,64,128]{2,1,0:T(8,128)(2,1)}), bf16[16,64,128]{2,1,0:T(8,128)(2,1)}, u32[]{:S(2)}, u32[]{:S(2)}) %all-to-all-start) | async-done | bytes 262176 | tf_op jit(solution)/shard_map/all_to_all | solution.py:774
  66.6 1.6 copy-done.3
  69.1 5.4 %forward.1 = (f32[256,512]{1,0:T(8,128)S(1)}, f32[256,512]{1,0:T(8,128)S(1)}, bf16[256,512]{1,0:T(8,128)(2,1)S(1)}, bf16[2,512,128]{2,1,0:T(8,128)(2,1)S(1)}, bf16[16,128,512]{2,1,0:T(8,128)(2,1)S(1)}) custom-call(s32[10]{0:T(128)S(1)} %copy-done.53, bf16[2,128,512]{2,1,0:T(8,128)(2,1)S(1)} %copy-done.13, f32[2,512]{1,0:T(2,128)S(1)} %copy-done.55, ...), custom_call_target="tpu_custom_call" | custom-call | flops 1000 | bytes 1000 | tf_op jit(solution)/shard_map/forward/pallas_call | solution.py:60
  75.3 2.1 collective-permute-done.19.far3
  77.5 7.5 %feed.1 = (bf16[2,128,512]{2,1,0:T(8,128)(2,1)}, f32[256,512]{1,0:T(8,128)S(1)}, f32[16,512]{1,0:T(8,128)S(1)}, bf16[16,64,512]{2,1,0:T(8,128)(2,1)S(1)}, bf16[1...) custom-call(s32[10]{0:T(128)S(1)} %copy-done.53, ...), custom_call_target="tpu_custom_call" | custom-call | flops 1000 | bytes 1000 | tf_op jit(solution)/shard_map/feed/pallas_call | solution.py:60
  85.6 4.3 %cross_back.1 = (bf16[256,512]{1,0:T(8,128)(2,1)S(1)}, bf16[2,1024,512]{2,1,0:T(8,128)(2,1)S(1)}) custom-call(s32[10]{0:T(128)S(1)} %copy-done.53, f32[256,512]{1,0:T(8,128)S(1)} %get-tuple-element.176.h2g, bf16[256,512]{1,0:T(8,128)(2,1)S(1)} %get-tuple-element.177.q, bf16[16,128,512]{2,1,0:T(8,128)(2,1)S(1)} %get-tuple-element.178.shares, ...), custom_call_target="tpu_custom_call" | custom-call | flops 1000 | bytes 1000 | tf_op jit(solution)/shard_map/cross_back/pallas_call | solution.py:60
  93.7 1.5 collective-permute-start.22
  95.2 3.4 %hidden_back.1 = (f32[256,512]{1,0:T(8,128)S(1)}, bf16[2,512,128]{2,1,0:T(8,128)(2,1)}, f32[16,512]{1,0:T(8,128)S(1)}) custom-call(s32[10]{0:T(128)S(1)} %copy-done.53, f32[256,512]{1,0:T(8,128)S(1)} %get-tuple-element.176.h2g, f32[256,512]{1,0:T(8,128)S(1)} %get-tuple-element.187.hidden1, bf16[256,512]{1,0:T(8,128)(2,1)S(1)} %get-tuple-element.179.dq, ...), custom_call_target="tpu_custom_call" | custom-call | flops 1000 | bytes 1000 | tf_op jit(solution)/shard_map/hidden_back/pallas_call | solution.py:60
  99.4 3.7 %all-to-all-start.1 = ((bf16[16,64,128]{2,1,0:T(8,128)(2,1)}), bf16[16,64,128]{2,1,0:T(8,128)(2,1)S(1)}, u32[]{:S(2)}, u32[]{:S(2)}) async-start(bf16[16,64,128]{2,1,0:T(8,128)(2,1)} %bitcast.10), calls=%async_computation.1 | async-start | bytes 524288 | tf_op jit(solution)/shard_map/all_to_all | solution.py:837
  103.2 7.2 %weights_back.1 = (bf16[8,80,512]{2,1,0:T(8,128)(2,1)}, bf16[8,80,512]{2,1,0:T(8,128)(2,1)}, bf16[8,80,512]{2,1,0:T(8,128)(2,1)}, bf16[8,80,512]{2,1,0:T(8,128)(...) custom-call(s32[10]{0:T(128)} %stack.40.meta, f32[256,512]{1,0:T(8,128)} %copy-done.6, ...), custom_call_target="tpu_custom_call" | custom-call | flops 1000 | bytes 1000 | tf_op jit(solution)/shard_map/weights_back/pallas_call | solution.py:60
  110.4 2.8 %all-to-all-done.1.grads = bf16[16,64,128]{2,1,0:T(8,128)(2,1)S(1)} async-done(((bf16[16,64,128]{2,1,0:T(8,128)(2,1)}), bf16[16,64,128]{2,1,0:T(8,128)(2,1)S(1)}, u32[]{:S(2)}, u32[]{:S(2)}) %all-to-all-start.1) | async-done | bytes 262176 | tf_op jit(solution)/shard_map/all_to_all | solution.py:837
  117.3 6.1 %attend_back_1.1 = (f32[64,2048]{1,0:T(8,128)S(1)}, bf16[128,1024]{1,0:T(8,128)(2,1)S(1)}) custom-call(bf16[192,2048]{1,0:T(8,128)(2,1)S(1)} %copy-done.9, f32[64,2048]{1,0:T(8,128)S(1)} %copy-done.15, f32[8,2048]{1,0:T(8,128)S(1)} %copy-done.39, bf16[16,64,128]{2,1,0:T(8,128)(2,1)S(1)} %all-to-all-done.1.grads), custom_call_target="tpu_custom_call" | custom-call | flops 1000 | bytes 1000 | tf_op jit(solution)/shard_map/attend_back_1/pallas_call | solution.py:60
  123.4 1.6 collective-permute-done.25.refs_3_
  127.9 1.5 collective-permute-start.31
  129.5 8.1 %attend_back_2.1 = (bf16[16,192,128]{2,1,0:T(8,128)(2,1)}, f32[208,256]{1,0:T(8,128)S(1)}, bf16[208,256]{1,0:T(8,128)(2,1)S(1)}) custom-call(s32[10]{0:T(128)S(1)} %copy-done.54, bf16[192,2048]{1,0:T(8,128)(2,1)S(1)} %copy-done.9, f32[64,2048]{1,0:T(8,128)S(1)} %copy-done.15, f32[8,2048]{1,0:T(8,128)S(1)} %copy-done.40, ...), custom_call_target="tpu_custom_call" | custom-call | flops 1000 | bytes 1000 | tf_op jit(solution)/shard_map/attend_back_2/pallas_call | solution.py:60
  140.9 3.6 %all-to-all-start.2 = ((bf16[16,192,128]{2,1,0:T(8,128)(2,1)}), bf16[16,192,128]{2,1,0:T(8,128)(2,1)S(1)}, u32[]{:S(2)}, u32[]{:S(2)}) async-start(bf16[16,192,128]{2,1,0:T(8,128)(2,1)} %get-tuple-element.246), calls=%async_computation.2 | async-start | bytes 1572864 | tf_op jit(solution)/shard_map/all_to_all | solution.py:896
  150.3 1.8 collective-permute-start.32
  152.2 3.9 %collective-permute-done.38.near = bf16[384,512]{1,0:T(8,128)(2,1)S(1)} collective-permute-done((bf16[384,512]{1,0:T(8,128)(2,1)}, bf16[384,512]{1,0:T(8,128)(2,1)S(1)}, u32[]{:S(2)}, u32[]{:S(2)}) %collective-permute-start.38) | collective-permute-done | bytes 393248 | tf_op jit(solution)/shard_map/ppermute | solution.py:668
  157.5 1.7 collective-permute-start.35
  159.2 2.4 %collective-permute-start.36 = (bf16[2,128,512]{2,1,0:T(8,128)(2,1)S(1)}, bf16[2,128,512]{2,1,0:T(8,128)(2,1)S(1)}, u32[]{:S(2)}, u32[]{:S(2)}) collective-permute-start(bf16[2,128,512]{2,1,0:T(8,128)(2,1)S(1)} %get-tuple-element.236.feed), channel_id=1, source_target_pairs={{0,16},{2,18},{4,20},{6,22},{8,24},{10,26},{12,28},{14,30},{16,0},... | collective-permute-start | bytes 786440 | tf_op jit(solution)/shard_map/ppermute | solution.py:664
  161.6 2.4 %collective-permute-done.32.refs_1_ = bf16[4,80,512]{2,1,0:T(8,128)(2,1)S(1)} collective-permute-done((bf16[4,80,512]{2,1,0:T(8,128)(2,1)S(1)}, bf16[4,80,512]{2,1,0:T(8,128)(2,1)S(1)}, u32[]{:S(2)}, u32[]{:S(2)}) %collective-permute-start.32) | collective-permute-done | bytes 327712 | tf_op jit(solution)/shard_map/ppermute | solution.py:664
  165.1 2.5 %collective-permute-start.34 = (bf16[2,80,512]{2,1,0:T(8,128)(2,1)S(1)}, bf16[2,80,512]{2,1,0:T(8,128)(2,1)S(1)}, u32[]{:S(2)}, u32[]{:S(2)}) collective-permute-start(bf16[2,80,512]{2,1,0:T(8,128)(2,1)S(1)} %get-tuple-element.234), channel_id=1, source_target_pairs={{0,8},{2,10},{4,12},{6,14},{8,0},{10,2},{12,4},{14,6},{16,24},{18,... | collective-permute-start | bytes 491528 | tf_op jit(solution)/shard_map/ppermute | solution.py:664
  168.7 2.4 %collective-permute-done.35.refs_3_ = bf16[2,128,512]{2,1,0:T(8,128)(2,1)S(1)} collective-permute-done((bf16[2,128,512]{2,1,0:T(8,128)(2,1)S(1)}, bf16[2,128,512]{2,1,0:T(8,128)(2,1)S(1)}, u32[]{:S(2)}, u32[]{:S(2)}) %collective-permute-start.35) | collective-permute-done | bytes 262176 | tf_op jit(solution)/shard_map/ppermute | solution.py:664
  171.2 6.0 %collective-permute-done.34.refs_1_ = bf16[2,80,512]{2,1,0:T(8,128)(2,1)S(1)} collective-permute-done((bf16[2,80,512]{2,1,0:T(8,128)(2,1)S(1)}, bf16[2,80,512]{2,1,0:T(8,128)(2,1)S(1)}, u32[]{:S(2)}, u32[]{:S(2)}) %collective-permute-start.34) | collective-permute-done | bytes 163872 | tf_op jit(solution)/shard_map/ppermute | solution.py:664
  178.0 3.3 %collective-permute-done.37.heads_got = bf16[1,208,256]{2,1,0:T(8,128)(2,1)S(1)} collective-permute-done((bf16[1,208,256]{2,1,0:T(8,128)(2,1)S(1)}, bf16[1,208,256]{2,1,0:T(8,128)(2,1)S(1)}, u32[]{:S(2)}, u32[]{:S(2)}) %collective-permute-start.37) | collective-permute-done | bytes 106528 | tf_op jit(solution)/shard_map/ppermute | solution.py:664
  184.2 2.0 collective-permute-start.42
  186.4 2.7 %collective-permute-start.40 = (bf16[1,128,512]{2,1,0:T(8,128)(2,1)}, bf16[1,128,512]{2,1,0:T(8,128)(2,1)}, u32[]{:S(2)}, u32[]{:S(2)}) collective-permute-start(bf16[1,128,512]{2,1,0:T(8,128)(2,1)} %get-tuple-element.248), channel_id=1, source_target_pairs={{0,16},{2,18},{4,20},{6,22},{8,24},{10,26},{12,28},{14,30},{16,0},... | collective-permute-start | bytes 393224 | tf_op jit(solution)/shard_map/ppermute | solution.py:664
  190.3 2.9 %start_grad.1 = f32[2,128,512]{2,1,0:T(8,128)} custom-call(s32[10]{0:T(128)S(1)} %copy-done.54, bf16[2,8,192,128]{3,2,1,0:T(8,128)(2,1)S(1)} %bitcast.17, bf16[2,128,512]{2,1,0:T(8,128)(2,1)S(1)} %copy-done.14, f32[2,512]{1,0:T(2,128)S(1)} %copy-done.55, f32[3,512]{1,0:T(4,128)S(1)} %copy-done.36, f32[256,512]{1,0:T(8,128)S(1)} %copy-done.19, ...), custom_call_target="tpu_custom_call" | custom-call | flops 1000 | bytes 1000 | tf_op jit(solution)/shard_map/start_grad/pallas_call | solution.py:60
  193.1 12.3 %collective-permute-done.40.got = bf16[1,128,512]{2,1,0:T(8,128)(2,1)} collective-permute-done((bf16[1,128,512]{2,1,0:T(8,128)(2,1)}, bf16[1,128,512]{2,1,0:T(8,128)(2,1)}, u32[]{:S(2)}, u32[]{:S(2)}) %collective-permute-start.40) | collective-permute-done | bytes 131104 | tf_op jit(solution)/shard_map/ppermute | solution.py:664
  206.1 2.4 %collective-permute-done.42.refs_1_ = bf16[1,368,512]{2,1,0:T(8,128)(2,1)} collective-permute-done((bf16[1,368,512]{2,1,0:T(8,128)(2,1)S(1)}, bf16[1,368,512]{2,1,0:T(8,128)(2,1)}, u32[]{:S(2)}, u32[]{:S(2)}) %collective-permute-start.42) | collective-permute-done | bytes 376864 | tf_op jit(solution)/shard_map/ppermute | solution.py:664
  212.1 2.3 %encoder_back.1 = f32[2,32,512]{2,1,0:T(8,128)} custom-call(bf16[1,128,512]{2,1,0:T(8,128)(2,1)S(1)} %copy-done.52, bf16[1,128,512]{2,1,0:T(8,128)(2,1)} %collective-permute-done.40.got, bf16[512,1024]{1,0:T(8,128)(2,1)S(1)} %copy-done.22), custom_call_target="tpu_custom_call" | custom-call | flops 1000 | bytes 1000 | tf_op jit(solution)/shard_map/encoder_back/pallas_call | solution.py:60
  214.4 4.4 %place.1 = (f32[256,2048]{1,0:T(8,128)}, f32[1024,512]{1,0:T(8,128)}, f32[256,1536]{1,0:T(8,128)}, f32[3,256]{1,0:T(4,128)}, f32[3,256]{1,0:T(4,128)}, /*index=5...) custom-call(s32[10]{0:T(128)S(1)} %copy-done.54, f32[1,512]{1,0:T(1,128)S(1)} %copy-done.58, ...), custom_call_target="tpu_custom_call" | custom-call | flops 1000 | bytes 1000 | tf_op jit(solution)/shard_map/place/pallas_call | solution.py:60
  221.4 2.2 place_cross.1
  (245 shorter events, 49.5 us)
Async XLA Ops:
  3.0 14.7 %collective-permute-start.4 = (bf16[192,512]{1,0:T(8,128)(2,1)}, bf16[192,512]{1,0:T(8,128)(2,1)S(1)}, u32[]{:S(2)}, u32[]{:S(2)}) collective-permute-start(bf16[192,512]{1,0:T(8,128)(2,1)} %get-tuple-element.155), channel_id=1, source_target_pairs={{0,16},{2,18},{4,20},{6,22},{8,24},{10,26},{12,28},{14,30},{16,0},... | collective-permute-start | bytes 589832 | tf_op jit(solution)/shard_map/ppermute | solution.py:664
  7.0 12.0 %collective-permute-start.3 = (bf16[192,512]{1,0:T(8,128)(2,1)}, bf16[192,512]{1,0:T(8,128)(2,1)S(1)}, u32[]{:S(2)}, u32[]{:S(2)}) collective-permute-start(bf16[192,512]{1,0:T(8,128)(2,1)} %get-tuple-element.156.refs_0_), channel_id=1, source_target_pairs={{0,12},{2,14},{4,8},{6,10},{8,4},{10,6},{12,0},{14,2},{16,28},{18,... | collective-permute-start | bytes 589832 | tf_op jit(solution)/shard_map/ppermute | solution.py:664
  9.6 9.5 %collective-permute-start.2 = (bf16[192,512]{1,0:T(8,128)(2,1)}, bf16[192,512]{1,0:T(8,128)(2,1)S(1)}, u32[]{:S(2)}, u32[]{:S(2)}) collective-permute-start(bf16[192,512]{1,0:T(8,128)(2,1)} %get-tuple-element.156.refs_0_), channel_id=1, source_target_pairs={{0,4},{2,6},{4,0},{6,2},{8,12},{10,14},{12,8},{14,10},{16,20},{18,... | collective-permute-start | bytes 589832 | tf_op jit(solution)/shard_map/ppermute | solution.py:664
  10.1 11.9 %collective-permute-start.1 = (bf16[192,512]{1,0:T(8,128)(2,1)}, bf16[192,512]{1,0:T(8,128)(2,1)}, u32[]{:S(2)}, u32[]{:S(2)}) collective-permute-start(bf16[192,512]{1,0:T(8,128)(2,1)} %get-tuple-element.156.refs_0_), channel_id=1, source_target_pairs={{0,8},{2,10},{4,12},{6,14},{8,0},{10,2},{12,4},{14,6},{16,24},{18,... | collective-permute-start | bytes 589832 | tf_op jit(solution)/shard_map/ppermute | solution.py:664
  12.5 5.2 %collective-permute-start = (bf16[256,256]{1,0:T(8,128)(2,1)}, bf16[256,256]{1,0:T(8,128)(2,1)S(1)}, u32[]{:S(2)}, u32[]{:S(2)}) collective-permute-start(bf16[256,256]{1,0:T(8,128)(2,1)} %prepare.1.mine), channel_id=1, source_target_pairs={{0,1},{1,0},{2,3},{3,2},{4,5},{5,4},{6,7},{7,6},{8,9},{9,8},{10,11... | collective-permute-start | bytes 393224 | tf_op jit(solution)/shard_map/ppermute | solution.py:668
  21.9 28.2 %collective-permute-start.16 = (bf16[1152,512]{1,0:T(8,128)(2,1)}, bf16[1152,512]{1,0:T(8,128)(2,1)S(1)}, u32[]{:S(2)}, u32[]{:S(2)}) collective-permute-start(bf16[1152,512]{1,0:T(8,128)(2,1)} %get-tuple-element.165), channel_id=1, source_target_pairs={{0,1},{1,0},{2,3},{3,2},{4,5},{5,4},{6,7},{7,6},{8,9},{9,8},{10,11... | collective-permute-start | bytes 3538952 | tf_op jit(solution)/shard_map/ppermute | solution.py:668
  23.5 8.4 %collective-permute-start.7 = (bf16[192,512]{1,0:T(8,128)(2,1)S(1)}, bf16[192,512]{1,0:T(8,128)(2,1)}, u32[]{:S(2)}, u32[]{:S(2)}) collective-permute-start(bf16[192,512]{1,0:T(8,128)(2,1)S(1)} %collective-permute-done.4.refs_4_), channel_id=1, source_target_pairs={{0,12},{2,14},{4,8},{6,10},{8,4},{10,6},{12,0},{14,2},{16,28},{18,... | collective-permute-start | bytes 589832 | tf_op jit(solution)/shard_map/ppermute | solution.py:664
  25.0 8.9 %collective-permute-start.6 = (bf16[192,512]{1,0:T(8,128)(2,1)S(1)}, bf16[192,512]{1,0:T(8,128)(2,1)}, u32[]{:S(2)}, u32[]{:S(2)}) collective-permute-start(bf16[192,512]{1,0:T(8,128)(2,1)S(1)} %collective-permute-done.4.refs_4_), channel_id=1, source_target_pairs={{0,4},{2,6},{4,0},{6,2},{8,12},{10,14},{12,8},{14,10},{16,20},{18,... | collective-permute-start | bytes 589832 | tf_op jit(solution)/shard_map/ppermute | solution.py:664
  25.5 8.4 %collective-permute-start.5 = (bf16[192,512]{1,0:T(8,128)(2,1)S(1)}, bf16[192,512]{1,0:T(8,128)(2,1)}, u32[]{:S(2)}, u32[]{:S(2)}) collective-permute-start(bf16[192,512]{1,0:T(8,128)(2,1)S(1)} %collective-permute-done.4.refs_4_), channel_id=1, source_target_pairs={{0,8},{2,10},{4,12},{6,14},{8,0},{10,2},{12,4},{14,6},{16,24},{18,... | collective-permute-start | bytes 589832 | tf_op jit(solution)/shard_map/ppermute | solution.py:664
  28.7 5.7 %collective-permute-start.8 = (bf16[192,512]{1,0:T(8,128)(2,1)S(1)}, bf16[192,512]{1,0:T(8,128)(2,1)S(1)}, u32[]{:S(2)}, u32[]{:S(2)}) collective-permute-start(bf16[192,512]{1,0:T(8,128)(2,1)S(1)} %copy-done.61), channel_id=1, source_target_pairs={{0,2},{2,0},{4,6},{6,4},{8,10},{10,8},{12,14},{14,12},{16,18},{18,... | collective-permute-start | bytes 589832 | tf_op jit(solution)/shard_map/ppermute | solution.py:664
  31.9 2.6 %collective-permute-start.9 = (bf16[192,512]{1,0:T(8,128)(2,1)}, bf16[192,512]{1,0:T(8,128)(2,1)S(1)}, u32[]{:S(2)}, u32[]{:S(2)}) collective-permute-start(bf16[192,512]{1,0:T(8,128)(2,1)} %collective-permute-done.1.refs_1_), channel_id=1, source_target_pairs={{0,2},{2,0},{4,6},{6,4},{8,10},{10,8},{12,14},{14,12},{16,18},{18,... | collective-permute-start | bytes 589832 | tf_op jit(solution)/shard_map/ppermute | solution.py:664
  50.2 5.2 %collective-permute-start.17 = (bf16[1152,512]{1,0:T(8,128)(2,1)S(1)}, bf16[1152,512]{1,0:T(8,128)(2,1)}, u32[]{:S(2)}, u32[]{:S(2)}) collective-permute-start(bf16[1152,512]{1,0:T(8,128)(2,1)S(1)} %collective-permute-done.16.near.near2), channel_id=1, source_target_pairs={{0,2},{2,0},{4,6},{6,4},{8,10},{10,8},{12,14},{14,12},{16,18},{18,... | collective-permute-start | bytes 3538952 | tf_op jit(solution)/shard_map/ppermute | solution.py:664
  50.5 24.8 %collective-permute-start.18 = (bf16[512,512]{1,0:T(8,128)(2,1)}, bf16[512,512]{1,0:T(8,128)(2,1)}, u32[]{:S(2)}, u32[]{:S(2)}) collective-permute-start(bf16[512,512]{1,0:T(8,128)(2,1)} %get-tuple-element.172), channel_id=1, source_target_pairs={{0,1},{1,0},{2,3},{3,2},{4,5},{5,4},{6,7},{7,6},{8,9},{9,8},{10,11... | collective-permute-start | bytes 1572872 | tf_op jit(solution)/shard_map/ppermute | solution.py:668
  51.0 14.2 %all-to-all-start = ((bf16[16,64,128]{2,1,0:T(8,128)(2,1)}), bf16[16,64,128]{2,1,0:T(8,128)(2,1)}, u32[]{:S(2)}, u32[]{:S(2)}) async-start(bf16[16,64,128]{2,1,0:T(8,128)(2,1)} %get-tuple-element.164), calls=%async_computation | async-start | bytes 524288 | tf_op jit(solution)/shard_map/all_to_all | solution.py:774
  85.0 6.3 %collective-permute-start.20 = (bf16[16,64,512]{2,1,0:T(8,128)(2,1)S(1)}, bf16[16,64,512]{2,1,0:T(8,128)(2,1)S(1)}, u32[]{:S(2)}, u32[]{:S(2)}) collective-permute-start(bf16[16,64,512]{2,1,0:T(8,128)(2,1)S(1)} %get-tuple-element.181), channel_id=1, source_target_pairs={{0,2},{2,0},{4,6},{6,4},{8,10},{10,8},{12,14},{14,12},{16,18},{18,... | collective-permute-start | bytes 3145736 | tf_op jit(solution)/shard_map/ppermute | solution.py:664
  85.2 6.1 %collective-permute-start.21 = (bf16[16,64,512]{2,1,0:T(8,128)(2,1)S(1)}, bf16[16,64,512]{2,1,0:T(8,128)(2,1)S(1)}, u32[]{:S(2)}, u32[]{:S(2)}) collective-permute-start(bf16[16,64,512]{2,1,0:T(8,128)(2,1)S(1)} %get-tuple-element.183), channel_id=1, source_target_pairs={{0,2},{2,0},{4,6},{6,4},{8,10},{10,8},{12,14},{14,12},{16,18},{18,... | collective-permute-start | bytes 3145736 | tf_op jit(solution)/shard_map/ppermute | solution.py:664
  93.5 19.6 %collective-permute-start.23 = (bf16[8,64,512]{2,1,0:T(8,128)(2,1)}, bf16[8,64,512]{2,1,0:T(8,128)(2,1)}, u32[]{:S(2)}, u32[]{:S(2)}) collective-permute-start(bf16[8,64,512]{2,1,0:T(8,128)(2,1)} %get-tuple-element.197), channel_id=1, source_target_pairs={{0,4},{2,6},{4,0},{6,2},{8,12},{10,14},{12,8},{14,10},{16,20},{18,... | collective-permute-start | bytes 1572872 | tf_op jit(solution)/shard_map/ppermute | solution.py:664
  93.7 19.5 %collective-permute-start.22 = (bf16[8,64,512]{2,1,0:T(8,128)(2,1)}, bf16[8,64,512]{2,1,0:T(8,128)(2,1)}, u32[]{:S(2)}, u32[]{:S(2)}) collective-permute-start(bf16[8,64,512]{2,1,0:T(8,128)(2,1)} %get-tuple-element.185), channel_id=1, source_target_pairs={{0,1},{1,0},{2,3},{3,2},{4,5},{5,4},{6,7},{7,6},{8,9},{9,8},{10,11... | collective-permute-start | bytes 1572872 | tf_op jit(solution)/shard_map/ppermute | solution.py:668
  99.4 13.8 %all-to-all-start.1 = ((bf16[16,64,128]{2,1,0:T(8,128)(2,1)}), bf16[16,64,128]{2,1,0:T(8,128)(2,1)S(1)}, u32[]{:S(2)}, u32[]{:S(2)}) async-start(bf16[16,64,128]{2,1,0:T(8,128)(2,1)} %bitcast.10), calls=%async_computation.1 | async-start | bytes 524288 | tf_op jit(solution)/shard_map/all_to_all | solution.py:837
  113.2 12.1 %collective-permute-start.28 = (bf16[8,128,512]{2,1,0:T(8,128)(2,1)}, bf16[8,128,512]{2,1,0:T(8,128)(2,1)S(1)}, u32[]{:S(2)}, u32[]{:S(2)}) collective-permute-start(bf16[8,128,512]{2,1,0:T(8,128)(2,1)} %get-tuple-element.215), channel_id=1, source_target_pairs={{0,2},{2,0},{4,6},{6,4},{8,10},{10,8},{12,14},{14,12},{16,18},{18,... | collective-permute-start | bytes 3145736 | tf_op jit(solution)/shard_map/ppermute | solution.py:664
  113.3 12.0 %collective-permute-start.26 = (bf16[8,80,512]{2,1,0:T(8,128)(2,1)}, bf16[8,80,512]{2,1,0:T(8,128)(2,1)S(1)}, u32[]{:S(2)}, u32[]{:S(2)}) collective-permute-start(bf16[8,80,512]{2,1,0:T(8,128)(2,1)} %get-tuple-element.209), channel_id=1, source_target_pairs={{0,2},{2,0},{4,6},{6,4},{8,10},{10,8},{12,14},{14,12},{16,18},{18,... | collective-permute-start | bytes 1966088 | tf_op jit(solution)/shard_map/ppermute | solution.py:664
  113.8 11.5 %collective-permute-start.27 = (bf16[8,80,512]{2,1,0:T(8,128)(2,1)}, bf16[8,80,512]{2,1,0:T(8,128)(2,1)S(1)}, u32[]{:S(2)}, u32[]{:S(2)}) collective-permute-start(bf16[8,80,512]{2,1,0:T(8,128)(2,1)} %get-tuple-element.212), channel_id=1, source_target_pairs={{0,2},{2,0},{4,6},{6,4},{8,10},{10,8},{12,14},{14,12},{16,18},{18,... | collective-permute-start | bytes 1966088 | tf_op jit(solution)/shard_map/ppermute | solution.py:664
  116.3 8.7 %collective-permute-start.25 = (bf16[4,64,512]{2,1,0:T(8,128)(2,1)S(1)}, bf16[4,64,512]{2,1,0:T(8,128)(2,1)S(1)}, u32[]{:S(2)}, u32[]{:S(2)}) collective-permute-start(bf16[4,64,512]{2,1,0:T(8,128)(2,1)S(1)} %get-tuple-element.207), channel_id=1, source_target_pairs={{0,1},{1,0},{2,3},{3,2},{4,5},{5,4},{6,7},{7,6},{8,9},{9,8},{10,11... | collective-permute-start | bytes 786440 | tf_op jit(solution)/shard_map/ppermute | solution.py:668
  116.9 8.4 %collective-permute-start.24 = (bf16[4,64,512]{2,1,0:T(8,128)(2,1)S(1)}, bf16[4,64,512]{2,1,0:T(8,128)(2,1)S(1)}, u32[]{:S(2)}, u32[]{:S(2)}) collective-permute-start(bf16[4,64,512]{2,1,0:T(8,128)(2,1)S(1)} %get-tuple-element.200), channel_id=1, source_target_pairs={{0,4},{2,6},{4,0},{6,2},{8,12},{10,14},{12,8},{14,10},{16,20},{18,... | collective-permute-start | bytes 786440 | tf_op jit(solution)/shard_map/ppermute | solution.py:664
  126.8 13.3 %collective-permute-start.30 = (bf16[4,128,512]{2,1,0:T(8,128)(2,1)S(1)}, bf16[4,128,512]{2,1,0:T(8,128)(2,1)S(1)}, u32[]{:S(2)}, u32[]{:S(2)}) collective-permute-start(bf16[4,128,512]{2,1,0:T(8,128)(2,1)S(1)} %get-tuple-element.223), channel_id=1, source_target_pairs={{0,4},{2,6},{4,0},{6,2},{8,12},{10,14},{12,8},{14,10},{16,20},{18,... | collective-permute-start | bytes 1572872 | tf_op jit(solution)/shard_map/ppermute | solution.py:664
  127.1 11.2 %collective-permute-start.29 = (bf16[2,128,512]{2,1,0:T(8,128)(2,1)S(1)}, bf16[2,128,512]{2,1,0:T(8,128)(2,1)S(1)}, u32[]{:S(2)}, u32[]{:S(2)}) collective-permute-start(bf16[2,128,512]{2,1,0:T(8,128)(2,1)S(1)} %get-tuple-element.217), channel_id=1, source_target_pairs={{0,8},{2,10},{4,12},{6,14},{8,0},{10,2},{12,4},{14,6},{16,24},{18,... | collective-permute-start | bytes 786440 | tf_op jit(solution)/shard_map/ppermute | solution.py:664
  127.9 18.1 %collective-permute-start.31 = (bf16[8,80,512]{2,1,0:T(8,128)(2,1)}, bf16[8,80,512]{2,1,0:T(8,128)(2,1)S(1)}, u32[]{:S(2)}, u32[]{:S(2)}) collective-permute-start(bf16[8,80,512]{2,1,0:T(8,128)(2,1)} %get-tuple-element.228), channel_id=1, source_target_pairs={{0,1},{1,0},{2,3},{3,2},{4,5},{5,4},{6,7},{7,6},{8,9},{9,8},{10,11... | collective-permute-start | bytes 1966088 | tf_op jit(solution)/shard_map/ppermute | solution.py:668
  140.9 48.3 %all-to-all-start.2 = ((bf16[16,192,128]{2,1,0:T(8,128)(2,1)}), bf16[16,192,128]{2,1,0:T(8,128)(2,1)S(1)}, u32[]{:S(2)}, u32[]{:S(2)}) async-start(bf16[16,192,128]{2,1,0:T(8,128)(2,1)} %get-tuple-element.246), calls=%async_computation.2 | async-start | bytes 1572864 | tf_op jit(solution)/shard_map/all_to_all | solution.py:896
  144.5 11.5 %collective-permute-start.38 = (bf16[384,512]{1,0:T(8,128)(2,1)}, bf16[384,512]{1,0:T(8,128)(2,1)S(1)}, u32[]{:S(2)}, u32[]{:S(2)}) collective-permute-start(bf16[384,512]{1,0:T(8,128)(2,1)} %get-tuple-element.239), channel_id=1, source_target_pairs={{0,1},{1,0},{2,3},{3,2},{4,5},{5,4},{6,7},{7,6},{8,9},{9,8},{10,11... | collective-permute-start | bytes 1179656 | tf_op jit(solution)/shard_map/ppermute | solution.py:668
  150.3 13.7 %collective-permute-start.32 = (bf16[4,80,512]{2,1,0:T(8,128)(2,1)S(1)}, bf16[4,80,512]{2,1,0:T(8,128)(2,1)S(1)}, u32[]{:S(2)}, u32[]{:S(2)}) collective-permute-start(bf16[4,80,512]{2,1,0:T(8,128)(2,1)S(1)} %get-tuple-element.230), channel_id=1, source_target_pairs={{0,4},{2,6},{4,0},{6,2},{8,12},{10,14},{12,8},{14,10},{16,20},{18,... | collective-permute-start | bytes 983048 | tf_op jit(solution)/shard_map/ppermute | solution.py:664
  156.0 25.4 %collective-permute-start.39 = (bf16[384,512]{1,0:T(8,128)(2,1)S(1)}, bf16[384,512]{1,0:T(8,128)(2,1)S(1)}, u32[]{:S(2)}, u32[]{:S(2)}) collective-permute-start(bf16[384,512]{1,0:T(8,128)(2,1)S(1)} %collective-permute-done.38.near), channel_id=1, source_target_pairs={{0,2},{2,0},{4,6},{6,4},{8,10},{10,8},{12,14},{14,12},{16,18},{18,... | collective-permute-start | bytes 1179656 | tf_op jit(solution)/shard_map/ppermute | solution.py:664
  156.0 5.6 %collective-permute-start.33 = (bf16[208,256]{1,0:T(8,128)(2,1)S(1)}, bf16[208,256]{1,0:T(8,128)(2,1)S(1)}, u32[]{:S(2)}, u32[]{:S(2)}) collective-permute-start(bf16[208,256]{1,0:T(8,128)(2,1)S(1)} %copy-done.60), channel_id=1, source_target_pairs={{0,1},{1,0},{2,3},{3,2},{4,5},{5,4},{6,7},{7,6},{8,9},{9,8},{10,11... | collective-permute-start | bytes 319496 | tf_op jit(solution)/shard_map/ppermute | solution.py:668
  157.5 13.6 %collective-permute-start.35 = (bf16[2,128,512]{2,1,0:T(8,128)(2,1)S(1)}, bf16[2,128,512]{2,1,0:T(8,128)(2,1)S(1)}, u32[]{:S(2)}, u32[]{:S(2)}) collective-permute-start(bf16[2,128,512]{2,1,0:T(8,128)(2,1)S(1)} %get-tuple-element.235), channel_id=1, source_target_pairs={{0,8},{2,10},{4,12},{6,14},{8,0},{10,2},{12,4},{14,6},{16,24},{18,... | collective-permute-start | bytes 786440 | tf_op jit(solution)/shard_map/ppermute | solution.py:664
  159.2 18.8 %collective-permute-start.36 = (bf16[2,128,512]{2,1,0:T(8,128)(2,1)S(1)}, bf16[2,128,512]{2,1,0:T(8,128)(2,1)S(1)}, u32[]{:S(2)}, u32[]{:S(2)}) collective-permute-start(bf16[2,128,512]{2,1,0:T(8,128)(2,1)S(1)} %get-tuple-element.236.feed), channel_id=1, source_target_pairs={{0,16},{2,18},{4,20},{6,22},{8,24},{10,26},{12,28},{14,30},{16,0},... | collective-permute-start | bytes 786440 | tf_op jit(solution)/shard_map/ppermute | solution.py:664
  165.1 12.0 %collective-permute-start.34 = (bf16[2,80,512]{2,1,0:T(8,128)(2,1)S(1)}, bf16[2,80,512]{2,1,0:T(8,128)(2,1)S(1)}, u32[]{:S(2)}, u32[]{:S(2)}) collective-permute-start(bf16[2,80,512]{2,1,0:T(8,128)(2,1)S(1)} %get-tuple-element.234), channel_id=1, source_target_pairs={{0,8},{2,10},{4,12},{6,14},{8,0},{10,2},{12,4},{14,6},{16,24},{18,... | collective-permute-start | bytes 491528 | tf_op jit(solution)/shard_map/ppermute | solution.py:664
  167.6 13.7 %collective-permute-start.37 = (bf16[1,208,256]{2,1,0:T(8,128)(2,1)S(1)}, bf16[1,208,256]{2,1,0:T(8,128)(2,1)S(1)}, u32[]{:S(2)}, u32[]{:S(2)}) collective-permute-start(bf16[1,208,256]{2,1,0:T(8,128)(2,1)S(1)} %get-tuple-element.237.heads), channel_id=1, source_target_pairs={{0,16},{2,18},{4,20},{6,22},{8,24},{10,26},{12,28},{14,30},{16,0},... | collective-permute-start | bytes 319496 | tf_op jit(solution)/shard_map/ppermute | solution.py:664
  182.7 22.8 %collective-permute-start.44 = (bf16[1,368,512]{2,1,0:T(8,128)(2,1)S(1)}, bf16[1,368,512]{2,1,0:T(8,128)(2,1)}, u32[]{:S(2)}, u32[]{:S(2)}) collective-permute-start(bf16[1,368,512]{2,1,0:T(8,128)(2,1)S(1)} %reduce_6.1.refs_0_), channel_id=1, source_target_pairs={{0,12},{2,14},{4,8},{6,10},{8,4},{10,6},{12,0},{14,2},{16,28},{18,... | collective-permute-start | bytes 1130504 | tf_op jit(solution)/shard_map/ppermute | solution.py:664
  182.7 23.3 %collective-permute-start.43 = (bf16[1,368,512]{2,1,0:T(8,128)(2,1)S(1)}, bf16[1,368,512]{2,1,0:T(8,128)(2,1)}, u32[]{:S(2)}, u32[]{:S(2)}) collective-permute-start(bf16[1,368,512]{2,1,0:T(8,128)(2,1)S(1)} %reduce_6.1.refs_0_), channel_id=1, source_target_pairs={{0,4},{2,6},{4,0},{6,2},{8,12},{10,14},{12,8},{14,10},{16,20},{18,... | collective-permute-start | bytes 1130504 | tf_op jit(solution)/shard_map/ppermute | solution.py:664
  184.2 24.3 %collective-permute-start.42 = (bf16[1,368,512]{2,1,0:T(8,128)(2,1)S(1)}, bf16[1,368,512]{2,1,0:T(8,128)(2,1)}, u32[]{:S(2)}, u32[]{:S(2)}) collective-permute-start(bf16[1,368,512]{2,1,0:T(8,128)(2,1)S(1)} %reduce_6.1.refs_0_), channel_id=1, source_target_pairs={{0,8},{2,10},{4,12},{6,14},{8,0},{10,2},{12,4},{14,6},{16,24},{18,... | collective-permute-start | bytes 1130504 | tf_op jit(solution)/shard_map/ppermute | solution.py:664
  186.2 19.2 %collective-permute-start.41 = (bf16[2,80,512]{2,1,0:T(8,128)(2,1)S(1)}, bf16[2,80,512]{2,1,0:T(8,128)(2,1)S(1)}, u32[]{:S(2)}, u32[]{:S(2)}) collective-permute-start(bf16[2,80,512]{2,1,0:T(8,128)(2,1)S(1)} %get-tuple-element.249.mine), channel_id=1, source_target_pairs={{0,16},{2,18},{4,20},{6,22},{8,24},{10,26},{12,28},{14,30},{16,0},... | collective-permute-start | bytes 491528 | tf_op jit(solution)/shard_map/ppermute | solution.py:664
  186.4 19.0 %collective-permute-start.40 = (bf16[1,128,512]{2,1,0:T(8,128)(2,1)}, bf16[1,128,512]{2,1,0:T(8,128)(2,1)}, u32[]{:S(2)}, u32[]{:S(2)}) collective-permute-start(bf16[1,128,512]{2,1,0:T(8,128)(2,1)} %get-tuple-element.248), channel_id=1, source_target_pairs={{0,16},{2,18},{4,20},{6,22},{8,24},{10,26},{12,28},{14,30},{16,0},... | collective-permute-start | bytes 393224 | tf_op jit(solution)/shard_map/ppermute | solution.py:664
  205.4 4.4 %collective-permute-start.45 = (bf16[1,368,512]{2,1,0:T(8,128)(2,1)S(1)}, bf16[1,368,512]{2,1,0:T(8,128)(2,1)S(1)}, u32[]{:S(2)}, u32[]{:S(2)}) collective-permute-start(bf16[1,368,512]{2,1,0:T(8,128)(2,1)S(1)} %reduce_6.1.refs_0_), channel_id=1, source_target_pairs={{0,2},{2,0},{4,6},{6,4},{8,10},{10,8},{12,14},{14,12},{16,18},{18,... | collective-permute-start | bytes 1130504 | tf_op jit(solution)/shard_map/ppermute | solution.py:664
  205.5 5.1 %collective-permute-start.48 = (bf16[1,368,512]{2,1,0:T(8,128)(2,1)}, bf16[1,368,512]{2,1,0:T(8,128)(2,1)S(1)}, u32[]{:S(2)}, u32[]{:S(2)}) collective-permute-start(bf16[1,368,512]{2,1,0:T(8,128)(2,1)} %collective-permute-done.44.refs_3_), channel_id=1, source_target_pairs={{0,2},{2,0},{4,6},{6,4},{8,10},{10,8},{12,14},{14,12},{16,18},{18,... | collective-permute-start | bytes 1130504 | tf_op jit(solution)/shard_map/ppermute | solution.py:664
  206.0 8.3 %collective-permute-start.47 = (bf16[1,368,512]{2,1,0:T(8,128)(2,1)}, bf16[1,368,512]{2,1,0:T(8,128)(2,1)S(1)}, u32[]{:S(2)}, u32[]{:S(2)}) collective-permute-start(bf16[1,368,512]{2,1,0:T(8,128)(2,1)} %collective-permute-done.43.refs_2_), channel_id=1, source_target_pairs={{0,2},{2,0},{4,6},{6,4},{8,10},{10,8},{12,14},{14,12},{16,18},{18,... | collective-permute-start | bytes 1130504 | tf_op jit(solution)/shard_map/ppermute | solution.py:664
  208.6 5.8 %collective-permute-start.46 = (bf16[1,368,512]{2,1,0:T(8,128)(2,1)}, bf16[1,368,512]{2,1,0:T(8,128)(2,1)S(1)}, u32[]{:S(2)}, u32[]{:S(2)}) collective-permute-start(bf16[1,368,512]{2,1,0:T(8,128)(2,1)} %collective-permute-done.42.refs_1_), channel_id=1, source_target_pairs={{0,2},{2,0},{4,6},{6,4},{8,10},{10,8},{12,14},{14,12},{16,18},{18,... | collective-permute-start | bytes 1130504 | tf_op jit(solution)/shard_map/ppermute | solution.py:664
  208.6 10.2 %collective-permute-start.51 = (bf16[2,80,512]{2,1,0:T(8,128)(2,1)S(1)}, bf16[2,80,512]{2,1,0:T(8,128)(2,1)S(1)}, u32[]{:S(2)}, u32[]{:S(2)}) collective-permute-start(bf16[2,80,512]{2,1,0:T(8,128)(2,1)S(1)} %reduce_8.1.refs_0_), channel_id=1, source_target_pairs={{0,12},{2,14},{4,8},{6,10},{8,4},{10,6},{12,0},{14,2},{16,28},{18,... | collective-permute-start | bytes 491528 | tf_op jit(solution)/shard_map/ppermute | solution.py:664
  209.9 9.4 %collective-permute-start.50 = (bf16[2,80,512]{2,1,0:T(8,128)(2,1)S(1)}, bf16[2,80,512]{2,1,0:T(8,128)(2,1)S(1)}, u32[]{:S(2)}, u32[]{:S(2)}) collective-permute-start(bf16[2,80,512]{2,1,0:T(8,128)(2,1)S(1)} %reduce_8.1.refs_0_), channel_id=1, source_target_pairs={{0,4},{2,6},{4,0},{6,2},{8,12},{10,14},{12,8},{14,10},{16,20},{18,... | collective-permute-start | bytes 491528 | tf_op jit(solution)/shard_map/ppermute | solution.py:664
  210.7 8.6 %collective-permute-start.49 = (bf16[2,80,512]{2,1,0:T(8,128)(2,1)S(1)}, bf16[2,80,512]{2,1,0:T(8,128)(2,1)S(1)}, u32[]{:S(2)}, u32[]{:S(2)}) collective-permute-start(bf16[2,80,512]{2,1,0:T(8,128)(2,1)S(1)} %reduce_8.1.refs_0_), channel_id=1, source_target_pairs={{0,8},{2,10},{4,12},{6,14},{8,0},{10,2},{12,4},{14,6},{16,24},{18,... | collective-permute-start | bytes 491528 | tf_op jit(solution)/shard_map/ppermute | solution.py:664
  (85 other events, 644.7 us)
